TPU v7x, 32 devices: a whole 2x2x4 slice. The times are simulated.
32 devices in a mesh: grp: 2 (over x), fa: 16 (over z, y, core).
Axes of the slice: x: 2, y: 2, z: 4, core: 2. Of those that a mesh axis runs over, the one named last changes fastest.
Arguments:
- hidden_f: bfloat16 [4096, 1024], P(('grp', 'fa')), parts along dimension 0, may hold values from -6 to 6
- hidden_t: bfloat16 [4096, 1024], P(('grp', 'fa')), parts along dimension 0, may hold values from -6 to 6
- hidden_b: bfloat16 [4096, 256], P(('grp', 'fa')), parts along dimension 0, may hold values from -6 to 6
- w_f: bfloat16 [1024, 256], replicated, may hold values from -0.1875 to 0.1875
- w_t: bfloat16 [1024, 256], replicated, may hold values from -0.1875 to 0.1875
- w_b: bfloat16 [256, 256], replicated, may hold values from -0.375 to 0.375
- latents: bfloat16 [1024, 256], P('grp'), parts along dimension 0, may hold values from -5 to 5
- latent_ids: int32 [4096], P(('grp', 'fa')), parts along dimension 0, may hold values from 0 to 511
- positives: int32 [4096], P(('grp', 'fa')), parts along dimension 0, may hold values from 0 to 2047, each once
Outputs:
- grad_wf: float32 [2048, 256], P('grp'), parts along dimension 0
- grad_wb: float32 [512, 256], P('grp'), parts along dimension 0
- loss: float32 [2], P('grp'), parts along dimension 0
There are 2 independent parts, one for each index of `grp`. A program takes and returns all parts, laid end to end along the dimension named above; an argument that names none is the same for every part. Nothing has to cross between parts.
Inputs may be any that keep to these rules, and one draw needn't show every extreme that they name: `positives`: each row index of 0 to 2047 appears exactly once.
All inputs are finite; a program needn't handle non-finite values.
Results may differ from a plain program's by a relative error of at most 0.0039.
Values may be sent and summed in bfloat16 or wider, within the bound.
No kernel may reach another device: no remote copies, remote signals or barrier semaphores. Data moves between devices by JAX's collectives and lax.ppermute only.
A program may use at most 128 MiB of HBM per device.

v0:
```python
import math

import jax
import jax.numpy as jnp
from jax import lax
from jax.sharding import PartitionSpec as P

GAMMA = 0.98
LAMBDA = 1.0
EPS = 1e-06


def contract_last(left, right):
    return lax.dot_general(
        left, right, (((1,), (1,)), ((), ())), preferred_element_type=jnp.float32
    )


def contract_first(left, right):
    return lax.dot_general(
        left, right, (((0,), (0,)), ((), ())), preferred_element_type=jnp.float32
    )


def body(hidden_f, hidden_t, hidden_b, w_f, w_t, w_b, latents, latent_ids, positives):
    rows = hidden_f.shape[0]
    width = w_f.shape[1]
    total = lax.axis_size("fa") * rows
    rowbase = lax.axis_index("fa") * rows
    pairs = float(total * (total - 1))
    onehot = (latent_ids[:, None] == jnp.arange(latents.shape[0], dtype=jnp.int32)[None, :]).astype(
        latents.dtype
    )
    zrows = jnp.dot(onehot, latents, preferred_element_type=jnp.float32)
    feat = (jnp.dot(hidden_f, w_f, preferred_element_type=jnp.float32) + zrows).astype(jnp.bfloat16)
    feat_t = (jnp.dot(hidden_t, w_t, preferred_element_type=jnp.float32) + zrows).astype(
        jnp.bfloat16
    )
    raw = jnp.dot(hidden_b, w_b, preferred_element_type=jnp.float32)
    scale_r = lax.rsqrt(jnp.mean(raw * raw, axis=-1, keepdims=True) + EPS)
    back = (raw * scale_r).astype(jnp.bfloat16)
    own_ids = rowbase + jnp.arange(rows, dtype=jnp.int32)
    start_acc = (
        jnp.zeros((rows, width), jnp.float32),
        jnp.zeros((rows, width), jnp.float32),
        jnp.zeros((), jnp.float32),
    )
    start_acc = start_acc + (jnp.zeros((rows, total), jnp.bfloat16),)
    piece = lax.all_gather(back, "fa", axis=0, tiled=True)
    count = piece.shape[0]
    sub = math.gcd(count, 2048)

    def inner(index, acc):
        offset = index * sub
        cols = lax.dynamic_slice_in_dim(piece, offset, sub, 0)
        col_ids = offset + jnp.arange(sub, dtype=jnp.int32)
        score = contract_last(feat, cols)
        score_t = contract_last(feat_t, cols)
        match = positives[:, None] == col_ids[None, :]
        offdiag = jnp.where(match, 0.0, score - GAMMA * score_t)
        weights = (offdiag / pairs - jnp.where(match, 1.0 / total, 0.0)).astype(jnp.bfloat16)
        cov = contract_last(back, cols)
        same = own_ids[:, None] == col_ids[None, :]
        cov_off = jnp.where(same, 0.0, cov)
        cov_w = (cov_off * (2.0 * LAMBDA / pairs)).astype(jnp.bfloat16)
        part = (
            jnp.sum(offdiag * offdiag) / (2.0 * pairs)
            - jnp.sum(jnp.where(match, score, 0.0)) / total
        )
        part = part + LAMBDA * (
            jnp.sum(cov_off * cov_off) / (2.0 * pairs) - jnp.sum(jnp.where(same, cov, 0.0)) / total
        )
        grad_f = acc[0] + jnp.dot(weights, cols, preferred_element_type=jnp.float32)
        ortho = acc[1] + jnp.dot(cov_w, cols, preferred_element_type=jnp.float32)
        tiles = lax.dynamic_update_slice_in_dim(acc[3], weights, offset, 1)
        return (grad_f, ortho, acc[2] + part, tiles)

    result = lax.fori_loop(0, count // sub, inner, start_acc)
    grad_f = result[0]
    ortho = result[1]
    loss_part = result[2]
    tiles = result[3]
    cross = lax.psum_scatter(contract_first(tiles, feat), "fa", scatter_dimension=0, tiled=True)
    grad_b = cross + ortho - 2.0 * LAMBDA / total * back.astype(jnp.float32)
    grad_u = (
        scale_r * grad_b - scale_r**3 / width * jnp.sum(grad_b * raw, axis=-1, keepdims=True) * raw
    )
    local_wf = contract_first(hidden_f, grad_f.astype(jnp.bfloat16))
    local_wb = contract_first(hidden_b, grad_u.astype(jnp.bfloat16))
    summed_wf, summed_wb, summed_loss = lax.psum((local_wf, local_wb, loss_part), "fa")
    factor_f = math.sqrt(hidden_f.shape[1])
    factor_b = math.sqrt(hidden_b.shape[1])
    return (summed_wf * factor_f, summed_wb * factor_b, (summed_loss / width).reshape(1))


def solution(mesh):
    placed = (
        P(("grp", "fa"), None),
        P(("grp", "fa"), None),
        P(("grp", "fa"), None),
        P(),
        P(),
        P(),
        P("grp", None),
        P(("grp", "fa")),
        P(("grp", "fa")),
    )
    return jax.shard_map(
        body,
        mesh=mesh,
        in_specs=placed,
        out_specs=(P("grp", None), P("grp", None), P("grp")),
        check_vma=False,
    )
```

profile of v0, /device:TPU:0, one launch (start us, length us, event | category | flops | bytes accessed | tf_op | source)
XLA Modules:
  0.0 228.7 jit_solution(6106895322144238327)
XLA Ops:
  7.2 0.0 copy-start
  7.2 0.0 copy-start.7
  7.2 0.0 copy-start.4
  7.2 0.0 all-gather.2.cloned.1.call-start
  7.2 1.3 multiply_reduce_fusion.3
  8.5 0.7 multiply_convert_fusion.2
  9.2 0.0 all-gather.2.cloned.1.call-update
  9.3 0.0 reduce-scatter.2.cloned.1.call-start
  9.3 1.2 fusion.9
  10.5 1.4 fusion.3
  11.9 39.6 %all-gather.2.cloned.1.call-done = bf16[2048,256]{1,0:T(8,128)(2,1)} async-done(((bf16[128,256]{1,0:T(8,128)(2,1)}), bf16[2048,256]{1,0:T(8,128)(2,1)}) %all-gather.2.cloned.1.call-update) | async-done | bytes 1048592 | tf_op jit(solution)/shard_map/all_gather | solution.py:49
  51.4 0.0 copy-start.1
  51.5 3.4 %select_reduce_fusion.1 = (f32[]{:T(128)}, f32[128,2048]{1,0:T(8,128)}) fusion(s32[128]{0:T(128)} %param.17, bf16[128,256]{1,0:T(8,128)(2,1)S(1)} %fusion.3, bf16[2048,256]{1,0:T(8,128)(2,1)} %all-gather.2.cloned.1.call-done), kind=kOutput, calls=%fused_computation.14 | convolution fusion | flops 135004160 | bytes 2163204 | tf_op jit(solution)/shard_map/while/body/eval_jaxpr/dot_general | solution.py:14
  54.8 0.0 copy-done
  54.8 0.0 copy-done.7
  54.8 0.0 copy-done.4
  54.8 0.0 copy-done.1
  54.8 2.6 %multiply_reduce_fusion.1 = (f32[]{:T(128)}, f32[128,2048]{1,0:T(8,128)S(1)}) fusion(f32[128,2048]{1,0:T(8,128)} %get-tuple-element.53, bf16[2048,256]{1,0:T(8,128)(2,1)S(1)} %copy-done.1, f32[128,256]{1,0:T(8,128)S(1)} %fusion.9, bf16[128,1024]{1,0:T(8,128)(2,1)S(1)} %copy-done.4, bf16[1024,256]{1,0:T(8,128)(2,1)S(1)} %copy-done, s32[128]{0:T(128)S(1)} %copy-done.7), kind=kOutput, calls=%fused_computation.15 | convolution fusion | flops 202964992 | bytes 4063748 | tf_op jit(solution)/shard_map/while/body/eval_jaxpr/dot_general | solution.py:14
  57.4 0.0 copy-start.3
  57.4 1.9 fusion.17
  59.3 0.0 copy-start.2
  59.3 0.0 reduce-scatter.2.cloned.1.call-update
  59.4 0.0 all-reduce.3.cloned.1.call-start
  59.4 0.0 copy-done.3
  59.4 2.1 select_reduce_fusion
  61.6 0.0 copy-done.2
  61.6 1.9 convolution_bitcast_fusion
  63.5 0.0 copy-start.5
  63.5 56.6 %reduce-scatter.2.cloned.1.call-done = f32[128,256]{1,0:T(8,128)} async-done(((f32[2048,256]{1,0:T(8,128)}), f32[128,256]{1,0:T(8,128)}) %reduce-scatter.2.cloned.1.call-update) | async-done | bytes 131088 | tf_op jit(solution)/shard_map/reduce_scatter | solution.py:83
  120.1 1.7 multiply_reduce_fusion.2
  121.7 0.0 copy-done.5
  121.7 1.0 convolution_bitcast_fusion.1
  122.7 0.0 all-reduce.3.cloned.1.call-update
  125.2 30.2 %psum.23 = f32[]{:T(128)} all-reduce(f32[]{:T(128)S(6)} %add.69), channel_id=1, replica_groups=mesh['grp'=2,'fa'=16] {'fa'}, use_global_device_ids=true, to_apply=%region_9.10 | all-reduce | flops 1 | bytes 8 | tf_op jit(solution)/shard_map/psum | solution.py:90
  156.1 61.4 %all-reduce.3.cloned.1.call-done = (f32[1024,256]{0,1:T(8,128)}, f32[256,256]{0,1:T(8,128)}) async-done(((f32[1024,256]{0,1:T(8,128)}, f32[256,256]{0,1:T(8,128)}), (f32[1024,256]{0,1:T(8,128)}, f32[256,256]{0,1:T(8,128)})) %all-reduce.3.cloned.1.call-update) | async-done | bytes 1310736 | tf_op jit(solution)/shard_map/psum | solution.py:90
  217.5 0.0 copy-start.6
  217.5 1.3 broadcast_multiply_fusion
  218.8 1.3 copy.12
  220.1 0.0 copy-done.6
  220.2 0.8 copy.13
  (4 shorter events, 0.0 us)
Async XLA Ops:
  7.2 47.7 %copy-start = (bf16[1024,256]{1,0:T(8,128)(2,1)S(1)}, bf16[1024,256]{1,0:T(8,128)(2,1)}, u32[]{:S(2)}) copy-start(bf16[1024,256]{1,0:T(8,128)(2,1)} %param.13) | copy-start | bytes 1572868
  7.2 47.6 %copy-start.7 = (s32[128]{0:T(128)S(1)}, s32[128]{0:T(128)}, u32[]{:S(2)}) copy-start(s32[128]{0:T(128)} %param.17) | copy-start | bytes 1540
  7.2 47.6 %copy-start.4 = (bf16[128,1024]{1,0:T(8,128)(2,1)S(1)}, bf16[128,1024]{1,0:T(8,128)(2,1)}, u32[]{:S(2)}) copy-start(bf16[128,1024]{1,0:T(8,128)(2,1)} %param.10) | copy-start | bytes 786436
  7.2 44.2 %all-gather.2.cloned.1.call-start = ((), (), s32[]{:S(2)}) async-start(), calls=%async_computation.1 | async-start | bytes 1114112 | tf_op jit(solution)/shard_map/all_gather | solution.py:49
  9.3 110.8 %reduce-scatter.2.cloned.1.call-start = ((), (), s32[]{:S(2)}) async-start(), calls=%async_computation.2 | async-start | bytes 2228224 | tf_op jit(solution)/shard_map/reduce_scatter | solution.py:83
  51.4 3.4 %copy-start.1 = (bf16[2048,256]{1,0:T(8,128)(2,1)S(1)}, bf16[2048,256]{1,0:T(8,128)(2,1)}, u32[]{:S(2)}) copy-start(bf16[2048,256]{1,0:T(8,128)(2,1)} %all-gather.2.cloned.1.call-done) | copy-start | bytes 3145732
  57.4 2.0 copy-start.3
  59.3 2.3 copy-start.2
  59.4 158.1 %all-reduce.3.cloned.1.call-start = ((), (), s32[]{:S(2)}) async-start(), calls=%async_computation.3 | async-start | bytes 2621440 | tf_op jit(solution)/shard_map/psum | solution.py:90
  63.5 58.3 %copy-start.5 = (bf16[128,256]{1,0:T(8,128)(2,1)S(1)}, bf16[128,256]{1,0:T(8,128)(2,1)}, u32[]{:S(2)}) copy-start(bf16[128,256]{1,0:T(8,128)(2,1)} %param.11) | copy-start | bytes 196612
  217.5 2.7 %copy-start.6 = (f32[256,256]{0,1:T(8,128)S(1)}, f32[256,256]{0,1:T(8,128)}, u32[]{:S(2)}) copy-start(f32[256,256]{0,1:T(8,128)} %get-tuple-element.33) | copy-start | bytes 786436
Sparse Core Ops, SparseCore 0:
  10.8 40.6 all-gather.1
  59.5 60.5 reduce-scatter.1
  124.6 92.8 all-reduce.2
where the time goes:
time: 229 us
  waiting for transfers between devices  158 us (69%)
  blocking collectives  30.2 us (13%)
  matrix products  18.4 us (8%)
  between operations  18.1 us (8%)
    psum x1, waiting for transfers between devices, body(): lax.psum((local_wf, local_wb, loss_part), 'fa')  61.4 us
    reduce_scatter x1, waiting for transfers between devices, body(): lax.psum_scatter(contract_first(tiles, feat), 'fa', scatter_dimension=0,...  56.6 us
    all_gather x1, waiting for transfers between devices, body(): piece = lax.all_gather(back, 'fa', axis=0, tiled=True)  39.6 us
    psum x1, blocking collectives, body(): lax.psum((local_wf, local_wb, loss_part), 'fa')  30.2 us
    dot_general x3, matrix products, contract_last(): lax.dot_general(left, right, (((1,), (1,)), ((), ())), preferred_element_...  8.1 us
    dot_general x3, matrix products, contract_first(): lax.dot_general(left, right, (((0,), (0,)), ((), ())), preferred_element_...  4.78 us
  transfers between devices with their start and end apart: 3, of which 3 were waited for; matrix products, arithmetic and copies ran while one was open for 3% of the time, Pallas kernels for 0%

commit v1 on v0

v1 whole, which is shorter than its diff:
```python
import functools
import math

import jax
import jax.numpy as jnp
from jax import lax
from jax.experimental import pallas as pl
from jax.experimental.pallas import tpu as pltpu
from jax.sharding import PartitionSpec as P

GAMMA = 0.98
LAMBDA = 1.0
EPS = 1e-06
BF = jnp.bfloat16
F32 = jnp.float32


def dot(left, right):
    return jnp.dot(left, right, preferred_element_type=F32)


def dot_t(left, right):
    return lax.dot_general(left, right, (((0,), (0,)), ((), ())), preferred_element_type=F32)


def halves(array):
    high = array.astype(BF)
    return high, (array - high.astype(F32)).astype(BF)


def swap(array, mask, size):
    return lax.ppermute(array, "fa", [(i, i ^ mask) for i in range(size)])


def masks_of(size):
    return [1 << k for k in range(size.bit_length() - 1)]


def reverse_bits(value, bits):
    out = value * 0
    for k in range(bits):
        out = out + (((value >> k) & 1) << (bits - 1 - k))
    return out


def gather_swapped(array, size):
    for mask in reversed(masks_of(size)):
        array = jnp.concatenate([array, swap(array, mask, size)], axis=0)
    return array


def assemble_kernel(place_ref, blocks_ref, wf_ref, wb_ref, *, count, wf_rows, wb_rows, factor_f, factor_b):
    place = place_ref[0]
    for e in range(count):
        at = place ^ e
        wf_ref[pl.ds(pl.multiple_of(at * wf_rows, wf_rows), wf_rows), :] = (
            blocks_ref[e, :wf_rows, :].astype(F32) * factor_f
        )
        wb_ref[pl.ds(pl.multiple_of(at * wb_rows, wb_rows), wb_rows), :] = (
            blocks_ref[e, wf_rows:, :].astype(F32) * factor_b
        )


def body(hidden_f, hidden_t, hidden_b, w_f, w_t, w_b, latents, latent_ids, positives):
    rows = hidden_f.shape[0]
    width = w_f.shape[1]
    size = lax.axis_size("fa")
    bits = size.bit_length() - 1
    me = lax.axis_index("fa")
    total = size * rows
    pairs = float(total * (total - 1))
    every_hb = gather_swapped(hidden_b, size)

    onehot = (latent_ids[:, None] == jnp.arange(latents.shape[0], dtype=jnp.int32)[None, :]).astype(BF)
    zrows = dot(onehot, latents)
    feat = (dot(hidden_f, w_f) + zrows).astype(BF)
    feat_t = (dot(hidden_t, w_t) + zrows).astype(BF)
    diff = feat.astype(F32) - GAMMA * feat_t.astype(F32)
    diff_hi, diff_lo = halves(diff)
    kmat = dot_t(diff_hi, feat) + dot_t(diff_lo, feat)

    blocks = me ^ reverse_bits(jnp.arange(size, dtype=jnp.int32), bits)
    col_ids = (blocks[:, None] * rows + jnp.arange(rows, dtype=jnp.int32)[None, :]).reshape(-1)
    pick = (positives[:, None] == col_ids[None, :]).astype(BF)

    def embed(hidden):
        raw = dot(hidden, w_b)
        scale = lax.rsqrt(jnp.mean(raw * raw, axis=-1, keepdims=True) + EPS)
        return raw, scale, (raw * scale).astype(BF)

    def through(grad, raw, scale):
        return (
            scale * grad - scale**3 / width * jnp.sum(grad * raw, axis=-1, keepdims=True) * raw
        ).astype(BF)

    raw, scale, back = embed(every_hb)
    smat = dot_t(back, back)
    s_hi, s_lo = halves(smat)
    own_hb = dot(pick, every_hb).astype(BF)
    own_raw, own_scale, own_back = embed(own_hb)
    ob = own_back.astype(F32)
    ds = dot(diff_hi, s_hi) + dot(diff_lo, s_hi) + dot(diff_hi, s_lo)
    db = jnp.sum(diff * ob, axis=-1, keepdims=True)
    coef = db / pairs + 1.0 / total
    grad_f = (ds / pairs - coef * ob).astype(BF)
    local_wf = dot_t(hidden_f, grad_f)
    norm = jnp.sum(ob * ob, axis=-1, keepdims=True)
    f32feat = feat.astype(F32)
    part = (
        (jnp.sum(diff * ds) - jnp.sum(db * db)) / (2.0 * pairs)
        - jnp.sum(f32feat * ob) / total
        + LAMBDA
        * ((jnp.sum(smat * smat) / size - jnp.sum(norm * norm)) / (2.0 * pairs) - jnp.sum(norm) / total)
    )
    amat = (kmat + (2.0 * LAMBDA / size) * smat) / pairs
    a_hi, a_lo = halves(amat)
    grad_all = through(dot(back, a_hi) + dot(back, a_lo), raw, scale)
    grad_own = through(
        -coef * f32feat - (2.0 * LAMBDA / pairs * norm + 2.0 * LAMBDA / total) * ob, own_raw, own_scale
    )
    local_wb = dot_t(every_hb, grad_all) + dot_t(own_hb, grad_own)

    wf_rows = local_wf.shape[0] // 16
    wb_rows = local_wb.shape[0] // 16
    each = wf_rows + wb_rows
    current = jnp.concatenate(
        [local_wf.reshape(16, wf_rows, width), local_wb.reshape(16, wb_rows, width)], axis=1
    )
    note = jnp.full((1, 8, width), part, F32)
    split = min(4, bits)
    for k, mask in enumerate(masks_of(size)):
        if k < split:
            count = current.shape[0] // 2
            mine = (me >> k) & 1
            keep = lax.dynamic_slice_in_dim(current, mine * count, count, 0)
            send = lax.dynamic_slice_in_dim(current, (1 - mine) * count, count, 0)
        else:
            count = current.shape[0]
            keep = send = current
        sent = jnp.concatenate([send.reshape(1, count * each, width), note], axis=1)
        got = swap(sent, mask, size)
        current = keep + got[:, : count * each].reshape(count, each, width)
        note = note + got[:, count * each :]
    result = current.astype(BF)
    for mask in reversed(masks_of(size)[:split]):
        result = jnp.concatenate([result, swap(result, mask, size)], axis=0)
    place = reverse_bits(me & ((1 << split) - 1), split).astype(jnp.int32).reshape(1)
    count = result.shape[0]
    grad_wf, grad_wb = pl.pallas_call(
        functools.partial(
            assemble_kernel,
            count=count,
            wf_rows=wf_rows * (16 // count),
            wb_rows=wb_rows * (16 // count),
            factor_f=math.sqrt(hidden_f.shape[1]),
            factor_b=math.sqrt(hidden_b.shape[1]),
        ),
        in_specs=[
            pl.BlockSpec(memory_space=pltpu.SMEM),
            pl.BlockSpec(memory_space=pltpu.VMEM),
        ],
        out_specs=[pl.BlockSpec(memory_space=pltpu.VMEM)] * 2,
        out_shape=[
            jax.ShapeDtypeStruct(local_wf.shape, F32),
            jax.ShapeDtypeStruct(local_wb.shape, F32),
        ],
        compiler_params=pltpu.CompilerParams(vmem_limit_bytes=16 * 2**20),
    )(place, result)
    return (grad_wf, grad_wb, (note[0, 0, :1] / width))


def solution(mesh):
    placed = (
        P(("grp", "fa"), None),
        P(("grp", "fa"), None),
        P(("grp", "fa"), None),
        P(),
        P(),
        P(),
        P("grp", None),
        P(("grp", "fa")),
        P(("grp", "fa")),
    )
    return jax.shard_map(
        body,
        mesh=mesh,
        in_specs=placed,
        out_specs=(P("grp", None), P("grp", None), P("grp")),
        check_vma=False,
    )
```

time: 229 us -> 95.8 us (0.42)
  waiting for transfers between devices: 158 us -> 36.1 us
  blocking collectives: 30.2 us -> 0 us
  starting transfers between devices: 0.12 us -> 18.4 us
  between operations: 18.1 us -> 7.39 us
  local copies, waits for them, and re-layouts: 2.18 us -> 9.58 us
  other arithmetic: 2.11 us -> 5.46 us
    psum x1 -> x0, waiting for transfers between devices: 61.4 us -> none  [body(): lax.psum((local_wf, local_wb, loss_part), 'fa')]
    reduce_scatter x1 -> x0, waiting for transfers between devices: 56.6 us -> none  [body(): lax.psum_scatter(contract_first(tiles, feat), 'fa', scatter_dimension=0,...]
    all_gather x1 -> x0, waiting for transfers between devices: 39.6 us -> none  [body(): piece = lax.all_gather(back, 'fa', axis=0, tiled=True)]
    ppermute x0 -> x12, waiting for transfers between devices: none -> 36.1 us  [swap(): return lax.ppermute(array, 'fa', [(i, i ^ mask) for i in range(size)])]
    psum x1 -> x0, blocking collectives: 30.2 us -> none  [body(): lax.psum((local_wf, local_wb, loss_part), 'fa')]
    ppermute x0 -> x12, starting transfers between devices: none -> 18.4 us  [swap(): return lax.ppermute(array, 'fa', [(i, i ^ mask) for i in range(size)])]
    reduce_sum x0 -> x2, other arithmetic: none -> 2.69 us  [the longest x1 1.44 us: body(): jnp.sum(f32feat * ob) / total]
    dot_general x0 -> x1, local copies, waits for them, and re-layouts: none -> 2.55 us  [dot_t(): lax.dot_general(left, right, (((0,), (0,)), ((), ())), preferred_element_...]
  transfers between devices with their start and end apart: 3 -> 12, of which waited for: 3 -> 11; matrix products, arithmetic and copies ran while one was open for 3% -> 8% of each run, Pallas kernels for 0% -> 0%
where the time goes in v1:
time: 95.8 us; the launch traced here: 95.3 us
  waiting for transfers between devices  36.1 us (38%)
  starting transfers between devices  18.4 us (19%)
  matrix products  17.3 us (18%)
  local copies, waits for them, and re-layouts  9.58 us (10%)
  between operations  7.39 us (8%)
  other arithmetic  5.46 us (6%)
  Pallas kernels  1.14 us (1%)
    ppermute x12, waiting for transfers between devices, swap(): return lax.ppermute(array, 'fa', [(i, i ^ mask) for i in range(size)])  36.1 us
    ppermute x12, starting transfers between devices, swap(): return lax.ppermute(array, 'fa', [(i, i ^ mask) for i in range(size)])  18.4 us
    dot_general x11, matrix products, dot(): return jnp.dot(left, right, preferred_element_type=F32)  11.5 us
    dot_general x6, matrix products, dot_t(): lax.dot_general(left, right, (((0,), (0,)), ((), ())), preferred_element_...  5.75 us
    unnamed x47, local copies, waits for them, and re-layouts  4.13 us
    dot_general x1, local copies, waits for them, and re-layouts, dot_t(): lax.dot_general(left, right, (((0,), (0,)), ((), ())), preferred_element_...  2.55 us
  transfers between devices with their start and end apart: 12, of which 11 were waited for; matrix products, arithmetic and copies ran while one was open for 8% of the time, Pallas kernels for 0%

profile of v1, /device:TPU:0, one launch (start us, length us, event | category | flops | bytes accessed | tf_op | source)
XLA Modules:
  0.0 95.3 jit_solution(12930932571856223176)
XLA Ops:
  0.6 0.0 copy-start
  0.7 4.1 %collective-permute-start = (bf16[128,256]{1,0:T(8,128)(2,1)}, bf16[128,256]{1,0:T(8,128)(2,1)S(1)}, u32[]{:S(2)}, u32[]{:S(2)}) collective-permute-start(bf16[128,256]{1,0:T(8,128)(2,1)} %param.11), channel_id=1, source_target_pairs={{0,8},{1,9},{2,10},{3,11},{4,12},{5,13},{6,14},{7,15},{8,0},{9,1},... | collective-permute-start | bytes 196616 | tf_op jit(solution)/shard_map/ppermute | solution.py:32
  4.8 1.2 %fusion.15 = f32[128,256]{1,0:T(8,128)S(1)} fusion(bf16[512,256]{1,0:T(8,128)(2,1)} %param.15, s32[128]{0:T(128)} %param.16), kind=kOutput, calls=%fused_computation.46 | convolution fusion | flops 33619968 | bytes 393728 | tf_op jit(solution)/shard_map/dot_general | solution.py:19
  6.0 1.2 %fusion.2 = bf16[128,256]{1,0:T(8,128)(2,1)S(1)} fusion(f32[128,256]{1,0:T(8,128)S(1)} %fusion.15, bf16[128,1024]{1,0:T(8,128)(2,1)} %param.9, bf16[1024,256]{1,0:T(8,128)(2,1)S(1)} %copy-done), kind=kOutput, calls=%fused_computation.19 | convolution fusion | flops 67174400 | bytes 983040 | tf_op jit(solution)/shard_map/dot_general | solution.py:19
  7.2 1.5 %collective-permute-done = bf16[128,256]{1,0:T(8,128)(2,1)S(1)} collective-permute-done((bf16[128,256]{1,0:T(8,128)(2,1)}, bf16[128,256]{1,0:T(8,128)(2,1)S(1)}, u32[]{:S(2)}, u32[]{:S(2)}) %collective-permute-start) | collective-permute-done | bytes 65568 | tf_op jit(solution)/shard_map/ppermute | solution.py:32
  8.6 0.8 pad_maximum_fusion.6
  9.5 0.7 collective-permute-start.1
  10.2 1.4 %fusion.6 = f32[128,256]{1,0:T(8,128)S(1)} fusion(f32[128,256]{1,0:T(8,128)S(1)} %fusion.15, bf16[128,1024]{1,0:T(8,128)(2,1)} %param.10, bf16[1024,256]{1,0:T(8,128)(2,1)} %param.13, bf16[128,256]{1,0:T(8,128)(2,1)S(1)} %fusion.2), kind=kOutput, calls=%fused_computation.23 | convolution fusion | flops 67305472 | bytes 1114112 | tf_op jit(solution)/shard_map/dot_general | solution.py:19
  11.6 0.0 copy-start.6
  11.6 0.6 constant_dynamic-update-slice_fusion.4
  12.2 2.3 %collective-permute-done.1 = bf16[256,256]{1,0:T(8,128)(2,1)S(1)} collective-permute-done((bf16[256,256]{1,0:T(8,128)(2,1)S(1)}, bf16[256,256]{1,0:T(8,128)(2,1)S(1)}, u32[]{:S(2)}, u32[]{:S(2)}) %collective-permute-start.1) | collective-permute-done | bytes 131104 | tf_op jit(solution)/shard_map/ppermute | solution.py:32
  14.5 1.8 %collective-permute-start.2 = (bf16[512,256]{1,0:T(8,128)(2,1)S(1)}, bf16[512,256]{1,0:T(8,128)(2,1)S(1)}, u32[]{:S(2)}, u32[]{:S(2)}) collective-permute-start(bf16[512,256]{1,0:T(8,128)(2,1)S(1)} %pad_maximum_fusion.3), channel_id=1, source_target_pairs={{0,2},{1,3},{2,0},{3,1},{4,6},{5,7},{6,4},{7,5},{8,10},{9,11},{10,... | collective-permute-start | bytes 786440 | tf_op jit(solution)/shard_map/ppermute | solution.py:32
  16.3 0.2 fusion.60
  16.5 4.4 %collective-permute-done.2 = bf16[512,256]{1,0:T(8,128)(2,1)S(1)} collective-permute-done((bf16[512,256]{1,0:T(8,128)(2,1)S(1)}, bf16[512,256]{1,0:T(8,128)(2,1)S(1)}, u32[]{:S(2)}, u32[]{:S(2)}) %collective-permute-start.2) | collective-permute-done | bytes 262176 | tf_op jit(solution)/shard_map/ppermute | solution.py:32
  21.0 0.1 collective-permute-start.3
  21.1 0.1 add_bitcast_fusion
  21.2 0.6 constant_dynamic-update-slice_fusion.3
  21.8 0.7 constant_dynamic-update-slice_fusion.2
  22.5 0.7 constant_dynamic-update-slice_fusion.1
  23.2 0.8 constant_dynamic-update-slice_fusion
  24.0 1.7 %multiply_reduce_fusion.1 = (f32[2048]{0:T(1024)S(1)}, f32[2048,256]{0,1:T(8,128)S(1)}) fusion(bf16[2048,256]{1,0:T(8,128)(2,1)} %constant_dynamic-update-slice_fusion, bf16[256,256]{1,0:T(8,128)(2,1)S(1)} %copy-done.6), kind=kOutput, calls=%fused_computation.4 | convolution fusion | flops 269481984 | bytes 3284992 | tf_op jit(solution)/shard_map/dot_general | solution.py:19
  25.8 0.0 copy-start.7
  25.8 1.1 %multiply_reduce_fusion.2 = (f32[]{:T(128)}, f32[256,256]{1,0:T(8,128)S(1)}) fusion(f32[2048,256]{0,1:T(8,128)S(1)} %get-tuple-element.22, f32[2048]{0:T(1024)S(1)} %add_rsqrt_fusion), kind=kOutput, calls=%fused_computation.37 | convolution fusion | flops 269615104 | bytes 2367492 | tf_op jit(solution)/shard_map/dot_general | solution.py:23
  26.9 0.2 fusion.56
  27.0 0.2 convolution_add_fusion.6
  27.2 1.6 %convolution_convert_fusion = bf16[128,256]{1,0:T(8,128)(2,1)S(1)} fusion(bf16[2048,256]{1,0:T(8,128)(2,1)} %constant_dynamic-update-slice_fusion, s32[2048]{0:T(1024)S(1)} %add_bitcast_fusion, s32[128]{0:T(128)S(1)} %copy-done.19), kind=kOutput, calls=%fused_computation.18 | convolution fusion | flops 134512640 | bytes 1122816 | tf_op jit(solution)/shard_map/dot_general | solution.py:19
  28.8 0.3 multiply_reduce_fusion.5
  29.1 0.6 copy-done.16
  29.6 1.5 %multiply_reduce_fusion.3 = (f32[]{:T(128)}, f32[128]{0:T(128)S(1)}, f32[]{:T(128)}, f32[128]{0:T(128)S(1)}, bf16[128,256]{1,0:T(8,128)(2,1)S(1)}, /*index=5*/f32[128,256]{1,0:T(8,128)}) fusion(f32[128,256]{1,0:T(8,128)S(1)} %fusion.6, f32[128,256]{1,0:T(8,128)S(1)} %get-tuple-element.24, f32[128]{0:T(128)S(1)} %add_rsqrt_fusion.1, ...), kind=kOutput, calls=%fused_computation.59 | convolution fusion | flops 17432320 | bytes 853512 | tf_op jit(solution)/shard_map/dot_general | solution.py:19
  31.1 1.2 %multiply_reduce_fusion.6 = (f32[]{:T(128)}, f32[128]{0:T(128)}, f32[128]{0:T(128)}, f32[128]{0:T(128)}, f32[]{:T(128)}) fusion(f32[128]{0:T(128)S(1)} %get-tuple-element.12, f32[128]{0:T(128)S(1)} %get-tuple-element.10), kind=kLoop, calls=%fused_computation.121 | loop fusion | flops 1150 | bytes 2568 | tf_op jit(solution)/shard_map/reduce_sum | solution.py:113
  35.5 1.4 %fusion.22 = (f32[]{:T(128)}, f32[128]{0:T(128)}) fusion(bf16[128,256]{1,0:T(8,128)(2,1)S(1)} %get-tuple-element.15, bf16[128,256]{1,0:T(8,128)(2,1)S(1)} %fusion.2, f32[128,256]{1,0:T(8,128)S(1)} %get-tuple-element.24, f32[128]{0:T(128)} %get-tuple-element.17, f32[128]{0:T(128)} %get-tuple-element.31), kind=kLoop, calls=%fused_computation.57 | loop fusion | flops 294783 | bytes 263684 | tf_op jit(solution)/shard_map/reduce_sum | solution.py:111
  37.6 0.2 fusion.1
  37.9 0.5 fusion.31
  38.4 0.0 copy-start.4
  38.5 1.9 %multiply_reduce_fusion = (f32[2048]{0:T(1024)S(1)}, f32[2048,256]{0,1:T(8,128)}) fusion(f32[2048,256]{0,1:T(8,128)S(1)} %get-tuple-element.22, f32[2048,256]{0,1:T(8,128)S(1)} %fusion.31, f32[256,256]{1,0:T(8,128)S(1)} %fusion.1, f32[2048]{0:T(1024)S(1)} %add_rsqrt_fusion), kind=kOutput, calls=%fused_computation.2 | convolution fusion | flops 271316992 | bytes 6569984 | tf_op jit(solution)/shard_map/dot_general | solution.py:19
  40.4 0.3 fusion.25
  40.8 1.4 %convolution_bitcast_fusion = f32[1024,256]{0,1:T(8,128)} fusion(bf16[128,1024]{1,0:T(8,128)(2,1)S(1)} %copy-done.4, bf16[128,256]{1,0:T(8,128)(2,1)S(1)} %get-tuple-element.15, f32[128,256]{1,0:T(8,128)S(1)} %copy-done.8, f32[128]{0:T(128)S(1)} %copy-done.15), kind=kOutput, calls=%fused_computation.7 | convolution fusion | flops 67272704 | bytes 1507840 | tf_op jit(solution)/shard_map/dot_general | solution.py:23
  42.2 2.5 %copy.12 = f32[1024,256]{1,0:T(8,128)} copy(f32[1024,256]{0,1:T(8,128)} %convolution_bitcast_fusion) | data formatting | bytes 2097152 | tf_op jit(solution)/shard_map/dot_general | solution.py:23
  44.7 2.6 %convolution_add_fusion.2 = f32[256,256]{1,0:T(8,128)S(1)} fusion(f32[256,256]{1,0:T(8,128)S(1)} %fusion.25, bf16[2048,256]{1,0:T(8,128)(2,1)} %constant_dynamic-update-slice_fusion, f32[2048,256]{0,1:T(8,128)S(1)} %get-tuple-element.22, f32[2048,256]{0,1:T(8,128)} %get-tuple-element.27, f32[2048]{0:T(1024)S(1)} %fusion.37, f32[2048]{0:T(1024)S(1)} %add_rsqrt_fusion), kind=kOutput, calls=%fused_computation.13 | convolution fusion | flops 270598144 | bytes 5783552 | tf_op jit(solution)/shard_map/dot_general | solution.py:23
  47.3 0.1 fusion.10
  47.4 0.9 concatenate.50
  48.3 0.5 collective-permute-start.4
  48.8 1.9 %collective-permute-done.4 = f32[1,648,256]{2,1,0:T(8,128)S(1)} collective-permute-done((f32[1,648,256]{2,1,0:T(8,128)}, f32[1,648,256]{2,1,0:T(8,128)S(1)}, u32[]{:S(2)}, u32[]{:S(2)}) %collective-permute-start.4) | collective-permute-done | bytes 663584 | tf_op jit(solution)/shard_map/ppermute | solution.py:32
  50.8 0.8 copy-done.5
  51.5 0.1 fusion.12
  51.7 0.7 slice_add_fusion.3
  52.4 1.8 %collective-permute-start.5 = (f32[1,328,256]{2,1,0:T(8,128)S(1)}, f32[1,328,256]{2,1,0:T(8,128)S(1)}, u32[]{:S(2)}, u32[]{:S(2)}) collective-permute-start(f32[1,328,256]{2,1,0:T(8,128)S(1)} %pad_maximum_fusion.1), channel_id=1, source_target_pairs={{0,2},{1,3},{2,0},{3,1},{4,6},{5,7},{6,4},{7,5},{8,10},{9,11},{10,... | collective-permute-start | bytes 1007624 | tf_op jit(solution)/shard_map/ppermute | solution.py:32
  54.2 8.4 %collective-permute-done.5 = f32[1,328,256]{2,1,0:T(8,128)S(1)} collective-permute-done((f32[1,328,256]{2,1,0:T(8,128)S(1)}, f32[1,328,256]{2,1,0:T(8,128)S(1)}, u32[]{:S(2)}, u32[]{:S(2)}) %collective-permute-start.5) | collective-permute-done | bytes 335904 | tf_op jit(solution)/shard_map/ppermute | solution.py:32
  62.8 0.7 slice_add_fusion.2
  63.5 0.9 collective-permute-start.6
  64.4 5.0 %collective-permute-done.6 = f32[1,168,256]{2,1,0:T(8,128)S(1)} collective-permute-done((f32[1,168,256]{2,1,0:T(8,128)S(1)}, f32[1,168,256]{2,1,0:T(8,128)S(1)}, u32[]{:S(2)}, u32[]{:S(2)}) %collective-permute-start.6) | collective-permute-done | bytes 172064 | tf_op jit(solution)/shard_map/ppermute | solution.py:32
  69.5 3.3 %collective-permute-start.7 = (f32[1,88,256]{2,1,0:T(8,128)S(1)}, f32[1,88,256]{2,1,0:T(8,128)S(1)}, u32[]{:S(2)}, u32[]{:S(2)}) collective-permute-start(f32[1,88,256]{2,1,0:T(8,128)S(1)} %pad_maximum_fusion.7), channel_id=1, source_target_pairs={{0,8},{1,9},{2,10},{3,11},{4,12},{5,13},{6,14},{7,15},{8,0},{9,1},... | collective-permute-start | bytes 270344 | tf_op jit(solution)/shard_map/ppermute | solution.py:32
  72.8 3.5 %collective-permute-done.7 = f32[1,88,256]{2,1,0:T(8,128)S(1)} collective-permute-done((f32[1,88,256]{2,1,0:T(8,128)S(1)}, f32[1,88,256]{2,1,0:T(8,128)S(1)}, u32[]{:S(2)}, u32[]{:S(2)}) %collective-permute-start.7) | collective-permute-done | bytes 90144 | tf_op jit(solution)/shard_map/ppermute | solution.py:32
  76.3 2.1 %collective-permute-start.8 = (bf16[1,80,256]{2,1,0:T(8,128)(2,1)S(1)}, bf16[1,80,256]{2,1,0:T(8,128)(2,1)S(1)}, u32[]{:S(2)}, u32[]{:S(2)}) collective-permute-start(bf16[1,80,256]{2,1,0:T(8,128)(2,1)S(1)} %get-tuple-element.14), channel_id=1, source_target_pairs={{0,8},{1,9},{2,10},{3,11},{4,12},{5,13},{6,14},{7,15},{8,0},{9,1},... | collective-permute-start | bytes 122888 | tf_op jit(solution)/shard_map/ppermute | solution.py:32
  78.4 2.9 %collective-permute-done.8 = bf16[1,80,256]{2,1,0:T(8,128)(2,1)S(1)} collective-permute-done((bf16[1,80,256]{2,1,0:T(8,128)(2,1)S(1)}, bf16[1,80,256]{2,1,0:T(8,128)(2,1)S(1)}, u32[]{:S(2)}, u32[]{:S(2)}) %collective-permute-start.8) | collective-permute-done | bytes 40992 | tf_op jit(solution)/shard_map/ppermute | solution.py:32
  81.4 1.4 %collective-permute-start.9 = (bf16[2,80,256]{2,1,0:T(8,128)(2,1)S(1)}, bf16[2,80,256]{2,1,0:T(8,128)(2,1)S(1)}, u32[]{:S(2)}, u32[]{:S(2)}) collective-permute-start(bf16[2,80,256]{2,1,0:T(8,128)(2,1)S(1)} %pad_maximum_fusion.8), channel_id=1, source_target_pairs={{0,4},{1,5},{2,6},{3,7},{4,0},{5,1},{6,2},{7,3},{8,12},{9,13},{10,... | collective-permute-start | bytes 245768 | tf_op jit(solution)/shard_map/ppermute | solution.py:32
  82.7 3.1 %collective-permute-done.9 = bf16[2,80,256]{2,1,0:T(8,128)(2,1)S(1)} collective-permute-done((bf16[2,80,256]{2,1,0:T(8,128)(2,1)S(1)}, bf16[2,80,256]{2,1,0:T(8,128)(2,1)S(1)}, u32[]{:S(2)}, u32[]{:S(2)}) %collective-permute-start.9) | collective-permute-done | bytes 81952 | tf_op jit(solution)/shard_map/ppermute | solution.py:32
  85.9 1.6 %collective-permute-start.10 = (bf16[4,80,256]{2,1,0:T(8,128)(2,1)S(1)}, bf16[4,80,256]{2,1,0:T(8,128)(2,1)S(1)}, u32[]{:S(2)}, u32[]{:S(2)}) collective-permute-start(bf16[4,80,256]{2,1,0:T(8,128)(2,1)S(1)} %pad_maximum_fusion.5), channel_id=1, source_target_pairs={{0,2},{1,3},{2,0},{3,1},{4,6},{5,7},{6,4},{7,5},{8,10},{9,11},{10,... | collective-permute-start | bytes 491528 | tf_op jit(solution)/shard_map/ppermute | solution.py:32
  87.5 0.5 slice.44
  88.0 0.5 slice.45
  89.8 1.5 %collective-permute-done.10 = bf16[4,80,256]{2,1,0:T(8,128)(2,1)S(1)} collective-permute-done((bf16[4,80,256]{2,1,0:T(8,128)(2,1)S(1)}, bf16[4,80,256]{2,1,0:T(8,128)(2,1)S(1)}, u32[]{:S(2)}, u32[]{:S(2)}) %collective-permute-start.10) | collective-permute-done | bytes 163872 | tf_op jit(solution)/shard_map/ppermute | solution.py:32
  91.3 0.1 collective-permute-start.11
  91.4 1.6 %collective-permute-done.11 = bf16[8,80,256]{2,1,0:T(8,128)(2,1)S(1)} collective-permute-done((bf16[8,80,256]{2,1,0:T(8,128)(2,1)S(1)}, bf16[8,80,256]{2,1,0:T(8,128)(2,1)S(1)}, u32[]{:S(2)}, u32[]{:S(2)}) %collective-permute-start.11) | collective-permute-done | bytes 327712 | tf_op jit(solution)/shard_map/ppermute | solution.py:32
  93.0 1.1 %shard_map.112 = (f32[1024,256]{1,0:T(8,128)}, f32[256,256]{1,0:T(8,128)}) custom-call(s32[1]{0:T(128)} %bitcast.place_ref, bf16[16,80,256]{2,1,0:T(8,128)(2,1)S(1)} %constant_dynamic-update-slice_fusion.5.blocks_ref), custom_call_target="tpu_custom_call" | custom-call | tf_op jit(solution)/shard_map/pallas_call | solution.py:149
  (62 shorter events, 0.6 us)
Async XLA Ops:
  0.6 5.3 %copy-start = (bf16[1024,256]{1,0:T(8,128)(2,1)S(1)}, bf16[1024,256]{1,0:T(8,128)(2,1)}, u32[]{:S(2)}) copy-start(bf16[1024,256]{1,0:T(8,128)(2,1)} %param.12) | copy-start | bytes 1572868
  0.6 10.9 %copy-start.3 = (bf16[128,256]{1,0:T(8,128)(2,1)S(1)}, bf16[128,256]{1,0:T(8,128)(2,1)}, u32[]{:S(2)}) copy-start(bf16[128,256]{1,0:T(8,128)(2,1)} %param.11) | copy-start | bytes 196612
  0.7 8.0 %collective-permute-start = (bf16[128,256]{1,0:T(8,128)(2,1)}, bf16[128,256]{1,0:T(8,128)(2,1)S(1)}, u32[]{:S(2)}, u32[]{:S(2)}) collective-permute-start(bf16[128,256]{1,0:T(8,128)(2,1)} %param.11), channel_id=1, source_target_pairs={{0,8},{1,9},{2,10},{3,11},{4,12},{5,13},{6,14},{7,15},{8,0},{9,1},... | collective-permute-start | bytes 196616 | tf_op jit(solution)/shard_map/ppermute | solution.py:32
  9.5 5.0 %collective-permute-start.1 = (bf16[256,256]{1,0:T(8,128)(2,1)S(1)}, bf16[256,256]{1,0:T(8,128)(2,1)S(1)}, u32[]{:S(2)}, u32[]{:S(2)}) collective-permute-start(bf16[256,256]{1,0:T(8,128)(2,1)S(1)} %pad_maximum_fusion.6), channel_id=1, source_target_pairs={{0,4},{1,5},{2,6},{3,7},{4,0},{5,1},{6,2},{7,3},{8,12},{9,13},{10,... | collective-permute-start | bytes 393224 | tf_op jit(solution)/shard_map/ppermute | solution.py:32
  11.6 12.4 %copy-start.6 = (bf16[256,256]{1,0:T(8,128)(2,1)S(1)}, bf16[256,256]{1,0:T(8,128)(2,1)}, u32[]{:S(2)}) copy-start(bf16[256,256]{1,0:T(8,128)(2,1)} %param.14) | copy-start | bytes 393220
  14.5 6.4 %collective-permute-start.2 = (bf16[512,256]{1,0:T(8,128)(2,1)S(1)}, bf16[512,256]{1,0:T(8,128)(2,1)S(1)}, u32[]{:S(2)}, u32[]{:S(2)}) collective-permute-start(bf16[512,256]{1,0:T(8,128)(2,1)S(1)} %pad_maximum_fusion.3), channel_id=1, source_target_pairs={{0,2},{1,3},{2,0},{3,1},{4,6},{5,7},{6,4},{7,5},{8,10},{9,11},{10,... | collective-permute-start | bytes 786440 | tf_op jit(solution)/shard_map/ppermute | solution.py:32
  21.0 2.2 %collective-permute-start.3 = (bf16[1024,256]{1,0:T(8,128)(2,1)S(1)}, bf16[1024,256]{1,0:T(8,128)(2,1)S(1)}, u32[]{:S(2)}, u32[]{:S(2)}) collective-permute-start(bf16[1024,256]{1,0:T(8,128)(2,1)S(1)} %pad_maximum_fusion), channel_id=1, source_target_pairs={{0,1},{1,0},{2,3},{3,2},{4,5},{5,4},{6,7},{7,6},{8,9},{9,8},{10,11... | collective-permute-start | bytes 1572872 | tf_op jit(solution)/shard_map/ppermute | solution.py:32
  25.7 1.4 %copy-start.19 = (s32[128]{0:T(128)S(1)}, s32[128]{0:T(128)}, u32[]{:S(2)}) copy-start(s32[128]{0:T(128)} %param.17) | copy-start | bytes 1540
  25.8 3.0 %copy-start.7 = (bf16[256,256]{1,0:T(8,128)(2,1)S(1)}, bf16[256,256]{1,0:T(8,128)(2,1)}, u32[]{:S(2)}) copy-start(bf16[256,256]{1,0:T(8,128)(2,1)} %param.14) | copy-start | bytes 393220
  28.8 2.4 %copy-start.9 = (bf16[128,256]{1,0:T(8,128)(2,1)}, bf16[128,256]{1,0:T(8,128)(2,1)S(1)}, u32[]{:S(2)}) copy-start(bf16[128,256]{1,0:T(8,128)(2,1)S(1)} %convolution_convert_fusion) | copy-start | bytes 196612
  29.1 0.6 copy-start.16
  29.6 1.5 %copy-start.13 = (f32[128]{0:T(128)}, f32[128]{0:T(128)S(1)}, u32[]{:S(2)}) copy-start(f32[128]{0:T(128)S(1)} %add_rsqrt_fusion.1) | copy-start | bytes 1540
  38.4 2.0 %copy-start.17 = (f32[128]{0:T(128)S(1)}, f32[128]{0:T(128)}, u32[]{:S(2)}) copy-start(f32[128]{0:T(128)} %copy-done.16) | copy-start | bytes 1540
  38.4 2.0 %copy-start.18 = (f32[128]{0:T(128)S(1)}, f32[128]{0:T(128)}, u32[]{:S(2)}) copy-start(f32[128]{0:T(128)} %get-tuple-element.8) | copy-start | bytes 1540
  38.4 2.0 %copy-start.10 = (bf16[128,256]{1,0:T(8,128)(2,1)S(1)}, bf16[128,256]{1,0:T(8,128)(2,1)}, u32[]{:S(2)}) copy-start(bf16[128,256]{1,0:T(8,128)(2,1)} %copy-done.9) | copy-start | bytes 196612
  38.4 2.0 %copy-start.11 = (f32[128]{0:T(128)S(1)}, f32[128]{0:T(128)}, u32[]{:S(2)}) copy-start(f32[128]{0:T(128)} %get-tuple-element.17) | copy-start | bytes 1540
  38.4 2.0 %copy-start.12 = (f32[128]{0:T(128)S(1)}, f32[128]{0:T(128)}, u32[]{:S(2)}) copy-start(f32[128]{0:T(128)} %get-tuple-element.31) | copy-start | bytes 1540
  38.4 2.0 %copy-start.14 = (f32[128]{0:T(128)S(1)}, f32[128]{0:T(128)}, u32[]{:S(2)}) copy-start(f32[128]{0:T(128)} %copy-done.13) | copy-start | bytes 1540
  38.4 2.3 %copy-start.4 = (bf16[128,1024]{1,0:T(8,128)(2,1)S(1)}, bf16[128,1024]{1,0:T(8,128)(2,1)}, u32[]{:S(2)}) copy-start(bf16[128,1024]{1,0:T(8,128)(2,1)} %param.9) | copy-start | bytes 786436
  38.4 2.3 %copy-start.8 = (f32[128,256]{1,0:T(8,128)S(1)}, f32[128,256]{1,0:T(8,128)}, u32[]{:S(2)}) copy-start(f32[128,256]{1,0:T(8,128)} %get-tuple-element.25) | copy-start | bytes 393220
  38.4 2.3 %copy-start.15 = (f32[128]{0:T(128)S(1)}, f32[128]{0:T(128)}, u32[]{:S(2)}) copy-start(f32[128]{0:T(128)} %get-tuple-element.30) | copy-start | bytes 1540
  44.7 2.6 %copy-start.1 = (f32[1024,256]{1,0:T(8,128)S(1)}, f32[1024,256]{1,0:T(8,128)}, u32[]{:S(2)}) copy-start(f32[1024,256]{1,0:T(8,128)} %copy.12) | copy-start | bytes 3145732
  47.3 4.2 %copy-start.2 = (f32[1024,256]{1,0:T(8,128)S(1)}, f32[1024,256]{1,0:T(8,128)}, u32[]{:S(2)}) copy-start(f32[1024,256]{1,0:T(8,128)} %copy.12) | copy-start | bytes 3145732
  48.3 2.4 %collective-permute-start.4 = (f32[1,648,256]{2,1,0:T(8,128)}, f32[1,648,256]{2,1,0:T(8,128)S(1)}, u32[]{:S(2)}, u32[]{:S(2)}) collective-permute-start(f32[1,648,256]{2,1,0:T(8,128)} %concatenate.50), channel_id=1, source_target_pairs={{0,1},{1,0},{2,3},{3,2},{4,5},{5,4},{6,7},{7,6},{8,9},{9,8},{10,11... | collective-permute-start | bytes 1990664 | tf_op jit(solution)/shard_map/ppermute | solution.py:32
  50.7 0.8 copy-start.5
  52.4 10.2 %collective-permute-start.5 = (f32[1,328,256]{2,1,0:T(8,128)S(1)}, f32[1,328,256]{2,1,0:T(8,128)S(1)}, u32[]{:S(2)}, u32[]{:S(2)}) collective-permute-start(f32[1,328,256]{2,1,0:T(8,128)S(1)} %pad_maximum_fusion.1), channel_id=1, source_target_pairs={{0,2},{1,3},{2,0},{3,1},{4,6},{5,7},{6,4},{7,5},{8,10},{9,11},{10,... | collective-permute-start | bytes 1007624 | tf_op jit(solution)/shard_map/ppermute | solution.py:32
  63.5 5.9 %collective-permute-start.6 = (f32[1,168,256]{2,1,0:T(8,128)S(1)}, f32[1,168,256]{2,1,0:T(8,128)S(1)}, u32[]{:S(2)}, u32[]{:S(2)}) collective-permute-start(f32[1,168,256]{2,1,0:T(8,128)S(1)} %pad_maximum_fusion.4), channel_id=1, source_target_pairs={{0,4},{1,5},{2,6},{3,7},{4,0},{5,1},{6,2},{7,3},{8,12},{9,13},{10,... | collective-permute-start | bytes 516104 | tf_op jit(solution)/shard_map/ppermute | solution.py:32
  69.5 6.8 %collective-permute-start.7 = (f32[1,88,256]{2,1,0:T(8,128)S(1)}, f32[1,88,256]{2,1,0:T(8,128)S(1)}, u32[]{:S(2)}, u32[]{:S(2)}) collective-permute-start(f32[1,88,256]{2,1,0:T(8,128)S(1)} %pad_maximum_fusion.7), channel_id=1, source_target_pairs={{0,8},{1,9},{2,10},{3,11},{4,12},{5,13},{6,14},{7,15},{8,0},{9,1},... | collective-permute-start | bytes 270344 | tf_op jit(solution)/shard_map/ppermute | solution.py:32
  76.3 5.1 %collective-permute-start.8 = (bf16[1,80,256]{2,1,0:T(8,128)(2,1)S(1)}, bf16[1,80,256]{2,1,0:T(8,128)(2,1)S(1)}, u32[]{:S(2)}, u32[]{:S(2)}) collective-permute-start(bf16[1,80,256]{2,1,0:T(8,128)(2,1)S(1)} %get-tuple-element.14), channel_id=1, source_target_pairs={{0,8},{1,9},{2,10},{3,11},{4,12},{5,13},{6,14},{7,15},{8,0},{9,1},... | collective-permute-start | bytes 122888 | tf_op jit(solution)/shard_map/ppermute | solution.py:32
  81.4 4.5 %collective-permute-start.9 = (bf16[2,80,256]{2,1,0:T(8,128)(2,1)S(1)}, bf16[2,80,256]{2,1,0:T(8,128)(2,1)S(1)}, u32[]{:S(2)}, u32[]{:S(2)}) collective-permute-start(bf16[2,80,256]{2,1,0:T(8,128)(2,1)S(1)} %pad_maximum_fusion.8), channel_id=1, source_target_pairs={{0,4},{1,5},{2,6},{3,7},{4,0},{5,1},{6,2},{7,3},{8,12},{9,13},{10,... | collective-permute-start | bytes 245768 | tf_op jit(solution)/shard_map/ppermute | solution.py:32
  85.9 5.4 %collective-permute-start.10 = (bf16[4,80,256]{2,1,0:T(8,128)(2,1)S(1)}, bf16[4,80,256]{2,1,0:T(8,128)(2,1)S(1)}, u32[]{:S(2)}, u32[]{:S(2)}) collective-permute-start(bf16[4,80,256]{2,1,0:T(8,128)(2,1)S(1)} %pad_maximum_fusion.5), channel_id=1, source_target_pairs={{0,2},{1,3},{2,0},{3,1},{4,6},{5,7},{6,4},{7,5},{8,10},{9,11},{10,... | collective-permute-start | bytes 491528 | tf_op jit(solution)/shard_map/ppermute | solution.py:32
  91.3 1.7 %collective-permute-start.11 = (bf16[8,80,256]{2,1,0:T(8,128)(2,1)S(1)}, bf16[8,80,256]{2,1,0:T(8,128)(2,1)S(1)}, u32[]{:S(2)}, u32[]{:S(2)}) collective-permute-start(bf16[8,80,256]{2,1,0:T(8,128)(2,1)S(1)} %pad_maximum_fusion.2), channel_id=1, source_target_pairs={{0,1},{1,0},{2,3},{3,2},{4,5},{5,4},{6,7},{7,6},{8,9},{9,8},{10,11... | collective-permute-start | bytes 983048 | tf_op jit(solution)/shard_map/ppermute | solution.py:32

commit v2 on v1

v2 whole, which is shorter than its diff:
```python
import functools
import math

import jax
import jax.numpy as jnp
from jax import lax
from jax.experimental import pallas as pl
from jax.experimental.pallas import tpu as pltpu
from jax.sharding import PartitionSpec as P

GAMMA = 0.98
LAMBDA = 1.0
EPS = 1e-06
BF = jnp.bfloat16
F32 = jnp.float32
GROUP = (0, 2, 1, 3)
PAD = 16


def dot(left, right):
    return jnp.dot(left, right, preferred_element_type=F32)


def dot_t(left, right):
    return lax.dot_general(left, right, (((0,), (0,)), ((), ())), preferred_element_type=F32)


def halves(array):
    high = array.astype(BF)
    return high, (array - high.astype(F32)).astype(BF)


def swap(array, mask, size):
    return lax.ppermute(array, "fa", [(i, i ^ mask) for i in range(size)])


def reverse_bits(value, bits):
    out = value * 0
    for k in range(bits):
        out = out + (((value >> k) & 1) << (bits - 1 - k))
    return out


def columns_of(row, rows):
    return jnp.transpose(jnp.broadcast_to(row, (rows, rows)))


def feature_kernel(
    quarter_ref, hf_ref, ht_ref, wf_ref, wt_ref, lat_ref, ids_ref, pos_ref, far_ref, near_ref, own_ref
):
    rows = hf_ref.shape[0]
    width = wf_ref.shape[1]
    cut = hf_ref.shape[1] // 4
    ids = columns_of(ids_ref[...].astype(F32), rows)
    lanes = lax.broadcasted_iota(jnp.int32, (rows, rows), 1).astype(F32)
    zrows = jnp.zeros((rows, width), F32)
    tiles = [
        jnp.where(ids == lanes + float(t * rows), 1.0, 0.0).astype(BF)
        for t in range(lat_ref.shape[0] // rows)
    ]
    zrows = dot(jnp.concatenate(tiles, axis=1), lat_ref[...])
    feat = (dot(hf_ref[...], wf_ref[...]) + zrows).astype(BF)
    feat_t = (dot(ht_ref[...], wt_ref[...]) + zrows).astype(BF)
    pos = pos_ref[...]
    line = lax.broadcasted_iota(jnp.int32, (PAD, rows), 0)
    high = jnp.broadcast_to(lax.shift_right_logical(pos, 7).astype(F32), (PAD, rows))
    low = jnp.broadcast_to((pos & 127).astype(F32), (PAD, rows))
    coded = jnp.where(line == 0, high, jnp.where(line == 1, low, 0.0)).astype(BF)
    for ref, start in ((far_ref, rows), (near_ref, 0)):
        ref[start : start + rows, :] = feat
        ref[start + rows : start + 2 * rows, :] = feat_t
        ref[start + 2 * rows : start + 2 * rows + PAD, :] = jnp.zeros((PAD, width), BF)
        ref[start + 2 * rows : start + 2 * rows + PAD, :rows] = coded

    def piece(slot):
        return hf_ref[:, pl.ds(pl.multiple_of(quarter_ref[slot] * cut, cut), cut)]

    end = 2 * rows + PAD
    own_ref[...] = piece(0)
    far_ref[:rows, :] = piece(1)
    near_ref[end : end + rows, :] = piece(2)
    far_ref[rows + end : 2 * rows + end, :] = piece(3)


def pair_kernel(
    base_ref,
    place_ref,
    hb0_ref,
    hb2_ref,
    hb1_ref,
    hb3_ref,
    own_ref,
    ff0_ref,
    ff2_ref,
    ff1_ref,
    ff3_ref,
    wb_ref,
    keep_ref,
    send_ref,
    raw_ref,
    back_ref,
    smat_ref,
    pick_ref,
    wfq_ref,
    wbq_ref,
    *,
    rows,
    total,
    chunk,
):
    width = wb_ref.shape[1]
    pairs = float(total * (total - 1))
    groups = total // (4 * rows)
    hb_refs = (hb0_ref, hb2_ref, hb1_ref, hb3_ref)
    each = hb0_ref.shape[0]
    steps = each // chunk
    tiles = chunk // rows
    wb = wb_ref[...]
    end = 2 * rows + PAD
    parts = ((ff0_ref, 0), (ff2_ref, rows), (ff1_ref, 0), (ff3_ref, rows))
    wanted = []
    for ref, start in parts:
        code = ref[start + 2 * rows : start + end, :rows].astype(F32)
        wanted.append(columns_of(code[0:1] * 128.0 + code[1:2], rows))
    lanes = lax.broadcasted_iota(jnp.int32, (rows, rows), 1)

    def embed(hidden):
        raw = dot(hidden, wb)
        scale = lax.rsqrt(jnp.mean(raw * raw, axis=-1, keepdims=True) + EPS)
        return raw, scale, (raw * scale).astype(BF)

    def through(grad, raw, scale):
        along = jnp.sum(grad * raw, axis=-1, keepdims=True)
        return (scale * grad - scale * scale * scale * (1.0 / width) * along * raw).astype(BF)

    def over_rows(step):
        for number, ref in enumerate(hb_refs):
            if steps == 1:
                step(number, ref, 0)
            else:
                lax.fori_loop(0, steps, lambda i, c: (step(number, ref, i), c)[1], 0)

    def at(number, index):
        return pl.ds(pl.multiple_of(number * each + index * chunk, chunk), chunk)

    smat_ref[...] = jnp.zeros_like(smat_ref)
    pick_ref[...] = jnp.zeros_like(pick_ref)
    wbq_ref[...] = jnp.zeros_like(wbq_ref)

    def first(number, ref, index):
        hidden = ref[pl.ds(pl.multiple_of(index * chunk, chunk), chunk), :]
        raw, _, back = embed(hidden)
        raw_ref[at(number, index), :] = raw
        back_ref[at(number, index), :] = back
        smat_ref[...] += dot_t(back, back)
        ids = [
            (lanes + base_ref[(number * steps + index) * tiles + t]).astype(F32) for t in range(tiles)
        ]
        mask = jnp.concatenate(
            [
                jnp.concatenate([jnp.where(want == i, 1.0, 0.0).astype(BF) for i in ids], axis=1)
                for want in wanted
            ],
            axis=0,
        )
        pick_ref[...] += dot(mask, hidden)

    over_rows(first)
    smat = smat_ref[...]
    s_hi, s_lo = halves(smat)
    kmat = jnp.zeros((width, width), F32)
    wfq = jnp.zeros((own_ref.shape[1], width), F32)
    sums = jnp.sum(smat * smat) / groups / (2.0 * pairs)
    cuts = (own_ref, (ff2_ref, 0), (ff1_ref, end), (ff3_ref, rows + end))
    for g, (ref, start) in enumerate(parts):
        feat = ref[start : start + rows, :]
        f32feat = feat.astype(F32)
        diff = f32feat - GAMMA * ref[start + rows : start + 2 * rows, :].astype(F32)
        d_hi, d_lo = halves(diff)
        hidden = pick_ref[g * rows : (g + 1) * rows, :].astype(BF)
        raw, scale, back = embed(hidden)
        ob = back.astype(F32)
        ds = dot(d_hi, s_hi) + dot(d_lo, s_hi) + dot(d_hi, s_lo)
        db = jnp.sum(diff * ob, axis=-1, keepdims=True)
        coef = db * (1.0 / pairs) + 1.0 / total
        norm = jnp.sum(ob * ob, axis=-1, keepdims=True)
        grad_f = (ds * (1.0 / pairs) - coef * ob).astype(BF)
        piece = cuts[g][...] if g == 0 else cuts[g][0][cuts[g][1] : cuts[g][1] + rows, :]
        wfq = wfq + dot_t(piece, grad_f)
        kmat = kmat + dot_t(d_hi, feat) + dot_t(d_lo, feat)
        sums = sums + (
            (jnp.sum(diff * ds) - jnp.sum(db * db) - LAMBDA * jnp.sum(norm * norm)) / (2.0 * pairs)
            - (jnp.sum(f32feat * ob) + LAMBDA * jnp.sum(norm)) / total
        )
        grad_own = through(
            -coef * f32feat - (norm * (2.0 * LAMBDA / pairs) + 2.0 * LAMBDA / total) * ob, raw, scale
        )
        wbq_ref[...] += dot_t(hidden, grad_own)
    wfq_ref[...] = wfq
    a_hi, a_lo = halves((kmat + (2.0 * LAMBDA / groups) * smat) * (1.0 / pairs))

    def second(number, ref, index):
        raw = raw_ref[at(number, index), :]
        back = back_ref[at(number, index), :]
        scale = lax.rsqrt(jnp.mean(raw * raw, axis=-1, keepdims=True) + EPS)
        grad = through(dot(back, a_hi) + dot(back, a_lo), raw, scale)
        hidden = ref[pl.ds(pl.multiple_of(index * chunk, chunk), chunk), :]
        wbq_ref[...] += dot_t(hidden, grad)

    over_rows(second)
    quarter, mine = place_ref[0], place_ref[1]
    wf_rows = wfq_ref.shape[0] // 4
    wb_rows = wbq_ref.shape[0] // 16
    size = wf_rows + wb_rows
    for ref, half in ((keep_ref, mine), (send_ref, 1 - mine)):
        for t in range(2):
            ref[t * size : t * size + wf_rows, :] = wfq_ref[
                pl.ds(pl.multiple_of((half * 2 + t) * wf_rows, wf_rows), wf_rows), :
            ]
            ref[t * size + wf_rows : (t + 1) * size, :] = wbq_ref[
                pl.ds(pl.multiple_of((quarter * 4 + half * 2 + t) * wb_rows, wb_rows), wb_rows), :
            ]
        ref[2 * size : 2 * size + 8, :] = jnp.full((8, width), sums, F32)


def assemble_kernel(place_ref, near_ref, far_ref, wf_ref, wb_ref, *, wf_rows, wb_rows, factor_f, factor_b):
    place = place_ref[0]
    for offset, ref in ((0, near_ref), (8, far_ref)):
        for e in range(8):
            to = place ^ (offset + e)
            wf_ref[pl.ds(pl.multiple_of(to * wf_rows, wf_rows), wf_rows), :] = (
                ref[e, :wf_rows, :].astype(F32) * factor_f
            )
            wb_ref[pl.ds(pl.multiple_of(to * wb_rows, wb_rows), wb_rows), :] = (
                ref[e, wf_rows:, :].astype(F32) * factor_b
            )


SMEM = pl.BlockSpec(memory_space=pltpu.SMEM)
VMEM = pl.BlockSpec(memory_space=pltpu.VMEM)


def body(hidden_f, hidden_t, hidden_b, w_f, w_t, w_b, latents, latent_ids, positives):
    rows, high = hidden_f.shape
    wide = hidden_b.shape[1]
    width = w_f.shape[1]
    size = lax.axis_size("fa")
    bits = size.bit_length() - 1
    outer = [1 << k for k in range(2, bits)]
    me = lax.axis_index("fa")
    total = size * rows
    cut = high // 4
    assert bits >= 4 and size == 1 << bits and cut == width

    hb0 = hidden_b
    for mask in reversed(outer):
        hb0 = jnp.concatenate([hb0, swap(hb0, mask, size)], axis=0)
    quarters = jnp.stack([reverse_bits((me ^ m) & 3, 2) for m in GROUP]).astype(jnp.int32)
    far, near, own = pl.pallas_call(
        feature_kernel,
        in_specs=[SMEM] + [VMEM] * 7,
        out_specs=[VMEM] * 3,
        out_shape=[
            jax.ShapeDtypeStruct((4 * rows + PAD, width), BF),
            jax.ShapeDtypeStruct((3 * rows + PAD, width), BF),
            jax.ShapeDtypeStruct((rows, width), BF),
        ],
        compiler_params=pltpu.CompilerParams(vmem_limit_bytes=24 * 2**20),
        cost_estimate=pl.CostEstimate(
            flops=4 * rows * high * width, bytes_accessed=4 * high * (rows + width), transcendentals=0
        ),
    )(
        quarters,
        hidden_f,
        hidden_t,
        w_f,
        w_t,
        latents,
        latent_ids.reshape(1, rows),
        positives.reshape(1, rows),
    )
    ff2 = swap(far, 2, size)
    ff1 = swap(near, 1, size)
    hb2 = swap(hb0, 2, size)
    hb1 = swap(hb0, 1, size)
    ff3 = swap(ff2, 1, size)
    hb3 = swap(hb2, 1, size)

    inner = reverse_bits(jnp.arange(size // 4, dtype=jnp.int32), bits - 2) << 2
    bases = jnp.concatenate([(me ^ m ^ inner) * rows for m in GROUP]).astype(jnp.int32)
    places = jnp.stack([quarters[0], ((me >> 2) & 1).astype(jnp.int32)])
    each = cut // 4 + wide // 16
    chunk = min(4 * rows, (size // 4) * rows)
    keep, send = pl.pallas_call(
        functools.partial(pair_kernel, rows=rows, total=total, chunk=chunk),
        in_specs=[SMEM] * 2 + [VMEM] * 10,
        out_specs=[VMEM] * 2,
        out_shape=[jax.ShapeDtypeStruct((2 * each + 8, width), F32)] * 2,
        scratch_shapes=[
            pltpu.VMEM((total, width), F32),
            pltpu.VMEM((total, width), BF),
            pltpu.VMEM((width, width), F32),
            pltpu.VMEM((4 * rows, wide), F32),
            pltpu.VMEM((cut, width), F32),
            pltpu.VMEM((wide, width), F32),
        ],
        compiler_params=pltpu.CompilerParams(vmem_limit_bytes=52 * 2**20),
    )(bases, places, hb0, hb2, hb1, hb3, own, near, ff2, ff1, ff3, w_b)

    current = keep + swap(send, outer[0], size)
    mine = (me >> 3) & 1
    note = current[2 * each :]
    keep = jnp.concatenate([lax.dynamic_slice_in_dim(current, mine * each, each, 0), note])
    send = jnp.concatenate([lax.dynamic_slice_in_dim(current, (1 - mine) * each, each, 0), note])
    current = keep + swap(send, outer[1], size)
    for mask in outer[2:]:
        current = current + swap(current, mask, size)
    result = current[:each].astype(BF).reshape(1, each, width)
    for mask in (8, 4, 2):
        result = jnp.concatenate([result, swap(result, mask, size)], axis=0)
    other = swap(result, 1, size)
    place = reverse_bits(me & 15, 4).astype(jnp.int32).reshape(1)
    grad_wf, grad_wb = pl.pallas_call(
        functools.partial(
            assemble_kernel,
            wf_rows=cut // 4,
            wb_rows=wide // 16,
            factor_f=math.sqrt(high),
            factor_b=math.sqrt(wide),
        ),
        in_specs=[SMEM, VMEM, VMEM],
        out_specs=[VMEM] * 2,
        out_shape=[
            jax.ShapeDtypeStruct((high, width), F32),
            jax.ShapeDtypeStruct((wide, width), F32),
        ],
        compiler_params=pltpu.CompilerParams(vmem_limit_bytes=16 * 2**20),
    )(place, result, other)
    return (grad_wf, grad_wb, current[each, :1] / width)


def solution(mesh):
    placed = (
        P(("grp", "fa"), None),
        P(("grp", "fa"), None),
        P(("grp", "fa"), None),
        P(),
        P(),
        P(),
        P("grp", None),
        P(("grp", "fa")),
        P(("grp", "fa")),
    )
    return jax.shard_map(
        body,
        mesh=mesh,
        in_specs=placed,
        out_specs=(P("grp", None), P("grp", None), P("grp")),
        check_vma=False,
    )
```

time: 95.8 us -> 65.6 us (0.68)
  matrix products: 17.3 us -> 0 us
  Pallas kernels: 1.14 us -> 8.29 us
  starting transfers between devices: 18.4 us -> 12.4 us
  other arithmetic: 5.46 us -> 0.36 us
  between operations: 7.39 us -> 2.56 us
  local copies, waits for them, and re-layouts: 9.58 us -> 6.18 us
    dot_general x17 -> x0, matrix products: 17.3 us -> none  [the longest x11 11.5 us: dot(): return jnp.dot(left, right, preferred_element_type=F32)]
    pallas_call x1 -> x3, Pallas kernels: 1.14 us -> 8.29 us  [the longest x1 6.23 us: body(): pl.pallas_call(functools.partial(pair_kernel, rows=rows, total=total, chu...]
    ppermute x12 -> x14, starting transfers between devices: 18.4 us -> 12.4 us  [swap(): return lax.ppermute(array, 'fa', [(i, i ^ mask) for i in range(size)])]
    reduce_sum x2 -> x0, other arithmetic: 2.69 us -> none  [the longest x1 1.44 us: body(): jnp.sum(f32feat * ob) / total]
    dot_general x1 -> x0, local copies, waits for them, and re-layouts: 2.55 us -> none  [dot_t(): lax.dot_general(left, right, (((0,), (0,)), ((), ())), preferred_element_...]
    concatenate x3 -> x1, local copies, waits for them, and re-layouts: 1.73 us -> 0.01 us  [body(): hb0 = jnp.concatenate([hb0, swap(hb0, mask, size)], axis=0)]
    add x7 -> x2, other arithmetic: 1.64 us -> 0.04 us  [the longest x1 0.02 us: body(): current = keep + swap(send, outer[0], size)]
    unnamed x47 -> x24, local copies, waits for them, and re-layouts: 4.13 us -> 5.63 us
  transfers between devices with their start and end apart: 12 -> 14, of which waited for: 11 -> 10; matrix products, arithmetic and copies ran while one was open for 8% -> 1% of each run, Pallas kernels for 0% -> 1%
where the time goes in v2:
time: 65.6 us; the launch traced here: 65.3 us
  waiting for transfers between devices  35.5 us (54%)
  starting transfers between devices  12.4 us (19%)
  Pallas kernels  8.29 us (13%)
  local copies, waits for them, and re-layouts  6.18 us (9%)
  between operations  2.56 us (4%)
    ppermute x14, waiting for transfers between devices, swap(): return lax.ppermute(array, 'fa', [(i, i ^ mask) for i in range(size)])  35.5 us
    ppermute x14, starting transfers between devices, swap(): return lax.ppermute(array, 'fa', [(i, i ^ mask) for i in range(size)])  12.4 us
    pallas_call x1, Pallas kernels, body(): pl.pallas_call(functools.partial(pair_kernel, rows=rows, total=total, chu...  6.23 us
    unnamed x24, local copies, waits for them, and re-layouts  5.63 us
  transfers between devices with their start and end apart: 14, of which 10 were waited for; matrix products, arithmetic and copies ran while one was open for 1% of the time, Pallas kernels for 1%

profile of v2, /device:TPU:0, one launch (start us, length us, event | category | flops | bytes accessed | tf_op | source)
XLA Modules:
  0.0 65.3 jit_solution(9704532858448164163)
XLA Ops:
  0.6 4.1 %collective-permute-start = (bf16[128,256]{1,0:T(8,128)(2,1)}, bf16[128,256]{1,0:T(8,128)(2,1)S(1)}, u32[]{:S(2)}, u32[]{:S(2)}) collective-permute-start(bf16[128,256]{1,0:T(8,128)(2,1)} %param.11), channel_id=1, source_target_pairs={{0,8},{1,9},{2,10},{3,11},{4,12},{5,13},{6,14},{7,15},{8,0},{9,1},... | collective-permute-start | bytes 196616 | tf_op jit(solution)/shard_map/ppermute | solution.py:34
  4.7 0.1 pad_add_fusion.2.quarter_ref
  4.8 0.0 copy-start.6
  4.8 0.0 copy-start.7
  4.8 0.7 copy-done.6
  5.5 0.0 copy-done.7
  5.5 0.0 copy-start
  5.5 1.0 %copy-done = bf16[1024,256]{1,0:T(8,128)(2,1)S(1)} copy-done((bf16[1024,256]{1,0:T(8,128)(2,1)S(1)}, bf16[1024,256]{1,0:T(8,128)(2,1)}, u32[]{:S(2)}) %copy-start) | copy-done | bytes 524312
  6.5 0.0 copy-start.1
  6.5 1.0 %copy-done.1 = bf16[1024,256]{1,0:T(8,128)(2,1)S(1)} copy-done((bf16[1024,256]{1,0:T(8,128)(2,1)S(1)}, bf16[1024,256]{1,0:T(8,128)(2,1)}, u32[]{:S(2)}) %copy-start.1) | copy-done | bytes 524312
  7.6 0.0 copy-start.2
  7.6 0.9 %copy-done.2 = bf16[128,1024]{1,0:T(8,128)(2,1)S(1)} copy-done((bf16[128,1024]{1,0:T(8,128)(2,1)S(1)}, bf16[128,1024]{1,0:T(8,128)(2,1)}, u32[]{:S(2)}) %copy-start.2) | copy-done | bytes 262168
  8.5 0.0 copy-start.3
  8.5 0.9 %copy-done.3 = bf16[128,1024]{1,0:T(8,128)(2,1)S(1)} copy-done((bf16[128,1024]{1,0:T(8,128)(2,1)S(1)}, bf16[128,1024]{1,0:T(8,128)(2,1)}, u32[]{:S(2)}) %copy-start.3) | copy-done | bytes 262168
  9.5 0.0 copy-start.4
  9.5 0.9 %copy-done.4 = bf16[512,256]{1,0:T(8,128)(2,1)S(1)} copy-done((bf16[512,256]{1,0:T(8,128)(2,1)S(1)}, bf16[512,256]{1,0:T(8,128)(2,1)}, u32[]{:S(2)}) %copy-start.4) | copy-done | bytes 262168
  10.4 0.0 copy-start.10
  10.4 0.9 %shard_map.112 = (bf16[528,256]{1,0:T(8,128)(2,1)S(1)}, bf16[400,256]{1,0:T(8,128)(2,1)S(1)}, bf16[128,256]{1,0:T(8,128)(2,1)S(1)}) custom-call(s32[4]{0:T(128)S(1)} %pad_add_fusion.2.quarter_ref, bf16[128,1024]{1,0:T(8,128)(2,1)S(1)} %copy-done.2, bf16[128,1024]{1,0:T(8,128)(2,1)S(1)} %copy-done.3, bf16[1024,256]{1,0:T(8,128)(2,1)S(1)} %copy-done, ...), custom_call_target="tpu_custom_call" | custom-call | flops 134217728 | bytes 1572864 | tf_op jit(solution)/shard_map/pallas_call | solution.py:259
  11.3 1.6 %collective-permute-start.5 = (bf16[528,256]{1,0:T(8,128)(2,1)S(1)}, bf16[528,256]{1,0:T(8,128)(2,1)S(1)}, u32[]{:S(2)}, u32[]{:S(2)}) collective-permute-start(bf16[528,256]{1,0:T(8,128)(2,1)S(1)} %get-tuple-element.12), channel_id=1, source_target_pairs={{0,2},{1,3},{2,0},{3,1},{4,6},{5,7},{6,4},{7,5},{8,10},{9,11},{10,... | collective-permute-start | bytes 811016 | tf_op jit(solution)/shard_map/ppermute | solution.py:34
  12.9 0.0 collective-permute-done
  12.9 0.0 copy-done.10
  13.0 1.6 %collective-permute-start.1 = (bf16[256,256]{1,0:T(8,128)(2,1)S(1)}, bf16[256,256]{1,0:T(8,128)(2,1)S(1)}, u32[]{:S(2)}, u32[]{:S(2)}) collective-permute-start(bf16[256,256]{1,0:T(8,128)(2,1)S(1)} %pad_maximum_fusion.2), channel_id=1, source_target_pairs={{0,4},{1,5},{2,6},{3,7},{4,0},{5,1},{6,2},{7,3},{8,12},{9,13},{10,... | collective-permute-start | bytes 393224 | tf_op jit(solution)/shard_map/ppermute | solution.py:34
  14.6 0.0 copy-start.5
  14.6 3.4 %collective-permute-done.1 = bf16[256,256]{1,0:T(8,128)(2,1)S(1)} collective-permute-done((bf16[256,256]{1,0:T(8,128)(2,1)S(1)}, bf16[256,256]{1,0:T(8,128)(2,1)S(1)}, u32[]{:S(2)}, u32[]{:S(2)}) %collective-permute-start.1) | collective-permute-done | bytes 131104 | tf_op jit(solution)/shard_map/ppermute | solution.py:34
  18.0 0.6 collective-permute-start.2
  18.6 0.0 collective-permute-start.6
  18.6 0.5 collective-permute-start.3
  19.1 0.5 collective-permute-done.5.ff2_ref
  19.6 0.0 copy-start.8
  19.6 0.0 collective-permute-start.7
  19.6 5.4 %collective-permute-done.2.hb2_ref = bf16[512,256]{1,0:T(8,128)(2,1)S(1)} collective-permute-done((bf16[512,256]{1,0:T(8,128)(2,1)S(1)}, bf16[512,256]{1,0:T(8,128)(2,1)S(1)}, u32[]{:S(2)}, u32[]{:S(2)}) %collective-permute-start.2) | collective-permute-done | bytes 262176 | tf_op jit(solution)/shard_map/ppermute | solution.py:34
  25.0 0.0 collective-permute-start.4
  25.0 0.1 pad_add_fusion.1.place_ref
  25.1 0.1 pad_add_fusion.base_ref
  25.1 0.0 collective-permute-done.6.ff1_ref
  25.1 0.0 collective-permute-done.3.hb1_ref
  25.1 0.0 collective-permute-done.7.ff3_ref
  25.2 0.0 copy-start.9
  25.2 1.3 %collective-permute-done.4.hb3_ref = bf16[512,256]{1,0:T(8,128)(2,1)S(1)} collective-permute-done((bf16[512,256]{1,0:T(8,128)(2,1)S(1)}, bf16[512,256]{1,0:T(8,128)(2,1)S(1)}, u32[]{:S(2)}, u32[]{:S(2)}) %collective-permute-start.4) | collective-permute-done | bytes 262176 | tf_op jit(solution)/shard_map/ppermute | solution.py:34
  26.5 0.0 copy-done.8
  26.5 0.0 copy-done.9
  26.5 0.0 copy-done.5
  26.5 6.2 %shard_map.113 = (f32[168,256]{1,0:T(8,128)S(1)}, f32[168,256]{1,0:T(8,128)S(1)}) custom-call(s32[16]{0:T(128)S(1)} %pad_add_fusion.base_ref, s32[2]{0:T(128)S(1)} %pad_add_fusion.1.place_ref, bf16[512,256]{1,0:T(8,128)(2,1)S(1)} %constant_dynamic-update-slice_fusion.hb0_ref, bf16[512,256]{1,0:T(8,128)(2,1)S(1)} %collective-permute-done.2.hb2_ref, ...), custom_call_target="tpu_custom_call" | custom-call | tf_op jit(solution)/shard_map/pallas_call | solution.py:294
  32.8 1.6 %collective-permute-start.8 = (f32[168,256]{1,0:T(8,128)S(1)}, f32[168,256]{1,0:T(8,128)S(1)}, u32[]{:S(2)}, u32[]{:S(2)}) collective-permute-start(f32[168,256]{1,0:T(8,128)S(1)} %get-tuple-element.14), channel_id=1, source_target_pairs={{0,4},{1,5},{2,6},{3,7},{4,0},{5,1},{6,2},{7,3},{8,12},{9,13},{10,... | collective-permute-start | bytes 516104 | tf_op jit(solution)/shard_map/ppermute | solution.py:34
  34.4 4.8 %collective-permute-done.8 = f32[168,256]{1,0:T(8,128)S(1)} collective-permute-done((f32[168,256]{1,0:T(8,128)S(1)}, f32[168,256]{1,0:T(8,128)S(1)}, u32[]{:S(2)}, u32[]{:S(2)}) %collective-permute-start.8) | collective-permute-done | bytes 172064 | tf_op jit(solution)/shard_map/ppermute | solution.py:34
  39.3 0.4 collective-permute-start.9
  39.7 6.4 %collective-permute-done.9 = f32[88,256]{1,0:T(8,128)S(1)} collective-permute-done((f32[88,256]{1,0:T(8,128)S(1)}, f32[88,256]{1,0:T(8,128)S(1)}, u32[]{:S(2)}, u32[]{:S(2)}) %collective-permute-start.9) | collective-permute-done | bytes 90144 | tf_op jit(solution)/shard_map/ppermute | solution.py:34
  46.1 0.1 collective-permute-start.10
  46.2 5.2 %collective-permute-done.10 = bf16[1,80,256]{2,1,0:T(8,128)(2,1)S(1)} collective-permute-done((bf16[1,80,256]{2,1,0:T(8,128)(2,1)S(1)}, bf16[1,80,256]{2,1,0:T(8,128)(2,1)S(1)}, u32[]{:S(2)}, u32[]{:S(2)}) %collective-permute-start.10) | collective-permute-done | bytes 40992 | tf_op jit(solution)/shard_map/ppermute | solution.py:34
  51.4 0.2 collective-permute-start.11
  51.6 4.3 %collective-permute-done.11 = bf16[2,80,256]{2,1,0:T(8,128)(2,1)S(1)} collective-permute-done((bf16[2,80,256]{2,1,0:T(8,128)(2,1)S(1)}, bf16[2,80,256]{2,1,0:T(8,128)(2,1)S(1)}, u32[]{:S(2)}, u32[]{:S(2)}) %collective-permute-start.11) | collective-permute-done | bytes 81952 | tf_op jit(solution)/shard_map/ppermute | solution.py:34
  55.9 1.6 %collective-permute-start.12 = (bf16[4,80,256]{2,1,0:T(8,128)(2,1)S(1)}, bf16[4,80,256]{2,1,0:T(8,128)(2,1)S(1)}, u32[]{:S(2)}, u32[]{:S(2)}) collective-permute-start(bf16[4,80,256]{2,1,0:T(8,128)(2,1)S(1)} %pad_maximum_fusion.1), channel_id=1, source_target_pairs={{0,2},{1,3},{2,0},{3,1},{4,6},{5,7},{6,4},{7,5},{8,10},{9,11},{10,... | collective-permute-start | bytes 491528 | tf_op jit(solution)/shard_map/ppermute | solution.py:34
  57.5 3.8 %collective-permute-done.12 = bf16[4,80,256]{2,1,0:T(8,128)(2,1)S(1)} collective-permute-done((bf16[4,80,256]{2,1,0:T(8,128)(2,1)S(1)}, bf16[4,80,256]{2,1,0:T(8,128)(2,1)S(1)}, u32[]{:S(2)}, u32[]{:S(2)}) %collective-permute-start.12) | collective-permute-done | bytes 163872 | tf_op jit(solution)/shard_map/ppermute | solution.py:34
  61.3 0.1 collective-permute-start.13
  61.4 0.5 slice.15
  62.6 0.4 collective-permute-done.13.far_ref
  63.0 1.1 %shard_map.114 = (f32[1024,256]{1,0:T(8,128)}, f32[256,256]{1,0:T(8,128)}) custom-call(s32[1]{0:T(128)} %bitcast.place_ref, bf16[8,80,256]{2,1,0:T(8,128)(2,1)S(1)} %pad_maximum_fusion.near_ref, bf16[8,80,256]{2,1,0:T(8,128)(2,1)S(1)} %collective-permute-done.13.far_ref), custom_call_target="tpu_custom_call" | custom-call | tf_op jit(solution)/shard_map/pallas_call | solution.py:323
  (15 shorter events, 0.2 us)
Async XLA Ops:
  0.6 12.3 %collective-permute-start = (bf16[128,256]{1,0:T(8,128)(2,1)}, bf16[128,256]{1,0:T(8,128)(2,1)S(1)}, u32[]{:S(2)}, u32[]{:S(2)}) collective-permute-start(bf16[128,256]{1,0:T(8,128)(2,1)} %param.11), channel_id=1, source_target_pairs={{0,8},{1,9},{2,10},{3,11},{4,12},{5,13},{6,14},{7,15},{8,0},{9,1},... | collective-permute-start | bytes 196616 | tf_op jit(solution)/shard_map/ppermute | solution.py:34
  4.8 0.7 %copy-start.6 = (s32[128]{0:T(128)S(1)}, s32[128]{0:T(128)}, u32[]{:S(2)}) copy-start(s32[128]{0:T(128)} %param.16) | copy-start | bytes 1540
  4.8 0.7 %copy-start.7 = (s32[128]{0:T(128)S(1)}, s32[128]{0:T(128)}, u32[]{:S(2)}) copy-start(s32[128]{0:T(128)} %param.17) | copy-start | bytes 1540
  5.5 1.0 %copy-start = (bf16[1024,256]{1,0:T(8,128)(2,1)S(1)}, bf16[1024,256]{1,0:T(8,128)(2,1)}, u32[]{:S(2)}) copy-start(bf16[1024,256]{1,0:T(8,128)(2,1)} %wf_ref.1) | copy-start | bytes 1572868
  6.5 1.0 %copy-start.1 = (bf16[1024,256]{1,0:T(8,128)(2,1)S(1)}, bf16[1024,256]{1,0:T(8,128)(2,1)}, u32[]{:S(2)}) copy-start(bf16[1024,256]{1,0:T(8,128)(2,1)} %wt_ref.1) | copy-start | bytes 1572868
  7.6 0.9 %copy-start.2 = (bf16[128,1024]{1,0:T(8,128)(2,1)S(1)}, bf16[128,1024]{1,0:T(8,128)(2,1)}, u32[]{:S(2)}) copy-start(bf16[128,1024]{1,0:T(8,128)(2,1)} %hf_ref.1) | copy-start | bytes 786436
  8.5 0.9 %copy-start.3 = (bf16[128,1024]{1,0:T(8,128)(2,1)S(1)}, bf16[128,1024]{1,0:T(8,128)(2,1)}, u32[]{:S(2)}) copy-start(bf16[128,1024]{1,0:T(8,128)(2,1)} %ht_ref.1) | copy-start | bytes 786436
  9.5 0.9 %copy-start.4 = (bf16[512,256]{1,0:T(8,128)(2,1)S(1)}, bf16[512,256]{1,0:T(8,128)(2,1)}, u32[]{:S(2)}) copy-start(bf16[512,256]{1,0:T(8,128)(2,1)} %lat_ref.1) | copy-start | bytes 786436
  10.4 2.5 %copy-start.10 = (bf16[128,256]{1,0:T(8,128)(2,1)S(1)}, bf16[128,256]{1,0:T(8,128)(2,1)}, u32[]{:S(2)}) copy-start(bf16[128,256]{1,0:T(8,128)(2,1)} %param.11) | copy-start | bytes 196612
  11.3 8.3 %collective-permute-start.5 = (bf16[528,256]{1,0:T(8,128)(2,1)S(1)}, bf16[528,256]{1,0:T(8,128)(2,1)S(1)}, u32[]{:S(2)}, u32[]{:S(2)}) collective-permute-start(bf16[528,256]{1,0:T(8,128)(2,1)S(1)} %get-tuple-element.12), channel_id=1, source_target_pairs={{0,2},{1,3},{2,0},{3,1},{4,6},{5,7},{6,4},{7,5},{8,10},{9,11},{10,... | collective-permute-start | bytes 811016 | tf_op jit(solution)/shard_map/ppermute | solution.py:34
  13.0 5.0 %collective-permute-start.1 = (bf16[256,256]{1,0:T(8,128)(2,1)S(1)}, bf16[256,256]{1,0:T(8,128)(2,1)S(1)}, u32[]{:S(2)}, u32[]{:S(2)}) collective-permute-start(bf16[256,256]{1,0:T(8,128)(2,1)S(1)} %pad_maximum_fusion.2), channel_id=1, source_target_pairs={{0,4},{1,5},{2,6},{3,7},{4,0},{5,1},{6,2},{7,3},{8,12},{9,13},{10,... | collective-permute-start | bytes 393224 | tf_op jit(solution)/shard_map/ppermute | solution.py:34
  14.6 11.9 %copy-start.5 = (bf16[256,256]{1,0:T(8,128)(2,1)S(1)}, bf16[256,256]{1,0:T(8,128)(2,1)}, u32[]{:S(2)}) copy-start(bf16[256,256]{1,0:T(8,128)(2,1)} %wb_ref.1) | copy-start | bytes 393220
  18.0 7.0 %collective-permute-start.2 = (bf16[512,256]{1,0:T(8,128)(2,1)S(1)}, bf16[512,256]{1,0:T(8,128)(2,1)S(1)}, u32[]{:S(2)}, u32[]{:S(2)}) collective-permute-start(bf16[512,256]{1,0:T(8,128)(2,1)S(1)} %constant_dynamic-update-slice_fusion.hb0_ref), channel_id=1, source_target_pairs={{0,2},{1,3},{2,0},{3,1},{4,6},{5,7},{6,4},{7,5},{8,10},{9,11},{10,... | collective-permute-start | bytes 786440 | tf_op jit(solution)/shard_map/ppermute | solution.py:34
  18.6 6.6 %collective-permute-start.6 = (bf16[400,256]{1,0:T(8,128)(2,1)S(1)}, bf16[400,256]{1,0:T(8,128)(2,1)S(1)}, u32[]{:S(2)}, u32[]{:S(2)}) collective-permute-start(bf16[400,256]{1,0:T(8,128)(2,1)S(1)} %get-tuple-element.11.ff0_ref), channel_id=1, source_target_pairs={{0,1},{1,0},{2,3},{3,2},{4,5},{5,4},{6,7},{7,6},{8,9},{9,8},{10,11... | collective-permute-start | bytes 614408 | tf_op jit(solution)/shard_map/ppermute | solution.py:34
  18.6 6.6 %collective-permute-start.3 = (bf16[512,256]{1,0:T(8,128)(2,1)S(1)}, bf16[512,256]{1,0:T(8,128)(2,1)S(1)}, u32[]{:S(2)}, u32[]{:S(2)}) collective-permute-start(bf16[512,256]{1,0:T(8,128)(2,1)S(1)} %constant_dynamic-update-slice_fusion.hb0_ref), channel_id=1, source_target_pairs={{0,1},{1,0},{2,3},{3,2},{4,5},{5,4},{6,7},{7,6},{8,9},{9,8},{10,11... | collective-permute-start | bytes 786440 | tf_op jit(solution)/shard_map/ppermute | solution.py:34
  19.6 6.9 %copy-start.8 = (bf16[528,256]{1,0:T(8,128)(2,1)}, bf16[528,256]{1,0:T(8,128)(2,1)S(1)}, u32[]{:S(2)}) copy-start(bf16[528,256]{1,0:T(8,128)(2,1)S(1)} %collective-permute-done.5.ff2_ref) | copy-start | bytes 811012
  19.6 5.5 %collective-permute-start.7 = (bf16[528,256]{1,0:T(8,128)(2,1)S(1)}, bf16[528,256]{1,0:T(8,128)(2,1)S(1)}, u32[]{:S(2)}, u32[]{:S(2)}) collective-permute-start(bf16[528,256]{1,0:T(8,128)(2,1)S(1)} %collective-permute-done.5.ff2_ref), channel_id=1, source_target_pairs={{0,1},{1,0},{2,3},{3,2},{4,5},{5,4},{6,7},{7,6},{8,9},{9,8},{10,11... | collective-permute-start | bytes 811016 | tf_op jit(solution)/shard_map/ppermute | solution.py:34
  25.0 1.5 %collective-permute-start.4 = (bf16[512,256]{1,0:T(8,128)(2,1)S(1)}, bf16[512,256]{1,0:T(8,128)(2,1)S(1)}, u32[]{:S(2)}, u32[]{:S(2)}) collective-permute-start(bf16[512,256]{1,0:T(8,128)(2,1)S(1)} %collective-permute-done.2.hb2_ref), channel_id=1, source_target_pairs={{0,1},{1,0},{2,3},{3,2},{4,5},{5,4},{6,7},{7,6},{8,9},{9,8},{10,11... | collective-permute-start | bytes 786440 | tf_op jit(solution)/shard_map/ppermute | solution.py:34
  25.2 1.4 %copy-start.9 = (bf16[528,256]{1,0:T(8,128)(2,1)}, bf16[528,256]{1,0:T(8,128)(2,1)S(1)}, u32[]{:S(2)}) copy-start(bf16[528,256]{1,0:T(8,128)(2,1)S(1)} %collective-permute-done.7.ff3_ref) | copy-start | bytes 811012
  32.8 6.5 %collective-permute-start.8 = (f32[168,256]{1,0:T(8,128)S(1)}, f32[168,256]{1,0:T(8,128)S(1)}, u32[]{:S(2)}, u32[]{:S(2)}) collective-permute-start(f32[168,256]{1,0:T(8,128)S(1)} %get-tuple-element.14), channel_id=1, source_target_pairs={{0,4},{1,5},{2,6},{3,7},{4,0},{5,1},{6,2},{7,3},{8,12},{9,13},{10,... | collective-permute-start | bytes 516104 | tf_op jit(solution)/shard_map/ppermute | solution.py:34
  39.3 6.8 %collective-permute-start.9 = (f32[88,256]{1,0:T(8,128)S(1)}, f32[88,256]{1,0:T(8,128)S(1)}, u32[]{:S(2)}, u32[]{:S(2)}) collective-permute-start(f32[88,256]{1,0:T(8,128)S(1)} %pad_maximum_fusion.3), channel_id=1, source_target_pairs={{0,8},{1,9},{2,10},{3,11},{4,12},{5,13},{6,14},{7,15},{8,0},{9,1},... | collective-permute-start | bytes 270344 | tf_op jit(solution)/shard_map/ppermute | solution.py:34
  46.1 5.2 %collective-permute-start.10 = (bf16[1,80,256]{2,1,0:T(8,128)(2,1)S(1)}, bf16[1,80,256]{2,1,0:T(8,128)(2,1)S(1)}, u32[]{:S(2)}, u32[]{:S(2)}) collective-permute-start(bf16[1,80,256]{2,1,0:T(8,128)(2,1)S(1)} %fusion.1), channel_id=1, source_target_pairs={{0,8},{1,9},{2,10},{3,11},{4,12},{5,13},{6,14},{7,15},{8,0},{9,1},... | collective-permute-start | bytes 122888 | tf_op jit(solution)/shard_map/ppermute | solution.py:34
  51.4 4.5 %collective-permute-start.11 = (bf16[2,80,256]{2,1,0:T(8,128)(2,1)S(1)}, bf16[2,80,256]{2,1,0:T(8,128)(2,1)S(1)}, u32[]{:S(2)}, u32[]{:S(2)}) collective-permute-start(bf16[2,80,256]{2,1,0:T(8,128)(2,1)S(1)} %pad_maximum_fusion.5), channel_id=1, source_target_pairs={{0,4},{1,5},{2,6},{3,7},{4,0},{5,1},{6,2},{7,3},{8,12},{9,13},{10,... | collective-permute-start | bytes 245768 | tf_op jit(solution)/shard_map/ppermute | solution.py:34
  55.9 5.4 %collective-permute-start.12 = (bf16[4,80,256]{2,1,0:T(8,128)(2,1)S(1)}, bf16[4,80,256]{2,1,0:T(8,128)(2,1)S(1)}, u32[]{:S(2)}, u32[]{:S(2)}) collective-permute-start(bf16[4,80,256]{2,1,0:T(8,128)(2,1)S(1)} %pad_maximum_fusion.1), channel_id=1, source_target_pairs={{0,2},{1,3},{2,0},{3,1},{4,6},{5,7},{6,4},{7,5},{8,10},{9,11},{10,... | collective-permute-start | bytes 491528 | tf_op jit(solution)/shard_map/ppermute | solution.py:34
  61.3 1.7 %collective-permute-start.13 = (bf16[8,80,256]{2,1,0:T(8,128)(2,1)S(1)}, bf16[8,80,256]{2,1,0:T(8,128)(2,1)S(1)}, u32[]{:S(2)}, u32[]{:S(2)}) collective-permute-start(bf16[8,80,256]{2,1,0:T(8,128)(2,1)S(1)} %pad_maximum_fusion.near_ref), channel_id=1, source_target_pairs={{0,1},{1,0},{2,3},{3,2},{4,5},{5,4},{6,7},{7,6},{8,9},{9,8},{10,11... | collective-permute-start | bytes 983048 | tf_op jit(solution)/shard_map/ppermute | solution.py:34

commit v3 on v2

v3 whole, which is shorter than its diff:
```python
import functools
import math

import jax
import jax.numpy as jnp
from jax import lax
from jax.experimental import pallas as pl
from jax.experimental.pallas import tpu as pltpu
from jax.sharding import PartitionSpec as P

GAMMA = 0.98
LAMBDA = 1.0
EPS = 1e-06
BF = jnp.bfloat16
F32 = jnp.float32
GROUP = (0, 2, 1, 3)
CUT_AT = (0, 0, 0, 1)
HEAD_AT = (0, 2, 1, 2)
PAD = 16
LINE = ((12, 3), (8, 1), (4, 2))


def dot(left, right):
    return jnp.dot(left, right, preferred_element_type=F32)


def dot_t(left, right):
    return lax.dot_general(left, right, (((0,), (0,)), ((), ())), preferred_element_type=F32)


def halves(array):
    high = array.astype(BF)
    return high, (array - high.astype(F32)).astype(BF)


def swap(array, mask, size):
    return lax.ppermute(array, "fa", [(i, i ^ mask) for i in range(size)])


def reverse_bits(value, bits):
    out = value * 0
    for k in range(bits):
        out = out + (((value >> k) & 1) << (bits - 1 - k))
    return out


def columns_of(row, rows):
    return jnp.transpose(jnp.broadcast_to(row, (rows, rows)))


def feature_kernel(
    hf_hbm, ht_hbm, wf_hbm, wt_hbm, lat_hbm, ids_hbm, pos_hbm, out_ref, hf, ht, wf, wt, lat, ids, pos, sems
):
    rows = hf.shape[0]
    width = wf.shape[1]
    moves = [
        pltpu.make_async_copy(source, target, sems.at[k])
        for k, (source, target) in enumerate(
            (
                (ids_hbm, ids),
                (pos_hbm, pos),
                (lat_hbm, lat),
                (hf_hbm, hf),
                (wf_hbm, wf),
                (ht_hbm, ht),
                (wt_hbm, wt),
            )
        )
    ]
    for move in moves:
        move.start()
    for move in moves[:3]:
        move.wait()
    who = columns_of(ids[...].astype(F32), rows)
    lanes = lax.broadcasted_iota(jnp.int32, (rows, rows), 1).astype(F32)
    tiles = [
        jnp.where(who == lanes + float(t * rows), 1.0, 0.0).astype(BF) for t in range(lat.shape[0] // rows)
    ]
    zrows = dot(jnp.concatenate(tiles, axis=1), lat[...])
    place = pos[...]
    line = lax.broadcasted_iota(jnp.int32, (PAD, rows), 0)
    high = jnp.broadcast_to(lax.shift_right_logical(place, 7).astype(F32), (PAD, rows))
    low = jnp.broadcast_to((place & 127).astype(F32), (PAD, rows))
    out_ref[2 * rows :, :] = jnp.zeros((PAD, width), BF)
    out_ref[2 * rows :, :rows] = jnp.where(line == 0, high, jnp.where(line == 1, low, 0.0)).astype(BF)
    moves[3].wait()
    moves[4].wait()
    out_ref[:rows, :] = (dot(hf[...], wf[...]) + zrows).astype(BF)
    moves[5].wait()
    moves[6].wait()
    out_ref[rows : 2 * rows, :] = (dot(ht[...], wt[...]) + zrows).astype(BF)


def pair_kernel(*refs, rows, total):
    base_ref, place_ref = refs[:2]
    head_ref, cut_ref, mails = refs[2], refs[3], refs[4:7]
    tails, feats, wb_ref = refs[7:11], refs[11:15], refs[15]
    keep_ref, sends = refs[16], refs[17:20]
    raw_ref, back_ref, smat_ref, pick_ref, wfq_ref, wbq_ref = refs[20:]
    heads, cuts = (head_ref,) + mails, (cut_ref,) + mails
    width = wb_ref.shape[1]
    pairs = float(total * (total - 1))
    groups = total // (4 * rows)
    span = total // 16
    wb = wb_ref[...]
    wanted = []
    for ref in feats:
        code = ref[2 * rows :, :rows].astype(F32)
        wanted.append(columns_of(code[0:1] * 128.0 + code[1:2], rows))
    lanes = lax.broadcasted_iota(jnp.int32, (rows, rows), 1)

    def embed(hidden):
        raw = dot(hidden, wb)
        scale = lax.rsqrt(jnp.mean(raw * raw, axis=-1, keepdims=True) + EPS)
        return raw, scale, (raw * scale).astype(BF)

    def through(grad, raw, scale):
        along = jnp.sum(grad * raw, axis=-1, keepdims=True)
        return (scale * grad - scale * scale * scale * (1.0 / width) * along * raw).astype(BF)

    def over_rows(step):
        for g in range(4):
            for ref, start, skip, chunk in (
                (heads[g], HEAD_AT[g] * rows, 0, rows),
                (tails[g], 0, span, 3 * rows),
            ):
                first = g * 4 * span + skip
                if span == rows:
                    step(ref, start, first, chunk)
                else:
                    lax.fori_loop(
                        0,
                        span // rows,
                        lambda i, c: (step(ref, start + i * chunk, first + i * chunk, chunk), c)[1],
                        0,
                    )

    def at(start, chunk):
        return pl.ds(pl.multiple_of(start, rows), chunk)

    smat_ref[...] = jnp.zeros_like(smat_ref)
    pick_ref[...] = jnp.zeros_like(pick_ref)
    wbq_ref[...] = jnp.zeros_like(wbq_ref)

    def first(ref, start, number, chunk):
        hidden = ref[at(start, chunk), :]
        raw, _, back = embed(hidden)
        raw_ref[at(number, chunk), :] = raw
        back_ref[at(number, chunk), :] = back
        smat_ref[...] += dot_t(back, back)
        ids = [(lanes + base_ref[number // rows + t]).astype(F32) for t in range(chunk // rows)]
        mask = jnp.concatenate(
            [
                jnp.concatenate([jnp.where(want == i, 1.0, 0.0).astype(BF) for i in ids], axis=1)
                for want in wanted
            ],
            axis=0,
        )
        pick_ref[...] += dot(mask, hidden)

    over_rows(first)
    smat = smat_ref[...]
    s_hi, s_lo = halves(smat)
    kmat = jnp.zeros((width, width), F32)
    wfq = jnp.zeros((cuts[0].shape[1], width), F32)
    sums = jnp.sum(smat * smat) / groups / (2.0 * pairs)
    for g, ref in enumerate(feats):
        feat = ref[:rows, :]
        f32feat = feat.astype(F32)
        diff = f32feat - GAMMA * ref[rows : 2 * rows, :].astype(F32)
        d_hi, d_lo = halves(diff)
        hidden = pick_ref[g * rows : (g + 1) * rows, :].astype(BF)
        raw, scale, back = embed(hidden)
        ob = back.astype(F32)
        ds = dot(d_hi, s_hi) + dot(d_lo, s_hi) + dot(d_hi, s_lo)
        db = jnp.sum(diff * ob, axis=-1, keepdims=True)
        coef = db * (1.0 / pairs) + 1.0 / total
        norm = jnp.sum(ob * ob, axis=-1, keepdims=True)
        grad_f = (ds * (1.0 / pairs) - coef * ob).astype(BF)
        wfq = wfq + dot_t(cuts[g][CUT_AT[g] * rows : (CUT_AT[g] + 1) * rows, :], grad_f)
        kmat = kmat + dot_t(d_hi, feat) + dot_t(d_lo, feat)
        sums = sums + (
            (jnp.sum(diff * ds) - jnp.sum(db * db) - LAMBDA * jnp.sum(norm * norm)) / (2.0 * pairs)
            - (jnp.sum(f32feat * ob) + LAMBDA * jnp.sum(norm)) / total
        )
        grad_own = through(
            -coef * f32feat - (norm * (2.0 * LAMBDA / pairs) + 2.0 * LAMBDA / total) * ob, raw, scale
        )
        wbq_ref[...] += dot_t(hidden, grad_own)
    wfq_ref[...] = wfq
    a_hi, a_lo = halves((kmat + (2.0 * LAMBDA / groups) * smat) * (1.0 / pairs))

    def second(ref, start, number, chunk):
        raw = raw_ref[at(number, chunk), :]
        scale = lax.rsqrt(jnp.mean(raw * raw, axis=-1, keepdims=True) + EPS)
        back = back_ref[at(number, chunk), :]
        grad = through(dot(back, a_hi) + dot(back, a_lo), raw, scale)
        wbq_ref[...] += dot_t(ref[at(start, chunk), :], grad)

    over_rows(second)
    quarter, mine = place_ref[0], place_ref[1]
    wf_rows = wfq_ref.shape[0] // 4
    wb_rows = wbq_ref.shape[0] // 16
    size = wf_rows + wb_rows

    def block(t):
        return (
            wfq_ref[pl.ds(pl.multiple_of(t * wf_rows, wf_rows), wf_rows), :],
            wbq_ref[pl.ds(pl.multiple_of((quarter * 4 + t) * wb_rows, wb_rows), wb_rows), :],
        )

    keep_ref[:wf_rows, :], keep_ref[wf_rows:size, :] = block(mine)
    note = jnp.full((PAD, width), sums, F32)
    keep_ref[size:, :] = note
    line = lax.broadcasted_iota(jnp.int32, (PAD, width), 0)
    n_hi = note.astype(BF)
    n_mid, n_lo = halves(note - n_hi.astype(F32))
    coded = jnp.where(
        line == 0,
        n_hi.astype(F32),
        jnp.where(line == 1, n_mid.astype(F32), jnp.where(line == 2, n_lo.astype(F32), 0.0)),
    ).astype(BF)
    for ref, (_, turn) in zip(sends, LINE):
        part_f, part_b = block(mine ^ turn)
        ref[:wf_rows, :] = part_f.astype(BF)
        ref[wf_rows:size, :] = part_b.astype(BF)
        ref[size:, :] = coded


def assemble_kernel(place_ref, *refs, wf_rows, wb_rows, factor_f, factor_b):
    place = place_ref[0]
    wf_ref, wb_ref = refs[4:]
    for offset, ref in zip((0, 4, 8, 12), refs):
        for e, turn in enumerate((0,) + tuple(turn for _, turn in LINE)):
            to = place ^ (offset + turn)
            wf_ref[pl.ds(pl.multiple_of(to * wf_rows, wf_rows), wf_rows), :] = (
                ref[e, :wf_rows, :].astype(F32) * factor_f
            )
            wb_ref[pl.ds(pl.multiple_of(to * wb_rows, wb_rows), wb_rows), :] = (
                ref[e, wf_rows:, :].astype(F32) * factor_b
            )


SMEM = pl.BlockSpec(memory_space=pltpu.SMEM)
VMEM = pl.BlockSpec(memory_space=pltpu.VMEM)
HBM = pl.BlockSpec(memory_space=pltpu.HBM)


def body(hidden_f, hidden_t, hidden_b, w_f, w_t, w_b, latents, latent_ids, positives):
    rows, high = hidden_f.shape
    wide = hidden_b.shape[1]
    width = w_f.shape[1]
    size = lax.axis_size("fa")
    bits = size.bit_length() - 1
    beyond = [1 << k for k in range(4, bits)]
    me = lax.axis_index("fa")
    total = size * rows
    cut = high // 4
    span = total // 16
    assert bits >= 4 and size == 1 << bits and cut == width == wide

    quarters = [reverse_bits((me ^ m) & 3, 2).astype(jnp.int32) for m in GROUP]
    cut0, cut2, cut1, cut3 = [
        lax.dynamic_slice_in_dim(hidden_f, q * cut, cut, 1) for q in quarters
    ]
    head0 = hidden_b
    for mask in reversed(beyond):
        head0 = jnp.concatenate([head0, swap(head0, mask, size)], axis=0)
    tail0 = jnp.concatenate([swap(head0, mask, size) for mask, _ in LINE], axis=0)
    mail2 = swap(jnp.concatenate([cut2, cut3, head0], axis=0), 2, size)
    mail1 = swap(jnp.concatenate([cut1, head0], axis=0), 1, size)
    mail3 = swap(mail2, 1, size)
    ff0 = pl.pallas_call(
        feature_kernel,
        in_specs=[HBM] * 7,
        out_specs=VMEM,
        out_shape=jax.ShapeDtypeStruct((2 * rows + PAD, width), BF),
        scratch_shapes=[
            pltpu.VMEM(hidden_f.shape, BF),
            pltpu.VMEM(hidden_t.shape, BF),
            pltpu.VMEM(w_f.shape, BF),
            pltpu.VMEM(w_t.shape, BF),
            pltpu.VMEM(latents.shape, BF),
            pltpu.VMEM((1, rows), jnp.int32),
            pltpu.VMEM((1, rows), jnp.int32),
            pltpu.SemaphoreType.DMA((7,)),
        ],
        compiler_params=pltpu.CompilerParams(vmem_limit_bytes=24 * 2**20),
        cost_estimate=pl.CostEstimate(
            flops=4 * rows * high * width, bytes_accessed=4 * high * (rows + width), transcendentals=0
        ),
    )(
        hidden_f,
        hidden_t,
        w_f,
        w_t,
        latents,
        latent_ids.reshape(1, rows),
        positives.reshape(1, rows),
    )
    ff2 = swap(ff0, 2, size)
    ff1 = swap(ff0, 1, size)
    tail2 = swap(tail0, 2, size)
    tail1 = swap(tail0, 1, size)
    ff3 = swap(ff2, 1, size)
    tail3 = swap(tail2, 1, size)

    inner = reverse_bits(jnp.arange(size // 16, dtype=jnp.int32), bits - 4) << 4
    bases = jnp.concatenate(
        [(me ^ m ^ o ^ inner) * rows for m in GROUP for o in (0,) + tuple(o for o, _ in LINE)]
    ).astype(jnp.int32)
    place = reverse_bits(me & 15, 4).astype(jnp.int32)
    places = jnp.stack([quarters[0], place & 3])
    each = cut // 4 + wide // 16
    keep, *sends = pl.pallas_call(
        functools.partial(pair_kernel, rows=rows, total=total),
        in_specs=[SMEM] * 2 + [VMEM] * 14,
        out_specs=[VMEM] * 4,
        out_shape=[jax.ShapeDtypeStruct((each + PAD, width), F32)]
        + [jax.ShapeDtypeStruct((each + PAD, width), BF)] * 3,
        scratch_shapes=[
            pltpu.VMEM((total, width), F32),
            pltpu.VMEM((total, width), BF),
            pltpu.VMEM((width, width), F32),
            pltpu.VMEM((4 * rows, wide), F32),
            pltpu.VMEM((cut, width), F32),
            pltpu.VMEM((wide, width), F32),
        ],
        compiler_params=pltpu.CompilerParams(vmem_limit_bytes=52 * 2**20),
    )(
        bases,
        places,
        head0,
        cut0,
        mail2,
        mail1,
        mail3,
        tail0,
        tail2,
        tail1,
        tail3,
        ff0,
        ff2,
        ff1,
        ff3,
        w_b,
    )

    got = [swap(part, mask, size).astype(F32) for part, (mask, _) in zip(sends, LINE)]
    current = keep[:each] + (got[0][:each] + got[1][:each] + got[2][:each])
    note = keep[each, :1]
    for part in got:
        note = note + (part[each, :1] + part[each + 1, :1] + part[each + 2, :1])
    for mask in beyond:
        current = current + swap(current, mask, size)
        note = note + swap(note, mask, size)
    result = current.astype(BF).reshape(1, each, width)
    pieces = [result] + [swap(result, mask, size) for mask, _ in LINE]
    crossed = [swap(piece, 2, size) for piece in pieces]
    near = jnp.concatenate(pieces, axis=0)
    near_y = jnp.concatenate(crossed, axis=0)
    far = swap(near, 1, size)
    far_y = swap(near_y, 1, size)
    grad_wf, grad_wb = pl.pallas_call(
        functools.partial(
            assemble_kernel,
            wf_rows=cut // 4,
            wb_rows=wide // 16,
            factor_f=math.sqrt(high),
            factor_b=math.sqrt(wide),
        ),
        in_specs=[SMEM] + [VMEM] * 4,
        out_specs=[VMEM] * 2,
        out_shape=[
            jax.ShapeDtypeStruct((high, width), F32),
            jax.ShapeDtypeStruct((wide, width), F32),
        ],
        compiler_params=pltpu.CompilerParams(vmem_limit_bytes=16 * 2**20),
    )(place.reshape(1), near, near_y, far, far_y)
    return (grad_wf, grad_wb, note / width)


def solution(mesh):
    placed = (
        P(("grp", "fa"), None),
        P(("grp", "fa"), None),
        P(("grp", "fa"), None),
        P(),
        P(),
        P(),
        P("grp", None),
        P(("grp", "fa")),
        P(("grp", "fa")),
    )
    return jax.shard_map(
        body,
        mesh=mesh,
        in_specs=placed,
        out_specs=(P("grp", None), P("grp", None), P("grp")),
        check_vma=False,
    )
```

time: 65.6 us -> 66 us (level)
  waiting for transfers between devices: 35.5 us -> 17.2 us
  starting transfers between devices: 12.4 us -> 23.3 us
  between operations: 2.56 us -> 8.32 us
  Pallas kernels: 8.29 us -> 9.99 us
    ppermute x14 -> x24, waiting for transfers between devices: 35.5 us -> 17.2 us  [swap(): return lax.ppermute(array, 'fa', [(i, i ^ mask) for i in range(size)])]
    ppermute x14 -> x24, starting transfers between devices: 12.4 us -> 23.3 us  [swap(): return lax.ppermute(array, 'fa', [(i, i ^ mask) for i in range(size)])]
    unnamed x24 -> x27, local copies, waits for them, and re-layouts: 5.63 us -> 3.27 us
    pallas_call x2, Pallas kernels: 7.15 us -> 8.85 us  [the longest x1 7.85 us: body(): pl.pallas_call(functools.partial(pair_kernel, rows=rows, total=total), in...]
    slice x2 -> x4, local copies, waits for them, and re-layouts: 0.52 us -> 2.16 us  [the longest x3 1.65 us: body(): note = note + (part[each, :1] + part[each + 1, :1] + part[each + 2, :1])]
    dynamic_slice x1, local copies, waits for them, and re-layouts: 0.02 us -> 1.03 us  [body(): lax.dynamic_slice_in_dim(hidden_f, q * cut, cut, 1)]
  transfers between devices with their start and end apart: 14 -> 24, of which waited for: 10 -> 11; matrix products, arithmetic and copies ran while one was open for 1% -> 5% of each run, Pallas kernels for 1% -> 2%
where the time goes in v3:
time: 66 us; the launch traced here: 65.6 us
  starting transfers between devices  23.3 us (35%)
  waiting for transfers between devices  17.2 us (26%)
  Pallas kernels  9.99 us (15%)
  between operations  8.32 us (13%)
  local copies, waits for them, and re-layouts  6.56 us (10%)
    ppermute x24, starting transfers between devices, swap(): return lax.ppermute(array, 'fa', [(i, i ^ mask) for i in range(size)])  23.3 us
    ppermute x24, waiting for transfers between devices, swap(): return lax.ppermute(array, 'fa', [(i, i ^ mask) for i in range(size)])  17.2 us
    pallas_call x1, Pallas kernels, body(): pl.pallas_call(functools.partial(pair_kernel, rows=rows, total=total), in...  7.85 us
    unnamed x27, local copies, waits for them, and re-layouts  3.27 us
    slice x3, local copies, waits for them, and re-layouts, body(): note = note + (part[each, :1] + part[each + 1, :1] + part[each + 2, :1])  1.65 us
  transfers between devices with their start and end apart: 24, of which 11 were waited for; matrix products, arithmetic and copies ran while one was open for 5% of the time, Pallas kernels for 2%

profile of v3, /device:TPU:0, one launch (start us, length us, event | category | flops | bytes accessed | tf_op | source)
XLA Modules:
  0.0 65.6 jit_solution(15067843747526609958)
XLA Ops:
  0.6 4.1 %collective-permute-start.4 = (bf16[128,256]{1,0:T(8,128)(2,1)}, bf16[128,256]{1,0:T(8,128)(2,1)S(1)}, u32[]{:S(2)}, u32[]{:S(2)}) collective-permute-start(bf16[128,256]{1,0:T(8,128)(2,1)} %refs_2_.1), channel_id=1, source_target_pairs={{0,8},{1,9},{2,10},{3,11},{4,12},{5,13},{6,14},{7,15},{8,0},{9,1},... | collective-permute-start | bytes 196616 | tf_op jit(solution)/shard_map/ppermute | solution.py:37
  4.7 1.3 %collective-permute-start.3 = (bf16[128,256]{1,0:T(8,128)(2,1)}, bf16[128,256]{1,0:T(8,128)(2,1)S(1)}, u32[]{:S(2)}, u32[]{:S(2)}) collective-permute-start(bf16[128,256]{1,0:T(8,128)(2,1)} %refs_2_.1), channel_id=1, source_target_pairs={{0,12},{1,13},{2,14},{3,15},{4,8},{5,9},{6,10},{7,11},{8,4},{9,5},... | collective-permute-start | bytes 196616 | tf_op jit(solution)/shard_map/ppermute | solution.py:37
  6.1 0.2 collective-permute-start.5
  6.3 1.0 %constant_dynamic-slice_fusion = (bf16[128,256]{1,0:T(8,128)(2,1)S(1)}, bf16[128,256]{1,0:T(8,128)(2,1)S(1)}, bf16[128,256]{1,0:T(8,128)(2,1)S(1)}, bf16[128,256]{1,0:T(8,128)(2,1)S(1)}) fusion(bf16[128,1024]{1,0:T(8,128)(2,1)} %hf_hbm.1, s32[]{:T(128)S(6)} %select_n.15, s32[]{:T(128)S(6)} %select_n.14, s32[]{:T(128)S(6)} %select_n.13, s32[]{:T(128)S(6)} %select_n.12), kind=kLoop, calls=%fused_computation.15 | loop fusion | bytes 524304 | tf_op jit(solution)/shard_map/dynamic_slice | solution.py:264
  7.3 0.0 copy-start.2
  7.4 0.0 copy-start
  7.4 1.6 %collective-permute-start = (bf16[384,256]{1,0:T(8,128)(2,1)S(1)}, bf16[384,256]{1,0:T(8,128)(2,1)S(1)}, u32[]{:S(2)}, u32[]{:S(2)}) collective-permute-start(bf16[384,256]{1,0:T(8,128)(2,1)S(1)} %pad_maximum_fusion), channel_id=1, source_target_pairs={{0,2},{1,3},{2,0},{3,1},{4,6},{5,7},{6,4},{7,5},{8,10},{9,11},{10,... | collective-permute-start | bytes 589832 | tf_op jit(solution)/shard_map/ppermute | solution.py:37
  9.0 2.2 %collective-permute-done.3 = bf16[128,256]{1,0:T(8,128)(2,1)S(1)} collective-permute-done((bf16[128,256]{1,0:T(8,128)(2,1)}, bf16[128,256]{1,0:T(8,128)(2,1)S(1)}, u32[]{:S(2)}, u32[]{:S(2)}) %collective-permute-start.3) | collective-permute-done | bytes 65568 | tf_op jit(solution)/shard_map/ppermute | solution.py:37
  11.2 0.0 collective-permute-done.4
  11.2 0.1 collective-permute-done.5
  11.3 1.5 %collective-permute-start.6 = (bf16[384,256]{1,0:T(8,128)(2,1)S(1)}, bf16[384,256]{1,0:T(8,128)(2,1)S(1)}, u32[]{:S(2)}, u32[]{:S(2)}) collective-permute-start(bf16[384,256]{1,0:T(8,128)(2,1)S(1)} %constant_dynamic-update-slice_fusion.refs_7_), channel_id=1, source_target_pairs={{0,2},{1,3},{2,0},{3,1},{4,6},{5,7},{6,4},{7,5},{8,10},{9,11},{10,... | collective-permute-start | bytes 589832 | tf_op jit(solution)/shard_map/ppermute | solution.py:37
  12.8 0.6 copy-done.7
  13.5 0.0 copy-done.8
  13.5 0.9 %copy-done.4 = bf16[128,1024]{1,0:T(8,128)(2,1)S(1)} copy-done((bf16[128,1024]{1,0:T(8,128)(2,1)S(1)}, bf16[128,1024]{1,0:T(8,128)(2,1)}, u32[]{:S(2)}) %copy-start.4) | copy-done | bytes 262168
  14.4 0.9 %copy-done.5 = bf16[512,256]{1,0:T(8,128)(2,1)S(1)} copy-done((bf16[512,256]{1,0:T(8,128)(2,1)S(1)}, bf16[512,256]{1,0:T(8,128)(2,1)}, u32[]{:S(2)}) %copy-start.5) | copy-done | bytes 262168
  15.4 1.0 %shard_map.112.refs_11_ = bf16[272,256]{1,0:T(8,128)(2,1)S(1)} custom-call(bf16[128,1024]{1,0:T(8,128)(2,1)S(1)} %copy-done, bf16[128,1024]{1,0:T(8,128)(2,1)S(1)} %copy-done.4, bf16[1024,256]{1,0:T(8,128)(2,1)S(1)} %copy-done.2, bf16[1024,256]{1,0:T(8,128)(2,1)S(1)} %copy-done.3, bf16[512,256]{1,0:T(8,128)(2,1)S(1)} %copy-done.5, s32[1,128]{1,0:T(1,128)S(1)} %bitcast.24, ...), custom_call_target="tpu_custom_call" | custom-call | flops 134217728 | bytes 1572864 | tf_op jit(solution)/shard_map/pallas_call | solution.py:273
  16.4 0.6 collective-permute-start.9
  17.0 0.0 copy-start.6
  17.0 0.1 collective-permute-start.1
  17.1 0.5 collective-permute-start.7
  17.6 0.0 collective-permute-done.refs_4_
  17.6 0.1 collective-permute-start.2
  17.7 0.5 collective-permute-done.6.refs_8_
  18.2 0.0 collective-permute-start.8
  18.2 0.2 collective-permute-done.1.refs_5_
  18.4 0.3 collective-permute-start.10
  18.7 2.8 %collective-permute-done.9.refs_12_ = bf16[272,256]{1,0:T(8,128)(2,1)S(1)} collective-permute-done((bf16[272,256]{1,0:T(8,128)(2,1)S(1)}, bf16[272,256]{1,0:T(8,128)(2,1)S(1)}, u32[]{:S(2)}, u32[]{:S(2)}) %collective-permute-start.9) | collective-permute-done | bytes 139296 | tf_op jit(solution)/shard_map/ppermute | solution.py:37
  21.5 0.0 collective-permute-start.11
  21.5 0.1 concatenate.18.refs_0_
  21.6 0.1 pad_add_fusion.refs_1_
  21.7 0.0 collective-permute-done.10.refs_13_
  21.7 0.0 collective-permute-done.7.refs_9_
  21.7 1.2 %collective-permute-done.11.refs_14_ = bf16[272,256]{1,0:T(8,128)(2,1)S(1)} collective-permute-done((bf16[272,256]{1,0:T(8,128)(2,1)S(1)}, bf16[272,256]{1,0:T(8,128)(2,1)S(1)}, u32[]{:S(2)}, u32[]{:S(2)}) %collective-permute-start.11) | collective-permute-done | bytes 139296 | tf_op jit(solution)/shard_map/ppermute | solution.py:37
  22.9 0.0 collective-permute-done.2.refs_6_
  22.9 0.0 collective-permute-done.8.refs_10_
  22.9 0.7 %copy-done.10 = bf16[384,256]{1,0:T(8,128)(2,1)} copy-done((bf16[384,256]{1,0:T(8,128)(2,1)}, bf16[384,256]{1,0:T(8,128)(2,1)S(1)}, u32[]{:S(2)}) %copy-start.10) | copy-done | bytes 196632
  23.6 7.9 %shard_map.113 = (f32[96,256]{1,0:T(8,128)S(1)}, bf16[96,256]{1,0:T(8,128)(2,1)S(1)}, bf16[96,256]{1,0:T(8,128)(2,1)S(1)}, bf16[96,256]{1,0:T(8,128)(2,1)S(1)}) custom-call(s32[16]{0:T(128)S(1)} %concatenate.18.refs_0_, s32[2]{0:T(128)S(1)} %pad_add_fusion.refs_1_, bf16[128,256]{1,0:T(8,128)(2,1)S(1)} %copy-done.1, ...), custom_call_target="tpu_custom_call" | custom-call | tf_op jit(solution)/shard_map/pallas_call | solution.py:315
  31.4 3.0 %collective-permute-start.12 = (bf16[96,256]{1,0:T(8,128)(2,1)S(1)}, bf16[96,256]{1,0:T(8,128)(2,1)S(1)}, u32[]{:S(2)}, u32[]{:S(2)}) collective-permute-start(bf16[96,256]{1,0:T(8,128)(2,1)S(1)} %get-tuple-element.10), channel_id=1, source_target_pairs={{0,12},{1,13},{2,14},{3,15},{4,8},{5,9},{6,10},{7,11},{8,4},{9,5},... | collective-permute-start | bytes 147464 | tf_op jit(solution)/shard_map/ppermute | solution.py:37
  34.5 0.0 collective-permute-start.13
  34.5 1.4 %collective-permute-start.14 = (bf16[96,256]{1,0:T(8,128)(2,1)S(1)}, bf16[96,256]{1,0:T(8,128)(2,1)S(1)}, u32[]{:S(2)}, u32[]{:S(2)}) collective-permute-start(bf16[96,256]{1,0:T(8,128)(2,1)S(1)} %get-tuple-element.12), channel_id=1, source_target_pairs={{0,4},{1,5},{2,6},{3,7},{4,0},{5,1},{6,2},{7,3},{8,12},{9,13},{10,... | collective-permute-start | bytes 147464 | tf_op jit(solution)/shard_map/ppermute | solution.py:37
  35.9 0.5 slice.46
  36.4 1.0 %collective-permute-done.12 = bf16[96,256]{1,0:T(8,128)(2,1)S(1)} collective-permute-done((bf16[96,256]{1,0:T(8,128)(2,1)S(1)}, bf16[96,256]{1,0:T(8,128)(2,1)S(1)}, u32[]{:S(2)}, u32[]{:S(2)}) %collective-permute-start.12) | collective-permute-done | bytes 49184 | tf_op jit(solution)/shard_map/ppermute | solution.py:37
  37.4 2.3 %collective-permute-done.13 = bf16[96,256]{1,0:T(8,128)(2,1)S(1)} collective-permute-done((bf16[96,256]{1,0:T(8,128)(2,1)S(1)}, bf16[96,256]{1,0:T(8,128)(2,1)S(1)}, u32[]{:S(2)}, u32[]{:S(2)}) %collective-permute-start.13) | collective-permute-done | bytes 49184 | tf_op jit(solution)/shard_map/ppermute | solution.py:37
  39.8 0.7 %collective-permute-start.18 = (bf16[1,80,256]{2,1,0:T(8,128)(2,1)S(1)}, bf16[1,80,256]{2,1,0:T(8,128)(2,1)S(1)}, u32[]{:S(2)}, u32[]{:S(2)}) collective-permute-start(bf16[1,80,256]{2,1,0:T(8,128)(2,1)S(1)} %fusion.2), channel_id=1, source_target_pairs={{0,2},{1,3},{2,0},{3,1},{4,6},{5,7},{6,4},{7,5},{8,10},{9,11},{10,... | collective-permute-start | bytes 122888 | tf_op jit(solution)/shard_map/ppermute | solution.py:37
  40.5 0.7 %collective-permute-start.17 = (bf16[1,80,256]{2,1,0:T(8,128)(2,1)S(1)}, bf16[1,80,256]{2,1,0:T(8,128)(2,1)S(1)}, u32[]{:S(2)}, u32[]{:S(2)}) collective-permute-start(bf16[1,80,256]{2,1,0:T(8,128)(2,1)S(1)} %fusion.2), channel_id=1, source_target_pairs={{0,4},{1,5},{2,6},{3,7},{4,0},{5,1},{6,2},{7,3},{8,12},{9,13},{10,... | collective-permute-start | bytes 122888 | tf_op jit(solution)/shard_map/ppermute | solution.py:37
  41.2 2.6 %collective-permute-start.16 = (bf16[1,80,256]{2,1,0:T(8,128)(2,1)S(1)}, bf16[1,80,256]{2,1,0:T(8,128)(2,1)S(1)}, u32[]{:S(2)}, u32[]{:S(2)}) collective-permute-start(bf16[1,80,256]{2,1,0:T(8,128)(2,1)S(1)} %fusion.2), channel_id=1, source_target_pairs={{0,8},{1,9},{2,10},{3,11},{4,12},{5,13},{6,14},{7,15},{8,0},{9,1},... | collective-permute-start | bytes 122888 | tf_op jit(solution)/shard_map/ppermute | solution.py:37
  43.8 1.1 %collective-permute-start.15 = (bf16[1,80,256]{2,1,0:T(8,128)(2,1)S(1)}, bf16[1,80,256]{2,1,0:T(8,128)(2,1)S(1)}, u32[]{:S(2)}, u32[]{:S(2)}) collective-permute-start(bf16[1,80,256]{2,1,0:T(8,128)(2,1)S(1)} %fusion.2), channel_id=1, source_target_pairs={{0,12},{1,13},{2,14},{3,15},{4,8},{5,9},{6,10},{7,11},{8,4},{9,5},... | collective-permute-start | bytes 122888 | tf_op jit(solution)/shard_map/ppermute | solution.py:37
  44.9 0.6 fusion.5
  45.5 0.7 %collective-permute-done.16 = bf16[1,80,256]{2,1,0:T(8,128)(2,1)S(1)} collective-permute-done((bf16[1,80,256]{2,1,0:T(8,128)(2,1)S(1)}, bf16[1,80,256]{2,1,0:T(8,128)(2,1)S(1)}, u32[]{:S(2)}, u32[]{:S(2)}) %collective-permute-start.16) | collective-permute-done | bytes 40992 | tf_op jit(solution)/shard_map/ppermute | solution.py:37
  46.1 3.5 %collective-permute-done.15 = bf16[1,80,256]{2,1,0:T(8,128)(2,1)S(1)} collective-permute-done((bf16[1,80,256]{2,1,0:T(8,128)(2,1)S(1)}, bf16[1,80,256]{2,1,0:T(8,128)(2,1)S(1)}, u32[]{:S(2)}, u32[]{:S(2)}) %collective-permute-start.15) | collective-permute-done | bytes 40992 | tf_op jit(solution)/shard_map/ppermute | solution.py:37
  49.6 0.1 collective-permute-start.22
  49.7 1.3 %collective-permute-start.21 = (bf16[1,80,256]{2,1,0:T(8,128)(2,1)S(1)}, bf16[1,80,256]{2,1,0:T(8,128)(2,1)S(1)}, u32[]{:S(2)}, u32[]{:S(2)}) collective-permute-start(bf16[1,80,256]{2,1,0:T(8,128)(2,1)S(1)} %collective-permute-done.17), channel_id=1, source_target_pairs={{0,2},{1,3},{2,0},{3,1},{4,6},{5,7},{6,4},{7,5},{8,10},{9,11},{10,... | collective-permute-start | bytes 122888 | tf_op jit(solution)/shard_map/ppermute | solution.py:37
  51.1 0.8 %collective-permute-start.20 = (bf16[1,80,256]{2,1,0:T(8,128)(2,1)S(1)}, bf16[1,80,256]{2,1,0:T(8,128)(2,1)S(1)}, u32[]{:S(2)}, u32[]{:S(2)}) collective-permute-start(bf16[1,80,256]{2,1,0:T(8,128)(2,1)S(1)} %collective-permute-done.16), channel_id=1, source_target_pairs={{0,2},{1,3},{2,0},{3,1},{4,6},{5,7},{6,4},{7,5},{8,10},{9,11},{10,... | collective-permute-start | bytes 122888 | tf_op jit(solution)/shard_map/ppermute | solution.py:37
  51.8 1.3 %collective-permute-start.19 = (bf16[1,80,256]{2,1,0:T(8,128)(2,1)S(1)}, bf16[1,80,256]{2,1,0:T(8,128)(2,1)S(1)}, u32[]{:S(2)}, u32[]{:S(2)}) collective-permute-start(bf16[1,80,256]{2,1,0:T(8,128)(2,1)S(1)} %collective-permute-done.15), channel_id=1, source_target_pairs={{0,2},{1,3},{2,0},{3,1},{4,6},{5,7},{6,4},{7,5},{8,10},{9,11},{10,... | collective-permute-start | bytes 122888 | tf_op jit(solution)/shard_map/ppermute | solution.py:37
  53.1 0.0 collective-permute-done.18
  53.1 2.7 %collective-permute-done.19 = bf16[1,80,256]{2,1,0:T(8,128)(2,1)S(1)} collective-permute-done((bf16[1,80,256]{2,1,0:T(8,128)(2,1)S(1)}, bf16[1,80,256]{2,1,0:T(8,128)(2,1)S(1)}, u32[]{:S(2)}, u32[]{:S(2)}) %collective-permute-start.19) | collective-permute-done | bytes 40992 | tf_op jit(solution)/shard_map/ppermute | solution.py:37
  55.8 0.0 collective-permute-done.20
  55.8 0.0 collective-permute-done.21
  55.9 0.1 collective-permute-start.23
  55.9 0.5 fusion.4
  60.9 0.5 fusion.3
  63.3 0.0 collective-permute-done.22.refs_2_
  63.4 0.0 collective-permute-done.23.refs_3_
  63.4 1.1 %shard_map.114 = (f32[1024,256]{1,0:T(8,128)}, f32[256,256]{1,0:T(8,128)}) custom-call(s32[1]{0:T(128)} %bitcast.place_ref, bf16[4,80,256]{2,1,0:T(8,128)(2,1)S(1)} %pad_maximum_fusion.1.refs_0_, bf16[4,80,256]{2,1,0:T(8,128)(2,1)S(1)} %constant_dynamic-update-slice_fusion.3.refs_1_, bf16[4,80,256]{2,1,0:T(8,128)(2,1)S(1)} %collective-permute-done.22.refs_2_, ...), custom_call_target="tpu_custom_call" | custom-call | tf_op jit(solution)/shard_map/pallas_call | solution.py:364
  (30 shorter events, 0.2 us)
Async XLA Ops:
  0.6 10.5 %collective-permute-start.4 = (bf16[128,256]{1,0:T(8,128)(2,1)}, bf16[128,256]{1,0:T(8,128)(2,1)S(1)}, u32[]{:S(2)}, u32[]{:S(2)}) collective-permute-start(bf16[128,256]{1,0:T(8,128)(2,1)} %refs_2_.1), channel_id=1, source_target_pairs={{0,8},{1,9},{2,10},{3,11},{4,12},{5,13},{6,14},{7,15},{8,0},{9,1},... | collective-permute-start | bytes 196616 | tf_op jit(solution)/shard_map/ppermute | solution.py:37
  4.7 6.4 %collective-permute-start.3 = (bf16[128,256]{1,0:T(8,128)(2,1)}, bf16[128,256]{1,0:T(8,128)(2,1)S(1)}, u32[]{:S(2)}, u32[]{:S(2)}) collective-permute-start(bf16[128,256]{1,0:T(8,128)(2,1)} %refs_2_.1), channel_id=1, source_target_pairs={{0,12},{1,13},{2,14},{3,15},{4,8},{5,9},{6,10},{7,11},{8,4},{9,5},... | collective-permute-start | bytes 196616 | tf_op jit(solution)/shard_map/ppermute | solution.py:37
  6.1 5.2 %collective-permute-start.5 = (bf16[128,256]{1,0:T(8,128)(2,1)}, bf16[128,256]{1,0:T(8,128)(2,1)S(1)}, u32[]{:S(2)}, u32[]{:S(2)}) collective-permute-start(bf16[128,256]{1,0:T(8,128)(2,1)} %refs_2_.1), channel_id=1, source_target_pairs={{0,4},{1,5},{2,6},{3,7},{4,0},{5,1},{6,2},{7,3},{8,12},{9,13},{10,... | collective-permute-start | bytes 196616 | tf_op jit(solution)/shard_map/ppermute | solution.py:37
  6.3 6.5 %copy-start.3 = (bf16[1024,256]{1,0:T(8,128)(2,1)S(1)}, bf16[1024,256]{1,0:T(8,128)(2,1)}, u32[]{:S(2)}) copy-start(bf16[1024,256]{1,0:T(8,128)(2,1)} %wt_hbm.1) | copy-start | bytes 1572868
  6.3 1.0 %copy-start.1 = (bf16[128,256]{1,0:T(8,128)(2,1)S(1)}, bf16[128,256]{1,0:T(8,128)(2,1)}, u32[]{:S(2)}) copy-start(bf16[128,256]{1,0:T(8,128)(2,1)} %refs_2_.1) | copy-start | bytes 196612
  7.3 5.5 %copy-start.2 = (bf16[1024,256]{1,0:T(8,128)(2,1)S(1)}, bf16[1024,256]{1,0:T(8,128)(2,1)}, u32[]{:S(2)}) copy-start(bf16[1024,256]{1,0:T(8,128)(2,1)} %wf_hbm.1) | copy-start | bytes 1572868
  7.4 5.4 %copy-start = (bf16[128,1024]{1,0:T(8,128)(2,1)S(1)}, bf16[128,1024]{1,0:T(8,128)(2,1)}, u32[]{:S(2)}) copy-start(bf16[128,1024]{1,0:T(8,128)(2,1)} %hf_hbm.1) | copy-start | bytes 786436
  7.4 10.2 %collective-permute-start = (bf16[384,256]{1,0:T(8,128)(2,1)S(1)}, bf16[384,256]{1,0:T(8,128)(2,1)S(1)}, u32[]{:S(2)}, u32[]{:S(2)}) collective-permute-start(bf16[384,256]{1,0:T(8,128)(2,1)S(1)} %pad_maximum_fusion), channel_id=1, source_target_pairs={{0,2},{1,3},{2,0},{3,1},{4,6},{5,7},{6,4},{7,5},{8,10},{9,11},{10,... | collective-permute-start | bytes 589832 | tf_op jit(solution)/shard_map/ppermute | solution.py:37
  11.3 6.9 %collective-permute-start.6 = (bf16[384,256]{1,0:T(8,128)(2,1)S(1)}, bf16[384,256]{1,0:T(8,128)(2,1)S(1)}, u32[]{:S(2)}, u32[]{:S(2)}) collective-permute-start(bf16[384,256]{1,0:T(8,128)(2,1)S(1)} %constant_dynamic-update-slice_fusion.refs_7_), channel_id=1, source_target_pairs={{0,2},{1,3},{2,0},{3,1},{4,6},{5,7},{6,4},{7,5},{8,10},{9,11},{10,... | collective-permute-start | bytes 589832 | tf_op jit(solution)/shard_map/ppermute | solution.py:37
  12.8 0.7 copy-start.7
  12.8 0.7 %copy-start.8 = (s32[128]{0:T(128)S(1)}, s32[128]{0:T(128)}, u32[]{:S(2)}) copy-start(s32[128]{0:T(128)} %param.17) | copy-start | bytes 1540
  13.5 0.9 %copy-start.4 = (bf16[128,1024]{1,0:T(8,128)(2,1)S(1)}, bf16[128,1024]{1,0:T(8,128)(2,1)}, u32[]{:S(2)}) copy-start(bf16[128,1024]{1,0:T(8,128)(2,1)} %ht_hbm.1) | copy-start | bytes 786436
  14.4 0.9 %copy-start.5 = (bf16[512,256]{1,0:T(8,128)(2,1)S(1)}, bf16[512,256]{1,0:T(8,128)(2,1)}, u32[]{:S(2)}) copy-start(bf16[512,256]{1,0:T(8,128)(2,1)} %lat_hbm.1) | copy-start | bytes 786436
  16.4 5.1 %collective-permute-start.9 = (bf16[272,256]{1,0:T(8,128)(2,1)S(1)}, bf16[272,256]{1,0:T(8,128)(2,1)S(1)}, u32[]{:S(2)}, u32[]{:S(2)}) collective-permute-start(bf16[272,256]{1,0:T(8,128)(2,1)S(1)} %shard_map.112.refs_11_), channel_id=1, source_target_pairs={{0,2},{1,3},{2,0},{3,1},{4,6},{5,7},{6,4},{7,5},{8,10},{9,11},{10,... | collective-permute-start | bytes 417800 | tf_op jit(solution)/shard_map/ppermute | solution.py:37
  17.0 6.6 %copy-start.6 = (bf16[256,256]{1,0:T(8,128)(2,1)S(1)}, bf16[256,256]{1,0:T(8,128)(2,1)}, u32[]{:S(2)}) copy-start(bf16[256,256]{1,0:T(8,128)(2,1)} %refs_15_.1) | copy-start | bytes 393220
  17.0 1.4 %collective-permute-start.1 = (bf16[256,256]{1,0:T(8,128)(2,1)S(1)}, bf16[256,256]{1,0:T(8,128)(2,1)S(1)}, u32[]{:S(2)}, u32[]{:S(2)}) collective-permute-start(bf16[256,256]{1,0:T(8,128)(2,1)S(1)} %pad_maximum_fusion.2), channel_id=1, source_target_pairs={{0,1},{1,0},{2,3},{3,2},{4,5},{5,4},{6,7},{7,6},{8,9},{9,8},{10,11... | collective-permute-start | bytes 393224 | tf_op jit(solution)/shard_map/ppermute | solution.py:37
  17.1 4.6 %collective-permute-start.7 = (bf16[384,256]{1,0:T(8,128)(2,1)S(1)}, bf16[384,256]{1,0:T(8,128)(2,1)S(1)}, u32[]{:S(2)}, u32[]{:S(2)}) collective-permute-start(bf16[384,256]{1,0:T(8,128)(2,1)S(1)} %constant_dynamic-update-slice_fusion.refs_7_), channel_id=1, source_target_pairs={{0,1},{1,0},{2,3},{3,2},{4,5},{5,4},{6,7},{7,6},{8,9},{9,8},{10,11... | collective-permute-start | bytes 589832 | tf_op jit(solution)/shard_map/ppermute | solution.py:37
  17.6 5.3 %collective-permute-start.2 = (bf16[384,256]{1,0:T(8,128)(2,1)S(1)}, bf16[384,256]{1,0:T(8,128)(2,1)S(1)}, u32[]{:S(2)}, u32[]{:S(2)}) collective-permute-start(bf16[384,256]{1,0:T(8,128)(2,1)S(1)} %collective-permute-done.refs_4_), channel_id=1, source_target_pairs={{0,1},{1,0},{2,3},{3,2},{4,5},{5,4},{6,7},{7,6},{8,9},{9,8},{10,11... | collective-permute-start | bytes 589832 | tf_op jit(solution)/shard_map/ppermute | solution.py:37
  18.2 4.7 %collective-permute-start.8 = (bf16[384,256]{1,0:T(8,128)(2,1)S(1)}, bf16[384,256]{1,0:T(8,128)(2,1)S(1)}, u32[]{:S(2)}, u32[]{:S(2)}) collective-permute-start(bf16[384,256]{1,0:T(8,128)(2,1)S(1)} %collective-permute-done.6.refs_8_), channel_id=1, source_target_pairs={{0,1},{1,0},{2,3},{3,2},{4,5},{5,4},{6,7},{7,6},{8,9},{9,8},{10,11... | collective-permute-start | bytes 589832 | tf_op jit(solution)/shard_map/ppermute | solution.py:37
  18.4 3.3 %collective-permute-start.10 = (bf16[272,256]{1,0:T(8,128)(2,1)S(1)}, bf16[272,256]{1,0:T(8,128)(2,1)S(1)}, u32[]{:S(2)}, u32[]{:S(2)}) collective-permute-start(bf16[272,256]{1,0:T(8,128)(2,1)S(1)} %shard_map.112.refs_11_), channel_id=1, source_target_pairs={{0,1},{1,0},{2,3},{3,2},{4,5},{5,4},{6,7},{7,6},{8,9},{9,8},{10,11... | collective-permute-start | bytes 417800 | tf_op jit(solution)/shard_map/ppermute | solution.py:37
  21.5 1.4 %collective-permute-start.11 = (bf16[272,256]{1,0:T(8,128)(2,1)S(1)}, bf16[272,256]{1,0:T(8,128)(2,1)S(1)}, u32[]{:S(2)}, u32[]{:S(2)}) collective-permute-start(bf16[272,256]{1,0:T(8,128)(2,1)S(1)} %collective-permute-done.9.refs_12_), channel_id=1, source_target_pairs={{0,1},{1,0},{2,3},{3,2},{4,5},{5,4},{6,7},{7,6},{8,9},{9,8},{10,11... | collective-permute-start | bytes 417800 | tf_op jit(solution)/shard_map/ppermute | solution.py:37
  21.7 1.2 %copy-start.9 = (bf16[384,256]{1,0:T(8,128)(2,1)}, bf16[384,256]{1,0:T(8,128)(2,1)S(1)}, u32[]{:S(2)}) copy-start(bf16[384,256]{1,0:T(8,128)(2,1)S(1)} %collective-permute-done.7.refs_9_) | copy-start | bytes 589828
  22.9 0.7 %copy-start.10 = (bf16[384,256]{1,0:T(8,128)(2,1)}, bf16[384,256]{1,0:T(8,128)(2,1)S(1)}, u32[]{:S(2)}) copy-start(bf16[384,256]{1,0:T(8,128)(2,1)S(1)} %collective-permute-done.8.refs_10_) | copy-start | bytes 589828
  31.4 6.0 %collective-permute-start.12 = (bf16[96,256]{1,0:T(8,128)(2,1)S(1)}, bf16[96,256]{1,0:T(8,128)(2,1)S(1)}, u32[]{:S(2)}, u32[]{:S(2)}) collective-permute-start(bf16[96,256]{1,0:T(8,128)(2,1)S(1)} %get-tuple-element.10), channel_id=1, source_target_pairs={{0,12},{1,13},{2,14},{3,15},{4,8},{5,9},{6,10},{7,11},{8,4},{9,5},... | collective-permute-start | bytes 147464 | tf_op jit(solution)/shard_map/ppermute | solution.py:37
  34.5 5.3 %collective-permute-start.13 = (bf16[96,256]{1,0:T(8,128)(2,1)S(1)}, bf16[96,256]{1,0:T(8,128)(2,1)S(1)}, u32[]{:S(2)}, u32[]{:S(2)}) collective-permute-start(bf16[96,256]{1,0:T(8,128)(2,1)S(1)} %get-tuple-element.11), channel_id=1, source_target_pairs={{0,8},{1,9},{2,10},{3,11},{4,12},{5,13},{6,14},{7,15},{8,0},{9,1},... | collective-permute-start | bytes 147464 | tf_op jit(solution)/shard_map/ppermute | solution.py:37
  34.5 5.3 %collective-permute-start.14 = (bf16[96,256]{1,0:T(8,128)(2,1)S(1)}, bf16[96,256]{1,0:T(8,128)(2,1)S(1)}, u32[]{:S(2)}, u32[]{:S(2)}) collective-permute-start(bf16[96,256]{1,0:T(8,128)(2,1)S(1)} %get-tuple-element.12), channel_id=1, source_target_pairs={{0,4},{1,5},{2,6},{3,7},{4,0},{5,1},{6,2},{7,3},{8,12},{9,13},{10,... | collective-permute-start | bytes 147464 | tf_op jit(solution)/shard_map/ppermute | solution.py:37
  39.8 13.3 %collective-permute-start.18 = (bf16[1,80,256]{2,1,0:T(8,128)(2,1)S(1)}, bf16[1,80,256]{2,1,0:T(8,128)(2,1)S(1)}, u32[]{:S(2)}, u32[]{:S(2)}) collective-permute-start(bf16[1,80,256]{2,1,0:T(8,128)(2,1)S(1)} %fusion.2), channel_id=1, source_target_pairs={{0,2},{1,3},{2,0},{3,1},{4,6},{5,7},{6,4},{7,5},{8,10},{9,11},{10,... | collective-permute-start | bytes 122888 | tf_op jit(solution)/shard_map/ppermute | solution.py:37
  40.5 5.0 %collective-permute-start.17 = (bf16[1,80,256]{2,1,0:T(8,128)(2,1)S(1)}, bf16[1,80,256]{2,1,0:T(8,128)(2,1)S(1)}, u32[]{:S(2)}, u32[]{:S(2)}) collective-permute-start(bf16[1,80,256]{2,1,0:T(8,128)(2,1)S(1)} %fusion.2), channel_id=1, source_target_pairs={{0,4},{1,5},{2,6},{3,7},{4,0},{5,1},{6,2},{7,3},{8,12},{9,13},{10,... | collective-permute-start | bytes 122888 | tf_op jit(solution)/shard_map/ppermute | solution.py:37
  41.2 4.9 %collective-permute-start.16 = (bf16[1,80,256]{2,1,0:T(8,128)(2,1)S(1)}, bf16[1,80,256]{2,1,0:T(8,128)(2,1)S(1)}, u32[]{:S(2)}, u32[]{:S(2)}) collective-permute-start(bf16[1,80,256]{2,1,0:T(8,128)(2,1)S(1)} %fusion.2), channel_id=1, source_target_pairs={{0,8},{1,9},{2,10},{3,11},{4,12},{5,13},{6,14},{7,15},{8,0},{9,1},... | collective-permute-start | bytes 122888 | tf_op jit(solution)/shard_map/ppermute | solution.py:37
  43.8 5.8 %collective-permute-start.15 = (bf16[1,80,256]{2,1,0:T(8,128)(2,1)S(1)}, bf16[1,80,256]{2,1,0:T(8,128)(2,1)S(1)}, u32[]{:S(2)}, u32[]{:S(2)}) collective-permute-start(bf16[1,80,256]{2,1,0:T(8,128)(2,1)S(1)} %fusion.2), channel_id=1, source_target_pairs={{0,12},{1,13},{2,14},{3,15},{4,8},{5,9},{6,10},{7,11},{8,4},{9,5},... | collective-permute-start | bytes 122888 | tf_op jit(solution)/shard_map/ppermute | solution.py:37
  49.6 13.7 %collective-permute-start.22 = (bf16[4,80,256]{2,1,0:T(8,128)(2,1)S(1)}, bf16[4,80,256]{2,1,0:T(8,128)(2,1)S(1)}, u32[]{:S(2)}, u32[]{:S(2)}) collective-permute-start(bf16[4,80,256]{2,1,0:T(8,128)(2,1)S(1)} %pad_maximum_fusion.1.refs_0_), channel_id=1, source_target_pairs={{0,1},{1,0},{2,3},{3,2},{4,5},{5,4},{6,7},{7,6},{8,9},{9,8},{10,11... | collective-permute-start | bytes 491528 | tf_op jit(solution)/shard_map/ppermute | solution.py:37
  49.7 6.1 %collective-permute-start.21 = (bf16[1,80,256]{2,1,0:T(8,128)(2,1)S(1)}, bf16[1,80,256]{2,1,0:T(8,128)(2,1)S(1)}, u32[]{:S(2)}, u32[]{:S(2)}) collective-permute-start(bf16[1,80,256]{2,1,0:T(8,128)(2,1)S(1)} %collective-permute-done.17), channel_id=1, source_target_pairs={{0,2},{1,3},{2,0},{3,1},{4,6},{5,7},{6,4},{7,5},{8,10},{9,11},{10,... | collective-permute-start | bytes 122888 | tf_op jit(solution)/shard_map/ppermute | solution.py:37
  51.1 4.8 %collective-permute-start.20 = (bf16[1,80,256]{2,1,0:T(8,128)(2,1)S(1)}, bf16[1,80,256]{2,1,0:T(8,128)(2,1)S(1)}, u32[]{:S(2)}, u32[]{:S(2)}) collective-permute-start(bf16[1,80,256]{2,1,0:T(8,128)(2,1)S(1)} %collective-permute-done.16), channel_id=1, source_target_pairs={{0,2},{1,3},{2,0},{3,1},{4,6},{5,7},{6,4},{7,5},{8,10},{9,11},{10,... | collective-permute-start | bytes 122888 | tf_op jit(solution)/shard_map/ppermute | solution.py:37
  51.8 4.0 %collective-permute-start.19 = (bf16[1,80,256]{2,1,0:T(8,128)(2,1)S(1)}, bf16[1,80,256]{2,1,0:T(8,128)(2,1)S(1)}, u32[]{:S(2)}, u32[]{:S(2)}) collective-permute-start(bf16[1,80,256]{2,1,0:T(8,128)(2,1)S(1)} %collective-permute-done.15), channel_id=1, source_target_pairs={{0,2},{1,3},{2,0},{3,1},{4,6},{5,7},{6,4},{7,5},{8,10},{9,11},{10,... | collective-permute-start | bytes 122888 | tf_op jit(solution)/shard_map/ppermute | solution.py:37
  55.9 7.5 %collective-permute-start.23 = (bf16[4,80,256]{2,1,0:T(8,128)(2,1)S(1)}, bf16[4,80,256]{2,1,0:T(8,128)(2,1)S(1)}, u32[]{:S(2)}, u32[]{:S(2)}) collective-permute-start(bf16[4,80,256]{2,1,0:T(8,128)(2,1)S(1)} %constant_dynamic-update-slice_fusion.3.refs_1_), channel_id=1, source_target_pairs={{0,1},{1,0},{2,3},{3,2},{4,5},{5,4},{6,7},{7,6},{8,9},{9,8},{10,11... | collective-permute-start | bytes 491528 | tf_op jit(solution)/shard_map/ppermute | solution.py:37

commit v4 on v3

--- a/solution.py
+++ b/solution.py
@@ -15,7 +15,8 @@
 F32 = jnp.float32
 GROUP = (0, 2, 1, 3)
 CUT_AT = (0, 0, 0, 1)
-HEAD_AT = (0, 2, 1, 2)
+HEAD_AT = (1, 2, 1, 2)
+FEAT_AT = (2, 3, 2, 3)
 PAD = 16
 LINE = ((12, 3), (8, 1), (4, 2))
 
@@ -49,7 +50,29 @@
 
 
 def feature_kernel(
-    hf_hbm, ht_hbm, wf_hbm, wt_hbm, lat_hbm, ids_hbm, pos_hbm, out_ref, hf, ht, wf, wt, lat, ids, pos, sems
+    quarter_ref,
+    hf_hbm,
+    ht_hbm,
+    hb_hbm,
+    wf_hbm,
+    wt_hbm,
+    wb_hbm,
+    lat_hbm,
+    ids_hbm,
+    pos_hbm,
+    far_ref,
+    near_ref,
+    cut_ref,
+    head_ref,
+    wb_ref,
+    hf,
+    ht,
+    wf,
+    wt,
+    lat,
+    ids,
+    pos,
+    sems,
 ):
     rows = hf.shape[0]
     width = wf.shape[1]
@@ -64,6 +87,8 @@
                 (wf_hbm, wf),
                 (ht_hbm, ht),
                 (wt_hbm, wt),
+                (hb_hbm, head_ref),
+                (wb_hbm, wb_ref),
             )
         )
     ]
@@ -81,31 +106,45 @@
     line = lax.broadcasted_iota(jnp.int32, (PAD, rows), 0)
     high = jnp.broadcast_to(lax.shift_right_logical(place, 7).astype(F32), (PAD, rows))
     low = jnp.broadcast_to((place & 127).astype(F32), (PAD, rows))
-    out_ref[2 * rows :, :] = jnp.zeros((PAD, width), BF)
-    out_ref[2 * rows :, :rows] = jnp.where(line == 0, high, jnp.where(line == 1, low, 0.0)).astype(BF)
+    coded = jnp.where(line == 0, high, jnp.where(line == 1, low, 0.0)).astype(BF)
+    coded = jnp.concatenate([coded] + [jnp.zeros((PAD, width - rows), BF)] * (width > rows), axis=1)
+
+    def piece(slot):
+        return hf[:, pl.ds(pl.multiple_of(quarter_ref[slot] * width, width), width)]
+
     moves[3].wait()
+    cut_ref[...] = piece(0)
+    far_ref[:rows, :] = piece(1)
+    near_ref[:rows, :] = piece(2)
+    far_ref[rows : 2 * rows, :] = piece(3)
     moves[4].wait()
-    out_ref[:rows, :] = (dot(hf[...], wf[...]) + zrows).astype(BF)
+    feat = (dot(hf[...], wf[...]) + zrows).astype(BF)
     moves[5].wait()
     moves[6].wait()
-    out_ref[rows : 2 * rows, :] = (dot(ht[...], wt[...]) + zrows).astype(BF)
+    feat_t = (dot(ht[...], wt[...]) + zrows).astype(BF)
+    moves[7].wait()
+    head = head_ref[...]
+    for ref, at in ((far_ref, HEAD_AT[1]), (near_ref, HEAD_AT[2])):
+        ref[at * rows : (at + 1) * rows, :] = head
+        ref[(at + 1) * rows : (at + 2) * rows, :] = feat
+        ref[(at + 2) * rows : (at + 3) * rows, :] = feat_t
+        ref[(at + 3) * rows :, :] = coded
+    moves[8].wait()
 
 
 def pair_kernel(*refs, rows, total):
     base_ref, place_ref = refs[:2]
-    head_ref, cut_ref, mails = refs[2], refs[3], refs[4:7]
-    tails, feats, wb_ref = refs[7:11], refs[11:15], refs[15]
-    keep_ref, sends = refs[16], refs[17:20]
-    raw_ref, back_ref, smat_ref, pick_ref, wfq_ref, wbq_ref = refs[20:]
-    heads, cuts = (head_ref,) + mails, (cut_ref,) + mails
+    mails, tails, cut_ref, wb_ref = refs[2:6], refs[6:10], refs[10], refs[11]
+    keep_ref, sends = refs[12], refs[13:16]
+    raw_ref, back_ref, smat_ref, pick_ref, wfq_ref, wbq_ref = refs[16:]
     width = wb_ref.shape[1]
     pairs = float(total * (total - 1))
     groups = total // (4 * rows)
-    span = total // 16
+    span = total // 4
     wb = wb_ref[...]
     wanted = []
-    for ref in feats:
-        code = ref[2 * rows :, :rows].astype(F32)
+    for g, ref in enumerate(mails):
+        code = ref[(FEAT_AT[g] + 2) * rows :, :rows].astype(F32)
         wanted.append(columns_of(code[0:1] * 128.0 + code[1:2], rows))
     lanes = lax.broadcasted_iota(jnp.int32, (rows, rows), 1)
 
@@ -120,20 +159,17 @@
 
     def over_rows(step):
         for g in range(4):
-            for ref, start, skip, chunk in (
-                (heads[g], HEAD_AT[g] * rows, 0, rows),
-                (tails[g], 0, span, 3 * rows),
-            ):
-                first = g * 4 * span + skip
-                if span == rows:
-                    step(ref, start, first, chunk)
-                else:
-                    lax.fori_loop(
-                        0,
-                        span // rows,
-                        lambda i, c: (step(ref, start + i * chunk, first + i * chunk, chunk), c)[1],
-                        0,
-                    )
+            step(mails[g], HEAD_AT[g] * rows, g * span, rows)
+            first = g * span + rows
+            if span == 4 * rows:
+                step(tails[g], 0, first, 3 * rows)
+            else:
+
+                def one(i, carry, ref=tails[g], first=first):
+                    step(ref, i * rows, first + i * rows, rows)
+                    return carry
+
+                lax.fori_loop(0, span // rows - 1, one, 0)
 
     def at(start, chunk):
         return pl.ds(pl.multiple_of(start, rows), chunk)
@@ -162,12 +198,13 @@
     smat = smat_ref[...]
     s_hi, s_lo = halves(smat)
     kmat = jnp.zeros((width, width), F32)
-    wfq = jnp.zeros((cuts[0].shape[1], width), F32)
+    wfq = jnp.zeros((cut_ref.shape[1], width), F32)
     sums = jnp.sum(smat * smat) / groups / (2.0 * pairs)
-    for g, ref in enumerate(feats):
-        feat = ref[:rows, :]
+    for g, ref in enumerate(mails):
+        start = FEAT_AT[g] * rows
+        feat = ref[start : start + rows, :]
         f32feat = feat.astype(F32)
-        diff = f32feat - GAMMA * ref[rows : 2 * rows, :].astype(F32)
+        diff = f32feat - GAMMA * ref[start + rows : start + 2 * rows, :].astype(F32)
         d_hi, d_lo = halves(diff)
         hidden = pick_ref[g * rows : (g + 1) * rows, :].astype(BF)
         raw, scale, back = embed(hidden)
@@ -177,7 +214,8 @@
         coef = db * (1.0 / pairs) + 1.0 / total
         norm = jnp.sum(ob * ob, axis=-1, keepdims=True)
         grad_f = (ds * (1.0 / pairs) - coef * ob).astype(BF)
-        wfq = wfq + dot_t(cuts[g][CUT_AT[g] * rows : (CUT_AT[g] + 1) * rows, :], grad_f)
+        cut = (cut_ref if g == 0 else ref)[CUT_AT[g] * rows : (CUT_AT[g] + 1) * rows, :]
+        wfq = wfq + dot_t(cut, grad_f)
         kmat = kmat + dot_t(d_hi, feat) + dot_t(d_lo, feat)
         sums = sums + (
             (jnp.sum(diff * ds) - jnp.sum(db * db) - LAMBDA * jnp.sum(norm * norm)) / (2.0 * pairs)
@@ -227,6 +265,19 @@
         ref[size:, :] = coded
 
 
+def add_kernel(keep_ref, *refs):
+    sum_ref, note_ref = refs[3:]
+    size, width = sum_ref.shape
+    total = keep_ref[:size, :]
+    note = keep_ref[size : size + 1, :1]
+    for ref in refs[:3]:
+        total = total + ref[:size, :].astype(F32)
+        coded = ref[size:, :].astype(F32)
+        note = note + (coded[0:1, :1] + coded[1:2, :1] + coded[2:3, :1])
+    sum_ref[...] = total.astype(sum_ref.dtype)
+    note_ref[...] = note * (1.0 / width)
+
+
 def assemble_kernel(place_ref, *refs, wf_rows, wb_rows, factor_f, factor_b):
     place = place_ref[0]
     wf_ref, wb_ref = refs[4:]
@@ -255,26 +306,21 @@
     beyond = [1 << k for k in range(4, bits)]
     me = lax.axis_index("fa")
     total = size * rows
-    cut = high // 4
-    span = total // 16
-    assert bits >= 4 and size == 1 << bits and cut == width == wide
+    assert bits >= 4 and size == 1 << bits and high // 4 == width == wide
 
     quarters = [reverse_bits((me ^ m) & 3, 2).astype(jnp.int32) for m in GROUP]
-    cut0, cut2, cut1, cut3 = [
-        lax.dynamic_slice_in_dim(hidden_f, q * cut, cut, 1) for q in quarters
-    ]
-    head0 = hidden_b
-    for mask in reversed(beyond):
-        head0 = jnp.concatenate([head0, swap(head0, mask, size)], axis=0)
-    tail0 = jnp.concatenate([swap(head0, mask, size) for mask, _ in LINE], axis=0)
-    mail2 = swap(jnp.concatenate([cut2, cut3, head0], axis=0), 2, size)
-    mail1 = swap(jnp.concatenate([cut1, head0], axis=0), 1, size)
-    mail3 = swap(mail2, 1, size)
-    ff0 = pl.pallas_call(
+    ends = [(at + 2) * rows + PAD for at in FEAT_AT]
+    far, near, cut, head, wb_copy = pl.pallas_call(
         feature_kernel,
-        in_specs=[HBM] * 7,
-        out_specs=VMEM,
-        out_shape=jax.ShapeDtypeStruct((2 * rows + PAD, width), BF),
+        in_specs=[SMEM] + [HBM] * 9,
+        out_specs=[VMEM] * 5,
+        out_shape=[
+            jax.ShapeDtypeStruct((ends[1], width), BF),
+            jax.ShapeDtypeStruct((ends[2], width), BF),
+            jax.ShapeDtypeStruct((rows, width), BF),
+            jax.ShapeDtypeStruct(hidden_b.shape, BF),
+            jax.ShapeDtypeStruct(w_b.shape, BF),
+        ],
         scratch_shapes=[
             pltpu.VMEM(hidden_f.shape, BF),
             pltpu.VMEM(hidden_t.shape, BF),
@@ -283,26 +329,31 @@
             pltpu.VMEM(latents.shape, BF),
             pltpu.VMEM((1, rows), jnp.int32),
             pltpu.VMEM((1, rows), jnp.int32),
-            pltpu.SemaphoreType.DMA((7,)),
+            pltpu.SemaphoreType.DMA((9,)),
         ],
-        compiler_params=pltpu.CompilerParams(vmem_limit_bytes=24 * 2**20),
-        cost_estimate=pl.CostEstimate(
-            flops=4 * rows * high * width, bytes_accessed=4 * high * (rows + width), transcendentals=0
-        ),
+        compiler_params=pltpu.CompilerParams(vmem_limit_bytes=60 * 2**20),
     )(
+        jnp.stack(quarters),
         hidden_f,
         hidden_t,
+        hidden_b,
         w_f,
         w_t,
+        w_b,
         latents,
         latent_ids.reshape(1, rows),
         positives.reshape(1, rows),
     )
-    ff2 = swap(ff0, 2, size)
-    ff1 = swap(ff0, 1, size)
+    far2 = swap(far, 2, size)
+    for mask in reversed(beyond):
+        head = jnp.concatenate([head, swap(head, mask, size)], axis=0)
+    tail0 = jnp.concatenate(
+        [head[rows:]] * (len(beyond) > 0) + [swap(head, mask, size) for mask, _ in LINE], axis=0
+    )
+    near1 = swap(near, 1, size)
     tail2 = swap(tail0, 2, size)
     tail1 = swap(tail0, 1, size)
-    ff3 = swap(ff2, 1, size)
+    far3 = swap(far2, 1, size)
     tail3 = swap(tail2, 1, size)
 
     inner = reverse_bits(jnp.arange(size // 16, dtype=jnp.int32), bits - 4) << 4
@@ -311,10 +362,11 @@
     ).astype(jnp.int32)
     place = reverse_bits(me & 15, 4).astype(jnp.int32)
     places = jnp.stack([quarters[0], place & 3])
-    each = cut // 4 + wide // 16
+    wf_rows, wb_rows = high // 16, wide // 16
+    each = wf_rows + wb_rows
     keep, *sends = pl.pallas_call(
         functools.partial(pair_kernel, rows=rows, total=total),
-        in_specs=[SMEM] * 2 + [VMEM] * 14,
+        in_specs=[SMEM] * 2 + [VMEM] * 10,
         out_specs=[VMEM] * 4,
         out_shape=[jax.ShapeDtypeStruct((each + PAD, width), F32)]
         + [jax.ShapeDtypeStruct((each + PAD, width), BF)] * 3,
@@ -323,49 +375,36 @@
             pltpu.VMEM((total, width), BF),
             pltpu.VMEM((width, width), F32),
             pltpu.VMEM((4 * rows, wide), F32),
-            pltpu.VMEM((cut, width), F32),
+            pltpu.VMEM((width, width), F32),
             pltpu.VMEM((wide, width), F32),
         ],
-        compiler_params=pltpu.CompilerParams(vmem_limit_bytes=52 * 2**20),
-    )(
-        bases,
-        places,
-        head0,
-        cut0,
-        mail2,
-        mail1,
-        mail3,
-        tail0,
-        tail2,
-        tail1,
-        tail3,
-        ff0,
-        ff2,
-        ff1,
-        ff3,
-        w_b,
-    )
-
-    got = [swap(part, mask, size).astype(F32) for part, (mask, _) in zip(sends, LINE)]
-    current = keep[:each] + (got[0][:each] + got[1][:each] + got[2][:each])
-    note = keep[each, :1]
-    for part in got:
-        note = note + (part[each, :1] + part[each + 1, :1] + part[each + 2, :1])
+        compiler_params=pltpu.CompilerParams(vmem_limit_bytes=12 * 2**20 + total * width * 8),
+    )(bases, places, near, far2, near1, far3, tail0, tail2, tail1, tail3, cut, wb_copy)
+
+    got = [swap(part, mask, size) for part, (mask, _) in zip(sends, LINE)]
+    result, note = pl.pallas_call(
+        add_kernel,
+        in_specs=[VMEM] * 4,
+        out_specs=[VMEM] * 2,
+        out_shape=[
+            jax.ShapeDtypeStruct((each, width), F32 if beyond else BF),
+            jax.ShapeDtypeStruct((1, 1), F32),
+        ],
+        compiler_params=pltpu.CompilerParams(vmem_limit_bytes=8 * 2**20),
+    )(keep, *got)
     for mask in beyond:
-        current = current + swap(current, mask, size)
+        result = result + swap(result, mask, size)
         note = note + swap(note, mask, size)
-    result = current.astype(BF).reshape(1, each, width)
-    pieces = [result] + [swap(result, mask, size) for mask, _ in LINE]
-    crossed = [swap(piece, 2, size) for piece in pieces]
-    near = jnp.concatenate(pieces, axis=0)
-    near_y = jnp.concatenate(crossed, axis=0)
+    result = result.astype(BF).reshape(1, each, width)
+    near = jnp.concatenate([result] + [swap(result, mask, size) for mask, _ in LINE], axis=0)
+    near_y = swap(near, 2, size)
     far = swap(near, 1, size)
     far_y = swap(near_y, 1, size)
     grad_wf, grad_wb = pl.pallas_call(
         functools.partial(
             assemble_kernel,
-            wf_rows=cut // 4,
-            wb_rows=wide // 16,
+            wf_rows=wf_rows,
+            wb_rows=wb_rows,
             factor_f=math.sqrt(high),
             factor_b=math.sqrt(wide),
         ),
@@ -377,7 +416,7 @@
         ],
         compiler_params=pltpu.CompilerParams(vmem_limit_bytes=16 * 2**20),
     )(place.reshape(1), near, near_y, far, far_y)
-    return (grad_wf, grad_wb, note / width)
+    return (grad_wf, grad_wb, note.reshape(1))
 
 
 def solution(mesh):

time: 66 us -> 58.5 us (0.89)
  between operations: 8.32 us -> 0.72 us
  waiting for transfers between devices: 17.2 us -> 24.3 us
  local copies, waits for them, and re-layouts: 6.56 us -> 0.12 us
  starting transfers between devices: 23.3 us -> 20 us
  Pallas kernels: 9.99 us -> 12.5 us
    ppermute x24 -> x18, waiting for transfers between devices: 17.2 us -> 24.3 us  [swap(): return lax.ppermute(array, 'fa', [(i, i ^ mask) for i in range(size)])]
    ppermute x24 -> x18, starting transfers between devices: 23.3 us -> 20 us  [swap(): return lax.ppermute(array, 'fa', [(i, i ^ mask) for i in range(size)])]
    unnamed x27 -> x8, local copies, waits for them, and re-layouts: 3.27 us -> 0.02 us
    pallas_call x2 -> x3, Pallas kernels: 2.14 us -> 5.15 us  [the longest x1 3.49 us: body(): pl.pallas_call(feature_kernel, in_specs=[SMEM] + [HBM] * 9, out_specs=[VM...]
    slice x4 -> x0, local copies, waits for them, and re-layouts: 2.16 us -> none  [the longest x3 1.65 us: body(): note = note + (part[each, :1] + part[each + 1, :1] + part[each + 2, :1])]
    dynamic_slice x1 -> x0, local copies, waits for them, and re-layouts: 1.03 us -> none  [body(): lax.dynamic_slice_in_dim(hidden_f, q * cut, cut, 1)]
  transfers between devices with their start and end apart: 24 -> 18, of which waited for: 11 -> 12; matrix products, arithmetic and copies ran while one was open for 5% -> 0% of each run, Pallas kernels for 2% -> 0%
where the time goes in v4:
time: 58.5 us; the launch traced here: 58.4 us
  waiting for transfers between devices  24.3 us (42%)
  starting transfers between devices  20 us (34%)
  Pallas kernels  12.5 us (21%)
  other arithmetic  0.75 us (1%)
  between operations  0.72 us (1%)
    ppermute x18, waiting for transfers between devices, swap(): return lax.ppermute(array, 'fa', [(i, i ^ mask) for i in range(size)])  24.3 us
    ppermute x18, starting transfers between devices, swap(): return lax.ppermute(array, 'fa', [(i, i ^ mask) for i in range(size)])  20 us
    pallas_call x1, Pallas kernels, body(): pl.pallas_call(functools.partial(pair_kernel, rows=rows, total=total), in...  7.35 us
    pallas_call x1, Pallas kernels, body(): pl.pallas_call(feature_kernel, in_specs=[SMEM] + [HBM] * 9, out_specs=[VM...  3.49 us
  transfers between devices with their start and end apart: 18, of which 12 were waited for; matrix products, arithmetic and copies ran while one was open for 0% of the time, Pallas kernels for 0%

profile of v4, /device:TPU:0, one launch (start us, length us, event | category | flops | bytes accessed | tf_op | source)
XLA Modules:
  0.0 58.4 jit_solution(14395152548921324854)
XLA Ops:
  0.6 0.7 %pad_add_fusion.1.quarter_ref = s32[4]{0:T(128)} fusion(s32[1]{0:T(128)} %bitcast.21, s32[1]{0:T(128)} %bitcast.20, s32[1]{0:T(128)} %bitcast.19, s32[1]{0:T(128)} %bitcast.17), kind=kLoop, calls=%fused_computation.5 | loop fusion | flops 12 | bytes 32 | tf_op jit(solution)/shard_map/stack | solution.py:336
  1.3 3.5 %shard_map.112 = (bf16[656,256]{1,0:T(8,128)(2,1)}, bf16[528,256]{1,0:T(8,128)(2,1)}, bf16[128,256]{1,0:T(8,128)(2,1)}, bf16[128,256]{1,0:T(8,128)(2,1)}, bf16[256,256]{1,0:T(8,128)(2,1)}) custom-call(s32[4]{0:T(128)} %pad_add_fusion.1.quarter_ref, bf16[128,1024]{1,0:T(8,128)(2,1)} %hf_hbm.1, bf16[128,1024]{1,0:T(8,128)(2,1)} %ht_hbm.1, ...), custom_call_target="tpu_custom_call" | custom-call | tf_op jit(solution)/shard_map/pallas_call | solution.py:313
  4.8 0.0 copy-start
  4.8 5.1 %collective-permute-start.3 = (bf16[128,256]{1,0:T(8,128)(2,1)}, bf16[128,256]{1,0:T(8,128)(2,1)S(1)}, u32[]{:S(2)}, u32[]{:S(2)}) collective-permute-start(bf16[128,256]{1,0:T(8,128)(2,1)} %get-tuple-element.18), channel_id=1, source_target_pairs={{0,12},{1,13},{2,14},{3,15},{4,8},{5,9},{6,10},{7,11},{8,4},{9,5},... | collective-permute-start | bytes 196616 | tf_op jit(solution)/shard_map/ppermute | solution.py:38
  9.9 0.0 collective-permute-start.5
  9.9 0.6 %collective-permute-start.4 = (bf16[128,256]{1,0:T(8,128)(2,1)}, bf16[128,256]{1,0:T(8,128)(2,1)S(1)}, u32[]{:S(2)}, u32[]{:S(2)}) collective-permute-start(bf16[128,256]{1,0:T(8,128)(2,1)} %get-tuple-element.18), channel_id=1, source_target_pairs={{0,8},{1,9},{2,10},{3,11},{4,12},{5,13},{6,14},{7,15},{8,0},{9,1},... | collective-permute-start | bytes 196616 | tf_op jit(solution)/shard_map/ppermute | solution.py:38
  10.6 1.7 %collective-permute-start = (bf16[656,256]{1,0:T(8,128)(2,1)}, bf16[656,256]{1,0:T(8,128)(2,1)S(1)}, u32[]{:S(2)}, u32[]{:S(2)}) collective-permute-start(bf16[656,256]{1,0:T(8,128)(2,1)} %get-tuple-element.17), channel_id=1, source_target_pairs={{0,2},{1,3},{2,0},{3,1},{4,6},{5,7},{6,4},{7,5},{8,10},{9,11},{10,... | collective-permute-start | bytes 1007624 | tf_op jit(solution)/shard_map/ppermute | solution.py:38
  12.2 0.8 %collective-permute-done.3 = bf16[128,256]{1,0:T(8,128)(2,1)S(1)} collective-permute-done((bf16[128,256]{1,0:T(8,128)(2,1)}, bf16[128,256]{1,0:T(8,128)(2,1)S(1)}, u32[]{:S(2)}, u32[]{:S(2)}) %collective-permute-start.3) | collective-permute-done | bytes 65568 | tf_op jit(solution)/shard_map/ppermute | solution.py:38
  13.0 2.7 %collective-permute-done.4 = bf16[128,256]{1,0:T(8,128)(2,1)S(1)} collective-permute-done((bf16[128,256]{1,0:T(8,128)(2,1)}, bf16[128,256]{1,0:T(8,128)(2,1)S(1)}, u32[]{:S(2)}, u32[]{:S(2)}) %collective-permute-start.4) | collective-permute-done | bytes 65568 | tf_op jit(solution)/shard_map/ppermute | solution.py:38
  15.8 0.0 copy-start.1
  15.8 0.0 collective-permute-done.5
  15.8 1.6 %collective-permute-start.6 = (bf16[384,256]{1,0:T(8,128)(2,1)S(1)}, bf16[384,256]{1,0:T(8,128)(2,1)S(1)}, u32[]{:S(2)}, u32[]{:S(2)}) collective-permute-start(bf16[384,256]{1,0:T(8,128)(2,1)S(1)} %constant_dynamic-update-slice_fusion.refs_6_), channel_id=1, source_target_pairs={{0,2},{1,3},{2,0},{3,1},{4,6},{5,7},{6,4},{7,5},{8,10},{9,11},{10,... | collective-permute-start | bytes 589832 | tf_op jit(solution)/shard_map/ppermute | solution.py:38
  17.4 4.2 %collective-permute-done.refs_3_ = bf16[656,256]{1,0:T(8,128)(2,1)S(1)} collective-permute-done((bf16[656,256]{1,0:T(8,128)(2,1)}, bf16[656,256]{1,0:T(8,128)(2,1)S(1)}, u32[]{:S(2)}, u32[]{:S(2)}) %collective-permute-start) | collective-permute-done | bytes 335904 | tf_op jit(solution)/shard_map/ppermute | solution.py:38
  21.6 0.0 collective-permute-start.2
  21.6 0.0 copy-done
  21.6 0.5 collective-permute-start.1
  22.1 0.0 collective-permute-start.7
  22.1 1.9 %collective-permute-done.6.refs_7_ = bf16[384,256]{1,0:T(8,128)(2,1)S(1)} collective-permute-done((bf16[384,256]{1,0:T(8,128)(2,1)S(1)}, bf16[384,256]{1,0:T(8,128)(2,1)S(1)}, u32[]{:S(2)}, u32[]{:S(2)}) %collective-permute-start.6) | collective-permute-done | bytes 196640 | tf_op jit(solution)/shard_map/ppermute | solution.py:38
  24.1 0.0 collective-permute-start.8
  24.1 0.0 copy-start.2
  24.1 0.1 concatenate.9.refs_0_
  24.2 0.1 pad_add_fusion.refs_1_
  24.2 0.0 collective-permute-done.7.refs_8_
  24.2 0.0 collective-permute-done.1.refs_4_
  24.2 1.3 %collective-permute-done.8.refs_9_ = bf16[384,256]{1,0:T(8,128)(2,1)S(1)} collective-permute-done((bf16[384,256]{1,0:T(8,128)(2,1)S(1)}, bf16[384,256]{1,0:T(8,128)(2,1)S(1)}, u32[]{:S(2)}, u32[]{:S(2)}) %collective-permute-start.8) | collective-permute-done | bytes 196640 | tf_op jit(solution)/shard_map/ppermute | solution.py:38
  25.5 0.0 collective-permute-done.2.refs_5_
  25.5 0.0 copy-done.1
  25.5 0.0 copy-done.2
  25.5 7.4 %shard_map.113 = (f32[96,256]{1,0:T(8,128)S(1)}, bf16[96,256]{1,0:T(8,128)(2,1)S(1)}, bf16[96,256]{1,0:T(8,128)(2,1)S(1)}, bf16[96,256]{1,0:T(8,128)(2,1)S(1)}) custom-call(s32[16]{0:T(128)S(1)} %concatenate.9.refs_0_, s32[2]{0:T(128)S(1)} %pad_add_fusion.refs_1_, bf16[528,256]{1,0:T(8,128)(2,1)S(1)} %copy-done, ...), custom_call_target="tpu_custom_call" | custom-call | tf_op jit(solution)/shard_map/pallas_call | solution.py:367
  32.9 3.5 %collective-permute-start.9 = (bf16[96,256]{1,0:T(8,128)(2,1)S(1)}, bf16[96,256]{1,0:T(8,128)(2,1)S(1)}, u32[]{:S(2)}, u32[]{:S(2)}) collective-permute-start(bf16[96,256]{1,0:T(8,128)(2,1)S(1)} %get-tuple-element.22), channel_id=1, source_target_pairs={{0,12},{1,13},{2,14},{3,15},{4,8},{5,9},{6,10},{7,11},{8,4},{9,5},... | collective-permute-start | bytes 147464 | tf_op jit(solution)/shard_map/ppermute | solution.py:38
  36.4 0.0 collective-permute-start.10
  36.4 0.9 %collective-permute-start.11 = (bf16[96,256]{1,0:T(8,128)(2,1)S(1)}, bf16[96,256]{1,0:T(8,128)(2,1)S(1)}, u32[]{:S(2)}, u32[]{:S(2)}) collective-permute-start(bf16[96,256]{1,0:T(8,128)(2,1)S(1)} %get-tuple-element.24), channel_id=1, source_target_pairs={{0,4},{1,5},{2,6},{3,7},{4,0},{5,1},{6,2},{7,3},{8,12},{9,13},{10,... | collective-permute-start | bytes 147464 | tf_op jit(solution)/shard_map/ppermute | solution.py:38
  37.3 1.8 %collective-permute-done.9.refs_0_ = bf16[96,256]{1,0:T(8,128)(2,1)S(1)} collective-permute-done((bf16[96,256]{1,0:T(8,128)(2,1)S(1)}, bf16[96,256]{1,0:T(8,128)(2,1)S(1)}, u32[]{:S(2)}, u32[]{:S(2)}) %collective-permute-start.9) | collective-permute-done | bytes 49184 | tf_op jit(solution)/shard_map/ppermute | solution.py:38
  39.1 2.3 %collective-permute-done.10.refs_1_ = bf16[96,256]{1,0:T(8,128)(2,1)S(1)} collective-permute-done((bf16[96,256]{1,0:T(8,128)(2,1)S(1)}, bf16[96,256]{1,0:T(8,128)(2,1)S(1)}, u32[]{:S(2)}, u32[]{:S(2)}) %collective-permute-start.10) | collective-permute-done | bytes 49184 | tf_op jit(solution)/shard_map/ppermute | solution.py:38
  41.4 0.1 collective-permute-done.11.refs_2_
  41.5 0.5 shard_map.114
  42.1 0.7 %collective-permute-start.14 = (bf16[1,80,256]{2,1,0:T(8,128)(2,1)S(1)}, bf16[1,80,256]{2,1,0:T(8,128)(2,1)S(1)}, u32[]{:S(2)}, u32[]{:S(2)}) collective-permute-start(bf16[1,80,256]{2,1,0:T(8,128)(2,1)S(1)} %bitcast.26), channel_id=1, source_target_pairs={{0,4},{1,5},{2,6},{3,7},{4,0},{5,1},{6,2},{7,3},{8,12},{9,13},{10,... | collective-permute-start | bytes 122888 | tf_op jit(solution)/shard_map/ppermute | solution.py:38
  42.8 1.8 %collective-permute-start.13 = (bf16[1,80,256]{2,1,0:T(8,128)(2,1)S(1)}, bf16[1,80,256]{2,1,0:T(8,128)(2,1)S(1)}, u32[]{:S(2)}, u32[]{:S(2)}) collective-permute-start(bf16[1,80,256]{2,1,0:T(8,128)(2,1)S(1)} %bitcast.27), channel_id=1, source_target_pairs={{0,8},{1,9},{2,10},{3,11},{4,12},{5,13},{6,14},{7,15},{8,0},{9,1},... | collective-permute-start | bytes 122888 | tf_op jit(solution)/shard_map/ppermute | solution.py:38
  44.6 1.8 %collective-permute-start.12 = (bf16[1,80,256]{2,1,0:T(8,128)(2,1)S(1)}, bf16[1,80,256]{2,1,0:T(8,128)(2,1)S(1)}, u32[]{:S(2)}, u32[]{:S(2)}) collective-permute-start(bf16[1,80,256]{2,1,0:T(8,128)(2,1)S(1)} %bitcast.28), channel_id=1, source_target_pairs={{0,12},{1,13},{2,14},{3,15},{4,8},{5,9},{6,10},{7,11},{8,4},{9,5},... | collective-permute-start | bytes 122888 | tf_op jit(solution)/shard_map/ppermute | solution.py:38
  46.5 0.0 collective-permute-done.14
  46.5 2.1 %collective-permute-done.13 = bf16[1,80,256]{2,1,0:T(8,128)(2,1)S(1)} collective-permute-done((bf16[1,80,256]{2,1,0:T(8,128)(2,1)S(1)}, bf16[1,80,256]{2,1,0:T(8,128)(2,1)S(1)}, u32[]{:S(2)}, u32[]{:S(2)}) %collective-permute-start.13) | collective-permute-done | bytes 40992 | tf_op jit(solution)/shard_map/ppermute | solution.py:38
  48.6 1.9 %collective-permute-done.12 = bf16[1,80,256]{2,1,0:T(8,128)(2,1)S(1)} collective-permute-done((bf16[1,80,256]{2,1,0:T(8,128)(2,1)S(1)}, bf16[1,80,256]{2,1,0:T(8,128)(2,1)S(1)}, u32[]{:S(2)}, u32[]{:S(2)}) %collective-permute-start.12) | collective-permute-done | bytes 40992 | tf_op jit(solution)/shard_map/ppermute | solution.py:38
  50.5 1.6 %collective-permute-start.15 = (bf16[4,80,256]{2,1,0:T(8,128)(2,1)S(1)}, bf16[4,80,256]{2,1,0:T(8,128)(2,1)S(1)}, u32[]{:S(2)}, u32[]{:S(2)}) collective-permute-start(bf16[4,80,256]{2,1,0:T(8,128)(2,1)S(1)} %pad_maximum_fusion.refs_0_), channel_id=1, source_target_pairs={{0,2},{1,3},{2,0},{3,1},{4,6},{5,7},{6,4},{7,5},{8,10},{9,11},{10,... | collective-permute-start | bytes 491528 | tf_op jit(solution)/shard_map/ppermute | solution.py:38
  52.1 0.0 collective-permute-start.16
  52.1 3.8 %collective-permute-done.15.refs_1_ = bf16[4,80,256]{2,1,0:T(8,128)(2,1)S(1)} collective-permute-done((bf16[4,80,256]{2,1,0:T(8,128)(2,1)S(1)}, bf16[4,80,256]{2,1,0:T(8,128)(2,1)S(1)}, u32[]{:S(2)}, u32[]{:S(2)}) %collective-permute-start.15) | collective-permute-done | bytes 163872 | tf_op jit(solution)/shard_map/ppermute | solution.py:38
  55.8 0.0 collective-permute-start.17
  55.9 0.0 collective-permute-done.16.refs_2_
  55.9 1.4 %collective-permute-done.17.refs_3_ = bf16[4,80,256]{2,1,0:T(8,128)(2,1)S(1)} collective-permute-done((bf16[4,80,256]{2,1,0:T(8,128)(2,1)S(1)}, bf16[4,80,256]{2,1,0:T(8,128)(2,1)S(1)}, u32[]{:S(2)}, u32[]{:S(2)}) %collective-permute-start.17) | collective-permute-done | bytes 163872 | tf_op jit(solution)/shard_map/ppermute | solution.py:38
  57.2 1.1 %shard_map.115 = (f32[1024,256]{1,0:T(8,128)}, f32[256,256]{1,0:T(8,128)}) custom-call(s32[1]{0:T(128)} %bitcast.place_ref, bf16[4,80,256]{2,1,0:T(8,128)(2,1)S(1)} %pad_maximum_fusion.refs_0_, bf16[4,80,256]{2,1,0:T(8,128)(2,1)S(1)} %collective-permute-done.15.refs_1_, bf16[4,80,256]{2,1,0:T(8,128)(2,1)S(1)} %collective-permute-done.16.refs_2_, ...), custom_call_target="tpu_custom_call" | custom-call | tf_op jit(solution)/shard_map/pallas_call | solution.py:403
  (4 shorter events, 0.0 us)
Async XLA Ops:
  4.8 16.8 %copy-start = (bf16[528,256]{1,0:T(8,128)(2,1)S(1)}, bf16[528,256]{1,0:T(8,128)(2,1)}, u32[]{:S(2)}) copy-start(bf16[528,256]{1,0:T(8,128)(2,1)} %get-tuple-element.16.refs_2_) | copy-start | bytes 811012
  4.8 8.2 %collective-permute-start.3 = (bf16[128,256]{1,0:T(8,128)(2,1)}, bf16[128,256]{1,0:T(8,128)(2,1)S(1)}, u32[]{:S(2)}, u32[]{:S(2)}) collective-permute-start(bf16[128,256]{1,0:T(8,128)(2,1)} %get-tuple-element.18), channel_id=1, source_target_pairs={{0,12},{1,13},{2,14},{3,15},{4,8},{5,9},{6,10},{7,11},{8,4},{9,5},... | collective-permute-start | bytes 196616 | tf_op jit(solution)/shard_map/ppermute | solution.py:38
  9.9 5.9 %collective-permute-start.5 = (bf16[128,256]{1,0:T(8,128)(2,1)}, bf16[128,256]{1,0:T(8,128)(2,1)S(1)}, u32[]{:S(2)}, u32[]{:S(2)}) collective-permute-start(bf16[128,256]{1,0:T(8,128)(2,1)} %get-tuple-element.18), channel_id=1, source_target_pairs={{0,4},{1,5},{2,6},{3,7},{4,0},{5,1},{6,2},{7,3},{8,12},{9,13},{10,... | collective-permute-start | bytes 196616 | tf_op jit(solution)/shard_map/ppermute | solution.py:38
  9.9 5.8 %collective-permute-start.4 = (bf16[128,256]{1,0:T(8,128)(2,1)}, bf16[128,256]{1,0:T(8,128)(2,1)S(1)}, u32[]{:S(2)}, u32[]{:S(2)}) collective-permute-start(bf16[128,256]{1,0:T(8,128)(2,1)} %get-tuple-element.18), channel_id=1, source_target_pairs={{0,8},{1,9},{2,10},{3,11},{4,12},{5,13},{6,14},{7,15},{8,0},{9,1},... | collective-permute-start | bytes 196616 | tf_op jit(solution)/shard_map/ppermute | solution.py:38
  10.6 11.0 %collective-permute-start = (bf16[656,256]{1,0:T(8,128)(2,1)}, bf16[656,256]{1,0:T(8,128)(2,1)S(1)}, u32[]{:S(2)}, u32[]{:S(2)}) collective-permute-start(bf16[656,256]{1,0:T(8,128)(2,1)} %get-tuple-element.17), channel_id=1, source_target_pairs={{0,2},{1,3},{2,0},{3,1},{4,6},{5,7},{6,4},{7,5},{8,10},{9,11},{10,... | collective-permute-start | bytes 1007624 | tf_op jit(solution)/shard_map/ppermute | solution.py:38
  15.8 9.7 %copy-start.1 = (bf16[256,256]{1,0:T(8,128)(2,1)S(1)}, bf16[256,256]{1,0:T(8,128)(2,1)}, u32[]{:S(2)}) copy-start(bf16[256,256]{1,0:T(8,128)(2,1)} %get-tuple-element.20.refs_11_) | copy-start | bytes 393220
  15.8 8.3 %collective-permute-start.6 = (bf16[384,256]{1,0:T(8,128)(2,1)S(1)}, bf16[384,256]{1,0:T(8,128)(2,1)S(1)}, u32[]{:S(2)}, u32[]{:S(2)}) collective-permute-start(bf16[384,256]{1,0:T(8,128)(2,1)S(1)} %constant_dynamic-update-slice_fusion.refs_6_), channel_id=1, source_target_pairs={{0,2},{1,3},{2,0},{3,1},{4,6},{5,7},{6,4},{7,5},{8,10},{9,11},{10,... | collective-permute-start | bytes 589832 | tf_op jit(solution)/shard_map/ppermute | solution.py:38
  21.6 3.9 %collective-permute-start.2 = (bf16[656,256]{1,0:T(8,128)(2,1)S(1)}, bf16[656,256]{1,0:T(8,128)(2,1)S(1)}, u32[]{:S(2)}, u32[]{:S(2)}) collective-permute-start(bf16[656,256]{1,0:T(8,128)(2,1)S(1)} %collective-permute-done.refs_3_), channel_id=1, source_target_pairs={{0,1},{1,0},{2,3},{3,2},{4,5},{5,4},{6,7},{7,6},{8,9},{9,8},{10,11... | collective-permute-start | bytes 1007624 | tf_op jit(solution)/shard_map/ppermute | solution.py:38
  21.6 2.6 %collective-permute-start.1 = (bf16[528,256]{1,0:T(8,128)(2,1)S(1)}, bf16[528,256]{1,0:T(8,128)(2,1)S(1)}, u32[]{:S(2)}, u32[]{:S(2)}) collective-permute-start(bf16[528,256]{1,0:T(8,128)(2,1)S(1)} %copy-done), channel_id=1, source_target_pairs={{0,1},{1,0},{2,3},{3,2},{4,5},{5,4},{6,7},{7,6},{8,9},{9,8},{10,11... | collective-permute-start | bytes 811016 | tf_op jit(solution)/shard_map/ppermute | solution.py:38
  22.1 2.1 %collective-permute-start.7 = (bf16[384,256]{1,0:T(8,128)(2,1)S(1)}, bf16[384,256]{1,0:T(8,128)(2,1)S(1)}, u32[]{:S(2)}, u32[]{:S(2)}) collective-permute-start(bf16[384,256]{1,0:T(8,128)(2,1)S(1)} %constant_dynamic-update-slice_fusion.refs_6_), channel_id=1, source_target_pairs={{0,1},{1,0},{2,3},{3,2},{4,5},{5,4},{6,7},{7,6},{8,9},{9,8},{10,11... | collective-permute-start | bytes 589832 | tf_op jit(solution)/shard_map/ppermute | solution.py:38
  24.1 1.4 %collective-permute-start.8 = (bf16[384,256]{1,0:T(8,128)(2,1)S(1)}, bf16[384,256]{1,0:T(8,128)(2,1)S(1)}, u32[]{:S(2)}, u32[]{:S(2)}) collective-permute-start(bf16[384,256]{1,0:T(8,128)(2,1)S(1)} %collective-permute-done.6.refs_7_), channel_id=1, source_target_pairs={{0,1},{1,0},{2,3},{3,2},{4,5},{5,4},{6,7},{7,6},{8,9},{9,8},{10,11... | collective-permute-start | bytes 589832 | tf_op jit(solution)/shard_map/ppermute | solution.py:38
  24.1 1.4 %copy-start.2 = (bf16[128,256]{1,0:T(8,128)(2,1)S(1)}, bf16[128,256]{1,0:T(8,128)(2,1)}, u32[]{:S(2)}) copy-start(bf16[128,256]{1,0:T(8,128)(2,1)} %get-tuple-element.19.refs_10_) | copy-start | bytes 196612
  32.9 6.3 %collective-permute-start.9 = (bf16[96,256]{1,0:T(8,128)(2,1)S(1)}, bf16[96,256]{1,0:T(8,128)(2,1)S(1)}, u32[]{:S(2)}, u32[]{:S(2)}) collective-permute-start(bf16[96,256]{1,0:T(8,128)(2,1)S(1)} %get-tuple-element.22), channel_id=1, source_target_pairs={{0,12},{1,13},{2,14},{3,15},{4,8},{5,9},{6,10},{7,11},{8,4},{9,5},... | collective-permute-start | bytes 147464 | tf_op jit(solution)/shard_map/ppermute | solution.py:38
  36.4 5.0 %collective-permute-start.10 = (bf16[96,256]{1,0:T(8,128)(2,1)S(1)}, bf16[96,256]{1,0:T(8,128)(2,1)S(1)}, u32[]{:S(2)}, u32[]{:S(2)}) collective-permute-start(bf16[96,256]{1,0:T(8,128)(2,1)S(1)} %get-tuple-element.23), channel_id=1, source_target_pairs={{0,8},{1,9},{2,10},{3,11},{4,12},{5,13},{6,14},{7,15},{8,0},{9,1},... | collective-permute-start | bytes 147464 | tf_op jit(solution)/shard_map/ppermute | solution.py:38
  36.4 5.1 %collective-permute-start.11 = (bf16[96,256]{1,0:T(8,128)(2,1)S(1)}, bf16[96,256]{1,0:T(8,128)(2,1)S(1)}, u32[]{:S(2)}, u32[]{:S(2)}) collective-permute-start(bf16[96,256]{1,0:T(8,128)(2,1)S(1)} %get-tuple-element.24), channel_id=1, source_target_pairs={{0,4},{1,5},{2,6},{3,7},{4,0},{5,1},{6,2},{7,3},{8,12},{9,13},{10,... | collective-permute-start | bytes 147464 | tf_op jit(solution)/shard_map/ppermute | solution.py:38
  42.1 4.4 %collective-permute-start.14 = (bf16[1,80,256]{2,1,0:T(8,128)(2,1)S(1)}, bf16[1,80,256]{2,1,0:T(8,128)(2,1)S(1)}, u32[]{:S(2)}, u32[]{:S(2)}) collective-permute-start(bf16[1,80,256]{2,1,0:T(8,128)(2,1)S(1)} %bitcast.26), channel_id=1, source_target_pairs={{0,4},{1,5},{2,6},{3,7},{4,0},{5,1},{6,2},{7,3},{8,12},{9,13},{10,... | collective-permute-start | bytes 122888 | tf_op jit(solution)/shard_map/ppermute | solution.py:38
  42.8 5.8 %collective-permute-start.13 = (bf16[1,80,256]{2,1,0:T(8,128)(2,1)S(1)}, bf16[1,80,256]{2,1,0:T(8,128)(2,1)S(1)}, u32[]{:S(2)}, u32[]{:S(2)}) collective-permute-start(bf16[1,80,256]{2,1,0:T(8,128)(2,1)S(1)} %bitcast.27), channel_id=1, source_target_pairs={{0,8},{1,9},{2,10},{3,11},{4,12},{5,13},{6,14},{7,15},{8,0},{9,1},... | collective-permute-start | bytes 122888 | tf_op jit(solution)/shard_map/ppermute | solution.py:38
  44.6 5.8 %collective-permute-start.12 = (bf16[1,80,256]{2,1,0:T(8,128)(2,1)S(1)}, bf16[1,80,256]{2,1,0:T(8,128)(2,1)S(1)}, u32[]{:S(2)}, u32[]{:S(2)}) collective-permute-start(bf16[1,80,256]{2,1,0:T(8,128)(2,1)S(1)} %bitcast.28), channel_id=1, source_target_pairs={{0,12},{1,13},{2,14},{3,15},{4,8},{5,9},{6,10},{7,11},{8,4},{9,5},... | collective-permute-start | bytes 122888 | tf_op jit(solution)/shard_map/ppermute | solution.py:38
  50.5 5.4 %collective-permute-start.15 = (bf16[4,80,256]{2,1,0:T(8,128)(2,1)S(1)}, bf16[4,80,256]{2,1,0:T(8,128)(2,1)S(1)}, u32[]{:S(2)}, u32[]{:S(2)}) collective-permute-start(bf16[4,80,256]{2,1,0:T(8,128)(2,1)S(1)} %pad_maximum_fusion.refs_0_), channel_id=1, source_target_pairs={{0,2},{1,3},{2,0},{3,1},{4,6},{5,7},{6,4},{7,5},{8,10},{9,11},{10,... | collective-permute-start | bytes 491528 | tf_op jit(solution)/shard_map/ppermute | solution.py:38
  52.1 3.8 %collective-permute-start.16 = (bf16[4,80,256]{2,1,0:T(8,128)(2,1)S(1)}, bf16[4,80,256]{2,1,0:T(8,128)(2,1)S(1)}, u32[]{:S(2)}, u32[]{:S(2)}) collective-permute-start(bf16[4,80,256]{2,1,0:T(8,128)(2,1)S(1)} %pad_maximum_fusion.refs_0_), channel_id=1, source_target_pairs={{0,1},{1,0},{2,3},{3,2},{4,5},{5,4},{6,7},{7,6},{8,9},{9,8},{10,11... | collective-permute-start | bytes 491528 | tf_op jit(solution)/shard_map/ppermute | solution.py:38
  55.8 1.4 %collective-permute-start.17 = (bf16[4,80,256]{2,1,0:T(8,128)(2,1)S(1)}, bf16[4,80,256]{2,1,0:T(8,128)(2,1)S(1)}, u32[]{:S(2)}, u32[]{:S(2)}) collective-permute-start(bf16[4,80,256]{2,1,0:T(8,128)(2,1)S(1)} %collective-permute-done.15.refs_1_), channel_id=1, source_target_pairs={{0,1},{1,0},{2,3},{3,2},{4,5},{5,4},{6,7},{7,6},{8,9},{9,8},{10,11... | collective-permute-start | bytes 491528 | tf_op jit(solution)/shard_map/ppermute | solution.py:38

commit v5 on v4

--- a/solution.py
+++ b/solution.py
@@ -13,12 +13,12 @@
 EPS = 1e-06
 BF = jnp.bfloat16
 F32 = jnp.float32
-GROUP = (0, 2, 1, 3)
-CUT_AT = (0, 0, 0, 1)
-HEAD_AT = (1, 2, 1, 2)
-FEAT_AT = (2, 3, 2, 3)
+GROUP = (0, 1)
+HEAD_AT = 2
+FEAT_AT = 3
 PAD = 16
 LINE = ((12, 3), (8, 1), (4, 2))
+TURNS = (0, 3, 1, 2, 4, 7, 5, 6)
 
 
 def dot(left, right):
@@ -50,7 +50,7 @@
 
 
 def feature_kernel(
-    quarter_ref,
+    core_ref,
     hf_hbm,
     ht_hbm,
     hb_hbm,
@@ -60,7 +60,6 @@
     lat_hbm,
     ids_hbm,
     pos_hbm,
-    far_ref,
     near_ref,
     cut_ref,
     head_ref,
@@ -109,42 +108,39 @@
     coded = jnp.where(line == 0, high, jnp.where(line == 1, low, 0.0)).astype(BF)
     coded = jnp.concatenate([coded] + [jnp.zeros((PAD, width - rows), BF)] * (width > rows), axis=1)
 
-    def piece(slot):
-        return hf[:, pl.ds(pl.multiple_of(quarter_ref[slot] * width, width), width)]
-
     moves[3].wait()
-    cut_ref[...] = piece(0)
-    far_ref[:rows, :] = piece(1)
-    near_ref[:rows, :] = piece(2)
-    far_ref[rows : 2 * rows, :] = piece(3)
+    core = core_ref[0]
+    for t in range(2):
+        for ref, half in ((cut_ref, core), (near_ref, 1 - core)):
+            ref[t * rows : (t + 1) * rows, :] = hf[
+                :, pl.ds(pl.multiple_of((half * 2 + t) * width, width), width)
+            ]
     moves[4].wait()
     feat = (dot(hf[...], wf[...]) + zrows).astype(BF)
     moves[5].wait()
     moves[6].wait()
     feat_t = (dot(ht[...], wt[...]) + zrows).astype(BF)
     moves[7].wait()
-    head = head_ref[...]
-    for ref, at in ((far_ref, HEAD_AT[1]), (near_ref, HEAD_AT[2])):
-        ref[at * rows : (at + 1) * rows, :] = head
-        ref[(at + 1) * rows : (at + 2) * rows, :] = feat
-        ref[(at + 2) * rows : (at + 3) * rows, :] = feat_t
-        ref[(at + 3) * rows :, :] = coded
+    near_ref[HEAD_AT * rows : FEAT_AT * rows, :] = head_ref[...]
+    near_ref[FEAT_AT * rows : (FEAT_AT + 1) * rows, :] = feat
+    near_ref[(FEAT_AT + 1) * rows : (FEAT_AT + 2) * rows, :] = feat_t
+    near_ref[(FEAT_AT + 2) * rows :, :] = coded
     moves[8].wait()
 
 
 def pair_kernel(*refs, rows, total):
     base_ref, place_ref = refs[:2]
-    mails, tails, cut_ref, wb_ref = refs[2:6], refs[6:10], refs[10], refs[11]
-    keep_ref, sends = refs[12], refs[13:16]
-    raw_ref, back_ref, smat_ref, pick_ref, wfq_ref, wbq_ref = refs[16:]
+    mails, tails, cut_ref, wb_ref = refs[2:4], refs[4:6], refs[6], refs[7]
+    keep_ref, send_ref = refs[8:10]
+    raw_ref, back_ref, smat_ref, pick_ref, wfq_ref, wbq_ref = refs[10:]
     width = wb_ref.shape[1]
     pairs = float(total * (total - 1))
-    groups = total // (4 * rows)
-    span = total // 4
+    groups = total // (2 * rows)
+    span = total // 2
     wb = wb_ref[...]
     wanted = []
-    for g, ref in enumerate(mails):
-        code = ref[(FEAT_AT[g] + 2) * rows :, :rows].astype(F32)
+    for ref in mails:
+        code = ref[(FEAT_AT + 2) * rows :, :rows].astype(F32)
         wanted.append(columns_of(code[0:1] * 128.0 + code[1:2], rows))
     lanes = lax.broadcasted_iota(jnp.int32, (rows, rows), 1)
 
@@ -158,11 +154,12 @@
         return (scale * grad - scale * scale * scale * (1.0 / width) * along * raw).astype(BF)
 
     def over_rows(step):
-        for g in range(4):
-            step(mails[g], HEAD_AT[g] * rows, g * span, rows)
+        for g in range(2):
+            step(mails[g], HEAD_AT * rows, g * span, rows)
             first = g * span + rows
-            if span == 4 * rows:
-                step(tails[g], 0, first, 3 * rows)
+            if span == 8 * rows:
+                step(tails[g], 0, first, 4 * rows)
+                step(tails[g], 4 * rows, first + 4 * rows, 3 * rows)
             else:
 
                 def one(i, carry, ref=tails[g], first=first):
@@ -198,10 +195,10 @@
     smat = smat_ref[...]
     s_hi, s_lo = halves(smat)
     kmat = jnp.zeros((width, width), F32)
-    wfq = jnp.zeros((cut_ref.shape[1], width), F32)
+    wfq = [jnp.zeros((width, width), F32)] * 2
     sums = jnp.sum(smat * smat) / groups / (2.0 * pairs)
     for g, ref in enumerate(mails):
-        start = FEAT_AT[g] * rows
+        start = FEAT_AT * rows
         feat = ref[start : start + rows, :]
         f32feat = feat.astype(F32)
         diff = f32feat - GAMMA * ref[start + rows : start + 2 * rows, :].astype(F32)
@@ -214,8 +211,8 @@
         coef = db * (1.0 / pairs) + 1.0 / total
         norm = jnp.sum(ob * ob, axis=-1, keepdims=True)
         grad_f = (ds * (1.0 / pairs) - coef * ob).astype(BF)
-        cut = (cut_ref if g == 0 else ref)[CUT_AT[g] * rows : (CUT_AT[g] + 1) * rows, :]
-        wfq = wfq + dot_t(cut, grad_f)
+        cut_from = cut_ref if g == 0 else ref
+        wfq = [wfq[t] + dot_t(cut_from[t * rows : (t + 1) * rows, :], grad_f) for t in range(2)]
         kmat = kmat + dot_t(d_hi, feat) + dot_t(d_lo, feat)
         sums = sums + (
             (jnp.sum(diff * ds) - jnp.sum(db * db) - LAMBDA * jnp.sum(norm * norm)) / (2.0 * pairs)
@@ -225,7 +222,8 @@
             -coef * f32feat - (norm * (2.0 * LAMBDA / pairs) + 2.0 * LAMBDA / total) * ob, raw, scale
         )
         wbq_ref[...] += dot_t(hidden, grad_own)
-    wfq_ref[...] = wfq
+    wfq_ref[:width, :] = wfq[0]
+    wfq_ref[width:, :] = wfq[1]
     a_hi, a_lo = halves((kmat + (2.0 * LAMBDA / groups) * smat) * (1.0 / pairs))
 
     def second(ref, start, number, chunk):
@@ -236,32 +234,54 @@
         wbq_ref[...] += dot_t(ref[at(start, chunk), :], grad)
 
     over_rows(second)
-    quarter, mine = place_ref[0], place_ref[1]
-    wf_rows = wfq_ref.shape[0] // 4
+    core, mine = place_ref[0], place_ref[1]
+    wf_rows = wfq_ref.shape[0] // 8
     wb_rows = wbq_ref.shape[0] // 16
     size = wf_rows + wb_rows
+    for ref, half in ((keep_ref, mine), (send_ref, 1 - mine)):
+        for t in range(4):
+            at_f, at_b = half * 4 + t, core * 8 + half * 4 + t
+            ref[t * size : t * size + wf_rows, :] = wfq_ref[
+                pl.ds(pl.multiple_of(at_f * wf_rows, wf_rows), wf_rows), :
+            ].astype(ref.dtype)
+            ref[t * size + wf_rows : (t + 1) * size, :] = wbq_ref[
+                pl.ds(pl.multiple_of(at_b * wb_rows, wb_rows), wb_rows), :
+            ].astype(ref.dtype)
+    note = jnp.full((PAD, width), sums, F32)
+    keep_ref[4 * size :, :] = note
+    send_ref[4 * size :, :] = coded_note(note)
+
+
+def coded_note(note):
+    line = lax.broadcasted_iota(jnp.int32, note.shape, 0)
+    high = note.astype(BF)
+    middle, low = halves(note - high.astype(F32))
+    return jnp.where(
+        line == 0,
+        high.astype(F32),
+        jnp.where(line == 1, middle.astype(F32), jnp.where(line == 2, low.astype(F32), 0.0)),
+    ).astype(BF)
+
+
+def read_note(coded):
+    return coded[0:1, :] + coded[1:2, :] + coded[2:3, :]
+
+
+def cross_kernel(place_ref, keep_ref, got_ref, own_ref, *sends):
+    mine = place_ref[0]
+    size = own_ref.shape[0] - PAD
+    note = keep_ref[4 * size : 4 * size + 1, :] + read_note(got_ref[4 * size :, :].astype(F32))
+    note = jnp.broadcast_to(note, (PAD, note.shape[1]))
 
     def block(t):
-        return (
-            wfq_ref[pl.ds(pl.multiple_of(t * wf_rows, wf_rows), wf_rows), :],
-            wbq_ref[pl.ds(pl.multiple_of((quarter * 4 + t) * wb_rows, wb_rows), wb_rows), :],
-        )
-
-    keep_ref[:wf_rows, :], keep_ref[wf_rows:size, :] = block(mine)
-    note = jnp.full((PAD, width), sums, F32)
-    keep_ref[size:, :] = note
-    line = lax.broadcasted_iota(jnp.int32, (PAD, width), 0)
-    n_hi = note.astype(BF)
-    n_mid, n_lo = halves(note - n_hi.astype(F32))
-    coded = jnp.where(
-        line == 0,
-        n_hi.astype(F32),
-        jnp.where(line == 1, n_mid.astype(F32), jnp.where(line == 2, n_lo.astype(F32), 0.0)),
-    ).astype(BF)
+        rows = pl.ds(pl.multiple_of(t * size, PAD), size)
+        return keep_ref[rows, :] + got_ref[rows, :].astype(F32)
+
+    own_ref[:size, :] = block(mine)
+    own_ref[size:, :] = note
+    coded = coded_note(note)
     for ref, (_, turn) in zip(sends, LINE):
-        part_f, part_b = block(mine ^ turn)
-        ref[:wf_rows, :] = part_f.astype(BF)
-        ref[wf_rows:size, :] = part_b.astype(BF)
+        ref[:size, :] = block(mine ^ turn).astype(BF)
         ref[size:, :] = coded
 
 
@@ -272,8 +292,7 @@
     note = keep_ref[size : size + 1, :1]
     for ref in refs[:3]:
         total = total + ref[:size, :].astype(F32)
-        coded = ref[size:, :].astype(F32)
-        note = note + (coded[0:1, :1] + coded[1:2, :1] + coded[2:3, :1])
+        note = note + read_note(ref[size:, :].astype(F32))[:, :1]
     sum_ref[...] = total.astype(sum_ref.dtype)
     note_ref[...] = note * (1.0 / width)
 
@@ -292,6 +311,20 @@
             )
 
 
+def assemble_kernel(place_ref, *refs, wf_rows, wb_rows, factor_f, factor_b):
+    place = place_ref[0]
+    wf_ref, wb_ref = refs[2:]
+    for offset, ref in zip((0, 8), refs):
+        for e, turn in enumerate(TURNS):
+            to = place ^ (offset + turn)
+            wf_ref[pl.ds(pl.multiple_of(to * wf_rows, wf_rows), wf_rows), :] = (
+                ref[e, :wf_rows, :].astype(F32) * factor_f
+            )
+            wb_ref[pl.ds(pl.multiple_of(to * wb_rows, wb_rows), wb_rows), :] = (
+                ref[e, wf_rows:, :].astype(F32) * factor_b
+            )
+
+
 SMEM = pl.BlockSpec(memory_space=pltpu.SMEM)
 VMEM = pl.BlockSpec(memory_space=pltpu.VMEM)
 HBM = pl.BlockSpec(memory_space=pltpu.HBM)
@@ -308,16 +341,14 @@
     total = size * rows
     assert bits >= 4 and size == 1 << bits and high // 4 == width == wide
 
-    quarters = [reverse_bits((me ^ m) & 3, 2).astype(jnp.int32) for m in GROUP]
-    ends = [(at + 2) * rows + PAD for at in FEAT_AT]
-    far, near, cut, head, wb_copy = pl.pallas_call(
+    core = (me & 1).astype(jnp.int32)
+    near, cut, head, wb_copy = pl.pallas_call(
         feature_kernel,
         in_specs=[SMEM] + [HBM] * 9,
-        out_specs=[VMEM] * 5,
+        out_specs=[VMEM] * 4,
         out_shape=[
-            jax.ShapeDtypeStruct((ends[1], width), BF),
-            jax.ShapeDtypeStruct((ends[2], width), BF),
-            jax.ShapeDtypeStruct((rows, width), BF),
+            jax.ShapeDtypeStruct(((FEAT_AT + 2) * rows + PAD, width), BF),
+            jax.ShapeDtypeStruct((2 * rows, width), BF),
             jax.ShapeDtypeStruct(hidden_b.shape, BF),
             jax.ShapeDtypeStruct(w_b.shape, BF),
         ],
@@ -333,7 +364,7 @@
         ],
         compiler_params=pltpu.CompilerParams(vmem_limit_bytes=60 * 2**20),
     )(
-        jnp.stack(quarters),
+        core.reshape(1),
         hidden_f,
         hidden_t,
         hidden_b,
@@ -344,42 +375,49 @@
         latent_ids.reshape(1, rows),
         positives.reshape(1, rows),
     )
-    far2 = swap(far, 2, size)
     for mask in reversed(beyond):
         head = jnp.concatenate([head, swap(head, mask, size)], axis=0)
-    tail0 = jnp.concatenate(
-        [head[rows:]] * (len(beyond) > 0) + [swap(head, mask, size) for mask, _ in LINE], axis=0
-    )
+    pieces = [head] + [swap(head, mask, size) for mask, _ in LINE]
+    pieces = pieces + [swap(piece, 2, size) for piece in pieces]
+    tail0 = jnp.concatenate([head[rows:]] * (len(beyond) > 0) + pieces[1:], axis=0)
     near1 = swap(near, 1, size)
-    tail2 = swap(tail0, 2, size)
     tail1 = swap(tail0, 1, size)
-    far3 = swap(far2, 1, size)
-    tail3 = swap(tail2, 1, size)
 
     inner = reverse_bits(jnp.arange(size // 16, dtype=jnp.int32), bits - 4) << 4
+    along = (0,) + tuple(mask for mask, _ in LINE)
     bases = jnp.concatenate(
-        [(me ^ m ^ o ^ inner) * rows for m in GROUP for o in (0,) + tuple(o for o, _ in LINE)]
+        [(me ^ m ^ y ^ z ^ inner) * rows for m in GROUP for y in (0, 2) for z in along]
     ).astype(jnp.int32)
     place = reverse_bits(me & 15, 4).astype(jnp.int32)
-    places = jnp.stack([quarters[0], place & 3])
+    places = jnp.stack([core, (place >> 2) & 1])
     wf_rows, wb_rows = high // 16, wide // 16
     each = wf_rows + wb_rows
-    keep, *sends = pl.pallas_call(
+    keep, send = pl.pallas_call(
         functools.partial(pair_kernel, rows=rows, total=total),
-        in_specs=[SMEM] * 2 + [VMEM] * 10,
-        out_specs=[VMEM] * 4,
-        out_shape=[jax.ShapeDtypeStruct((each + PAD, width), F32)]
-        + [jax.ShapeDtypeStruct((each + PAD, width), BF)] * 3,
+        in_specs=[SMEM] * 2 + [VMEM] * 6,
+        out_specs=[VMEM] * 2,
+        out_shape=[
+            jax.ShapeDtypeStruct((4 * each + PAD, width), F32),
+            jax.ShapeDtypeStruct((4 * each + PAD, width), BF),
+        ],
         scratch_shapes=[
             pltpu.VMEM((total, width), F32),
             pltpu.VMEM((total, width), BF),
             pltpu.VMEM((width, width), F32),
-            pltpu.VMEM((4 * rows, wide), F32),
-            pltpu.VMEM((width, width), F32),
+            pltpu.VMEM((2 * rows, wide), F32),
+            pltpu.VMEM((2 * width, width), F32),
             pltpu.VMEM((wide, width), F32),
         ],
         compiler_params=pltpu.CompilerParams(vmem_limit_bytes=12 * 2**20 + total * width * 8),
-    )(bases, places, near, far2, near1, far3, tail0, tail2, tail1, tail3, cut, wb_copy)
+    )(bases, places, near, near1, tail0, tail1, cut, wb_copy)
+    keep, *sends = pl.pallas_call(
+        cross_kernel,
+        in_specs=[SMEM] + [VMEM] * 2,
+        out_specs=[VMEM] * 4,
+        out_shape=[jax.ShapeDtypeStruct((each + PAD, width), F32)]
+        + [jax.ShapeDtypeStruct((each + PAD, width), BF)] * 3,
+        compiler_params=pltpu.CompilerParams(vmem_limit_bytes=8 * 2**20),
+    )((place & 3).reshape(1), keep, swap(send, 2, size))
 
     got = [swap(part, mask, size) for part, (mask, _) in zip(sends, LINE)]
     result, note = pl.pallas_call(
@@ -396,10 +434,9 @@
         result = result + swap(result, mask, size)
         note = note + swap(note, mask, size)
     result = result.astype(BF).reshape(1, each, width)
-    near = jnp.concatenate([result] + [swap(result, mask, size) for mask, _ in LINE], axis=0)
-    near_y = swap(near, 2, size)
+    pieces = [result] + [swap(result, mask, size) for mask, _ in LINE]
+    near = jnp.concatenate(pieces + [swap(piece, 2, size) for piece in pieces], axis=0)
     far = swap(near, 1, size)
-    far_y = swap(near_y, 1, size)
     grad_wf, grad_wb = pl.pallas_call(
         functools.partial(
             assemble_kernel,
@@ -408,14 +445,14 @@
             factor_f=math.sqrt(high),
             factor_b=math.sqrt(wide),
         ),
-        in_specs=[SMEM] + [VMEM] * 4,
+        in_specs=[SMEM] + [VMEM] * 2,
         out_specs=[VMEM] * 2,
         out_shape=[
             jax.ShapeDtypeStruct((high, width), F32),
             jax.ShapeDtypeStruct((wide, width), F32),
         ],
         compiler_params=pltpu.CompilerParams(vmem_limit_bytes=16 * 2**20),
-    )(place.reshape(1), near, near_y, far, far_y)
+    )(place.reshape(1), near, far)
     return (grad_wf, grad_wb, note.reshape(1))
 
 

time: 58.5 us -> 58 us (level)
  starting transfers between devices: 20 us -> 25.4 us
  waiting for transfers between devices: 24.3 us -> 21.4 us
  Pallas kernels: 12.5 us -> 10 us
  other arithmetic: 0.75 us -> 0.08 us
    ppermute x18 -> x21, starting transfers between devices: 20 us -> 25.4 us  [swap(): return lax.ppermute(array, 'fa', [(i, i ^ mask) for i in range(size)])]
    ppermute x18 -> x21, waiting for transfers between devices: 24.3 us -> 21.4 us  [swap(): return lax.ppermute(array, 'fa', [(i, i ^ mask) for i in range(size)])]
    pallas_call x1, Pallas kernels: 7.35 us -> 5.55 us  [body(): pl.pallas_call(functools.partial(pair_kernel, rows=rows, total=total), in...]
    pallas_call x1, Pallas kernels: 3.49 us -> 2.76 us  [body(): pl.pallas_call(feature_kernel, in_specs=[SMEM] + [HBM] * 9, out_specs=[VM...]
    another operation x2 -> x1, other arithmetic: 0.73 us -> 0.08 us  [body(): places = jnp.stack([core, place >> 2 & 1])]
  transfers between devices with their start and end apart: 18 -> 21, of which waited for: 12 -> 14; matrix products, arithmetic and copies ran while one was open for 0% -> 0% of each run, Pallas kernels for 0% -> 0%
where the time goes in v5:
time: 58 us; the launch traced here: 57.8 us
  starting transfers between devices  25.4 us (44%)
  waiting for transfers between devices  21.4 us (37%)
  Pallas kernels  10 us (17%)
  between operations  0.75 us (1%)
    ppermute x21, starting transfers between devices, swap(): return lax.ppermute(array, 'fa', [(i, i ^ mask) for i in range(size)])  25.4 us
    ppermute x21, waiting for transfers between devices, swap(): return lax.ppermute(array, 'fa', [(i, i ^ mask) for i in range(size)])  21.4 us
    pallas_call x1, Pallas kernels, body(): pl.pallas_call(functools.partial(pair_kernel, rows=rows, total=total), in...  5.55 us
    pallas_call x1, Pallas kernels, body(): pl.pallas_call(feature_kernel, in_specs=[SMEM] + [HBM] * 9, out_specs=[VM...  2.76 us
  transfers between devices with their start and end apart: 21, of which 14 were waited for; matrix products, arithmetic and copies ran while one was open for 0% of the time, Pallas kernels for 0%

profile of v5, /device:TPU:0, one launch (start us, length us, event | category | flops | bytes accessed | tf_op | source)
XLA Modules:
  0.0 57.8 jit_solution(3750674971367478245)
XLA Ops:
  0.6 2.8 %shard_map.112 = (bf16[656,256]{1,0:T(8,128)(2,1)}, bf16[256,256]{1,0:T(8,128)(2,1)}, bf16[128,256]{1,0:T(8,128)(2,1)}, bf16[256,256]{1,0:T(8,128)(2,1)}) custom-call(s32[1]{0:T(128)} %bitcast.18.core_ref, bf16[128,1024]{1,0:T(8,128)(2,1)} %hf_hbm.1, bf16[128,1024]{1,0:T(8,128)(2,1)} %ht_hbm.1, bf16[128,256]{1,0:T(8,128)(2,1)} %hb_hbm.1, ...), custom_call_target="tpu_custom_call" | custom-call | tf_op jit(solution)/shard_map/pallas_call | solution.py:345
  3.4 5.1 %collective-permute-start.1 = (bf16[128,256]{1,0:T(8,128)(2,1)}, bf16[128,256]{1,0:T(8,128)(2,1)S(1)}, u32[]{:S(2)}, u32[]{:S(2)}) collective-permute-start(bf16[128,256]{1,0:T(8,128)(2,1)} %get-tuple-element.18), channel_id=1, source_target_pairs={{0,12},{1,13},{2,14},{3,15},{4,8},{5,9},{6,10},{7,11},{8,4},{9,5},... | collective-permute-start | bytes 196616 | tf_op jit(solution)/shard_map/ppermute | solution.py:38
  8.5 0.0 collective-permute-start.2
  8.5 0.6 %collective-permute-start.3 = (bf16[128,256]{1,0:T(8,128)(2,1)}, bf16[128,256]{1,0:T(8,128)(2,1)S(1)}, u32[]{:S(2)}, u32[]{:S(2)}) collective-permute-start(bf16[128,256]{1,0:T(8,128)(2,1)} %get-tuple-element.18), channel_id=1, source_target_pairs={{0,4},{1,5},{2,6},{3,7},{4,0},{5,1},{6,2},{7,3},{8,12},{9,13},{10,... | collective-permute-start | bytes 196616 | tf_op jit(solution)/shard_map/ppermute | solution.py:38
  9.2 1.7 %collective-permute-start.4 = (bf16[128,256]{1,0:T(8,128)(2,1)}, bf16[128,256]{1,0:T(8,128)(2,1)S(1)}, u32[]{:S(2)}, u32[]{:S(2)}) collective-permute-start(bf16[128,256]{1,0:T(8,128)(2,1)} %get-tuple-element.18), channel_id=1, source_target_pairs={{0,2},{1,3},{2,0},{3,1},{4,6},{5,7},{6,4},{7,5},{8,10},{9,11},{10,... | collective-permute-start | bytes 196616 | tf_op jit(solution)/shard_map/ppermute | solution.py:38
  10.8 0.5 collective-permute-done.1
  11.3 1.9 %collective-permute-start.5 = (bf16[128,256]{1,0:T(8,128)(2,1)S(1)}, bf16[128,256]{1,0:T(8,128)(2,1)S(1)}, u32[]{:S(2)}, u32[]{:S(2)}) collective-permute-start(bf16[128,256]{1,0:T(8,128)(2,1)S(1)} %collective-permute-done.1), channel_id=1, source_target_pairs={{0,2},{1,3},{2,0},{3,1},{4,6},{5,7},{6,4},{7,5},{8,10},{9,11},{10,... | collective-permute-start | bytes 196616 | tf_op jit(solution)/shard_map/ppermute | solution.py:38
  13.2 1.1 %collective-permute-done.2 = bf16[128,256]{1,0:T(8,128)(2,1)S(1)} collective-permute-done((bf16[128,256]{1,0:T(8,128)(2,1)}, bf16[128,256]{1,0:T(8,128)(2,1)S(1)}, u32[]{:S(2)}, u32[]{:S(2)}) %collective-permute-start.2) | collective-permute-done | bytes 65568 | tf_op jit(solution)/shard_map/ppermute | solution.py:38
  14.3 1.5 %collective-permute-start.6 = (bf16[128,256]{1,0:T(8,128)(2,1)S(1)}, bf16[128,256]{1,0:T(8,128)(2,1)S(1)}, u32[]{:S(2)}, u32[]{:S(2)}) collective-permute-start(bf16[128,256]{1,0:T(8,128)(2,1)S(1)} %collective-permute-done.2), channel_id=1, source_target_pairs={{0,2},{1,3},{2,0},{3,1},{4,6},{5,7},{6,4},{7,5},{8,10},{9,11},{10,... | collective-permute-start | bytes 196616 | tf_op jit(solution)/shard_map/ppermute | solution.py:38
  15.9 0.0 copy-start
  15.9 0.0 collective-permute-done.3
  15.9 0.6 collective-permute-start.7
  16.4 0.0 collective-permute-done.4
  16.5 0.0 collective-permute-done.5
  16.5 2.6 %collective-permute-done.6 = bf16[128,256]{1,0:T(8,128)(2,1)S(1)} collective-permute-done((bf16[128,256]{1,0:T(8,128)(2,1)S(1)}, bf16[128,256]{1,0:T(8,128)(2,1)S(1)}, u32[]{:S(2)}, u32[]{:S(2)}) %collective-permute-start.6) | collective-permute-done | bytes 65568 | tf_op jit(solution)/shard_map/ppermute | solution.py:38
  19.1 0.0 copy-start.1
  19.1 0.0 copy-start.2
  19.1 1.1 %collective-permute-done.7 = bf16[128,256]{1,0:T(8,128)(2,1)S(1)} collective-permute-done((bf16[128,256]{1,0:T(8,128)(2,1)S(1)}, bf16[128,256]{1,0:T(8,128)(2,1)S(1)}, u32[]{:S(2)}, u32[]{:S(2)}) %collective-permute-start.7) | collective-permute-done | bytes 65568 | tf_op jit(solution)/shard_map/ppermute | solution.py:38
  20.2 0.0 collective-permute-start.8
  20.2 0.0 copy-done
  20.2 0.5 collective-permute-start
  20.7 0.1 concatenate.9.refs_0_
  20.8 0.1 pad_add_fusion.refs_1_
  20.9 1.6 %collective-permute-done.refs_3_ = bf16[656,256]{1,0:T(8,128)(2,1)S(1)} collective-permute-done((bf16[656,256]{1,0:T(8,128)(2,1)S(1)}, bf16[656,256]{1,0:T(8,128)(2,1)S(1)}, u32[]{:S(2)}, u32[]{:S(2)}) %collective-permute-start) | collective-permute-done | bytes 335904 | tf_op jit(solution)/shard_map/ppermute | solution.py:38
  22.5 0.0 collective-permute-done.8.refs_5_
  22.5 0.0 copy-done.1
  22.5 0.0 copy-done.2
  22.5 5.5 %shard_map.113 = (f32[336,256]{1,0:T(8,128)S(1)}, bf16[336,256]{1,0:T(8,128)(2,1)S(1)}) custom-call(s32[16]{0:T(128)S(1)} %concatenate.9.refs_0_, s32[2]{0:T(128)S(1)} %pad_add_fusion.refs_1_, bf16[656,256]{1,0:T(8,128)(2,1)S(1)} %copy-done, bf16[656,256]{1,0:T(8,128)(2,1)S(1)} %collective-permute-done.refs_3_, ...), custom_call_target="tpu_custom_call" | custom-call | tf_op jit(solution)/shard_map/pallas_call | solution.py:395
  28.1 1.0 %collective-permute-start.9 = (bf16[336,256]{1,0:T(8,128)(2,1)S(1)}, bf16[336,256]{1,0:T(8,128)(2,1)S(1)}, u32[]{:S(2)}, u32[]{:S(2)}) collective-permute-start(bf16[336,256]{1,0:T(8,128)(2,1)S(1)} %get-tuple-element.22), channel_id=1, source_target_pairs={{0,2},{1,3},{2,0},{3,1},{4,6},{5,7},{6,4},{7,5},{8,10},{9,11},{10,... | collective-permute-start | bytes 516104 | tf_op jit(solution)/shard_map/ppermute | solution.py:38
  29.0 5.5 %collective-permute-done.9.got_ref = bf16[336,256]{1,0:T(8,128)(2,1)S(1)} collective-permute-done((bf16[336,256]{1,0:T(8,128)(2,1)S(1)}, bf16[336,256]{1,0:T(8,128)(2,1)S(1)}, u32[]{:S(2)}, u32[]{:S(2)}) %collective-permute-start.9) | collective-permute-done | bytes 172064 | tf_op jit(solution)/shard_map/ppermute | solution.py:38
  34.6 2.8 %collective-permute-start.10 = (bf16[96,256]{1,0:T(8,128)(2,1)S(1)}, bf16[96,256]{1,0:T(8,128)(2,1)S(1)}, u32[]{:S(2)}, u32[]{:S(2)}) collective-permute-start(bf16[96,256]{1,0:T(8,128)(2,1)S(1)} %get-tuple-element.24), channel_id=1, source_target_pairs={{0,12},{1,13},{2,14},{3,15},{4,8},{5,9},{6,10},{7,11},{8,4},{9,5},... | collective-permute-start | bytes 147464 | tf_op jit(solution)/shard_map/ppermute | solution.py:38
  37.4 0.0 collective-permute-start.11
  37.4 1.7 %collective-permute-start.12 = (bf16[96,256]{1,0:T(8,128)(2,1)S(1)}, bf16[96,256]{1,0:T(8,128)(2,1)S(1)}, u32[]{:S(2)}, u32[]{:S(2)}) collective-permute-start(bf16[96,256]{1,0:T(8,128)(2,1)S(1)} %get-tuple-element.26), channel_id=1, source_target_pairs={{0,4},{1,5},{2,6},{3,7},{4,0},{5,1},{6,2},{7,3},{8,12},{9,13},{10,... | collective-permute-start | bytes 147464 | tf_op jit(solution)/shard_map/ppermute | solution.py:38
  39.0 1.6 %collective-permute-done.10.refs_0_ = bf16[96,256]{1,0:T(8,128)(2,1)S(1)} collective-permute-done((bf16[96,256]{1,0:T(8,128)(2,1)S(1)}, bf16[96,256]{1,0:T(8,128)(2,1)S(1)}, u32[]{:S(2)}, u32[]{:S(2)}) %collective-permute-start.10) | collective-permute-done | bytes 49184 | tf_op jit(solution)/shard_map/ppermute | solution.py:38
  40.6 1.7 %collective-permute-done.11.refs_1_ = bf16[96,256]{1,0:T(8,128)(2,1)S(1)} collective-permute-done((bf16[96,256]{1,0:T(8,128)(2,1)S(1)}, bf16[96,256]{1,0:T(8,128)(2,1)S(1)}, u32[]{:S(2)}, u32[]{:S(2)}) %collective-permute-start.11) | collective-permute-done | bytes 49184 | tf_op jit(solution)/shard_map/ppermute | solution.py:38
  42.4 0.0 collective-permute-done.12.refs_2_
  42.4 0.5 shard_map.115
  42.9 2.0 %collective-permute-start.13 = (bf16[1,80,256]{2,1,0:T(8,128)(2,1)S(1)}, bf16[1,80,256]{2,1,0:T(8,128)(2,1)S(1)}, u32[]{:S(2)}, u32[]{:S(2)}) collective-permute-start(bf16[1,80,256]{2,1,0:T(8,128)(2,1)S(1)} %bitcast.25), channel_id=1, source_target_pairs={{0,12},{1,13},{2,14},{3,15},{4,8},{5,9},{6,10},{7,11},{8,4},{9,5},... | collective-permute-start | bytes 122888 | tf_op jit(solution)/shard_map/ppermute | solution.py:38
  44.9 0.3 collective-permute-start.14
  45.1 2.2 %collective-permute-start.15 = (bf16[1,80,256]{2,1,0:T(8,128)(2,1)S(1)}, bf16[1,80,256]{2,1,0:T(8,128)(2,1)S(1)}, u32[]{:S(2)}, u32[]{:S(2)}) collective-permute-start(bf16[1,80,256]{2,1,0:T(8,128)(2,1)S(1)} %bitcast.27), channel_id=1, source_target_pairs={{0,4},{1,5},{2,6},{3,7},{4,0},{5,1},{6,2},{7,3},{8,12},{9,13},{10,... | collective-permute-start | bytes 122888 | tf_op jit(solution)/shard_map/ppermute | solution.py:38
  47.3 0.8 %collective-permute-start.16 = (bf16[1,80,256]{2,1,0:T(8,128)(2,1)S(1)}, bf16[1,80,256]{2,1,0:T(8,128)(2,1)S(1)}, u32[]{:S(2)}, u32[]{:S(2)}) collective-permute-start(bf16[1,80,256]{2,1,0:T(8,128)(2,1)S(1)} %bitcast.28), channel_id=1, source_target_pairs={{0,2},{1,3},{2,0},{3,1},{4,6},{5,7},{6,4},{7,5},{8,10},{9,11},{10,... | collective-permute-start | bytes 122888 | tf_op jit(solution)/shard_map/ppermute | solution.py:38
  48.1 0.6 %collective-permute-done.13 = bf16[1,80,256]{2,1,0:T(8,128)(2,1)S(1)} collective-permute-done((bf16[1,80,256]{2,1,0:T(8,128)(2,1)S(1)}, bf16[1,80,256]{2,1,0:T(8,128)(2,1)S(1)}, u32[]{:S(2)}, u32[]{:S(2)}) %collective-permute-start.13) | collective-permute-done | bytes 40992 | tf_op jit(solution)/shard_map/ppermute | solution.py:38
  48.7 0.9 %collective-permute-start.17 = (bf16[1,80,256]{2,1,0:T(8,128)(2,1)S(1)}, bf16[1,80,256]{2,1,0:T(8,128)(2,1)S(1)}, u32[]{:S(2)}, u32[]{:S(2)}) collective-permute-start(bf16[1,80,256]{2,1,0:T(8,128)(2,1)S(1)} %collective-permute-done.13), channel_id=1, source_target_pairs={{0,2},{1,3},{2,0},{3,1},{4,6},{5,7},{6,4},{7,5},{8,10},{9,11},{10,... | collective-permute-start | bytes 122888 | tf_op jit(solution)/shard_map/ppermute | solution.py:38
  49.6 0.6 %collective-permute-done.14 = bf16[1,80,256]{2,1,0:T(8,128)(2,1)S(1)} collective-permute-done((bf16[1,80,256]{2,1,0:T(8,128)(2,1)S(1)}, bf16[1,80,256]{2,1,0:T(8,128)(2,1)S(1)}, u32[]{:S(2)}, u32[]{:S(2)}) %collective-permute-start.14) | collective-permute-done | bytes 40992 | tf_op jit(solution)/shard_map/ppermute | solution.py:38
  50.2 0.9 %collective-permute-start.18 = (bf16[1,80,256]{2,1,0:T(8,128)(2,1)S(1)}, bf16[1,80,256]{2,1,0:T(8,128)(2,1)S(1)}, u32[]{:S(2)}, u32[]{:S(2)}) collective-permute-start(bf16[1,80,256]{2,1,0:T(8,128)(2,1)S(1)} %collective-permute-done.14), channel_id=1, source_target_pairs={{0,2},{1,3},{2,0},{3,1},{4,6},{5,7},{6,4},{7,5},{8,10},{9,11},{10,... | collective-permute-start | bytes 122888 | tf_op jit(solution)/shard_map/ppermute | solution.py:38
  51.1 0.0 collective-permute-done.15
  51.1 1.2 %collective-permute-start.19 = (bf16[1,80,256]{2,1,0:T(8,128)(2,1)S(1)}, bf16[1,80,256]{2,1,0:T(8,128)(2,1)S(1)}, u32[]{:S(2)}, u32[]{:S(2)}) collective-permute-start(bf16[1,80,256]{2,1,0:T(8,128)(2,1)S(1)} %collective-permute-done.15), channel_id=1, source_target_pairs={{0,2},{1,3},{2,0},{3,1},{4,6},{5,7},{6,4},{7,5},{8,10},{9,11},{10,... | collective-permute-start | bytes 122888 | tf_op jit(solution)/shard_map/ppermute | solution.py:38
  52.2 0.0 collective-permute-done.16
  52.2 0.4 collective-permute-done.17
  52.7 1.5 %collective-permute-done.18 = bf16[1,80,256]{2,1,0:T(8,128)(2,1)S(1)} collective-permute-done((bf16[1,80,256]{2,1,0:T(8,128)(2,1)S(1)}, bf16[1,80,256]{2,1,0:T(8,128)(2,1)S(1)}, u32[]{:S(2)}, u32[]{:S(2)}) %collective-permute-start.18) | collective-permute-done | bytes 40992 | tf_op jit(solution)/shard_map/ppermute | solution.py:38
  54.2 0.9 %collective-permute-done.19 = bf16[1,80,256]{2,1,0:T(8,128)(2,1)S(1)} collective-permute-done((bf16[1,80,256]{2,1,0:T(8,128)(2,1)S(1)}, bf16[1,80,256]{2,1,0:T(8,128)(2,1)S(1)}, u32[]{:S(2)}, u32[]{:S(2)}) %collective-permute-start.19) | collective-permute-done | bytes 40992 | tf_op jit(solution)/shard_map/ppermute | solution.py:38
  55.1 0.0 collective-permute-start.20
  55.1 1.6 %collective-permute-done.20.refs_1_ = bf16[8,80,256]{2,1,0:T(8,128)(2,1)S(1)} collective-permute-done((bf16[8,80,256]{2,1,0:T(8,128)(2,1)S(1)}, bf16[8,80,256]{2,1,0:T(8,128)(2,1)S(1)}, u32[]{:S(2)}, u32[]{:S(2)}) %collective-permute-start.20) | collective-permute-done | bytes 327712 | tf_op jit(solution)/shard_map/ppermute | solution.py:38
  56.7 1.1 %shard_map.116 = (f32[1024,256]{1,0:T(8,128)}, f32[256,256]{1,0:T(8,128)}) custom-call(s32[1]{0:T(128)} %bitcast.place_ref, bf16[8,80,256]{2,1,0:T(8,128)(2,1)S(1)} %constant_dynamic-update-slice_fusion.7.refs_0_, bf16[8,80,256]{2,1,0:T(8,128)(2,1)S(1)} %collective-permute-done.20.refs_1_), custom_call_target="tpu_custom_call" | custom-call | tf_op jit(solution)/shard_map/pallas_call | solution.py:440
  (16 shorter events, 0.1 us)
Async XLA Ops:
  3.4 7.9 %collective-permute-start.1 = (bf16[128,256]{1,0:T(8,128)(2,1)}, bf16[128,256]{1,0:T(8,128)(2,1)S(1)}, u32[]{:S(2)}, u32[]{:S(2)}) collective-permute-start(bf16[128,256]{1,0:T(8,128)(2,1)} %get-tuple-element.18), channel_id=1, source_target_pairs={{0,12},{1,13},{2,14},{3,15},{4,8},{5,9},{6,10},{7,11},{8,4},{9,5},... | collective-permute-start | bytes 196616 | tf_op jit(solution)/shard_map/ppermute | solution.py:38
  8.5 5.8 %collective-permute-start.2 = (bf16[128,256]{1,0:T(8,128)(2,1)}, bf16[128,256]{1,0:T(8,128)(2,1)S(1)}, u32[]{:S(2)}, u32[]{:S(2)}) collective-permute-start(bf16[128,256]{1,0:T(8,128)(2,1)} %get-tuple-element.18), channel_id=1, source_target_pairs={{0,8},{1,9},{2,10},{3,11},{4,12},{5,13},{6,14},{7,15},{8,0},{9,1},... | collective-permute-start | bytes 196616 | tf_op jit(solution)/shard_map/ppermute | solution.py:38
  8.5 7.3 %collective-permute-start.3 = (bf16[128,256]{1,0:T(8,128)(2,1)}, bf16[128,256]{1,0:T(8,128)(2,1)S(1)}, u32[]{:S(2)}, u32[]{:S(2)}) collective-permute-start(bf16[128,256]{1,0:T(8,128)(2,1)} %get-tuple-element.18), channel_id=1, source_target_pairs={{0,4},{1,5},{2,6},{3,7},{4,0},{5,1},{6,2},{7,3},{8,12},{9,13},{10,... | collective-permute-start | bytes 196616 | tf_op jit(solution)/shard_map/ppermute | solution.py:38
  9.2 7.3 %collective-permute-start.4 = (bf16[128,256]{1,0:T(8,128)(2,1)}, bf16[128,256]{1,0:T(8,128)(2,1)S(1)}, u32[]{:S(2)}, u32[]{:S(2)}) collective-permute-start(bf16[128,256]{1,0:T(8,128)(2,1)} %get-tuple-element.18), channel_id=1, source_target_pairs={{0,2},{1,3},{2,0},{3,1},{4,6},{5,7},{6,4},{7,5},{8,10},{9,11},{10,... | collective-permute-start | bytes 196616 | tf_op jit(solution)/shard_map/ppermute | solution.py:38
  11.3 5.1 %collective-permute-start.5 = (bf16[128,256]{1,0:T(8,128)(2,1)S(1)}, bf16[128,256]{1,0:T(8,128)(2,1)S(1)}, u32[]{:S(2)}, u32[]{:S(2)}) collective-permute-start(bf16[128,256]{1,0:T(8,128)(2,1)S(1)} %collective-permute-done.1), channel_id=1, source_target_pairs={{0,2},{1,3},{2,0},{3,1},{4,6},{5,7},{6,4},{7,5},{8,10},{9,11},{10,... | collective-permute-start | bytes 196616 | tf_op jit(solution)/shard_map/ppermute | solution.py:38
  14.3 4.8 %collective-permute-start.6 = (bf16[128,256]{1,0:T(8,128)(2,1)S(1)}, bf16[128,256]{1,0:T(8,128)(2,1)S(1)}, u32[]{:S(2)}, u32[]{:S(2)}) collective-permute-start(bf16[128,256]{1,0:T(8,128)(2,1)S(1)} %collective-permute-done.2), channel_id=1, source_target_pairs={{0,2},{1,3},{2,0},{3,1},{4,6},{5,7},{6,4},{7,5},{8,10},{9,11},{10,... | collective-permute-start | bytes 196616 | tf_op jit(solution)/shard_map/ppermute | solution.py:38
  15.9 4.4 %copy-start = (bf16[656,256]{1,0:T(8,128)(2,1)S(1)}, bf16[656,256]{1,0:T(8,128)(2,1)}, u32[]{:S(2)}) copy-start(bf16[656,256]{1,0:T(8,128)(2,1)} %get-tuple-element.17.refs_2_) | copy-start | bytes 1007620
  15.9 4.3 %collective-permute-start.7 = (bf16[128,256]{1,0:T(8,128)(2,1)S(1)}, bf16[128,256]{1,0:T(8,128)(2,1)S(1)}, u32[]{:S(2)}, u32[]{:S(2)}) collective-permute-start(bf16[128,256]{1,0:T(8,128)(2,1)S(1)} %collective-permute-done.3), channel_id=1, source_target_pairs={{0,2},{1,3},{2,0},{3,1},{4,6},{5,7},{6,4},{7,5},{8,10},{9,11},{10,... | collective-permute-start | bytes 196616 | tf_op jit(solution)/shard_map/ppermute | solution.py:38
  19.1 3.4 %copy-start.1 = (bf16[256,256]{1,0:T(8,128)(2,1)S(1)}, bf16[256,256]{1,0:T(8,128)(2,1)}, u32[]{:S(2)}) copy-start(bf16[256,256]{1,0:T(8,128)(2,1)} %get-tuple-element.19.refs_6_) | copy-start | bytes 393220
  19.1 3.4 %copy-start.2 = (bf16[256,256]{1,0:T(8,128)(2,1)S(1)}, bf16[256,256]{1,0:T(8,128)(2,1)}, u32[]{:S(2)}) copy-start(bf16[256,256]{1,0:T(8,128)(2,1)} %get-tuple-element.20.refs_7_) | copy-start | bytes 393220
  20.2 2.3 %collective-permute-start.8 = (bf16[896,256]{1,0:T(8,128)(2,1)S(1)}, bf16[896,256]{1,0:T(8,128)(2,1)S(1)}, u32[]{:S(2)}, u32[]{:S(2)}) collective-permute-start(bf16[896,256]{1,0:T(8,128)(2,1)S(1)} %constant_dynamic-update-slice_fusion.refs_4_), channel_id=1, source_target_pairs={{0,1},{1,0},{2,3},{3,2},{4,5},{5,4},{6,7},{7,6},{8,9},{9,8},{10,11... | collective-permute-start | bytes 1376264 | tf_op jit(solution)/shard_map/ppermute | solution.py:38
  20.2 2.3 %collective-permute-start = (bf16[656,256]{1,0:T(8,128)(2,1)S(1)}, bf16[656,256]{1,0:T(8,128)(2,1)S(1)}, u32[]{:S(2)}, u32[]{:S(2)}) collective-permute-start(bf16[656,256]{1,0:T(8,128)(2,1)S(1)} %copy-done), channel_id=1, source_target_pairs={{0,1},{1,0},{2,3},{3,2},{4,5},{5,4},{6,7},{7,6},{8,9},{9,8},{10,11... | collective-permute-start | bytes 1007624 | tf_op jit(solution)/shard_map/ppermute | solution.py:38
  28.1 6.5 %collective-permute-start.9 = (bf16[336,256]{1,0:T(8,128)(2,1)S(1)}, bf16[336,256]{1,0:T(8,128)(2,1)S(1)}, u32[]{:S(2)}, u32[]{:S(2)}) collective-permute-start(bf16[336,256]{1,0:T(8,128)(2,1)S(1)} %get-tuple-element.22), channel_id=1, source_target_pairs={{0,2},{1,3},{2,0},{3,1},{4,6},{5,7},{6,4},{7,5},{8,10},{9,11},{10,... | collective-permute-start | bytes 516104 | tf_op jit(solution)/shard_map/ppermute | solution.py:38
  34.6 6.1 %collective-permute-start.10 = (bf16[96,256]{1,0:T(8,128)(2,1)S(1)}, bf16[96,256]{1,0:T(8,128)(2,1)S(1)}, u32[]{:S(2)}, u32[]{:S(2)}) collective-permute-start(bf16[96,256]{1,0:T(8,128)(2,1)S(1)} %get-tuple-element.24), channel_id=1, source_target_pairs={{0,12},{1,13},{2,14},{3,15},{4,8},{5,9},{6,10},{7,11},{8,4},{9,5},... | collective-permute-start | bytes 147464 | tf_op jit(solution)/shard_map/ppermute | solution.py:38
  37.4 5.0 %collective-permute-start.11 = (bf16[96,256]{1,0:T(8,128)(2,1)S(1)}, bf16[96,256]{1,0:T(8,128)(2,1)S(1)}, u32[]{:S(2)}, u32[]{:S(2)}) collective-permute-start(bf16[96,256]{1,0:T(8,128)(2,1)S(1)} %get-tuple-element.25), channel_id=1, source_target_pairs={{0,8},{1,9},{2,10},{3,11},{4,12},{5,13},{6,14},{7,15},{8,0},{9,1},... | collective-permute-start | bytes 147464 | tf_op jit(solution)/shard_map/ppermute | solution.py:38
  37.4 5.0 %collective-permute-start.12 = (bf16[96,256]{1,0:T(8,128)(2,1)S(1)}, bf16[96,256]{1,0:T(8,128)(2,1)S(1)}, u32[]{:S(2)}, u32[]{:S(2)}) collective-permute-start(bf16[96,256]{1,0:T(8,128)(2,1)S(1)} %get-tuple-element.26), channel_id=1, source_target_pairs={{0,4},{1,5},{2,6},{3,7},{4,0},{5,1},{6,2},{7,3},{8,12},{9,13},{10,... | collective-permute-start | bytes 147464 | tf_op jit(solution)/shard_map/ppermute | solution.py:38
  42.9 5.8 %collective-permute-start.13 = (bf16[1,80,256]{2,1,0:T(8,128)(2,1)S(1)}, bf16[1,80,256]{2,1,0:T(8,128)(2,1)S(1)}, u32[]{:S(2)}, u32[]{:S(2)}) collective-permute-start(bf16[1,80,256]{2,1,0:T(8,128)(2,1)S(1)} %bitcast.25), channel_id=1, source_target_pairs={{0,12},{1,13},{2,14},{3,15},{4,8},{5,9},{6,10},{7,11},{8,4},{9,5},... | collective-permute-start | bytes 122888 | tf_op jit(solution)/shard_map/ppermute | solution.py:38
  44.9 5.3 %collective-permute-start.14 = (bf16[1,80,256]{2,1,0:T(8,128)(2,1)S(1)}, bf16[1,80,256]{2,1,0:T(8,128)(2,1)S(1)}, u32[]{:S(2)}, u32[]{:S(2)}) collective-permute-start(bf16[1,80,256]{2,1,0:T(8,128)(2,1)S(1)} %bitcast.26), channel_id=1, source_target_pairs={{0,8},{1,9},{2,10},{3,11},{4,12},{5,13},{6,14},{7,15},{8,0},{9,1},... | collective-permute-start | bytes 122888 | tf_op jit(solution)/shard_map/ppermute | solution.py:38
  45.1 5.9 %collective-permute-start.15 = (bf16[1,80,256]{2,1,0:T(8,128)(2,1)S(1)}, bf16[1,80,256]{2,1,0:T(8,128)(2,1)S(1)}, u32[]{:S(2)}, u32[]{:S(2)}) collective-permute-start(bf16[1,80,256]{2,1,0:T(8,128)(2,1)S(1)} %bitcast.27), channel_id=1, source_target_pairs={{0,4},{1,5},{2,6},{3,7},{4,0},{5,1},{6,2},{7,3},{8,12},{9,13},{10,... | collective-permute-start | bytes 122888 | tf_op jit(solution)/shard_map/ppermute | solution.py:38
  47.3 5.0 %collective-permute-start.16 = (bf16[1,80,256]{2,1,0:T(8,128)(2,1)S(1)}, bf16[1,80,256]{2,1,0:T(8,128)(2,1)S(1)}, u32[]{:S(2)}, u32[]{:S(2)}) collective-permute-start(bf16[1,80,256]{2,1,0:T(8,128)(2,1)S(1)} %bitcast.28), channel_id=1, source_target_pairs={{0,2},{1,3},{2,0},{3,1},{4,6},{5,7},{6,4},{7,5},{8,10},{9,11},{10,... | collective-permute-start | bytes 122888 | tf_op jit(solution)/shard_map/ppermute | solution.py:38
  48.7 4.0 %collective-permute-start.17 = (bf16[1,80,256]{2,1,0:T(8,128)(2,1)S(1)}, bf16[1,80,256]{2,1,0:T(8,128)(2,1)S(1)}, u32[]{:S(2)}, u32[]{:S(2)}) collective-permute-start(bf16[1,80,256]{2,1,0:T(8,128)(2,1)S(1)} %collective-permute-done.13), channel_id=1, source_target_pairs={{0,2},{1,3},{2,0},{3,1},{4,6},{5,7},{6,4},{7,5},{8,10},{9,11},{10,... | collective-permute-start | bytes 122888 | tf_op jit(solution)/shard_map/ppermute | solution.py:38
  50.2 4.0 %collective-permute-start.18 = (bf16[1,80,256]{2,1,0:T(8,128)(2,1)S(1)}, bf16[1,80,256]{2,1,0:T(8,128)(2,1)S(1)}, u32[]{:S(2)}, u32[]{:S(2)}) collective-permute-start(bf16[1,80,256]{2,1,0:T(8,128)(2,1)S(1)} %collective-permute-done.14), channel_id=1, source_target_pairs={{0,2},{1,3},{2,0},{3,1},{4,6},{5,7},{6,4},{7,5},{8,10},{9,11},{10,... | collective-permute-start | bytes 122888 | tf_op jit(solution)/shard_map/ppermute | solution.py:38
  51.1 4.0 %collective-permute-start.19 = (bf16[1,80,256]{2,1,0:T(8,128)(2,1)S(1)}, bf16[1,80,256]{2,1,0:T(8,128)(2,1)S(1)}, u32[]{:S(2)}, u32[]{:S(2)}) collective-permute-start(bf16[1,80,256]{2,1,0:T(8,128)(2,1)S(1)} %collective-permute-done.15), channel_id=1, source_target_pairs={{0,2},{1,3},{2,0},{3,1},{4,6},{5,7},{6,4},{7,5},{8,10},{9,11},{10,... | collective-permute-start | bytes 122888 | tf_op jit(solution)/shard_map/ppermute | solution.py:38
  55.1 1.6 %collective-permute-start.20 = (bf16[8,80,256]{2,1,0:T(8,128)(2,1)S(1)}, bf16[8,80,256]{2,1,0:T(8,128)(2,1)S(1)}, u32[]{:S(2)}, u32[]{:S(2)}) collective-permute-start(bf16[8,80,256]{2,1,0:T(8,128)(2,1)S(1)} %constant_dynamic-update-slice_fusion.7.refs_0_), channel_id=1, source_target_pairs={{0,1},{1,0},{2,3},{3,2},{4,5},{5,4},{6,7},{7,6},{8,9},{9,8},{10,11... | collective-permute-start | bytes 983048 | tf_op jit(solution)/shard_map/ppermute | solution.py:38

commit v6 on v4

--- a/solution.py
+++ b/solution.py
@@ -14,11 +14,9 @@
 BF = jnp.bfloat16
 F32 = jnp.float32
 GROUP = (0, 2, 1, 3)
-CUT_AT = (0, 0, 0, 1)
-HEAD_AT = (1, 2, 1, 2)
-FEAT_AT = (2, 3, 2, 3)
 PAD = 16
 LINE = ((12, 3), (8, 1), (4, 2))
+TURNS = (0, 3, 1, 2, 4, 7, 5, 6)
 
 
 def dot(left, right):
@@ -49,22 +47,44 @@
     return jnp.transpose(jnp.broadcast_to(row, (rows, rows)))
 
 
+def message_kernel(me_ref, hf_hbm, hb_hbm, wb_hbm, far_ref, near_ref, cut_ref, wb_ref, sems):
+    rows, width = cut_ref.shape
+    me = me_ref[0]
+
+    def columns(mask):
+        other = me ^ mask
+        quarter = (other & 1) * 2 + ((other >> 1) & 1)
+        return hf_hbm.at[:, pl.ds(pl.multiple_of(quarter * width, width), width)]
+
+    moves = [
+        pltpu.make_async_copy(source, target, sems.at[k])
+        for k, (source, target) in enumerate(
+            (
+                (columns(2), far_ref.at[:rows, :]),
+                (columns(3), far_ref.at[rows : 2 * rows, :]),
+                (hb_hbm, far_ref.at[2 * rows :, :]),
+                (columns(1), near_ref.at[:rows, :]),
+                (hb_hbm, near_ref.at[rows:, :]),
+                (columns(0), cut_ref),
+                (wb_hbm, wb_ref),
+            )
+        )
+    ]
+    for move in moves:
+        move.start()
+    for move in moves:
+        move.wait()
+
+
 def feature_kernel(
-    quarter_ref,
     hf_hbm,
     ht_hbm,
-    hb_hbm,
     wf_hbm,
     wt_hbm,
-    wb_hbm,
     lat_hbm,
     ids_hbm,
     pos_hbm,
-    far_ref,
-    near_ref,
-    cut_ref,
-    head_ref,
-    wb_ref,
+    out_ref,
     hf,
     ht,
     wf,
@@ -87,8 +107,6 @@
                 (wf_hbm, wf),
                 (ht_hbm, ht),
                 (wt_hbm, wt),
-                (hb_hbm, head_ref),
-                (wb_hbm, wb_ref),
             )
         )
     ]
@@ -109,42 +127,54 @@
     coded = jnp.where(line == 0, high, jnp.where(line == 1, low, 0.0)).astype(BF)
     coded = jnp.concatenate([coded] + [jnp.zeros((PAD, width - rows), BF)] * (width > rows), axis=1)
 
-    def piece(slot):
-        return hf[:, pl.ds(pl.multiple_of(quarter_ref[slot] * width, width), width)]
-
+    out_ref[2 * rows :, :] = coded
     moves[3].wait()
-    cut_ref[...] = piece(0)
-    far_ref[:rows, :] = piece(1)
-    near_ref[:rows, :] = piece(2)
-    far_ref[rows : 2 * rows, :] = piece(3)
     moves[4].wait()
-    feat = (dot(hf[...], wf[...]) + zrows).astype(BF)
+    out_ref[:rows, :] = (dot(hf[...], wf[...]) + zrows).astype(BF)
     moves[5].wait()
     moves[6].wait()
-    feat_t = (dot(ht[...], wt[...]) + zrows).astype(BF)
-    moves[7].wait()
-    head = head_ref[...]
-    for ref, at in ((far_ref, HEAD_AT[1]), (near_ref, HEAD_AT[2])):
-        ref[at * rows : (at + 1) * rows, :] = head
-        ref[(at + 1) * rows : (at + 2) * rows, :] = feat
-        ref[(at + 2) * rows : (at + 3) * rows, :] = feat_t
-        ref[(at + 3) * rows :, :] = coded
-    moves[8].wait()
+    out_ref[rows : 2 * rows, :] = (dot(ht[...], wt[...]) + zrows).astype(BF)
+
+
+def pack_kernel(near_ref, feats_ref, piece_ref, over_y_ref, to_core_ref):
+    end = feats_ref.shape[0]
+    over_y_ref[:end, :] = feats_ref[...]
+    over_y_ref[end:, :] = piece_ref[...]
+    at = 0
+    for ref in (near_ref, feats_ref):
+        to_core_ref[at : at + ref.shape[0], :] = ref[...]
+        at = at + ref.shape[0]
 
 
 def pair_kernel(*refs, rows, total):
     base_ref, place_ref = refs[:2]
-    mails, tails, cut_ref, wb_ref = refs[2:6], refs[6:10], refs[10], refs[11]
-    keep_ref, sends = refs[12], refs[13:16]
-    raw_ref, back_ref, smat_ref, pick_ref, wfq_ref, wbq_ref = refs[16:]
+    near_ref, far_ref, core_ref, far3_ref, feats_ref = refs[2:7]
+    second_refs, rest_refs = refs[7:9], refs[9:11]
+    cut_ref, wb_ref, keep_ref, sends = refs[11], refs[12], refs[13], refs[14:17]
+    raw_ref, back_ref, smat_ref, pick_ref, wfq_ref, wbq_ref = refs[17:]
     width = wb_ref.shape[1]
     pairs = float(total * (total - 1))
     groups = total // (4 * rows)
-    span = total // 4
+    span = total // 16
     wb = wb_ref[...]
+    end = 2 * rows + PAD
+    feats = ((feats_ref, 0), (second_refs[0], 0), (core_ref, 2 * rows), (second_refs[1], 0))
+    cuts = ((cut_ref, 0), (far_ref, 0), (core_ref, 0), (far3_ref, rows))
+    segments = []
+    for own, far, second, rest in (
+        (near_ref, far_ref, second_refs[0], rest_refs[0]),
+        (core_ref, far3_ref, second_refs[1], rest_refs[1]),
+    ):
+        segments += [
+            (own, rows, rows),
+            (rest, 0, 4 * span - rows),
+            (far, 2 * rows, rows),
+            (second, end, span),
+            (rest, 4 * span - rows, 3 * span - rows),
+        ]
     wanted = []
-    for g, ref in enumerate(mails):
-        code = ref[(FEAT_AT[g] + 2) * rows :, :rows].astype(F32)
+    for ref, start in feats:
+        code = ref[start + 2 * rows : start + end, :rows].astype(F32)
         wanted.append(columns_of(code[0:1] * 128.0 + code[1:2], rows))
     lanes = lax.broadcasted_iota(jnp.int32, (rows, rows), 1)
 
@@ -158,21 +188,21 @@
         return (scale * grad - scale * scale * scale * (1.0 / width) * along * raw).astype(BF)
 
     def over_rows(step):
-        for g in range(4):
-            step(mails[g], HEAD_AT[g] * rows, g * span, rows)
-            first = g * span + rows
-            if span == 4 * rows:
-                step(tails[g], 0, first, 3 * rows)
+        first = 0
+        for ref, start, length in segments:
+            if length <= 4 * rows:
+                step(ref, start, first, length)
             else:
 
-                def one(i, carry, ref=tails[g], first=first):
-                    step(ref, i * rows, first + i * rows, rows)
+                def one(i, carry, ref=ref, start=start, first=first):
+                    step(ref, start + i * rows, first + i * rows, rows)
                     return carry
 
-                lax.fori_loop(0, span // rows - 1, one, 0)
+                lax.fori_loop(0, length // rows, one, 0)
+            first = first + length
 
     def at(start, chunk):
-        return pl.ds(pl.multiple_of(start, rows), chunk)
+        return pl.ds(pl.multiple_of(start, PAD), chunk)
 
     smat_ref[...] = jnp.zeros_like(smat_ref)
     pick_ref[...] = jnp.zeros_like(pick_ref)
@@ -200,8 +230,7 @@
     kmat = jnp.zeros((width, width), F32)
     wfq = jnp.zeros((cut_ref.shape[1], width), F32)
     sums = jnp.sum(smat * smat) / groups / (2.0 * pairs)
-    for g, ref in enumerate(mails):
-        start = FEAT_AT[g] * rows
+    for g, (ref, start) in enumerate(feats):
         feat = ref[start : start + rows, :]
         f32feat = feat.astype(F32)
         diff = f32feat - GAMMA * ref[start + rows : start + 2 * rows, :].astype(F32)
@@ -214,7 +243,7 @@
         coef = db * (1.0 / pairs) + 1.0 / total
         norm = jnp.sum(ob * ob, axis=-1, keepdims=True)
         grad_f = (ds * (1.0 / pairs) - coef * ob).astype(BF)
-        cut = (cut_ref if g == 0 else ref)[CUT_AT[g] * rows : (CUT_AT[g] + 1) * rows, :]
+        cut = cuts[g][0][cuts[g][1] : cuts[g][1] + rows, :]
         wfq = wfq + dot_t(cut, grad_f)
         kmat = kmat + dot_t(d_hi, feat) + dot_t(d_lo, feat)
         sums = sums + (
@@ -292,6 +321,20 @@
             )
 
 
+def assemble_kernel(place_ref, *refs, wf_rows, wb_rows, factor_f, factor_b):
+    place = place_ref[0]
+    wf_ref, wb_ref = refs[2:]
+    for offset, ref in zip((0, 8), refs):
+        for e, turn in enumerate(TURNS):
+            to = place ^ (offset + turn)
+            wf_ref[pl.ds(pl.multiple_of(to * wf_rows, wf_rows), wf_rows), :] = (
+                ref[e, :wf_rows, :].astype(F32) * factor_f
+            )
+            wb_ref[pl.ds(pl.multiple_of(to * wb_rows, wb_rows), wb_rows), :] = (
+                ref[e, wf_rows:, :].astype(F32) * factor_b
+            )
+
+
 SMEM = pl.BlockSpec(memory_space=pltpu.SMEM)
 VMEM = pl.BlockSpec(memory_space=pltpu.VMEM)
 HBM = pl.BlockSpec(memory_space=pltpu.HBM)
@@ -308,19 +351,28 @@
     total = size * rows
     assert bits >= 4 and size == 1 << bits and high // 4 == width == wide
 
-    quarters = [reverse_bits((me ^ m) & 3, 2).astype(jnp.int32) for m in GROUP]
-    ends = [(at + 2) * rows + PAD for at in FEAT_AT]
-    far, near, cut, head, wb_copy = pl.pallas_call(
-        feature_kernel,
-        in_specs=[SMEM] + [HBM] * 9,
-        out_specs=[VMEM] * 5,
+    head = hidden_b
+    for mask in reversed(beyond):
+        head = jnp.concatenate([head, swap(head, mask, size)], axis=0)
+    piece12, piece8, piece4 = [swap(head, mask, size) for mask, _ in LINE]
+    far, near, cut, wb_copy = pl.pallas_call(
+        message_kernel,
+        in_specs=[SMEM] + [HBM] * 3,
+        out_specs=[VMEM] * 4,
         out_shape=[
-            jax.ShapeDtypeStruct((ends[1], width), BF),
-            jax.ShapeDtypeStruct((ends[2], width), BF),
+            jax.ShapeDtypeStruct((3 * rows, width), BF),
+            jax.ShapeDtypeStruct((2 * rows, width), BF),
             jax.ShapeDtypeStruct((rows, width), BF),
-            jax.ShapeDtypeStruct(hidden_b.shape, BF),
             jax.ShapeDtypeStruct(w_b.shape, BF),
         ],
+        scratch_shapes=[pltpu.SemaphoreType.DMA((7,))],
+        compiler_params=pltpu.CompilerParams(vmem_limit_bytes=60 * 2**20),
+    )(me.astype(jnp.int32).reshape(1), hidden_f, hidden_b, w_b)
+    feats0 = pl.pallas_call(
+        feature_kernel,
+        in_specs=[HBM] * 7,
+        out_specs=VMEM,
+        out_shape=jax.ShapeDtypeStruct((2 * rows + PAD, width), BF),
         scratch_shapes=[
             pltpu.VMEM(hidden_f.shape, BF),
             pltpu.VMEM(hidden_t.shape, BF),
@@ -329,44 +381,58 @@
             pltpu.VMEM(latents.shape, BF),
             pltpu.VMEM((1, rows), jnp.int32),
             pltpu.VMEM((1, rows), jnp.int32),
-            pltpu.SemaphoreType.DMA((9,)),
+            pltpu.SemaphoreType.DMA((7,)),
         ],
         compiler_params=pltpu.CompilerParams(vmem_limit_bytes=60 * 2**20),
+        cost_estimate=pl.CostEstimate(
+            flops=4 * rows * high * width, bytes_accessed=4 * high * (rows + width), transcendentals=0
+        ),
     )(
-        jnp.stack(quarters),
         hidden_f,
         hidden_t,
-        hidden_b,
         w_f,
         w_t,
-        w_b,
         latents,
         latent_ids.reshape(1, rows),
         positives.reshape(1, rows),
     )
     far2 = swap(far, 2, size)
-    for mask in reversed(beyond):
-        head = jnp.concatenate([head, swap(head, mask, size)], axis=0)
-    tail0 = jnp.concatenate(
-        [head[rows:]] * (len(beyond) > 0) + [swap(head, mask, size) for mask, _ in LINE], axis=0
+    second, to_core = pl.pallas_call(
+        pack_kernel,
+        in_specs=[VMEM] * 3,
+        out_specs=[VMEM] * 2,
+        out_shape=[
+            jax.ShapeDtypeStruct((feats0.shape[0] + piece4.shape[0], width), BF),
+            jax.ShapeDtypeStruct((2 * rows + feats0.shape[0], width), BF),
+        ],
+        compiler_params=pltpu.CompilerParams(vmem_limit_bytes=16 * 2**20),
+    )(near, feats0, piece4)
+    second2 = swap(second, 2, size)
+    over_y = [swap(piece, 2, size) for piece in (piece8, piece12)]
+    more = [head[rows:]] * (len(beyond) > 0)
+    rest0 = jnp.concatenate(
+        [piece4, piece8, piece12] + more + over_y + [swap(piece, 2, size) for piece in more], axis=0
     )
-    near1 = swap(near, 1, size)
-    tail2 = swap(tail0, 2, size)
-    tail1 = swap(tail0, 1, size)
+    from_core = swap(to_core, 1, size)
     far3 = swap(far2, 1, size)
-    tail3 = swap(tail2, 1, size)
+    second3 = swap(second2, 1, size)
+    rest1 = swap(rest0, 1, size)
 
     inner = reverse_bits(jnp.arange(size // 16, dtype=jnp.int32), bits - 4) << 4
-    bases = jnp.concatenate(
-        [(me ^ m ^ o ^ inner) * rows for m in GROUP for o in (0,) + tuple(o for o, _ in LINE)]
-    ).astype(jnp.int32)
+    first, others = inner[:1], inner[1:]
+    bases = []
+    for core in (0, 1):
+        bases += [core ^ first] + [core ^ mask ^ inner for mask in (4, 8, 12)] + [core ^ others]
+        core = core ^ 2
+        bases += [core ^ first] + [core ^ mask ^ inner for mask in (4, 8, 12)] + [core ^ others]
+    bases = ((me ^ jnp.concatenate(bases)) * rows).astype(jnp.int32)
     place = reverse_bits(me & 15, 4).astype(jnp.int32)
-    places = jnp.stack([quarters[0], place & 3])
+    places = jnp.stack([place >> 2, place & 3])
     wf_rows, wb_rows = high // 16, wide // 16
     each = wf_rows + wb_rows
     keep, *sends = pl.pallas_call(
         functools.partial(pair_kernel, rows=rows, total=total),
-        in_specs=[SMEM] * 2 + [VMEM] * 10,
+        in_specs=[SMEM] * 2 + [VMEM] * 11,
         out_specs=[VMEM] * 4,
         out_shape=[jax.ShapeDtypeStruct((each + PAD, width), F32)]
         + [jax.ShapeDtypeStruct((each + PAD, width), BF)] * 3,
@@ -379,7 +445,7 @@
             pltpu.VMEM((wide, width), F32),
         ],
         compiler_params=pltpu.CompilerParams(vmem_limit_bytes=12 * 2**20 + total * width * 8),
-    )(bases, places, near, far2, near1, far3, tail0, tail2, tail1, tail3, cut, wb_copy)
+    )(bases, places, near, far2, from_core, far3, feats0, second2, second3, rest0, rest1, cut, wb_copy)
 
     got = [swap(part, mask, size) for part, (mask, _) in zip(sends, LINE)]
     result, note = pl.pallas_call(
@@ -396,10 +462,9 @@
         result = result + swap(result, mask, size)
         note = note + swap(note, mask, size)
     result = result.astype(BF).reshape(1, each, width)
-    near = jnp.concatenate([result] + [swap(result, mask, size) for mask, _ in LINE], axis=0)
-    near_y = swap(near, 2, size)
+    pieces = [result] + [swap(result, mask, size) for mask, _ in LINE]
+    near = jnp.concatenate(pieces + [swap(piece, 2, size) for piece in pieces], axis=0)
     far = swap(near, 1, size)
-    far_y = swap(near_y, 1, size)
     grad_wf, grad_wb = pl.pallas_call(
         functools.partial(
             assemble_kernel,
@@ -408,14 +473,14 @@
             factor_f=math.sqrt(high),
             factor_b=math.sqrt(wide),
         ),
-        in_specs=[SMEM] + [VMEM] * 4,
+        in_specs=[SMEM] + [VMEM] * 2,
         out_specs=[VMEM] * 2,
         out_shape=[
             jax.ShapeDtypeStruct((high, width), F32),
             jax.ShapeDtypeStruct((wide, width), F32),
         ],
         compiler_params=pltpu.CompilerParams(vmem_limit_bytes=16 * 2**20),
-    )(place.reshape(1), near, near_y, far, far_y)
+    )(place.reshape(1), near, far)
     return (grad_wf, grad_wb, note.reshape(1))
 
 

time: 58.5 us -> 56.9 us (0.973)
  waiting for transfers between devices: 24.3 us -> 17.3 us
  starting transfers between devices: 20 us -> 23.5 us
  Pallas kernels: 12.5 us -> 14.1 us
  local copies, waits for them, and re-layouts: 0.12 us -> 0.98 us
  other arithmetic: 0.75 us -> 0.08 us
    ppermute x18 -> x22, waiting for transfers between devices: 24.3 us -> 17.3 us  [swap(): return lax.ppermute(array, 'fa', [(i, i ^ mask) for i in range(size)])]
    ppermute x18 -> x22, starting transfers between devices: 20 us -> 23.5 us  [swap(): return lax.ppermute(array, 'fa', [(i, i ^ mask) for i in range(size)])]
    pallas_call x1 -> x3, Pallas kernels: 3.49 us -> 4.54 us  [the longest x1 2.56 us: body(): pl.pallas_call(feature_kernel, in_specs=[HBM] * 7, out_specs=VMEM, out_sh...]
    unnamed x8 -> x23, local copies, waits for them, and re-layouts: 0.02 us -> 0.97 us
    another operation x2 -> x1, other arithmetic: 0.73 us -> 0.08 us  [body(): places = jnp.stack([place >> 2, place & 3])]
  transfers between devices with their start and end apart: 18 -> 22, of which waited for: 12 -> 12; matrix products, arithmetic and copies ran while one was open for 0% -> 0% of each run, Pallas kernels for 0% -> 8%
where the time goes in v6:
time: 56.9 us; the launch traced here: 56.7 us
  starting transfers between devices  23.5 us (41%)
  waiting for transfers between devices  17.3 us (30%)
  Pallas kernels  14.1 us (25%)
  local copies, waits for them, and re-layouts  0.98 us (2%)
  between operations  0.75 us (1%)
    ppermute x22, starting transfers between devices, swap(): return lax.ppermute(array, 'fa', [(i, i ^ mask) for i in range(size)])  23.5 us
    ppermute x22, waiting for transfers between devices, swap(): return lax.ppermute(array, 'fa', [(i, i ^ mask) for i in range(size)])  17.3 us
    pallas_call x1, Pallas kernels, body(): pl.pallas_call(functools.partial(pair_kernel, rows=rows, total=total), in...  7.87 us
    pallas_call x1, Pallas kernels, body(): pl.pallas_call(feature_kernel, in_specs=[HBM] * 7, out_specs=VMEM, out_sh...  2.56 us
    pallas_call x1, Pallas kernels, body(): pl.pallas_call(message_kernel, in_specs=[SMEM] + [HBM] * 3, out_specs=[VM...  1.95 us
  transfers between devices with their start and end apart: 22, of which 12 were waited for; matrix products, arithmetic and copies ran while one was open for 0% of the time, Pallas kernels for 8%

profile of v6, /device:TPU:0, one launch (start us, length us, event | category | flops | bytes accessed | tf_op | source)
XLA Modules:
  0.0 56.7 jit_solution(8819879080613873816)
XLA Ops:
  0.6 3.1 %collective-permute-start.1 = (bf16[128,256]{1,0:T(8,128)(2,1)}, bf16[128,256]{1,0:T(8,128)(2,1)S(1)}, u32[]{:S(2)}, u32[]{:S(2)}) collective-permute-start(bf16[128,256]{1,0:T(8,128)(2,1)} %hb_hbm.1), channel_id=1, source_target_pairs={{0,4},{1,5},{2,6},{3,7},{4,0},{5,1},{6,2},{7,3},{8,12},{9,13},{10,... | collective-permute-start | bytes 196616 | tf_op jit(solution)/shard_map/ppermute | solution.py:36
  3.7 2.6 %collective-permute-start.6 = (bf16[128,256]{1,0:T(8,128)(2,1)}, bf16[128,256]{1,0:T(8,128)(2,1)S(1)}, u32[]{:S(2)}, u32[]{:S(2)}) collective-permute-start(bf16[128,256]{1,0:T(8,128)(2,1)} %hb_hbm.1), channel_id=1, source_target_pairs={{0,8},{1,9},{2,10},{3,11},{4,12},{5,13},{6,14},{7,15},{8,0},{9,1},... | collective-permute-start | bytes 196616 | tf_op jit(solution)/shard_map/ppermute | solution.py:36
  6.3 0.0 collective-permute-start.7
  6.3 1.9 %shard_map.112 = (bf16[384,256]{1,0:T(8,128)(2,1)}, bf16[256,256]{1,0:T(8,128)(2,1)}, bf16[128,256]{1,0:T(8,128)(2,1)}, bf16[256,256]{1,0:T(8,128)(2,1)}) custom-call(s32[1]{0:T(128)} %bitcast.3.me_ref, bf16[128,1024]{1,0:T(8,128)(2,1)} %hf_hbm.3, bf16[128,256]{1,0:T(8,128)(2,1)} %hb_hbm.1, bf16[256,256]{1,0:T(8,128)(2,1)} %wb_hbm.1), custom_call_target="tpu_custom_call" | custom-call | tf_op jit(solution)/shard_map/pallas_call | solution.py:358
  8.3 1.8 %collective-permute-start = (bf16[384,256]{1,0:T(8,128)(2,1)}, bf16[384,256]{1,0:T(8,128)(2,1)S(1)}, u32[]{:S(2)}, u32[]{:S(2)}) collective-permute-start(bf16[384,256]{1,0:T(8,128)(2,1)} %get-tuple-element.18), channel_id=1, source_target_pairs={{0,2},{1,3},{2,0},{3,1},{4,6},{5,7},{6,4},{7,5},{8,10},{9,11},{10,... | collective-permute-start | bytes 589832 | tf_op jit(solution)/shard_map/ppermute | solution.py:36
  10.1 0.0 copy-start.2
  10.1 2.6 %shard_map.113.feats_ref.refs_6_ = bf16[272,256]{1,0:T(8,128)(2,1)} custom-call(bf16[128,1024]{1,0:T(8,128)(2,1)} %hf_hbm.3, bf16[128,1024]{1,0:T(8,128)(2,1)} %ht_hbm.1, bf16[1024,256]{1,0:T(8,128)(2,1)} %wf_hbm.1, bf16[1024,256]{1,0:T(8,128)(2,1)} %wt_hbm.1, bf16[512,256]{1,0:T(8,128)(2,1)} %lat_hbm.1, s32[1,128]{1,0:T(1,128)} %bitcast.13, s32[1,128]{1,0:T(1,128)} %bitcast.14), custom_call_target="tpu_custom_call" | custom-call | flops 134217728 | bytes 1572864 | tf_op jit(solution)/shard_map/pallas_call | solution.py:371
  12.6 0.0 collective-permute-done.1.piece_ref
  12.6 0.0 copy-done.2
  12.7 0.0 copy-start
  12.7 0.9 %copy-done = bf16[272,256]{1,0:T(8,128)(2,1)S(1)} copy-done((bf16[272,256]{1,0:T(8,128)(2,1)S(1)}, bf16[272,256]{1,0:T(8,128)(2,1)}, u32[]{:S(2)}) %copy-start) | copy-done | bytes 139288
  13.6 0.4 collective-permute-start.4
  14.0 0.0 collective-permute-start.2
  14.0 0.0 collective-permute-done.6
  14.0 1.8 %collective-permute-start.8 = (bf16[128,256]{1,0:T(8,128)(2,1)S(1)}, bf16[128,256]{1,0:T(8,128)(2,1)S(1)}, u32[]{:S(2)}, u32[]{:S(2)}) collective-permute-start(bf16[128,256]{1,0:T(8,128)(2,1)S(1)} %collective-permute-done.6), channel_id=1, source_target_pairs={{0,2},{1,3},{2,0},{3,1},{4,6},{5,7},{6,4},{7,5},{8,10},{9,11},{10,... | collective-permute-start | bytes 196616 | tf_op jit(solution)/shard_map/ppermute | solution.py:36
  15.8 0.0 collective-permute-done.7
  15.8 0.4 collective-permute-start.9
  16.1 0.0 copy-start.5
  16.2 0.0 copy-start.4
  16.2 0.0 copy-start.1
  16.2 0.0 copy-start.3
  16.2 5.3 %collective-permute-done.8 = bf16[128,256]{1,0:T(8,128)(2,1)S(1)} collective-permute-done((bf16[128,256]{1,0:T(8,128)(2,1)S(1)}, bf16[128,256]{1,0:T(8,128)(2,1)S(1)}, u32[]{:S(2)}, u32[]{:S(2)}) %collective-permute-start.8) | collective-permute-done | bytes 65568 | tf_op jit(solution)/shard_map/ppermute | solution.py:36
  21.5 0.7 %collective-permute-done.9 = bf16[128,256]{1,0:T(8,128)(2,1)S(1)} collective-permute-done((bf16[128,256]{1,0:T(8,128)(2,1)S(1)}, bf16[128,256]{1,0:T(8,128)(2,1)S(1)}, u32[]{:S(2)}, u32[]{:S(2)}) %collective-permute-start.9) | collective-permute-done | bytes 65568 | tf_op jit(solution)/shard_map/ppermute | solution.py:36
  22.2 0.0 collective-permute-start.10
  22.3 0.1 pad_add_fusion.refs_1_
  22.3 0.0 collective-permute-done.refs_3_
  22.3 0.5 collective-permute-start.3
  22.8 0.0 collective-permute-done.4.refs_7_
  22.8 0.1 collective-permute-start.5
  22.9 0.0 copy-done.5
  22.9 0.0 collective-permute-done.2.refs_4_
  22.9 1.2 %collective-permute-done.3.refs_5_ = bf16[384,256]{1,0:T(8,128)(2,1)S(1)} collective-permute-done((bf16[384,256]{1,0:T(8,128)(2,1)S(1)}, bf16[384,256]{1,0:T(8,128)(2,1)S(1)}, u32[]{:S(2)}, u32[]{:S(2)}) %collective-permute-start.3) | collective-permute-done | bytes 196640 | tf_op jit(solution)/shard_map/ppermute | solution.py:36
  24.2 0.0 collective-permute-done.10.refs_10_
  24.2 0.3 collective-permute-done.5.refs_8_
  24.4 0.0 copy-done.4
  24.4 0.0 copy-done.1
  24.5 0.0 copy-done.3
  24.5 7.9 %shard_map.115 = (f32[96,256]{1,0:T(8,128)S(1)}, bf16[96,256]{1,0:T(8,128)(2,1)S(1)}, bf16[96,256]{1,0:T(8,128)(2,1)S(1)}, bf16[96,256]{1,0:T(8,128)(2,1)S(1)}) custom-call(s32[16]{0:T(128)S(1)} %xor_multiply_fusion.refs_0_, s32[2]{0:T(128)S(1)} %pad_add_fusion.refs_1_, bf16[256,256]{1,0:T(8,128)(2,1)S(1)} %copy-done.2, ...), custom_call_target="tpu_custom_call" | custom-call | tf_op jit(solution)/shard_map/pallas_call | solution.py:433
  32.3 3.7 %collective-permute-start.11 = (bf16[96,256]{1,0:T(8,128)(2,1)S(1)}, bf16[96,256]{1,0:T(8,128)(2,1)S(1)}, u32[]{:S(2)}, u32[]{:S(2)}) collective-permute-start(bf16[96,256]{1,0:T(8,128)(2,1)S(1)} %get-tuple-element.24), channel_id=1, source_target_pairs={{0,12},{1,13},{2,14},{3,15},{4,8},{5,9},{6,10},{7,11},{8,4},{9,5},... | collective-permute-start | bytes 147464 | tf_op jit(solution)/shard_map/ppermute | solution.py:36
  36.0 0.0 collective-permute-start.12
  36.0 0.8 %collective-permute-start.13 = (bf16[96,256]{1,0:T(8,128)(2,1)S(1)}, bf16[96,256]{1,0:T(8,128)(2,1)S(1)}, u32[]{:S(2)}, u32[]{:S(2)}) collective-permute-start(bf16[96,256]{1,0:T(8,128)(2,1)S(1)} %get-tuple-element.26), channel_id=1, source_target_pairs={{0,4},{1,5},{2,6},{3,7},{4,0},{5,1},{6,2},{7,3},{8,12},{9,13},{10,... | collective-permute-start | bytes 147464 | tf_op jit(solution)/shard_map/ppermute | solution.py:36
  36.8 1.8 %collective-permute-done.11.refs_0_ = bf16[96,256]{1,0:T(8,128)(2,1)S(1)} collective-permute-done((bf16[96,256]{1,0:T(8,128)(2,1)S(1)}, bf16[96,256]{1,0:T(8,128)(2,1)S(1)}, u32[]{:S(2)}, u32[]{:S(2)}) %collective-permute-start.11) | collective-permute-done | bytes 49184 | tf_op jit(solution)/shard_map/ppermute | solution.py:36
  38.6 2.4 %collective-permute-done.12.refs_1_ = bf16[96,256]{1,0:T(8,128)(2,1)S(1)} collective-permute-done((bf16[96,256]{1,0:T(8,128)(2,1)S(1)}, bf16[96,256]{1,0:T(8,128)(2,1)S(1)}, u32[]{:S(2)}, u32[]{:S(2)}) %collective-permute-start.12) | collective-permute-done | bytes 49184 | tf_op jit(solution)/shard_map/ppermute | solution.py:36
  41.0 0.0 collective-permute-done.13.refs_2_
  41.0 0.5 shard_map.116
  41.5 2.2 %collective-permute-start.14 = (bf16[1,80,256]{2,1,0:T(8,128)(2,1)S(1)}, bf16[1,80,256]{2,1,0:T(8,128)(2,1)S(1)}, u32[]{:S(2)}, u32[]{:S(2)}) collective-permute-start(bf16[1,80,256]{2,1,0:T(8,128)(2,1)S(1)} %bitcast.9), channel_id=1, source_target_pairs={{0,12},{1,13},{2,14},{3,15},{4,8},{5,9},{6,10},{7,11},{8,4},{9,5},... | collective-permute-start | bytes 122888 | tf_op jit(solution)/shard_map/ppermute | solution.py:36
  43.7 0.2 collective-permute-start.15
  43.9 2.0 %collective-permute-start.16 = (bf16[1,80,256]{2,1,0:T(8,128)(2,1)S(1)}, bf16[1,80,256]{2,1,0:T(8,128)(2,1)S(1)}, u32[]{:S(2)}, u32[]{:S(2)}) collective-permute-start(bf16[1,80,256]{2,1,0:T(8,128)(2,1)S(1)} %bitcast.11), channel_id=1, source_target_pairs={{0,4},{1,5},{2,6},{3,7},{4,0},{5,1},{6,2},{7,3},{8,12},{9,13},{10,... | collective-permute-start | bytes 122888 | tf_op jit(solution)/shard_map/ppermute | solution.py:36
  45.9 1.0 %collective-permute-start.17 = (bf16[1,80,256]{2,1,0:T(8,128)(2,1)S(1)}, bf16[1,80,256]{2,1,0:T(8,128)(2,1)S(1)}, u32[]{:S(2)}, u32[]{:S(2)}) collective-permute-start(bf16[1,80,256]{2,1,0:T(8,128)(2,1)S(1)} %bitcast.12), channel_id=1, source_target_pairs={{0,2},{1,3},{2,0},{3,1},{4,6},{5,7},{6,4},{7,5},{8,10},{9,11},{10,... | collective-permute-start | bytes 122888 | tf_op jit(solution)/shard_map/ppermute | solution.py:36
  46.9 0.8 %collective-permute-done.14 = bf16[1,80,256]{2,1,0:T(8,128)(2,1)S(1)} collective-permute-done((bf16[1,80,256]{2,1,0:T(8,128)(2,1)S(1)}, bf16[1,80,256]{2,1,0:T(8,128)(2,1)S(1)}, u32[]{:S(2)}, u32[]{:S(2)}) %collective-permute-start.14) | collective-permute-done | bytes 40992 | tf_op jit(solution)/shard_map/ppermute | solution.py:36
  47.7 1.0 %collective-permute-start.18 = (bf16[1,80,256]{2,1,0:T(8,128)(2,1)S(1)}, bf16[1,80,256]{2,1,0:T(8,128)(2,1)S(1)}, u32[]{:S(2)}, u32[]{:S(2)}) collective-permute-start(bf16[1,80,256]{2,1,0:T(8,128)(2,1)S(1)} %collective-permute-done.14), channel_id=1, source_target_pairs={{0,2},{1,3},{2,0},{3,1},{4,6},{5,7},{6,4},{7,5},{8,10},{9,11},{10,... | collective-permute-start | bytes 122888 | tf_op jit(solution)/shard_map/ppermute | solution.py:36
  48.7 0.2 collective-permute-done.15
  48.9 1.0 %collective-permute-start.19 = (bf16[1,80,256]{2,1,0:T(8,128)(2,1)S(1)}, bf16[1,80,256]{2,1,0:T(8,128)(2,1)S(1)}, u32[]{:S(2)}, u32[]{:S(2)}) collective-permute-start(bf16[1,80,256]{2,1,0:T(8,128)(2,1)S(1)} %collective-permute-done.15), channel_id=1, source_target_pairs={{0,2},{1,3},{2,0},{3,1},{4,6},{5,7},{6,4},{7,5},{8,10},{9,11},{10,... | collective-permute-start | bytes 122888 | tf_op jit(solution)/shard_map/ppermute | solution.py:36
  49.9 0.0 collective-permute-done.16
  49.9 1.0 %collective-permute-start.20 = (bf16[1,80,256]{2,1,0:T(8,128)(2,1)S(1)}, bf16[1,80,256]{2,1,0:T(8,128)(2,1)S(1)}, u32[]{:S(2)}, u32[]{:S(2)}) collective-permute-start(bf16[1,80,256]{2,1,0:T(8,128)(2,1)S(1)} %collective-permute-done.16), channel_id=1, source_target_pairs={{0,2},{1,3},{2,0},{3,1},{4,6},{5,7},{6,4},{7,5},{8,10},{9,11},{10,... | collective-permute-start | bytes 122888 | tf_op jit(solution)/shard_map/ppermute | solution.py:36
  50.9 0.0 collective-permute-done.17
  50.9 0.8 %collective-permute-done.18 = bf16[1,80,256]{2,1,0:T(8,128)(2,1)S(1)} collective-permute-done((bf16[1,80,256]{2,1,0:T(8,128)(2,1)S(1)}, bf16[1,80,256]{2,1,0:T(8,128)(2,1)S(1)}, u32[]{:S(2)}, u32[]{:S(2)}) %collective-permute-start.18) | collective-permute-done | bytes 40992 | tf_op jit(solution)/shard_map/ppermute | solution.py:36
  51.7 1.2 %collective-permute-done.19 = bf16[1,80,256]{2,1,0:T(8,128)(2,1)S(1)} collective-permute-done((bf16[1,80,256]{2,1,0:T(8,128)(2,1)S(1)}, bf16[1,80,256]{2,1,0:T(8,128)(2,1)S(1)}, u32[]{:S(2)}, u32[]{:S(2)}) %collective-permute-start.19) | collective-permute-done | bytes 40992 | tf_op jit(solution)/shard_map/ppermute | solution.py:36
  52.9 1.0 %collective-permute-done.20 = bf16[1,80,256]{2,1,0:T(8,128)(2,1)S(1)} collective-permute-done((bf16[1,80,256]{2,1,0:T(8,128)(2,1)S(1)}, bf16[1,80,256]{2,1,0:T(8,128)(2,1)S(1)}, u32[]{:S(2)}, u32[]{:S(2)}) %collective-permute-start.20) | collective-permute-done | bytes 40992 | tf_op jit(solution)/shard_map/ppermute | solution.py:36
  53.9 0.0 collective-permute-start.21
  53.9 1.6 %collective-permute-done.21.refs_1_ = bf16[8,80,256]{2,1,0:T(8,128)(2,1)S(1)} collective-permute-done((bf16[8,80,256]{2,1,0:T(8,128)(2,1)S(1)}, bf16[8,80,256]{2,1,0:T(8,128)(2,1)S(1)}, u32[]{:S(2)}, u32[]{:S(2)}) %collective-permute-start.21) | collective-permute-done | bytes 327712 | tf_op jit(solution)/shard_map/ppermute | solution.py:36
  55.6 1.1 %shard_map.117 = (f32[1024,256]{1,0:T(8,128)}, f32[256,256]{1,0:T(8,128)}) custom-call(s32[1]{0:T(128)} %bitcast.place_ref, bf16[8,80,256]{2,1,0:T(8,128)(2,1)S(1)} %constant_dynamic-update-slice_fusion.5.refs_0_, bf16[8,80,256]{2,1,0:T(8,128)(2,1)S(1)} %collective-permute-done.21.refs_1_), custom_call_target="tpu_custom_call" | custom-call | tf_op jit(solution)/shard_map/pallas_call | solution.py:468
  (15 shorter events, 0.1 us)
Async XLA Ops:
  0.6 12.0 %collective-permute-start.1 = (bf16[128,256]{1,0:T(8,128)(2,1)}, bf16[128,256]{1,0:T(8,128)(2,1)S(1)}, u32[]{:S(2)}, u32[]{:S(2)}) collective-permute-start(bf16[128,256]{1,0:T(8,128)(2,1)} %hb_hbm.1), channel_id=1, source_target_pairs={{0,4},{1,5},{2,6},{3,7},{4,0},{5,1},{6,2},{7,3},{8,12},{9,13},{10,... | collective-permute-start | bytes 196616 | tf_op jit(solution)/shard_map/ppermute | solution.py:36
  3.7 10.3 %collective-permute-start.6 = (bf16[128,256]{1,0:T(8,128)(2,1)}, bf16[128,256]{1,0:T(8,128)(2,1)S(1)}, u32[]{:S(2)}, u32[]{:S(2)}) collective-permute-start(bf16[128,256]{1,0:T(8,128)(2,1)} %hb_hbm.1), channel_id=1, source_target_pairs={{0,8},{1,9},{2,10},{3,11},{4,12},{5,13},{6,14},{7,15},{8,0},{9,1},... | collective-permute-start | bytes 196616 | tf_op jit(solution)/shard_map/ppermute | solution.py:36
  6.3 9.5 %collective-permute-start.7 = (bf16[128,256]{1,0:T(8,128)(2,1)}, bf16[128,256]{1,0:T(8,128)(2,1)S(1)}, u32[]{:S(2)}, u32[]{:S(2)}) collective-permute-start(bf16[128,256]{1,0:T(8,128)(2,1)} %hb_hbm.1), channel_id=1, source_target_pairs={{0,12},{1,13},{2,14},{3,15},{4,8},{5,9},{6,10},{7,11},{8,4},{9,5},... | collective-permute-start | bytes 196616 | tf_op jit(solution)/shard_map/ppermute | solution.py:36
  8.3 14.1 %collective-permute-start = (bf16[384,256]{1,0:T(8,128)(2,1)}, bf16[384,256]{1,0:T(8,128)(2,1)S(1)}, u32[]{:S(2)}, u32[]{:S(2)}) collective-permute-start(bf16[384,256]{1,0:T(8,128)(2,1)} %get-tuple-element.18), channel_id=1, source_target_pairs={{0,2},{1,3},{2,0},{3,1},{4,6},{5,7},{6,4},{7,5},{8,10},{9,11},{10,... | collective-permute-start | bytes 589832 | tf_op jit(solution)/shard_map/ppermute | solution.py:36
  10.1 2.6 %copy-start.2 = (bf16[256,256]{1,0:T(8,128)(2,1)S(1)}, bf16[256,256]{1,0:T(8,128)(2,1)}, u32[]{:S(2)}) copy-start(bf16[256,256]{1,0:T(8,128)(2,1)} %get-tuple-element.17.near_ref.refs_2_) | copy-start | bytes 393220
  12.7 0.9 %copy-start = (bf16[272,256]{1,0:T(8,128)(2,1)S(1)}, bf16[272,256]{1,0:T(8,128)(2,1)}, u32[]{:S(2)}) copy-start(bf16[272,256]{1,0:T(8,128)(2,1)} %shard_map.113.feats_ref.refs_6_) | copy-start | bytes 417796
  13.6 9.2 %collective-permute-start.4 = (bf16[400,256]{1,0:T(8,128)(2,1)S(1)}, bf16[400,256]{1,0:T(8,128)(2,1)S(1)}, u32[]{:S(2)}, u32[]{:S(2)}) collective-permute-start(bf16[400,256]{1,0:T(8,128)(2,1)S(1)} %get-tuple-element.20), channel_id=1, source_target_pairs={{0,2},{1,3},{2,0},{3,1},{4,6},{5,7},{6,4},{7,5},{8,10},{9,11},{10,... | collective-permute-start | bytes 614408 | tf_op jit(solution)/shard_map/ppermute | solution.py:36
  14.0 9.0 %collective-permute-start.2 = (bf16[528,256]{1,0:T(8,128)(2,1)S(1)}, bf16[528,256]{1,0:T(8,128)(2,1)S(1)}, u32[]{:S(2)}, u32[]{:S(2)}) collective-permute-start(bf16[528,256]{1,0:T(8,128)(2,1)S(1)} %get-tuple-element.19), channel_id=1, source_target_pairs={{0,1},{1,0},{2,3},{3,2},{4,5},{5,4},{6,7},{7,6},{8,9},{9,8},{10,11... | collective-permute-start | bytes 811016 | tf_op jit(solution)/shard_map/ppermute | solution.py:36
  14.0 7.6 %collective-permute-start.8 = (bf16[128,256]{1,0:T(8,128)(2,1)S(1)}, bf16[128,256]{1,0:T(8,128)(2,1)S(1)}, u32[]{:S(2)}, u32[]{:S(2)}) collective-permute-start(bf16[128,256]{1,0:T(8,128)(2,1)S(1)} %collective-permute-done.6), channel_id=1, source_target_pairs={{0,2},{1,3},{2,0},{3,1},{4,6},{5,7},{6,4},{7,5},{8,10},{9,11},{10,... | collective-permute-start | bytes 196616 | tf_op jit(solution)/shard_map/ppermute | solution.py:36
  15.8 6.4 %collective-permute-start.9 = (bf16[128,256]{1,0:T(8,128)(2,1)S(1)}, bf16[128,256]{1,0:T(8,128)(2,1)S(1)}, u32[]{:S(2)}, u32[]{:S(2)}) collective-permute-start(bf16[128,256]{1,0:T(8,128)(2,1)S(1)} %collective-permute-done.7), channel_id=1, source_target_pairs={{0,2},{1,3},{2,0},{3,1},{4,6},{5,7},{6,4},{7,5},{8,10},{9,11},{10,... | collective-permute-start | bytes 196616 | tf_op jit(solution)/shard_map/ppermute | solution.py:36
  16.1 6.8 %copy-start.5 = (s32[16]{0:T(128)S(1)}, s32[16]{0:T(128)}, u32[]{:S(2)}) copy-start(s32[16]{0:T(128)} %constant.48.clone.1) | copy-start | bytes 196
  16.2 8.3 %copy-start.4 = (bf16[128,256]{1,0:T(8,128)(2,1)S(1)}, bf16[128,256]{1,0:T(8,128)(2,1)}, u32[]{:S(2)}) copy-start(bf16[128,256]{1,0:T(8,128)(2,1)} %get-tuple-element.21.refs_11_) | copy-start | bytes 196612
  16.2 8.3 %copy-start.1 = (bf16[272,256]{1,0:T(8,128)(2,1)S(1)}, bf16[272,256]{1,0:T(8,128)(2,1)}, u32[]{:S(2)}) copy-start(bf16[272,256]{1,0:T(8,128)(2,1)} %shard_map.113.feats_ref.refs_6_) | copy-start | bytes 417796
  16.2 8.3 %copy-start.3 = (bf16[256,256]{1,0:T(8,128)(2,1)S(1)}, bf16[256,256]{1,0:T(8,128)(2,1)}, u32[]{:S(2)}) copy-start(bf16[256,256]{1,0:T(8,128)(2,1)} %get-tuple-element.22.refs_12_) | copy-start | bytes 393220
  22.2 1.9 %collective-permute-start.10 = (bf16[640,256]{1,0:T(8,128)(2,1)S(1)}, bf16[640,256]{1,0:T(8,128)(2,1)S(1)}, u32[]{:S(2)}, u32[]{:S(2)}) collective-permute-start(bf16[640,256]{1,0:T(8,128)(2,1)S(1)} %constant_dynamic-update-slice_fusion.refs_9_), channel_id=1, source_target_pairs={{0,1},{1,0},{2,3},{3,2},{4,5},{5,4},{6,7},{7,6},{8,9},{9,8},{10,11... | collective-permute-start | bytes 983048 | tf_op jit(solution)/shard_map/ppermute | solution.py:36
  22.3 1.8 %collective-permute-start.3 = (bf16[384,256]{1,0:T(8,128)(2,1)S(1)}, bf16[384,256]{1,0:T(8,128)(2,1)S(1)}, u32[]{:S(2)}, u32[]{:S(2)}) collective-permute-start(bf16[384,256]{1,0:T(8,128)(2,1)S(1)} %collective-permute-done.refs_3_), channel_id=1, source_target_pairs={{0,1},{1,0},{2,3},{3,2},{4,5},{5,4},{6,7},{7,6},{8,9},{9,8},{10,11... | collective-permute-start | bytes 589832 | tf_op jit(solution)/shard_map/ppermute | solution.py:36
  22.8 1.6 %collective-permute-start.5 = (bf16[400,256]{1,0:T(8,128)(2,1)S(1)}, bf16[400,256]{1,0:T(8,128)(2,1)S(1)}, u32[]{:S(2)}, u32[]{:S(2)}) collective-permute-start(bf16[400,256]{1,0:T(8,128)(2,1)S(1)} %collective-permute-done.4.refs_7_), channel_id=1, source_target_pairs={{0,1},{1,0},{2,3},{3,2},{4,5},{5,4},{6,7},{7,6},{8,9},{9,8},{10,11... | collective-permute-start | bytes 614408 | tf_op jit(solution)/shard_map/ppermute | solution.py:36
  32.3 6.2 %collective-permute-start.11 = (bf16[96,256]{1,0:T(8,128)(2,1)S(1)}, bf16[96,256]{1,0:T(8,128)(2,1)S(1)}, u32[]{:S(2)}, u32[]{:S(2)}) collective-permute-start(bf16[96,256]{1,0:T(8,128)(2,1)S(1)} %get-tuple-element.24), channel_id=1, source_target_pairs={{0,12},{1,13},{2,14},{3,15},{4,8},{5,9},{6,10},{7,11},{8,4},{9,5},... | collective-permute-start | bytes 147464 | tf_op jit(solution)/shard_map/ppermute | solution.py:36
  36.0 5.0 %collective-permute-start.12 = (bf16[96,256]{1,0:T(8,128)(2,1)S(1)}, bf16[96,256]{1,0:T(8,128)(2,1)S(1)}, u32[]{:S(2)}, u32[]{:S(2)}) collective-permute-start(bf16[96,256]{1,0:T(8,128)(2,1)S(1)} %get-tuple-element.25), channel_id=1, source_target_pairs={{0,8},{1,9},{2,10},{3,11},{4,12},{5,13},{6,14},{7,15},{8,0},{9,1},... | collective-permute-start | bytes 147464 | tf_op jit(solution)/shard_map/ppermute | solution.py:36
  36.0 5.0 %collective-permute-start.13 = (bf16[96,256]{1,0:T(8,128)(2,1)S(1)}, bf16[96,256]{1,0:T(8,128)(2,1)S(1)}, u32[]{:S(2)}, u32[]{:S(2)}) collective-permute-start(bf16[96,256]{1,0:T(8,128)(2,1)S(1)} %get-tuple-element.26), channel_id=1, source_target_pairs={{0,4},{1,5},{2,6},{3,7},{4,0},{5,1},{6,2},{7,3},{8,12},{9,13},{10,... | collective-permute-start | bytes 147464 | tf_op jit(solution)/shard_map/ppermute | solution.py:36
  41.5 6.2 %collective-permute-start.14 = (bf16[1,80,256]{2,1,0:T(8,128)(2,1)S(1)}, bf16[1,80,256]{2,1,0:T(8,128)(2,1)S(1)}, u32[]{:S(2)}, u32[]{:S(2)}) collective-permute-start(bf16[1,80,256]{2,1,0:T(8,128)(2,1)S(1)} %bitcast.9), channel_id=1, source_target_pairs={{0,12},{1,13},{2,14},{3,15},{4,8},{5,9},{6,10},{7,11},{8,4},{9,5},... | collective-permute-start | bytes 122888 | tf_op jit(solution)/shard_map/ppermute | solution.py:36
  43.7 5.2 %collective-permute-start.15 = (bf16[1,80,256]{2,1,0:T(8,128)(2,1)S(1)}, bf16[1,80,256]{2,1,0:T(8,128)(2,1)S(1)}, u32[]{:S(2)}, u32[]{:S(2)}) collective-permute-start(bf16[1,80,256]{2,1,0:T(8,128)(2,1)S(1)} %bitcast.10), channel_id=1, source_target_pairs={{0,8},{1,9},{2,10},{3,11},{4,12},{5,13},{6,14},{7,15},{8,0},{9,1},... | collective-permute-start | bytes 122888 | tf_op jit(solution)/shard_map/ppermute | solution.py:36
  43.9 6.1 %collective-permute-start.16 = (bf16[1,80,256]{2,1,0:T(8,128)(2,1)S(1)}, bf16[1,80,256]{2,1,0:T(8,128)(2,1)S(1)}, u32[]{:S(2)}, u32[]{:S(2)}) collective-permute-start(bf16[1,80,256]{2,1,0:T(8,128)(2,1)S(1)} %bitcast.11), channel_id=1, source_target_pairs={{0,4},{1,5},{2,6},{3,7},{4,0},{5,1},{6,2},{7,3},{8,12},{9,13},{10,... | collective-permute-start | bytes 122888 | tf_op jit(solution)/shard_map/ppermute | solution.py:36
  45.9 5.0 %collective-permute-start.17 = (bf16[1,80,256]{2,1,0:T(8,128)(2,1)S(1)}, bf16[1,80,256]{2,1,0:T(8,128)(2,1)S(1)}, u32[]{:S(2)}, u32[]{:S(2)}) collective-permute-start(bf16[1,80,256]{2,1,0:T(8,128)(2,1)S(1)} %bitcast.12), channel_id=1, source_target_pairs={{0,2},{1,3},{2,0},{3,1},{4,6},{5,7},{6,4},{7,5},{8,10},{9,11},{10,... | collective-permute-start | bytes 122888 | tf_op jit(solution)/shard_map/ppermute | solution.py:36
  47.7 4.0 %collective-permute-start.18 = (bf16[1,80,256]{2,1,0:T(8,128)(2,1)S(1)}, bf16[1,80,256]{2,1,0:T(8,128)(2,1)S(1)}, u32[]{:S(2)}, u32[]{:S(2)}) collective-permute-start(bf16[1,80,256]{2,1,0:T(8,128)(2,1)S(1)} %collective-permute-done.14), channel_id=1, source_target_pairs={{0,2},{1,3},{2,0},{3,1},{4,6},{5,7},{6,4},{7,5},{8,10},{9,11},{10,... | collective-permute-start | bytes 122888 | tf_op jit(solution)/shard_map/ppermute | solution.py:36
  48.9 4.0 %collective-permute-start.19 = (bf16[1,80,256]{2,1,0:T(8,128)(2,1)S(1)}, bf16[1,80,256]{2,1,0:T(8,128)(2,1)S(1)}, u32[]{:S(2)}, u32[]{:S(2)}) collective-permute-start(bf16[1,80,256]{2,1,0:T(8,128)(2,1)S(1)} %collective-permute-done.15), channel_id=1, source_target_pairs={{0,2},{1,3},{2,0},{3,1},{4,6},{5,7},{6,4},{7,5},{8,10},{9,11},{10,... | collective-permute-start | bytes 122888 | tf_op jit(solution)/shard_map/ppermute | solution.py:36
  49.9 4.0 %collective-permute-start.20 = (bf16[1,80,256]{2,1,0:T(8,128)(2,1)S(1)}, bf16[1,80,256]{2,1,0:T(8,128)(2,1)S(1)}, u32[]{:S(2)}, u32[]{:S(2)}) collective-permute-start(bf16[1,80,256]{2,1,0:T(8,128)(2,1)S(1)} %collective-permute-done.16), channel_id=1, source_target_pairs={{0,2},{1,3},{2,0},{3,1},{4,6},{5,7},{6,4},{7,5},{8,10},{9,11},{10,... | collective-permute-start | bytes 122888 | tf_op jit(solution)/shard_map/ppermute | solution.py:36
  53.9 1.6 %collective-permute-start.21 = (bf16[8,80,256]{2,1,0:T(8,128)(2,1)S(1)}, bf16[8,80,256]{2,1,0:T(8,128)(2,1)S(1)}, u32[]{:S(2)}, u32[]{:S(2)}) collective-permute-start(bf16[8,80,256]{2,1,0:T(8,128)(2,1)S(1)} %constant_dynamic-update-slice_fusion.5.refs_0_), channel_id=1, source_target_pairs={{0,1},{1,0},{2,3},{3,2},{4,5},{5,4},{6,7},{7,6},{8,9},{9,8},{10,11... | collective-permute-start | bytes 983048 | tf_op jit(solution)/shard_map/ppermute | solution.py:36

commit v7 on v6

--- a/solution.py
+++ b/solution.py
@@ -151,7 +151,7 @@
     near_ref, far_ref, core_ref, far3_ref, feats_ref = refs[2:7]
     second_refs, rest_refs = refs[7:9], refs[9:11]
     cut_ref, wb_ref, keep_ref, sends = refs[11], refs[12], refs[13], refs[14:17]
-    raw_ref, back_ref, smat_ref, pick_ref, wfq_ref, wbq_ref = refs[17:]
+    hid_ref, raw_ref, back_ref, mask_ref, smat_ref, pick_ref, own_ref, wfq_ref, wbq_ref = refs[17:]
     width = wb_ref.shape[1]
     pairs = float(total * (total - 1))
     groups = total // (4 * rows)
@@ -172,108 +172,118 @@
             (second, end, span),
             (rest, 4 * span - rows, 3 * span - rows),
         ]
+    first = 0
+    for ref, start, length in segments:
+        if length <= 4 * rows:
+            hid_ref[first : first + length, :] = ref[start : start + length, :]
+        else:
+
+            def one(i, carry, ref=ref, start=start, first=first):
+                hid_ref[pl.ds(pl.multiple_of(first + i * rows, PAD), rows), :] = ref[
+                    pl.ds(pl.multiple_of(start + i * rows, PAD), rows), :
+                ]
+                return carry
+
+            lax.fori_loop(0, length // rows, one, 0)
+        first = first + length
+
+    def embed(hidden):
+        raw = dot(hidden, wb)
+        scale = lax.rsqrt(jnp.mean(raw * raw, axis=-1, keepdims=True) + EPS)
+        return raw, scale, (raw * scale).astype(BF)
+
+    def through(grad, raw, scale):
+        along = jnp.sum(grad * raw, axis=-1, keepdims=True)
+        return (scale * grad - scale * scale * scale * (1.0 / width) * along * raw).astype(BF)
+
+    big, small = mask_ref.shape[1], 4 * rows
+
+    def over_rows(step):
+        if big == total:
+            step(0)
+        else:
+            lax.fori_loop(0, total // big, lambda i, carry: (step(i), carry)[1], 0)
+
+    def at(start, length):
+        return pl.ds(pl.multiple_of(start, rows), length)
+
     wanted = []
     for ref, start in feats:
         code = ref[start + 2 * rows : start + end, :rows].astype(F32)
         wanted.append(columns_of(code[0:1] * 128.0 + code[1:2], rows))
     lanes = lax.broadcasted_iota(jnp.int32, (rows, rows), 1)
-
-    def embed(hidden):
-        raw = dot(hidden, wb)
-        scale = lax.rsqrt(jnp.mean(raw * raw, axis=-1, keepdims=True) + EPS)
-        return raw, scale, (raw * scale).astype(BF)
-
-    def through(grad, raw, scale):
-        along = jnp.sum(grad * raw, axis=-1, keepdims=True)
-        return (scale * grad - scale * scale * scale * (1.0 / width) * along * raw).astype(BF)
-
-    def over_rows(step):
-        first = 0
-        for ref, start, length in segments:
-            if length <= 4 * rows:
-                step(ref, start, first, length)
-            else:
-
-                def one(i, carry, ref=ref, start=start, first=first):
-                    step(ref, start + i * rows, first + i * rows, rows)
-                    return carry
-
-                lax.fori_loop(0, length // rows, one, 0)
-            first = first + length
-
-    def at(start, chunk):
-        return pl.ds(pl.multiple_of(start, PAD), chunk)
-
     smat_ref[...] = jnp.zeros_like(smat_ref)
     pick_ref[...] = jnp.zeros_like(pick_ref)
-    wbq_ref[...] = jnp.zeros_like(wbq_ref)
-
-    def first(ref, start, number, chunk):
-        hidden = ref[at(start, chunk), :]
-        raw, _, back = embed(hidden)
-        raw_ref[at(number, chunk), :] = raw
-        back_ref[at(number, chunk), :] = back
-        smat_ref[...] += dot_t(back, back)
-        ids = [(lanes + base_ref[number // rows + t]).astype(F32) for t in range(chunk // rows)]
-        mask = jnp.concatenate(
-            [
-                jnp.concatenate([jnp.where(want == i, 1.0, 0.0).astype(BF) for i in ids], axis=1)
-                for want in wanted
-            ],
-            axis=0,
-        )
-        pick_ref[...] += dot(mask, hidden)
-
-    over_rows(first)
+
+    def first_pass(step):
+        for i in range(big // small):
+            here = at(step * big + i * small, small)
+            raw, _, back = embed(hid_ref[here, :])
+            raw_ref[here, :] = raw
+            back_ref[here, :] = back
+        for t in range(big // rows):
+            ids = (lanes + base_ref[step * (big // rows) + t]).astype(F32)
+            for g, want in enumerate(wanted):
+                mask_ref[g * rows : (g + 1) * rows, t * rows : (t + 1) * rows] = jnp.where(
+                    want == ids, 1.0, 0.0
+                ).astype(BF)
+        here = at(step * big, big)
+        smat_ref[...] += dot_t(back_ref[here, :], back_ref[here, :])
+        pick_ref[...] += dot(mask_ref[...], hid_ref[here, :])
+
+    over_rows(first_pass)
     smat = smat_ref[...]
     s_hi, s_lo = halves(smat)
-    kmat = jnp.zeros((width, width), F32)
-    wfq = jnp.zeros((cut_ref.shape[1], width), F32)
-    sums = jnp.sum(smat * smat) / groups / (2.0 * pairs)
-    for g, (ref, start) in enumerate(feats):
-        feat = ref[start : start + rows, :]
-        f32feat = feat.astype(F32)
-        diff = f32feat - GAMMA * ref[start + rows : start + 2 * rows, :].astype(F32)
-        d_hi, d_lo = halves(diff)
-        hidden = pick_ref[g * rows : (g + 1) * rows, :].astype(BF)
-        raw, scale, back = embed(hidden)
-        ob = back.astype(F32)
-        ds = dot(d_hi, s_hi) + dot(d_lo, s_hi) + dot(d_hi, s_lo)
-        db = jnp.sum(diff * ob, axis=-1, keepdims=True)
-        coef = db * (1.0 / pairs) + 1.0 / total
-        norm = jnp.sum(ob * ob, axis=-1, keepdims=True)
-        grad_f = (ds * (1.0 / pairs) - coef * ob).astype(BF)
-        cut = cuts[g][0][cuts[g][1] : cuts[g][1] + rows, :]
-        wfq = wfq + dot_t(cut, grad_f)
-        kmat = kmat + dot_t(d_hi, feat) + dot_t(d_lo, feat)
-        sums = sums + (
-            (jnp.sum(diff * ds) - jnp.sum(db * db) - LAMBDA * jnp.sum(norm * norm)) / (2.0 * pairs)
-            - (jnp.sum(f32feat * ob) + LAMBDA * jnp.sum(norm)) / total
-        )
-        grad_own = through(
-            -coef * f32feat - (norm * (2.0 * LAMBDA / pairs) + 2.0 * LAMBDA / total) * ob, raw, scale
-        )
-        wbq_ref[...] += dot_t(hidden, grad_own)
-    wfq_ref[...] = wfq
+    quarter, mine = place_ref[0], place_ref[1]
+    half = wbq_ref.shape[0]
+    columns = pl.ds(pl.multiple_of((quarter >> 1) * half, half), half)
+
+    def rows_of(places, offset):
+        return jnp.concatenate([ref[at + offset : at + offset + rows, :] for ref, at in places], axis=0)
+
+    feat = rows_of(feats, 0)
+    f32feat = feat.astype(F32)
+    diff = f32feat - GAMMA * rows_of(feats, rows).astype(F32)
+    d_hi, d_lo = halves(diff)
+    kmat = dot_t(d_hi, feat) + dot_t(d_lo, feat)
+    hidden = pick_ref[...].astype(BF)
+    own_ref[...] = hidden
+    raw, scale, back = embed(hidden)
+    ob = back.astype(F32)
+    ds = dot(d_hi, s_hi) + dot(d_lo, s_hi) + dot(d_hi, s_lo)
+    db = jnp.sum(diff * ob, axis=-1, keepdims=True)
+    coef = db * (1.0 / pairs) + 1.0 / total
+    norm = jnp.sum(ob * ob, axis=-1, keepdims=True)
+    grad_f = (ds * (1.0 / pairs) - coef * ob).astype(BF)
+    wfq_ref[...] = dot_t(rows_of(cuts, 0), grad_f)
+    squares = jnp.sum(diff * ds) - jnp.sum(db * db)
+    squares = squares + LAMBDA * (jnp.sum(smat * smat) / groups - jnp.sum(norm * norm))
+    sums = squares / (2.0 * pairs) - (jnp.sum(f32feat * ob) + LAMBDA * jnp.sum(norm)) / total
+    grad_own = through(
+        -coef * f32feat - (norm * (2.0 * LAMBDA / pairs) + 2.0 * LAMBDA / total) * ob, raw, scale
+    )
+    wbq_ref[...] = dot_t(own_ref[:, columns], grad_own)
     a_hi, a_lo = halves((kmat + (2.0 * LAMBDA / groups) * smat) * (1.0 / pairs))
 
-    def second(ref, start, number, chunk):
-        raw = raw_ref[at(number, chunk), :]
-        scale = lax.rsqrt(jnp.mean(raw * raw, axis=-1, keepdims=True) + EPS)
-        back = back_ref[at(number, chunk), :]
-        grad = through(dot(back, a_hi) + dot(back, a_lo), raw, scale)
-        wbq_ref[...] += dot_t(ref[at(start, chunk), :], grad)
-
-    over_rows(second)
-    quarter, mine = place_ref[0], place_ref[1]
+    def second_pass(step):
+        for i in range(big // small):
+            here = at(step * big + i * small, small)
+            raw = raw_ref[here, :]
+            scale = lax.rsqrt(jnp.mean(raw * raw, axis=-1, keepdims=True) + EPS)
+            back = back_ref[here, :]
+            back_ref[here, :] = through(dot(back, a_hi) + dot(back, a_lo), raw, scale)
+        here = at(step * big, big)
+        wbq_ref[...] += dot_t(hid_ref[here, columns], back_ref[here, :])
+
+    over_rows(second_pass)
     wf_rows = wfq_ref.shape[0] // 4
-    wb_rows = wbq_ref.shape[0] // 16
+    wb_rows = wbq_ref.shape[0] // 8
     size = wf_rows + wb_rows
 
     def block(t):
         return (
             wfq_ref[pl.ds(pl.multiple_of(t * wf_rows, wf_rows), wf_rows), :],
-            wbq_ref[pl.ds(pl.multiple_of((quarter * 4 + t) * wb_rows, wb_rows), wb_rows), :],
+            wbq_ref[pl.ds(pl.multiple_of(((quarter & 1) * 4 + t) * wb_rows, wb_rows), wb_rows), :],
         )
 
     keep_ref[:wf_rows, :], keep_ref[wf_rows:size, :] = block(mine)
@@ -437,14 +447,17 @@
         out_shape=[jax.ShapeDtypeStruct((each + PAD, width), F32)]
         + [jax.ShapeDtypeStruct((each + PAD, width), BF)] * 3,
         scratch_shapes=[
+            pltpu.VMEM((total, wide), BF),
             pltpu.VMEM((total, width), F32),
             pltpu.VMEM((total, width), BF),
+            pltpu.VMEM((4 * rows, min(total, 16 * rows)), BF),
             pltpu.VMEM((width, width), F32),
             pltpu.VMEM((4 * rows, wide), F32),
+            pltpu.VMEM((4 * rows, wide), BF),
             pltpu.VMEM((width, width), F32),
-            pltpu.VMEM((wide, width), F32),
+            pltpu.VMEM((wide // 2, width), F32),
         ],
-        compiler_params=pltpu.CompilerParams(vmem_limit_bytes=12 * 2**20 + total * width * 8),
+        compiler_params=pltpu.CompilerParams(vmem_limit_bytes=15 * 2**20 + total * width * 10),
     )(bases, places, near, far2, from_core, far3, feats0, second2, second3, rest0, rest1, cut, wb_copy)
 
     got = [swap(part, mask, size) for part, (mask, _) in zip(sends, LINE)]

time: 56.9 us -> 53.1 us (0.933)
  Pallas kernels: 14.1 us -> 10.3 us
    pallas_call x1, Pallas kernels: 7.87 us -> 4.08 us  [body(): pl.pallas_call(functools.partial(pair_kernel, rows=rows, total=total), in...]
  transfers between devices with their start and end apart: 22 -> 22, of which waited for: 12 -> 12; matrix products, arithmetic and copies ran while one was open for 0% -> 0% of each run, Pallas kernels for 8% -> 9%
where the time goes in v7:
time: 53.1 us; the launch traced here: 52.9 us
  starting transfers between devices  23.5 us (44%)
  waiting for transfers between devices  17.3 us (33%)
  Pallas kernels  10.3 us (19%)
  local copies, waits for them, and re-layouts  0.98 us (2%)
  between operations  0.76 us (1%)
    ppermute x22, starting transfers between devices, swap(): return lax.ppermute(array, 'fa', [(i, i ^ mask) for i in range(size)])  23.5 us
    ppermute x22, waiting for transfers between devices, swap(): return lax.ppermute(array, 'fa', [(i, i ^ mask) for i in range(size)])  17.3 us
    pallas_call x1, Pallas kernels, body(): pl.pallas_call(functools.partial(pair_kernel, rows=rows, total=total), in...  4.08 us
    pallas_call x1, Pallas kernels, body(): pl.pallas_call(feature_kernel, in_specs=[HBM] * 7, out_specs=VMEM, out_sh...  2.56 us
    pallas_call x1, Pallas kernels, body(): pl.pallas_call(message_kernel, in_specs=[SMEM] + [HBM] * 3, out_specs=[VM...  1.95 us
    pallas_call x1, Pallas kernels, body(): pl.pallas_call(functools.partial(assemble_kernel, wf_rows=wf_rows, wb_row...  1.14 us
  transfers between devices with their start and end apart: 22, of which 12 were waited for; matrix products, arithmetic and copies ran while one was open for 0% of the time, Pallas kernels for 9%

profile of v7, /device:TPU:0, one launch (start us, length us, event | category | flops | bytes accessed | tf_op | source)
XLA Modules:
  0.0 52.9 jit_solution(16699524153780572341)
XLA Ops:
  0.6 3.1 %collective-permute-start.1 = (bf16[128,256]{1,0:T(8,128)(2,1)}, bf16[128,256]{1,0:T(8,128)(2,1)S(1)}, u32[]{:S(2)}, u32[]{:S(2)}) collective-permute-start(bf16[128,256]{1,0:T(8,128)(2,1)} %hb_hbm.1), channel_id=1, source_target_pairs={{0,4},{1,5},{2,6},{3,7},{4,0},{5,1},{6,2},{7,3},{8,12},{9,13},{10,... | collective-permute-start | bytes 196616 | tf_op jit(solution)/shard_map/ppermute | solution.py:36
  3.7 2.6 %collective-permute-start.6 = (bf16[128,256]{1,0:T(8,128)(2,1)}, bf16[128,256]{1,0:T(8,128)(2,1)S(1)}, u32[]{:S(2)}, u32[]{:S(2)}) collective-permute-start(bf16[128,256]{1,0:T(8,128)(2,1)} %hb_hbm.1), channel_id=1, source_target_pairs={{0,8},{1,9},{2,10},{3,11},{4,12},{5,13},{6,14},{7,15},{8,0},{9,1},... | collective-permute-start | bytes 196616 | tf_op jit(solution)/shard_map/ppermute | solution.py:36
  6.3 0.0 collective-permute-start.7
  6.3 1.9 %shard_map.112 = (bf16[384,256]{1,0:T(8,128)(2,1)}, bf16[256,256]{1,0:T(8,128)(2,1)}, bf16[128,256]{1,0:T(8,128)(2,1)}, bf16[256,256]{1,0:T(8,128)(2,1)}) custom-call(s32[1]{0:T(128)} %bitcast.3.me_ref, bf16[128,1024]{1,0:T(8,128)(2,1)} %hf_hbm.3, bf16[128,256]{1,0:T(8,128)(2,1)} %hb_hbm.1, bf16[256,256]{1,0:T(8,128)(2,1)} %wb_hbm.1), custom_call_target="tpu_custom_call" | custom-call | tf_op jit(solution)/shard_map/pallas_call | solution.py:368
  8.3 1.8 %collective-permute-start = (bf16[384,256]{1,0:T(8,128)(2,1)}, bf16[384,256]{1,0:T(8,128)(2,1)S(1)}, u32[]{:S(2)}, u32[]{:S(2)}) collective-permute-start(bf16[384,256]{1,0:T(8,128)(2,1)} %get-tuple-element.18), channel_id=1, source_target_pairs={{0,2},{1,3},{2,0},{3,1},{4,6},{5,7},{6,4},{7,5},{8,10},{9,11},{10,... | collective-permute-start | bytes 589832 | tf_op jit(solution)/shard_map/ppermute | solution.py:36
  10.1 0.0 copy-start.2
  10.1 2.6 %shard_map.113.feats_ref.refs_6_ = bf16[272,256]{1,0:T(8,128)(2,1)} custom-call(bf16[128,1024]{1,0:T(8,128)(2,1)} %hf_hbm.3, bf16[128,1024]{1,0:T(8,128)(2,1)} %ht_hbm.1, bf16[1024,256]{1,0:T(8,128)(2,1)} %wf_hbm.1, bf16[1024,256]{1,0:T(8,128)(2,1)} %wt_hbm.1, bf16[512,256]{1,0:T(8,128)(2,1)} %lat_hbm.1, s32[1,128]{1,0:T(1,128)} %bitcast.13, s32[1,128]{1,0:T(1,128)} %bitcast.14), custom_call_target="tpu_custom_call" | custom-call | flops 134217728 | bytes 1572864 | tf_op jit(solution)/shard_map/pallas_call | solution.py:381
  12.6 0.0 collective-permute-done.1.piece_ref
  12.6 0.0 copy-done.2
  12.7 0.0 copy-start
  12.7 0.9 %copy-done = bf16[272,256]{1,0:T(8,128)(2,1)S(1)} copy-done((bf16[272,256]{1,0:T(8,128)(2,1)S(1)}, bf16[272,256]{1,0:T(8,128)(2,1)}, u32[]{:S(2)}) %copy-start) | copy-done | bytes 139288
  13.6 0.4 collective-permute-start.4
  14.0 0.0 collective-permute-start.2
  14.0 0.0 collective-permute-done.6
  14.0 1.8 %collective-permute-start.8 = (bf16[128,256]{1,0:T(8,128)(2,1)S(1)}, bf16[128,256]{1,0:T(8,128)(2,1)S(1)}, u32[]{:S(2)}, u32[]{:S(2)}) collective-permute-start(bf16[128,256]{1,0:T(8,128)(2,1)S(1)} %collective-permute-done.6), channel_id=1, source_target_pairs={{0,2},{1,3},{2,0},{3,1},{4,6},{5,7},{6,4},{7,5},{8,10},{9,11},{10,... | collective-permute-start | bytes 196616 | tf_op jit(solution)/shard_map/ppermute | solution.py:36
  15.8 0.0 collective-permute-done.7
  15.8 0.4 collective-permute-start.9
  16.1 0.0 copy-start.5
  16.2 0.0 copy-start.4
  16.2 0.0 copy-start.1
  16.2 0.0 copy-start.3
  16.2 5.3 %collective-permute-done.8 = bf16[128,256]{1,0:T(8,128)(2,1)S(1)} collective-permute-done((bf16[128,256]{1,0:T(8,128)(2,1)S(1)}, bf16[128,256]{1,0:T(8,128)(2,1)S(1)}, u32[]{:S(2)}, u32[]{:S(2)}) %collective-permute-start.8) | collective-permute-done | bytes 65568 | tf_op jit(solution)/shard_map/ppermute | solution.py:36
  21.5 0.7 %collective-permute-done.9 = bf16[128,256]{1,0:T(8,128)(2,1)S(1)} collective-permute-done((bf16[128,256]{1,0:T(8,128)(2,1)S(1)}, bf16[128,256]{1,0:T(8,128)(2,1)S(1)}, u32[]{:S(2)}, u32[]{:S(2)}) %collective-permute-start.9) | collective-permute-done | bytes 65568 | tf_op jit(solution)/shard_map/ppermute | solution.py:36
  22.2 0.0 collective-permute-start.10
  22.3 0.1 pad_add_fusion.refs_1_
  22.3 0.0 collective-permute-done.refs_3_
  22.3 0.5 collective-permute-start.3
  22.8 0.0 collective-permute-done.4.refs_7_
  22.8 0.1 collective-permute-start.5
  22.9 0.0 copy-done.5
  22.9 0.0 collective-permute-done.2.refs_4_
  22.9 1.2 %collective-permute-done.3.refs_5_ = bf16[384,256]{1,0:T(8,128)(2,1)S(1)} collective-permute-done((bf16[384,256]{1,0:T(8,128)(2,1)S(1)}, bf16[384,256]{1,0:T(8,128)(2,1)S(1)}, u32[]{:S(2)}, u32[]{:S(2)}) %collective-permute-start.3) | collective-permute-done | bytes 196640 | tf_op jit(solution)/shard_map/ppermute | solution.py:36
  24.2 0.0 collective-permute-done.10.refs_10_
  24.2 0.3 collective-permute-done.5.refs_8_
  24.4 0.0 copy-done.4
  24.4 0.0 copy-done.1
  24.5 0.0 copy-done.3
  24.5 4.1 %shard_map.115 = (f32[96,256]{1,0:T(8,128)S(1)}, bf16[96,256]{1,0:T(8,128)(2,1)S(1)}, bf16[96,256]{1,0:T(8,128)(2,1)S(1)}, bf16[96,256]{1,0:T(8,128)(2,1)S(1)}) custom-call(s32[16]{0:T(128)S(1)} %xor_multiply_fusion.refs_0_, s32[2]{0:T(128)S(1)} %pad_add_fusion.refs_1_, bf16[256,256]{1,0:T(8,128)(2,1)S(1)} %copy-done.2, ...), custom_call_target="tpu_custom_call" | custom-call | tf_op jit(solution)/shard_map/pallas_call | solution.py:443
  28.5 3.7 %collective-permute-start.11 = (bf16[96,256]{1,0:T(8,128)(2,1)S(1)}, bf16[96,256]{1,0:T(8,128)(2,1)S(1)}, u32[]{:S(2)}, u32[]{:S(2)}) collective-permute-start(bf16[96,256]{1,0:T(8,128)(2,1)S(1)} %get-tuple-element.24), channel_id=1, source_target_pairs={{0,12},{1,13},{2,14},{3,15},{4,8},{5,9},{6,10},{7,11},{8,4},{9,5},... | collective-permute-start | bytes 147464 | tf_op jit(solution)/shard_map/ppermute | solution.py:36
  32.2 0.0 collective-permute-start.12
  32.2 0.8 %collective-permute-start.13 = (bf16[96,256]{1,0:T(8,128)(2,1)S(1)}, bf16[96,256]{1,0:T(8,128)(2,1)S(1)}, u32[]{:S(2)}, u32[]{:S(2)}) collective-permute-start(bf16[96,256]{1,0:T(8,128)(2,1)S(1)} %get-tuple-element.26), channel_id=1, source_target_pairs={{0,4},{1,5},{2,6},{3,7},{4,0},{5,1},{6,2},{7,3},{8,12},{9,13},{10,... | collective-permute-start | bytes 147464 | tf_op jit(solution)/shard_map/ppermute | solution.py:36
  33.0 1.8 %collective-permute-done.11.refs_0_ = bf16[96,256]{1,0:T(8,128)(2,1)S(1)} collective-permute-done((bf16[96,256]{1,0:T(8,128)(2,1)S(1)}, bf16[96,256]{1,0:T(8,128)(2,1)S(1)}, u32[]{:S(2)}, u32[]{:S(2)}) %collective-permute-start.11) | collective-permute-done | bytes 49184 | tf_op jit(solution)/shard_map/ppermute | solution.py:36
  34.8 2.4 %collective-permute-done.12.refs_1_ = bf16[96,256]{1,0:T(8,128)(2,1)S(1)} collective-permute-done((bf16[96,256]{1,0:T(8,128)(2,1)S(1)}, bf16[96,256]{1,0:T(8,128)(2,1)S(1)}, u32[]{:S(2)}, u32[]{:S(2)}) %collective-permute-start.12) | collective-permute-done | bytes 49184 | tf_op jit(solution)/shard_map/ppermute | solution.py:36
  37.2 0.0 collective-permute-done.13.refs_2_
  37.2 0.5 shard_map.116
  37.7 2.2 %collective-permute-start.14 = (bf16[1,80,256]{2,1,0:T(8,128)(2,1)S(1)}, bf16[1,80,256]{2,1,0:T(8,128)(2,1)S(1)}, u32[]{:S(2)}, u32[]{:S(2)}) collective-permute-start(bf16[1,80,256]{2,1,0:T(8,128)(2,1)S(1)} %bitcast.9), channel_id=1, source_target_pairs={{0,12},{1,13},{2,14},{3,15},{4,8},{5,9},{6,10},{7,11},{8,4},{9,5},... | collective-permute-start | bytes 122888 | tf_op jit(solution)/shard_map/ppermute | solution.py:36
  39.9 0.2 collective-permute-start.15
  40.1 2.0 %collective-permute-start.16 = (bf16[1,80,256]{2,1,0:T(8,128)(2,1)S(1)}, bf16[1,80,256]{2,1,0:T(8,128)(2,1)S(1)}, u32[]{:S(2)}, u32[]{:S(2)}) collective-permute-start(bf16[1,80,256]{2,1,0:T(8,128)(2,1)S(1)} %bitcast.11), channel_id=1, source_target_pairs={{0,4},{1,5},{2,6},{3,7},{4,0},{5,1},{6,2},{7,3},{8,12},{9,13},{10,... | collective-permute-start | bytes 122888 | tf_op jit(solution)/shard_map/ppermute | solution.py:36
  42.1 1.0 %collective-permute-start.17 = (bf16[1,80,256]{2,1,0:T(8,128)(2,1)S(1)}, bf16[1,80,256]{2,1,0:T(8,128)(2,1)S(1)}, u32[]{:S(2)}, u32[]{:S(2)}) collective-permute-start(bf16[1,80,256]{2,1,0:T(8,128)(2,1)S(1)} %bitcast.12), channel_id=1, source_target_pairs={{0,2},{1,3},{2,0},{3,1},{4,6},{5,7},{6,4},{7,5},{8,10},{9,11},{10,... | collective-permute-start | bytes 122888 | tf_op jit(solution)/shard_map/ppermute | solution.py:36
  43.2 0.7 %collective-permute-done.14 = bf16[1,80,256]{2,1,0:T(8,128)(2,1)S(1)} collective-permute-done((bf16[1,80,256]{2,1,0:T(8,128)(2,1)S(1)}, bf16[1,80,256]{2,1,0:T(8,128)(2,1)S(1)}, u32[]{:S(2)}, u32[]{:S(2)}) %collective-permute-start.14) | collective-permute-done | bytes 40992 | tf_op jit(solution)/shard_map/ppermute | solution.py:36
  43.9 1.1 %collective-permute-start.18 = (bf16[1,80,256]{2,1,0:T(8,128)(2,1)S(1)}, bf16[1,80,256]{2,1,0:T(8,128)(2,1)S(1)}, u32[]{:S(2)}, u32[]{:S(2)}) collective-permute-start(bf16[1,80,256]{2,1,0:T(8,128)(2,1)S(1)} %collective-permute-done.14), channel_id=1, source_target_pairs={{0,2},{1,3},{2,0},{3,1},{4,6},{5,7},{6,4},{7,5},{8,10},{9,11},{10,... | collective-permute-start | bytes 122888 | tf_op jit(solution)/shard_map/ppermute | solution.py:36
  45.0 0.1 collective-permute-done.15
  45.1 1.0 %collective-permute-start.19 = (bf16[1,80,256]{2,1,0:T(8,128)(2,1)S(1)}, bf16[1,80,256]{2,1,0:T(8,128)(2,1)S(1)}, u32[]{:S(2)}, u32[]{:S(2)}) collective-permute-start(bf16[1,80,256]{2,1,0:T(8,128)(2,1)S(1)} %collective-permute-done.15), channel_id=1, source_target_pairs={{0,2},{1,3},{2,0},{3,1},{4,6},{5,7},{6,4},{7,5},{8,10},{9,11},{10,... | collective-permute-start | bytes 122888 | tf_op jit(solution)/shard_map/ppermute | solution.py:36
  46.1 0.0 collective-permute-done.16
  46.1 1.0 %collective-permute-start.20 = (bf16[1,80,256]{2,1,0:T(8,128)(2,1)S(1)}, bf16[1,80,256]{2,1,0:T(8,128)(2,1)S(1)}, u32[]{:S(2)}, u32[]{:S(2)}) collective-permute-start(bf16[1,80,256]{2,1,0:T(8,128)(2,1)S(1)} %collective-permute-done.16), channel_id=1, source_target_pairs={{0,2},{1,3},{2,0},{3,1},{4,6},{5,7},{6,4},{7,5},{8,10},{9,11},{10,... | collective-permute-start | bytes 122888 | tf_op jit(solution)/shard_map/ppermute | solution.py:36
  47.1 0.0 collective-permute-done.17
  47.1 0.8 %collective-permute-done.18 = bf16[1,80,256]{2,1,0:T(8,128)(2,1)S(1)} collective-permute-done((bf16[1,80,256]{2,1,0:T(8,128)(2,1)S(1)}, bf16[1,80,256]{2,1,0:T(8,128)(2,1)S(1)}, u32[]{:S(2)}, u32[]{:S(2)}) %collective-permute-start.18) | collective-permute-done | bytes 40992 | tf_op jit(solution)/shard_map/ppermute | solution.py:36
  47.9 1.2 %collective-permute-done.19 = bf16[1,80,256]{2,1,0:T(8,128)(2,1)S(1)} collective-permute-done((bf16[1,80,256]{2,1,0:T(8,128)(2,1)S(1)}, bf16[1,80,256]{2,1,0:T(8,128)(2,1)S(1)}, u32[]{:S(2)}, u32[]{:S(2)}) %collective-permute-start.19) | collective-permute-done | bytes 40992 | tf_op jit(solution)/shard_map/ppermute | solution.py:36
  49.1 1.0 %collective-permute-done.20 = bf16[1,80,256]{2,1,0:T(8,128)(2,1)S(1)} collective-permute-done((bf16[1,80,256]{2,1,0:T(8,128)(2,1)S(1)}, bf16[1,80,256]{2,1,0:T(8,128)(2,1)S(1)}, u32[]{:S(2)}, u32[]{:S(2)}) %collective-permute-start.20) | collective-permute-done | bytes 40992 | tf_op jit(solution)/shard_map/ppermute | solution.py:36
  50.2 0.0 collective-permute-start.21
  50.2 1.6 %collective-permute-done.21.refs_1_ = bf16[8,80,256]{2,1,0:T(8,128)(2,1)S(1)} collective-permute-done((bf16[8,80,256]{2,1,0:T(8,128)(2,1)S(1)}, bf16[8,80,256]{2,1,0:T(8,128)(2,1)S(1)}, u32[]{:S(2)}, u32[]{:S(2)}) %collective-permute-start.21) | collective-permute-done | bytes 327712 | tf_op jit(solution)/shard_map/ppermute | solution.py:36
  51.8 1.1 %shard_map.117 = (f32[1024,256]{1,0:T(8,128)}, f32[256,256]{1,0:T(8,128)}) custom-call(s32[1]{0:T(128)} %bitcast.place_ref, bf16[8,80,256]{2,1,0:T(8,128)(2,1)S(1)} %constant_dynamic-update-slice_fusion.5.refs_0_, bf16[8,80,256]{2,1,0:T(8,128)(2,1)S(1)} %collective-permute-done.21.refs_1_), custom_call_target="tpu_custom_call" | custom-call | tf_op jit(solution)/shard_map/pallas_call | solution.py:481
  (15 shorter events, 0.1 us)
Async XLA Ops:
  0.6 12.0 %collective-permute-start.1 = (bf16[128,256]{1,0:T(8,128)(2,1)}, bf16[128,256]{1,0:T(8,128)(2,1)S(1)}, u32[]{:S(2)}, u32[]{:S(2)}) collective-permute-start(bf16[128,256]{1,0:T(8,128)(2,1)} %hb_hbm.1), channel_id=1, source_target_pairs={{0,4},{1,5},{2,6},{3,7},{4,0},{5,1},{6,2},{7,3},{8,12},{9,13},{10,... | collective-permute-start | bytes 196616 | tf_op jit(solution)/shard_map/ppermute | solution.py:36
  3.7 10.3 %collective-permute-start.6 = (bf16[128,256]{1,0:T(8,128)(2,1)}, bf16[128,256]{1,0:T(8,128)(2,1)S(1)}, u32[]{:S(2)}, u32[]{:S(2)}) collective-permute-start(bf16[128,256]{1,0:T(8,128)(2,1)} %hb_hbm.1), channel_id=1, source_target_pairs={{0,8},{1,9},{2,10},{3,11},{4,12},{5,13},{6,14},{7,15},{8,0},{9,1},... | collective-permute-start | bytes 196616 | tf_op jit(solution)/shard_map/ppermute | solution.py:36
  6.3 9.5 %collective-permute-start.7 = (bf16[128,256]{1,0:T(8,128)(2,1)}, bf16[128,256]{1,0:T(8,128)(2,1)S(1)}, u32[]{:S(2)}, u32[]{:S(2)}) collective-permute-start(bf16[128,256]{1,0:T(8,128)(2,1)} %hb_hbm.1), channel_id=1, source_target_pairs={{0,12},{1,13},{2,14},{3,15},{4,8},{5,9},{6,10},{7,11},{8,4},{9,5},... | collective-permute-start | bytes 196616 | tf_op jit(solution)/shard_map/ppermute | solution.py:36
  8.3 14.1 %collective-permute-start = (bf16[384,256]{1,0:T(8,128)(2,1)}, bf16[384,256]{1,0:T(8,128)(2,1)S(1)}, u32[]{:S(2)}, u32[]{:S(2)}) collective-permute-start(bf16[384,256]{1,0:T(8,128)(2,1)} %get-tuple-element.18), channel_id=1, source_target_pairs={{0,2},{1,3},{2,0},{3,1},{4,6},{5,7},{6,4},{7,5},{8,10},{9,11},{10,... | collective-permute-start | bytes 589832 | tf_op jit(solution)/shard_map/ppermute | solution.py:36
  10.1 2.6 %copy-start.2 = (bf16[256,256]{1,0:T(8,128)(2,1)S(1)}, bf16[256,256]{1,0:T(8,128)(2,1)}, u32[]{:S(2)}) copy-start(bf16[256,256]{1,0:T(8,128)(2,1)} %get-tuple-element.17.near_ref.refs_2_) | copy-start | bytes 393220
  12.7 0.9 %copy-start = (bf16[272,256]{1,0:T(8,128)(2,1)S(1)}, bf16[272,256]{1,0:T(8,128)(2,1)}, u32[]{:S(2)}) copy-start(bf16[272,256]{1,0:T(8,128)(2,1)} %shard_map.113.feats_ref.refs_6_) | copy-start | bytes 417796
  13.6 9.2 %collective-permute-start.4 = (bf16[400,256]{1,0:T(8,128)(2,1)S(1)}, bf16[400,256]{1,0:T(8,128)(2,1)S(1)}, u32[]{:S(2)}, u32[]{:S(2)}) collective-permute-start(bf16[400,256]{1,0:T(8,128)(2,1)S(1)} %get-tuple-element.20), channel_id=1, source_target_pairs={{0,2},{1,3},{2,0},{3,1},{4,6},{5,7},{6,4},{7,5},{8,10},{9,11},{10,... | collective-permute-start | bytes 614408 | tf_op jit(solution)/shard_map/ppermute | solution.py:36
  14.0 9.0 %collective-permute-start.2 = (bf16[528,256]{1,0:T(8,128)(2,1)S(1)}, bf16[528,256]{1,0:T(8,128)(2,1)S(1)}, u32[]{:S(2)}, u32[]{:S(2)}) collective-permute-start(bf16[528,256]{1,0:T(8,128)(2,1)S(1)} %get-tuple-element.19), channel_id=1, source_target_pairs={{0,1},{1,0},{2,3},{3,2},{4,5},{5,4},{6,7},{7,6},{8,9},{9,8},{10,11... | collective-permute-start | bytes 811016 | tf_op jit(solution)/shard_map/ppermute | solution.py:36
  14.0 7.6 %collective-permute-start.8 = (bf16[128,256]{1,0:T(8,128)(2,1)S(1)}, bf16[128,256]{1,0:T(8,128)(2,1)S(1)}, u32[]{:S(2)}, u32[]{:S(2)}) collective-permute-start(bf16[128,256]{1,0:T(8,128)(2,1)S(1)} %collective-permute-done.6), channel_id=1, source_target_pairs={{0,2},{1,3},{2,0},{3,1},{4,6},{5,7},{6,4},{7,5},{8,10},{9,11},{10,... | collective-permute-start | bytes 196616 | tf_op jit(solution)/shard_map/ppermute | solution.py:36
  15.8 6.4 %collective-permute-start.9 = (bf16[128,256]{1,0:T(8,128)(2,1)S(1)}, bf16[128,256]{1,0:T(8,128)(2,1)S(1)}, u32[]{:S(2)}, u32[]{:S(2)}) collective-permute-start(bf16[128,256]{1,0:T(8,128)(2,1)S(1)} %collective-permute-done.7), channel_id=1, source_target_pairs={{0,2},{1,3},{2,0},{3,1},{4,6},{5,7},{6,4},{7,5},{8,10},{9,11},{10,... | collective-permute-start | bytes 196616 | tf_op jit(solution)/shard_map/ppermute | solution.py:36
  16.1 6.8 %copy-start.5 = (s32[16]{0:T(128)S(1)}, s32[16]{0:T(128)}, u32[]{:S(2)}) copy-start(s32[16]{0:T(128)} %constant.48.clone.1) | copy-start | bytes 196
  16.2 8.3 %copy-start.4 = (bf16[128,256]{1,0:T(8,128)(2,1)S(1)}, bf16[128,256]{1,0:T(8,128)(2,1)}, u32[]{:S(2)}) copy-start(bf16[128,256]{1,0:T(8,128)(2,1)} %get-tuple-element.21.refs_11_) | copy-start | bytes 196612
  16.2 8.3 %copy-start.1 = (bf16[272,256]{1,0:T(8,128)(2,1)S(1)}, bf16[272,256]{1,0:T(8,128)(2,1)}, u32[]{:S(2)}) copy-start(bf16[272,256]{1,0:T(8,128)(2,1)} %shard_map.113.feats_ref.refs_6_) | copy-start | bytes 417796
  16.2 8.3 %copy-start.3 = (bf16[256,256]{1,0:T(8,128)(2,1)S(1)}, bf16[256,256]{1,0:T(8,128)(2,1)}, u32[]{:S(2)}) copy-start(bf16[256,256]{1,0:T(8,128)(2,1)} %get-tuple-element.22.refs_12_) | copy-start | bytes 393220
  22.2 1.9 %collective-permute-start.10 = (bf16[640,256]{1,0:T(8,128)(2,1)S(1)}, bf16[640,256]{1,0:T(8,128)(2,1)S(1)}, u32[]{:S(2)}, u32[]{:S(2)}) collective-permute-start(bf16[640,256]{1,0:T(8,128)(2,1)S(1)} %constant_dynamic-update-slice_fusion.refs_9_), channel_id=1, source_target_pairs={{0,1},{1,0},{2,3},{3,2},{4,5},{5,4},{6,7},{7,6},{8,9},{9,8},{10,11... | collective-permute-start | bytes 983048 | tf_op jit(solution)/shard_map/ppermute | solution.py:36
  22.3 1.8 %collective-permute-start.3 = (bf16[384,256]{1,0:T(8,128)(2,1)S(1)}, bf16[384,256]{1,0:T(8,128)(2,1)S(1)}, u32[]{:S(2)}, u32[]{:S(2)}) collective-permute-start(bf16[384,256]{1,0:T(8,128)(2,1)S(1)} %collective-permute-done.refs_3_), channel_id=1, source_target_pairs={{0,1},{1,0},{2,3},{3,2},{4,5},{5,4},{6,7},{7,6},{8,9},{9,8},{10,11... | collective-permute-start | bytes 589832 | tf_op jit(solution)/shard_map/ppermute | solution.py:36
  22.8 1.6 %collective-permute-start.5 = (bf16[400,256]{1,0:T(8,128)(2,1)S(1)}, bf16[400,256]{1,0:T(8,128)(2,1)S(1)}, u32[]{:S(2)}, u32[]{:S(2)}) collective-permute-start(bf16[400,256]{1,0:T(8,128)(2,1)S(1)} %collective-permute-done.4.refs_7_), channel_id=1, source_target_pairs={{0,1},{1,0},{2,3},{3,2},{4,5},{5,4},{6,7},{7,6},{8,9},{9,8},{10,11... | collective-permute-start | bytes 614408 | tf_op jit(solution)/shard_map/ppermute | solution.py:36
  28.5 6.2 %collective-permute-start.11 = (bf16[96,256]{1,0:T(8,128)(2,1)S(1)}, bf16[96,256]{1,0:T(8,128)(2,1)S(1)}, u32[]{:S(2)}, u32[]{:S(2)}) collective-permute-start(bf16[96,256]{1,0:T(8,128)(2,1)S(1)} %get-tuple-element.24), channel_id=1, source_target_pairs={{0,12},{1,13},{2,14},{3,15},{4,8},{5,9},{6,10},{7,11},{8,4},{9,5},... | collective-permute-start | bytes 147464 | tf_op jit(solution)/shard_map/ppermute | solution.py:36
  32.2 5.0 %collective-permute-start.12 = (bf16[96,256]{1,0:T(8,128)(2,1)S(1)}, bf16[96,256]{1,0:T(8,128)(2,1)S(1)}, u32[]{:S(2)}, u32[]{:S(2)}) collective-permute-start(bf16[96,256]{1,0:T(8,128)(2,1)S(1)} %get-tuple-element.25), channel_id=1, source_target_pairs={{0,8},{1,9},{2,10},{3,11},{4,12},{5,13},{6,14},{7,15},{8,0},{9,1},... | collective-permute-start | bytes 147464 | tf_op jit(solution)/shard_map/ppermute | solution.py:36
  32.2 5.0 %collective-permute-start.13 = (bf16[96,256]{1,0:T(8,128)(2,1)S(1)}, bf16[96,256]{1,0:T(8,128)(2,1)S(1)}, u32[]{:S(2)}, u32[]{:S(2)}) collective-permute-start(bf16[96,256]{1,0:T(8,128)(2,1)S(1)} %get-tuple-element.26), channel_id=1, source_target_pairs={{0,4},{1,5},{2,6},{3,7},{4,0},{5,1},{6,2},{7,3},{8,12},{9,13},{10,... | collective-permute-start | bytes 147464 | tf_op jit(solution)/shard_map/ppermute | solution.py:36
  37.7 6.2 %collective-permute-start.14 = (bf16[1,80,256]{2,1,0:T(8,128)(2,1)S(1)}, bf16[1,80,256]{2,1,0:T(8,128)(2,1)S(1)}, u32[]{:S(2)}, u32[]{:S(2)}) collective-permute-start(bf16[1,80,256]{2,1,0:T(8,128)(2,1)S(1)} %bitcast.9), channel_id=1, source_target_pairs={{0,12},{1,13},{2,14},{3,15},{4,8},{5,9},{6,10},{7,11},{8,4},{9,5},... | collective-permute-start | bytes 122888 | tf_op jit(solution)/shard_map/ppermute | solution.py:36
  39.9 5.2 %collective-permute-start.15 = (bf16[1,80,256]{2,1,0:T(8,128)(2,1)S(1)}, bf16[1,80,256]{2,1,0:T(8,128)(2,1)S(1)}, u32[]{:S(2)}, u32[]{:S(2)}) collective-permute-start(bf16[1,80,256]{2,1,0:T(8,128)(2,1)S(1)} %bitcast.10), channel_id=1, source_target_pairs={{0,8},{1,9},{2,10},{3,11},{4,12},{5,13},{6,14},{7,15},{8,0},{9,1},... | collective-permute-start | bytes 122888 | tf_op jit(solution)/shard_map/ppermute | solution.py:36
  40.1 6.1 %collective-permute-start.16 = (bf16[1,80,256]{2,1,0:T(8,128)(2,1)S(1)}, bf16[1,80,256]{2,1,0:T(8,128)(2,1)S(1)}, u32[]{:S(2)}, u32[]{:S(2)}) collective-permute-start(bf16[1,80,256]{2,1,0:T(8,128)(2,1)S(1)} %bitcast.11), channel_id=1, source_target_pairs={{0,4},{1,5},{2,6},{3,7},{4,0},{5,1},{6,2},{7,3},{8,12},{9,13},{10,... | collective-permute-start | bytes 122888 | tf_op jit(solution)/shard_map/ppermute | solution.py:36
  42.1 5.0 %collective-permute-start.17 = (bf16[1,80,256]{2,1,0:T(8,128)(2,1)S(1)}, bf16[1,80,256]{2,1,0:T(8,128)(2,1)S(1)}, u32[]{:S(2)}, u32[]{:S(2)}) collective-permute-start(bf16[1,80,256]{2,1,0:T(8,128)(2,1)S(1)} %bitcast.12), channel_id=1, source_target_pairs={{0,2},{1,3},{2,0},{3,1},{4,6},{5,7},{6,4},{7,5},{8,10},{9,11},{10,... | collective-permute-start | bytes 122888 | tf_op jit(solution)/shard_map/ppermute | solution.py:36
  43.9 4.0 %collective-permute-start.18 = (bf16[1,80,256]{2,1,0:T(8,128)(2,1)S(1)}, bf16[1,80,256]{2,1,0:T(8,128)(2,1)S(1)}, u32[]{:S(2)}, u32[]{:S(2)}) collective-permute-start(bf16[1,80,256]{2,1,0:T(8,128)(2,1)S(1)} %collective-permute-done.14), channel_id=1, source_target_pairs={{0,2},{1,3},{2,0},{3,1},{4,6},{5,7},{6,4},{7,5},{8,10},{9,11},{10,... | collective-permute-start | bytes 122888 | tf_op jit(solution)/shard_map/ppermute | solution.py:36
  45.1 4.0 %collective-permute-start.19 = (bf16[1,80,256]{2,1,0:T(8,128)(2,1)S(1)}, bf16[1,80,256]{2,1,0:T(8,128)(2,1)S(1)}, u32[]{:S(2)}, u32[]{:S(2)}) collective-permute-start(bf16[1,80,256]{2,1,0:T(8,128)(2,1)S(1)} %collective-permute-done.15), channel_id=1, source_target_pairs={{0,2},{1,3},{2,0},{3,1},{4,6},{5,7},{6,4},{7,5},{8,10},{9,11},{10,... | collective-permute-start | bytes 122888 | tf_op jit(solution)/shard_map/ppermute | solution.py:36
  46.1 4.0 %collective-permute-start.20 = (bf16[1,80,256]{2,1,0:T(8,128)(2,1)S(1)}, bf16[1,80,256]{2,1,0:T(8,128)(2,1)S(1)}, u32[]{:S(2)}, u32[]{:S(2)}) collective-permute-start(bf16[1,80,256]{2,1,0:T(8,128)(2,1)S(1)} %collective-permute-done.16), channel_id=1, source_target_pairs={{0,2},{1,3},{2,0},{3,1},{4,6},{5,7},{6,4},{7,5},{8,10},{9,11},{10,... | collective-permute-start | bytes 122888 | tf_op jit(solution)/shard_map/ppermute | solution.py:36
  50.2 1.6 %collective-permute-start.21 = (bf16[8,80,256]{2,1,0:T(8,128)(2,1)S(1)}, bf16[8,80,256]{2,1,0:T(8,128)(2,1)S(1)}, u32[]{:S(2)}, u32[]{:S(2)}) collective-permute-start(bf16[8,80,256]{2,1,0:T(8,128)(2,1)S(1)} %constant_dynamic-update-slice_fusion.5.refs_0_), channel_id=1, source_target_pairs={{0,1},{1,0},{2,3},{3,2},{4,5},{5,4},{6,7},{7,6},{8,9},{9,8},{10,11... | collective-permute-start | bytes 983048 | tf_op jit(solution)/shard_map/ppermute | solution.py:36

commit v8 on v7

--- a/solution.py
+++ b/solution.py
@@ -47,7 +47,7 @@
     return jnp.transpose(jnp.broadcast_to(row, (rows, rows)))
 
 
-def message_kernel(me_ref, hf_hbm, hb_hbm, wb_hbm, far_ref, near_ref, cut_ref, wb_ref, sems):
+def message_kernel(me_ref, hf_hbm, hb_hbm, wb_hbm, far_ref, near_ref, cut_ref, head_ref, wb_ref, sems):
     rows, width = cut_ref.shape
     me = me_ref[0]
 
@@ -66,6 +66,7 @@
                 (columns(1), near_ref.at[:rows, :]),
                 (hb_hbm, near_ref.at[rows:, :]),
                 (columns(0), cut_ref),
+                (hb_hbm, head_ref),
                 (wb_hbm, wb_ref),
             )
         )
@@ -136,42 +137,40 @@
     out_ref[rows : 2 * rows, :] = (dot(ht[...], wt[...]) + zrows).astype(BF)
 
 
-def pack_kernel(near_ref, feats_ref, piece_ref, over_y_ref, to_core_ref):
-    end = feats_ref.shape[0]
-    over_y_ref[:end, :] = feats_ref[...]
-    over_y_ref[end:, :] = piece_ref[...]
+def pack_kernel(*refs):
     at = 0
-    for ref in (near_ref, feats_ref):
-        to_core_ref[at : at + ref.shape[0], :] = ref[...]
+    for ref in refs[:-2]:
+        refs[-1][at : at + ref.shape[0], :] = ref[...]
         at = at + ref.shape[0]
+
+
+def pack(*arrays, after):
+    return pl.pallas_call(
+        pack_kernel,
+        in_specs=[VMEM] * (len(arrays) + 1),
+        out_specs=VMEM,
+        out_shape=jax.ShapeDtypeStruct((sum(x.shape[0] for x in arrays), arrays[0].shape[1]), BF),
+        compiler_params=pltpu.CompilerParams(vmem_limit_bytes=20 * 2**20),
+    )(*arrays, after)
 
 
 def pair_kernel(*refs, rows, total):
     base_ref, place_ref = refs[:2]
-    near_ref, far_ref, core_ref, far3_ref, feats_ref = refs[2:7]
-    second_refs, rest_refs = refs[7:9], refs[9:11]
-    cut_ref, wb_ref, keep_ref, sends = refs[11], refs[12], refs[13], refs[14:17]
-    hid_ref, raw_ref, back_ref, mask_ref, smat_ref, pick_ref, own_ref, wfq_ref, wbq_ref = refs[17:]
+    near_ref, far_ref, core_ref = refs[2:5]
+    feats = [(ref, 0) for ref in refs[5:9]]
+    cut_ref, wb_ref, keep_ref, sends = refs[9], refs[10], refs[11], refs[12:15]
+    hid_ref, raw_ref, back_ref, mask_ref, smat_ref, pick_ref, own_ref, wfq_ref, wbq_ref = refs[15:]
     width = wb_ref.shape[1]
     pairs = float(total * (total - 1))
     groups = total // (4 * rows)
     span = total // 16
     wb = wb_ref[...]
     end = 2 * rows + PAD
-    feats = ((feats_ref, 0), (second_refs[0], 0), (core_ref, 2 * rows), (second_refs[1], 0))
-    cuts = ((cut_ref, 0), (far_ref, 0), (core_ref, 0), (far3_ref, rows))
+    heads = ((near_ref, rows), (far_ref, 2 * rows), (core_ref, rows), (core_ref, 4 * rows))
+    cuts = ((cut_ref, 0), (far_ref, 0), (core_ref, 0), (core_ref, 3 * rows))
     segments = []
-    for own, far, second, rest in (
-        (near_ref, far_ref, second_refs[0], rest_refs[0]),
-        (core_ref, far3_ref, second_refs[1], rest_refs[1]),
-    ):
-        segments += [
-            (own, rows, rows),
-            (rest, 0, 4 * span - rows),
-            (far, 2 * rows, rows),
-            (second, end, span),
-            (rest, 4 * span - rows, 3 * span - rows),
-        ]
+    for (head, start), (line, _) in zip(heads, feats):
+        segments += [(head, start, rows), (line, end, 4 * span - rows)]
     first = 0
     for ref, start, length in segments:
         if length <= 4 * rows:
@@ -361,22 +360,19 @@
     total = size * rows
     assert bits >= 4 and size == 1 << bits and high // 4 == width == wide
 
-    head = hidden_b
-    for mask in reversed(beyond):
-        head = jnp.concatenate([head, swap(head, mask, size)], axis=0)
-    piece12, piece8, piece4 = [swap(head, mask, size) for mask, _ in LINE]
-    far, near, cut, wb_copy = pl.pallas_call(
+    far, near, cut, head, wb_copy = pl.pallas_call(
         message_kernel,
         in_specs=[SMEM] + [HBM] * 3,
-        out_specs=[VMEM] * 4,
+        out_specs=[VMEM] * 5,
         out_shape=[
             jax.ShapeDtypeStruct((3 * rows, width), BF),
             jax.ShapeDtypeStruct((2 * rows, width), BF),
             jax.ShapeDtypeStruct((rows, width), BF),
+            jax.ShapeDtypeStruct(hidden_b.shape, BF),
             jax.ShapeDtypeStruct(w_b.shape, BF),
         ],
-        scratch_shapes=[pltpu.SemaphoreType.DMA((7,))],
-        compiler_params=pltpu.CompilerParams(vmem_limit_bytes=60 * 2**20),
+        scratch_shapes=[pltpu.SemaphoreType.DMA((8,))],
+        compiler_params=pltpu.CompilerParams(vmem_limit_bytes=59 * 2**20),
     )(me.astype(jnp.int32).reshape(1), hidden_f, hidden_b, w_b)
     feats0 = pl.pallas_call(
         feature_kernel,
@@ -393,7 +389,7 @@
             pltpu.VMEM((1, rows), jnp.int32),
             pltpu.SemaphoreType.DMA((7,)),
         ],
-        compiler_params=pltpu.CompilerParams(vmem_limit_bytes=60 * 2**20),
+        compiler_params=pltpu.CompilerParams(vmem_limit_bytes=59 * 2**20),
         cost_estimate=pl.CostEstimate(
             flops=4 * rows * high * width, bytes_accessed=4 * high * (rows + width), transcendentals=0
         ),
@@ -407,26 +403,16 @@
         positives.reshape(1, rows),
     )
     far2 = swap(far, 2, size)
-    second, to_core = pl.pallas_call(
-        pack_kernel,
-        in_specs=[VMEM] * 3,
-        out_specs=[VMEM] * 2,
-        out_shape=[
-            jax.ShapeDtypeStruct((feats0.shape[0] + piece4.shape[0], width), BF),
-            jax.ShapeDtypeStruct((2 * rows + feats0.shape[0], width), BF),
-        ],
-        compiler_params=pltpu.CompilerParams(vmem_limit_bytes=16 * 2**20),
-    )(near, feats0, piece4)
-    second2 = swap(second, 2, size)
-    over_y = [swap(piece, 2, size) for piece in (piece8, piece12)]
+    for mask in reversed(beyond):
+        head = jnp.concatenate([head, swap(head, mask, size)], axis=0)
+    piece12, piece8, piece4 = [swap(head, mask, size) for mask, _ in LINE]
+    to_core = pack(near, far2, after=near)
     more = [head[rows:]] * (len(beyond) > 0)
-    rest0 = jnp.concatenate(
-        [piece4, piece8, piece12] + more + over_y + [swap(piece, 2, size) for piece in more], axis=0
-    )
+    second0 = pack(feats0, piece4, piece8, piece12, *more, after=to_core)
+    second2 = swap(second0, 2, size)
     from_core = swap(to_core, 1, size)
-    far3 = swap(far2, 1, size)
+    second1 = swap(second0, 1, size)
     second3 = swap(second2, 1, size)
-    rest1 = swap(rest0, 1, size)
 
     inner = reverse_bits(jnp.arange(size // 16, dtype=jnp.int32), bits - 4) << 4
     first, others = inner[:1], inner[1:]
@@ -442,7 +428,7 @@
     each = wf_rows + wb_rows
     keep, *sends = pl.pallas_call(
         functools.partial(pair_kernel, rows=rows, total=total),
-        in_specs=[SMEM] * 2 + [VMEM] * 11,
+        in_specs=[SMEM] * 2 + [VMEM] * 9,
         out_specs=[VMEM] * 4,
         out_shape=[jax.ShapeDtypeStruct((each + PAD, width), F32)]
         + [jax.ShapeDtypeStruct((each + PAD, width), BF)] * 3,
@@ -458,7 +444,7 @@
             pltpu.VMEM((wide // 2, width), F32),
         ],
         compiler_params=pltpu.CompilerParams(vmem_limit_bytes=15 * 2**20 + total * width * 10),
-    )(bases, places, near, far2, from_core, far3, feats0, second2, second3, rest0, rest1, cut, wb_copy)
+    )(bases, places, near, far2, from_core, second0, second2, second1, second3, cut, wb_copy)
 
     got = [swap(part, mask, size) for part, (mask, _) in zip(sends, LINE)]
     result, note = pl.pallas_call(

time: 53.1 us -> 53.7 us (1.011)
  waiting for transfers between devices: 17.3 us -> 19.5 us
  starting transfers between devices: 23.5 us -> 22.2 us
    ppermute x22 -> x19, waiting for transfers between devices: 17.3 us -> 19.5 us  [swap(): return lax.ppermute(array, 'fa', [(i, i ^ mask) for i in range(size)])]
    ppermute x22 -> x19, starting transfers between devices: 23.5 us -> 22.2 us  [swap(): return lax.ppermute(array, 'fa', [(i, i ^ mask) for i in range(size)])]
  transfers between devices with their start and end apart: 22 -> 19, of which waited for: 12 -> 10; matrix products, arithmetic and copies ran while one was open for 0% -> 0% of each run, Pallas kernels for 9% -> 5%
where the time goes in v8:
time: 53.7 us; the launch traced here: 53.5 us
  starting transfers between devices  22.2 us (41%)
  waiting for transfers between devices  19.5 us (36%)
  Pallas kernels  10.3 us (19%)
  between operations  0.78 us (1%)
  local copies, waits for them, and re-layouts  0.63 us (1%)
    ppermute x19, starting transfers between devices, swap(): return lax.ppermute(array, 'fa', [(i, i ^ mask) for i in range(size)])  22.2 us
    ppermute x19, waiting for transfers between devices, swap(): return lax.ppermute(array, 'fa', [(i, i ^ mask) for i in range(size)])  19.5 us
    pallas_call x1, Pallas kernels, body(): pl.pallas_call(functools.partial(pair_kernel, rows=rows, total=total), in...  4.06 us
    pallas_call x1, Pallas kernels, body(): pl.pallas_call(feature_kernel, in_specs=[HBM] * 7, out_specs=VMEM, out_sh...  2.56 us
    pallas_call x1, Pallas kernels, body(): pl.pallas_call(message_kernel, in_specs=[SMEM] + [HBM] * 3, out_specs=[VM...  2.01 us
    pallas_call x1, Pallas kernels, body(): pl.pallas_call(functools.partial(assemble_kernel, wf_rows=wf_rows, wb_row...  1.14 us
  transfers between devices with their start and end apart: 19, of which 10 were waited for; matrix products, arithmetic and copies ran while one was open for 0% of the time, Pallas kernels for 5%

profile of v8, /device:TPU:0, one launch (start us, length us, event | category | flops | bytes accessed | tf_op | source)
XLA Modules:
  0.0 53.5 jit_solution(3150197662688439390)
XLA Ops:
  0.6 2.0 %shard_map.112 = (bf16[384,256]{1,0:T(8,128)(2,1)}, bf16[256,256]{1,0:T(8,128)(2,1)}, bf16[128,256]{1,0:T(8,128)(2,1)}, bf16[128,256]{1,0:T(8,128)(2,1)}, bf16[256,256]{1,0:T(8,128)(2,1)}) custom-call(s32[1]{0:T(128)} %bitcast.3.me_ref, bf16[128,1024]{1,0:T(8,128)(2,1)} %hf_hbm.3, bf16[128,256]{1,0:T(8,128)(2,1)} %hb_hbm.1, bf16[256,256]{1,0:T(8,128)(2,1)} %wb_hbm.1), custom_call_target="tpu_custom_call" | custom-call | tf_op jit(solution)/shard_map/pallas_call | solution.py:363
  2.7 3.0 %collective-permute-start = (bf16[384,256]{1,0:T(8,128)(2,1)}, bf16[384,256]{1,0:T(8,128)(2,1)S(1)}, u32[]{:S(2)}, u32[]{:S(2)}) collective-permute-start(bf16[384,256]{1,0:T(8,128)(2,1)} %get-tuple-element.17), channel_id=1, source_target_pairs={{0,2},{1,3},{2,0},{3,1},{4,6},{5,7},{6,4},{7,5},{8,10},{9,11},{10,... | collective-permute-start | bytes 589832 | tf_op jit(solution)/shard_map/ppermute | solution.py:36
  5.7 3.6 %collective-permute-start.4 = (bf16[128,256]{1,0:T(8,128)(2,1)}, bf16[128,256]{1,0:T(8,128)(2,1)S(1)}, u32[]{:S(2)}, u32[]{:S(2)}) collective-permute-start(bf16[128,256]{1,0:T(8,128)(2,1)} %get-tuple-element.18), channel_id=1, source_target_pairs={{0,12},{1,13},{2,14},{3,15},{4,8},{5,9},{6,10},{7,11},{8,4},{9,5},... | collective-permute-start | bytes 196616 | tf_op jit(solution)/shard_map/ppermute | solution.py:36
  9.3 0.0 collective-permute-start.3
  9.3 0.8 %collective-permute-start.2 = (bf16[128,256]{1,0:T(8,128)(2,1)}, bf16[128,256]{1,0:T(8,128)(2,1)S(1)}, u32[]{:S(2)}, u32[]{:S(2)}) collective-permute-start(bf16[128,256]{1,0:T(8,128)(2,1)} %get-tuple-element.18), channel_id=1, source_target_pairs={{0,4},{1,5},{2,6},{3,7},{4,0},{5,1},{6,2},{7,3},{8,12},{9,13},{10,... | collective-permute-start | bytes 196616 | tf_op jit(solution)/shard_map/ppermute | solution.py:36
  10.1 0.0 copy-start
  10.1 2.6 %shard_map.114.refs_0_ = bf16[272,256]{1,0:T(8,128)(2,1)} custom-call(bf16[128,1024]{1,0:T(8,128)(2,1)} %hf_hbm.3, bf16[128,1024]{1,0:T(8,128)(2,1)} %ht_hbm.1, bf16[1024,256]{1,0:T(8,128)(2,1)} %wf_hbm.1, bf16[1024,256]{1,0:T(8,128)(2,1)} %wt_hbm.1, bf16[512,256]{1,0:T(8,128)(2,1)} %lat_hbm.1, s32[1,128]{1,0:T(1,128)} %bitcast.13, s32[1,128]{1,0:T(1,128)} %bitcast.14), custom_call_target="tpu_custom_call" | custom-call | flops 134217728 | bytes 1572864 | tf_op jit(solution)/shard_map/pallas_call | solution.py:377
  12.6 0.0 collective-permute-done.refs_1_.refs_3_
  12.7 0.0 copy-done
  12.7 0.0 copy-start.1
  12.7 0.1 collective-permute-done.4.refs_3_
  12.8 2.1 %collective-permute-done.3.refs_2_ = bf16[128,256]{1,0:T(8,128)(2,1)S(1)} collective-permute-done((bf16[128,256]{1,0:T(8,128)(2,1)}, bf16[128,256]{1,0:T(8,128)(2,1)S(1)}, u32[]{:S(2)}, u32[]{:S(2)}) %collective-permute-start.3) | collective-permute-done | bytes 65568 | tf_op jit(solution)/shard_map/ppermute | solution.py:36
  14.9 0.1 collective-permute-done.2.refs_1_
  14.9 0.0 copy-done.1
  14.9 0.0 copy-start.2
  14.9 0.0 copy-start.3
  15.0 0.5 collective-permute-start.5
  15.5 0.0 collective-permute-start.1
  15.5 0.5 collective-permute-start.6
  16.0 8.3 %collective-permute-done.5.refs_6_ = bf16[656,256]{1,0:T(8,128)(2,1)S(1)} collective-permute-done((bf16[656,256]{1,0:T(8,128)(2,1)S(1)}, bf16[656,256]{1,0:T(8,128)(2,1)S(1)}, u32[]{:S(2)}, u32[]{:S(2)}) %collective-permute-start.5) | collective-permute-done | bytes 335904 | tf_op jit(solution)/shard_map/ppermute | solution.py:36
  24.2 0.0 collective-permute-start.7
  24.2 0.0 copy-start.4
  24.2 0.1 pad_add_fusion.refs_1_
  24.3 0.6 %copy-done.4 = s32[16]{0:T(128)S(1)} copy-done((s32[16]{0:T(128)S(1)}, s32[16]{0:T(128)}, u32[]{:S(2)}) %copy-start.4) | copy-done | bytes 88
  24.9 0.0 collective-permute-done.1.refs_4_
  24.9 0.0 collective-permute-done.6.refs_7_
  24.9 1.0 %collective-permute-done.7.refs_8_ = bf16[656,256]{1,0:T(8,128)(2,1)S(1)} collective-permute-done((bf16[656,256]{1,0:T(8,128)(2,1)S(1)}, bf16[656,256]{1,0:T(8,128)(2,1)S(1)}, u32[]{:S(2)}, u32[]{:S(2)}) %collective-permute-start.7) | collective-permute-done | bytes 335904 | tf_op jit(solution)/shard_map/ppermute | solution.py:36
  25.9 0.0 copy-done.2
  25.9 0.0 copy-done.3
  25.9 4.1 %shard_map.116 = (f32[96,256]{1,0:T(8,128)S(1)}, bf16[96,256]{1,0:T(8,128)(2,1)S(1)}, bf16[96,256]{1,0:T(8,128)(2,1)S(1)}, bf16[96,256]{1,0:T(8,128)(2,1)S(1)}) custom-call(s32[16]{0:T(128)S(1)} %xor_multiply_fusion.refs_0_, s32[2]{0:T(128)S(1)} %pad_add_fusion.refs_1_, bf16[256,256]{1,0:T(8,128)(2,1)S(1)} %copy-done, ...), custom_call_target="tpu_custom_call" | custom-call | tf_op jit(solution)/shard_map/pallas_call | solution.py:429
  29.9 1.6 %collective-permute-start.8 = (bf16[96,256]{1,0:T(8,128)(2,1)S(1)}, bf16[96,256]{1,0:T(8,128)(2,1)S(1)}, u32[]{:S(2)}, u32[]{:S(2)}) collective-permute-start(bf16[96,256]{1,0:T(8,128)(2,1)S(1)} %get-tuple-element.22), channel_id=1, source_target_pairs={{0,12},{1,13},{2,14},{3,15},{4,8},{5,9},{6,10},{7,11},{8,4},{9,5},... | collective-permute-start | bytes 147464 | tf_op jit(solution)/shard_map/ppermute | solution.py:36
  31.6 0.2 collective-permute-start.9
  31.7 2.7 %collective-permute-start.10 = (bf16[96,256]{1,0:T(8,128)(2,1)S(1)}, bf16[96,256]{1,0:T(8,128)(2,1)S(1)}, u32[]{:S(2)}, u32[]{:S(2)}) collective-permute-start(bf16[96,256]{1,0:T(8,128)(2,1)S(1)} %get-tuple-element.24), channel_id=1, source_target_pairs={{0,4},{1,5},{2,6},{3,7},{4,0},{5,1},{6,2},{7,3},{8,12},{9,13},{10,... | collective-permute-start | bytes 147464 | tf_op jit(solution)/shard_map/ppermute | solution.py:36
  34.4 1.8 %collective-permute-done.8.refs_0_ = bf16[96,256]{1,0:T(8,128)(2,1)S(1)} collective-permute-done((bf16[96,256]{1,0:T(8,128)(2,1)S(1)}, bf16[96,256]{1,0:T(8,128)(2,1)S(1)}, u32[]{:S(2)}, u32[]{:S(2)}) %collective-permute-start.8) | collective-permute-done | bytes 49184 | tf_op jit(solution)/shard_map/ppermute | solution.py:36
  36.2 1.5 %collective-permute-done.9.refs_1_ = bf16[96,256]{1,0:T(8,128)(2,1)S(1)} collective-permute-done((bf16[96,256]{1,0:T(8,128)(2,1)S(1)}, bf16[96,256]{1,0:T(8,128)(2,1)S(1)}, u32[]{:S(2)}, u32[]{:S(2)}) %collective-permute-start.9) | collective-permute-done | bytes 49184 | tf_op jit(solution)/shard_map/ppermute | solution.py:36
  37.7 0.0 collective-permute-done.10.refs_2_
  37.7 0.5 shard_map.117
  38.2 0.5 collective-permute-start.14
  38.7 0.8 %collective-permute-start.13 = (bf16[1,80,256]{2,1,0:T(8,128)(2,1)S(1)}, bf16[1,80,256]{2,1,0:T(8,128)(2,1)S(1)}, u32[]{:S(2)}, u32[]{:S(2)}) collective-permute-start(bf16[1,80,256]{2,1,0:T(8,128)(2,1)S(1)} %bitcast.10), channel_id=1, source_target_pairs={{0,4},{1,5},{2,6},{3,7},{4,0},{5,1},{6,2},{7,3},{8,12},{9,13},{10,... | collective-permute-start | bytes 122888 | tf_op jit(solution)/shard_map/ppermute | solution.py:36
  39.5 1.3 %collective-permute-start.12 = (bf16[1,80,256]{2,1,0:T(8,128)(2,1)S(1)}, bf16[1,80,256]{2,1,0:T(8,128)(2,1)S(1)}, u32[]{:S(2)}, u32[]{:S(2)}) collective-permute-start(bf16[1,80,256]{2,1,0:T(8,128)(2,1)S(1)} %bitcast.11), channel_id=1, source_target_pairs={{0,8},{1,9},{2,10},{3,11},{4,12},{5,13},{6,14},{7,15},{8,0},{9,1},... | collective-permute-start | bytes 122888 | tf_op jit(solution)/shard_map/ppermute | solution.py:36
  40.8 2.3 %collective-permute-start.11 = (bf16[1,80,256]{2,1,0:T(8,128)(2,1)S(1)}, bf16[1,80,256]{2,1,0:T(8,128)(2,1)S(1)}, u32[]{:S(2)}, u32[]{:S(2)}) collective-permute-start(bf16[1,80,256]{2,1,0:T(8,128)(2,1)S(1)} %bitcast.12), channel_id=1, source_target_pairs={{0,12},{1,13},{2,14},{3,15},{4,8},{5,9},{6,10},{7,11},{8,4},{9,5},... | collective-permute-start | bytes 122888 | tf_op jit(solution)/shard_map/ppermute | solution.py:36
  43.1 0.0 collective-permute-done.13
  43.1 1.5 %collective-permute-start.17 = (bf16[1,80,256]{2,1,0:T(8,128)(2,1)S(1)}, bf16[1,80,256]{2,1,0:T(8,128)(2,1)S(1)}, u32[]{:S(2)}, u32[]{:S(2)}) collective-permute-start(bf16[1,80,256]{2,1,0:T(8,128)(2,1)S(1)} %collective-permute-done.13), channel_id=1, source_target_pairs={{0,2},{1,3},{2,0},{3,1},{4,6},{5,7},{6,4},{7,5},{8,10},{9,11},{10,... | collective-permute-start | bytes 122888 | tf_op jit(solution)/shard_map/ppermute | solution.py:36
  44.6 0.0 collective-permute-done.12
  44.6 1.3 %collective-permute-start.16 = (bf16[1,80,256]{2,1,0:T(8,128)(2,1)S(1)}, bf16[1,80,256]{2,1,0:T(8,128)(2,1)S(1)}, u32[]{:S(2)}, u32[]{:S(2)}) collective-permute-start(bf16[1,80,256]{2,1,0:T(8,128)(2,1)S(1)} %collective-permute-done.12), channel_id=1, source_target_pairs={{0,2},{1,3},{2,0},{3,1},{4,6},{5,7},{6,4},{7,5},{8,10},{9,11},{10,... | collective-permute-start | bytes 122888 | tf_op jit(solution)/shard_map/ppermute | solution.py:36
  45.9 0.7 %collective-permute-done.11 = bf16[1,80,256]{2,1,0:T(8,128)(2,1)S(1)} collective-permute-done((bf16[1,80,256]{2,1,0:T(8,128)(2,1)S(1)}, bf16[1,80,256]{2,1,0:T(8,128)(2,1)S(1)}, u32[]{:S(2)}, u32[]{:S(2)}) %collective-permute-start.11) | collective-permute-done | bytes 40992 | tf_op jit(solution)/shard_map/ppermute | solution.py:36
  46.6 1.5 %collective-permute-start.15 = (bf16[1,80,256]{2,1,0:T(8,128)(2,1)S(1)}, bf16[1,80,256]{2,1,0:T(8,128)(2,1)S(1)}, u32[]{:S(2)}, u32[]{:S(2)}) collective-permute-start(bf16[1,80,256]{2,1,0:T(8,128)(2,1)S(1)} %collective-permute-done.11), channel_id=1, source_target_pairs={{0,2},{1,3},{2,0},{3,1},{4,6},{5,7},{6,4},{7,5},{8,10},{9,11},{10,... | collective-permute-start | bytes 122888 | tf_op jit(solution)/shard_map/ppermute | solution.py:36
  48.2 0.0 collective-permute-done.14
  48.2 2.4 %collective-permute-done.15 = bf16[1,80,256]{2,1,0:T(8,128)(2,1)S(1)} collective-permute-done((bf16[1,80,256]{2,1,0:T(8,128)(2,1)S(1)}, bf16[1,80,256]{2,1,0:T(8,128)(2,1)S(1)}, u32[]{:S(2)}, u32[]{:S(2)}) %collective-permute-start.15) | collective-permute-done | bytes 40992 | tf_op jit(solution)/shard_map/ppermute | solution.py:36
  50.6 0.0 collective-permute-done.16
  50.7 0.0 collective-permute-done.17
  50.7 0.1 collective-permute-start.18
  50.8 1.6 %collective-permute-done.18.refs_1_ = bf16[8,80,256]{2,1,0:T(8,128)(2,1)S(1)} collective-permute-done((bf16[8,80,256]{2,1,0:T(8,128)(2,1)S(1)}, bf16[8,80,256]{2,1,0:T(8,128)(2,1)S(1)}, u32[]{:S(2)}, u32[]{:S(2)}) %collective-permute-start.18) | collective-permute-done | bytes 327712 | tf_op jit(solution)/shard_map/ppermute | solution.py:36
  52.4 1.1 %shard_map.118 = (f32[1024,256]{1,0:T(8,128)}, f32[256,256]{1,0:T(8,128)}) custom-call(s32[1]{0:T(128)} %bitcast.place_ref, bf16[8,80,256]{2,1,0:T(8,128)(2,1)S(1)} %constant_dynamic-update-slice_fusion.refs_0_, bf16[8,80,256]{2,1,0:T(8,128)(2,1)S(1)} %collective-permute-done.18.refs_1_), custom_call_target="tpu_custom_call" | custom-call | tf_op jit(solution)/shard_map/pallas_call | solution.py:467
  (11 shorter events, 0.1 us)
Async XLA Ops:
  2.7 10.0 %collective-permute-start = (bf16[384,256]{1,0:T(8,128)(2,1)}, bf16[384,256]{1,0:T(8,128)(2,1)S(1)}, u32[]{:S(2)}, u32[]{:S(2)}) collective-permute-start(bf16[384,256]{1,0:T(8,128)(2,1)} %get-tuple-element.17), channel_id=1, source_target_pairs={{0,2},{1,3},{2,0},{3,1},{4,6},{5,7},{6,4},{7,5},{8,10},{9,11},{10,... | collective-permute-start | bytes 589832 | tf_op jit(solution)/shard_map/ppermute | solution.py:36
  5.7 7.1 %collective-permute-start.4 = (bf16[128,256]{1,0:T(8,128)(2,1)}, bf16[128,256]{1,0:T(8,128)(2,1)S(1)}, u32[]{:S(2)}, u32[]{:S(2)}) collective-permute-start(bf16[128,256]{1,0:T(8,128)(2,1)} %get-tuple-element.18), channel_id=1, source_target_pairs={{0,12},{1,13},{2,14},{3,15},{4,8},{5,9},{6,10},{7,11},{8,4},{9,5},... | collective-permute-start | bytes 196616 | tf_op jit(solution)/shard_map/ppermute | solution.py:36
  9.3 5.6 %collective-permute-start.3 = (bf16[128,256]{1,0:T(8,128)(2,1)}, bf16[128,256]{1,0:T(8,128)(2,1)S(1)}, u32[]{:S(2)}, u32[]{:S(2)}) collective-permute-start(bf16[128,256]{1,0:T(8,128)(2,1)} %get-tuple-element.18), channel_id=1, source_target_pairs={{0,8},{1,9},{2,10},{3,11},{4,12},{5,13},{6,14},{7,15},{8,0},{9,1},... | collective-permute-start | bytes 196616 | tf_op jit(solution)/shard_map/ppermute | solution.py:36
  9.3 5.6 %collective-permute-start.2 = (bf16[128,256]{1,0:T(8,128)(2,1)}, bf16[128,256]{1,0:T(8,128)(2,1)S(1)}, u32[]{:S(2)}, u32[]{:S(2)}) collective-permute-start(bf16[128,256]{1,0:T(8,128)(2,1)} %get-tuple-element.18), channel_id=1, source_target_pairs={{0,4},{1,5},{2,6},{3,7},{4,0},{5,1},{6,2},{7,3},{8,12},{9,13},{10,... | collective-permute-start | bytes 196616 | tf_op jit(solution)/shard_map/ppermute | solution.py:36
  10.1 2.6 %copy-start = (bf16[256,256]{1,0:T(8,128)(2,1)S(1)}, bf16[256,256]{1,0:T(8,128)(2,1)}, u32[]{:S(2)}) copy-start(bf16[256,256]{1,0:T(8,128)(2,1)} %get-tuple-element.16.refs_0_.refs_2_) | copy-start | bytes 393220
  12.7 2.3 %copy-start.1 = (bf16[272,256]{1,0:T(8,128)(2,1)S(1)}, bf16[272,256]{1,0:T(8,128)(2,1)}, u32[]{:S(2)}) copy-start(bf16[272,256]{1,0:T(8,128)(2,1)} %shard_map.114.refs_0_) | copy-start | bytes 417796
  14.9 10.9 %copy-start.2 = (bf16[256,256]{1,0:T(8,128)(2,1)S(1)}, bf16[256,256]{1,0:T(8,128)(2,1)}, u32[]{:S(2)}) copy-start(bf16[256,256]{1,0:T(8,128)(2,1)} %get-tuple-element.20.refs_10_) | copy-start | bytes 393220
  14.9 10.9 %copy-start.3 = (bf16[128,256]{1,0:T(8,128)(2,1)S(1)}, bf16[128,256]{1,0:T(8,128)(2,1)}, u32[]{:S(2)}) copy-start(bf16[128,256]{1,0:T(8,128)(2,1)} %get-tuple-element.19.refs_9_) | copy-start | bytes 196612
  15.0 9.3 %collective-permute-start.5 = (bf16[656,256]{1,0:T(8,128)(2,1)S(1)}, bf16[656,256]{1,0:T(8,128)(2,1)S(1)}, u32[]{:S(2)}, u32[]{:S(2)}) collective-permute-start(bf16[656,256]{1,0:T(8,128)(2,1)S(1)} %shard_map.115.refs_5_), channel_id=1, source_target_pairs={{0,2},{1,3},{2,0},{3,1},{4,6},{5,7},{6,4},{7,5},{8,10},{9,11},{10,... | collective-permute-start | bytes 1007624 | tf_op jit(solution)/shard_map/ppermute | solution.py:36
  15.5 9.4 %collective-permute-start.1 = (bf16[640,256]{1,0:T(8,128)(2,1)S(1)}, bf16[640,256]{1,0:T(8,128)(2,1)S(1)}, u32[]{:S(2)}, u32[]{:S(2)}) collective-permute-start(bf16[640,256]{1,0:T(8,128)(2,1)S(1)} %shard_map.113.refs_4_), channel_id=1, source_target_pairs={{0,1},{1,0},{2,3},{3,2},{4,5},{5,4},{6,7},{7,6},{8,9},{9,8},{10,11... | collective-permute-start | bytes 983048 | tf_op jit(solution)/shard_map/ppermute | solution.py:36
  15.5 9.4 %collective-permute-start.6 = (bf16[656,256]{1,0:T(8,128)(2,1)S(1)}, bf16[656,256]{1,0:T(8,128)(2,1)S(1)}, u32[]{:S(2)}, u32[]{:S(2)}) collective-permute-start(bf16[656,256]{1,0:T(8,128)(2,1)S(1)} %shard_map.115.refs_5_), channel_id=1, source_target_pairs={{0,1},{1,0},{2,3},{3,2},{4,5},{5,4},{6,7},{7,6},{8,9},{9,8},{10,11... | collective-permute-start | bytes 1007624 | tf_op jit(solution)/shard_map/ppermute | solution.py:36
  24.2 1.6 %collective-permute-start.7 = (bf16[656,256]{1,0:T(8,128)(2,1)S(1)}, bf16[656,256]{1,0:T(8,128)(2,1)S(1)}, u32[]{:S(2)}, u32[]{:S(2)}) collective-permute-start(bf16[656,256]{1,0:T(8,128)(2,1)S(1)} %collective-permute-done.5.refs_6_), channel_id=1, source_target_pairs={{0,1},{1,0},{2,3},{3,2},{4,5},{5,4},{6,7},{7,6},{8,9},{9,8},{10,11... | collective-permute-start | bytes 1007624 | tf_op jit(solution)/shard_map/ppermute | solution.py:36
  24.2 0.7 %copy-start.4 = (s32[16]{0:T(128)S(1)}, s32[16]{0:T(128)}, u32[]{:S(2)}) copy-start(s32[16]{0:T(128)} %constant.48.clone.1) | copy-start | bytes 196
  29.9 6.3 %collective-permute-start.8 = (bf16[96,256]{1,0:T(8,128)(2,1)S(1)}, bf16[96,256]{1,0:T(8,128)(2,1)S(1)}, u32[]{:S(2)}, u32[]{:S(2)}) collective-permute-start(bf16[96,256]{1,0:T(8,128)(2,1)S(1)} %get-tuple-element.22), channel_id=1, source_target_pairs={{0,12},{1,13},{2,14},{3,15},{4,8},{5,9},{6,10},{7,11},{8,4},{9,5},... | collective-permute-start | bytes 147464 | tf_op jit(solution)/shard_map/ppermute | solution.py:36
  31.6 6.1 %collective-permute-start.9 = (bf16[96,256]{1,0:T(8,128)(2,1)S(1)}, bf16[96,256]{1,0:T(8,128)(2,1)S(1)}, u32[]{:S(2)}, u32[]{:S(2)}) collective-permute-start(bf16[96,256]{1,0:T(8,128)(2,1)S(1)} %get-tuple-element.23), channel_id=1, source_target_pairs={{0,8},{1,9},{2,10},{3,11},{4,12},{5,13},{6,14},{7,15},{8,0},{9,1},... | collective-permute-start | bytes 147464 | tf_op jit(solution)/shard_map/ppermute | solution.py:36
  31.7 6.0 %collective-permute-start.10 = (bf16[96,256]{1,0:T(8,128)(2,1)S(1)}, bf16[96,256]{1,0:T(8,128)(2,1)S(1)}, u32[]{:S(2)}, u32[]{:S(2)}) collective-permute-start(bf16[96,256]{1,0:T(8,128)(2,1)S(1)} %get-tuple-element.24), channel_id=1, source_target_pairs={{0,4},{1,5},{2,6},{3,7},{4,0},{5,1},{6,2},{7,3},{8,12},{9,13},{10,... | collective-permute-start | bytes 147464 | tf_op jit(solution)/shard_map/ppermute | solution.py:36
  38.2 10.0 %collective-permute-start.14 = (bf16[1,80,256]{2,1,0:T(8,128)(2,1)S(1)}, bf16[1,80,256]{2,1,0:T(8,128)(2,1)S(1)}, u32[]{:S(2)}, u32[]{:S(2)}) collective-permute-start(bf16[1,80,256]{2,1,0:T(8,128)(2,1)S(1)} %bitcast.9), channel_id=1, source_target_pairs={{0,2},{1,3},{2,0},{3,1},{4,6},{5,7},{6,4},{7,5},{8,10},{9,11},{10,... | collective-permute-start | bytes 122888 | tf_op jit(solution)/shard_map/ppermute | solution.py:36
  38.7 4.4 %collective-permute-start.13 = (bf16[1,80,256]{2,1,0:T(8,128)(2,1)S(1)}, bf16[1,80,256]{2,1,0:T(8,128)(2,1)S(1)}, u32[]{:S(2)}, u32[]{:S(2)}) collective-permute-start(bf16[1,80,256]{2,1,0:T(8,128)(2,1)S(1)} %bitcast.10), channel_id=1, source_target_pairs={{0,4},{1,5},{2,6},{3,7},{4,0},{5,1},{6,2},{7,3},{8,12},{9,13},{10,... | collective-permute-start | bytes 122888 | tf_op jit(solution)/shard_map/ppermute | solution.py:36
  39.5 5.1 %collective-permute-start.12 = (bf16[1,80,256]{2,1,0:T(8,128)(2,1)S(1)}, bf16[1,80,256]{2,1,0:T(8,128)(2,1)S(1)}, u32[]{:S(2)}, u32[]{:S(2)}) collective-permute-start(bf16[1,80,256]{2,1,0:T(8,128)(2,1)S(1)} %bitcast.11), channel_id=1, source_target_pairs={{0,8},{1,9},{2,10},{3,11},{4,12},{5,13},{6,14},{7,15},{8,0},{9,1},... | collective-permute-start | bytes 122888 | tf_op jit(solution)/shard_map/ppermute | solution.py:36
  40.8 5.8 %collective-permute-start.11 = (bf16[1,80,256]{2,1,0:T(8,128)(2,1)S(1)}, bf16[1,80,256]{2,1,0:T(8,128)(2,1)S(1)}, u32[]{:S(2)}, u32[]{:S(2)}) collective-permute-start(bf16[1,80,256]{2,1,0:T(8,128)(2,1)S(1)} %bitcast.12), channel_id=1, source_target_pairs={{0,12},{1,13},{2,14},{3,15},{4,8},{5,9},{6,10},{7,11},{8,4},{9,5},... | collective-permute-start | bytes 122888 | tf_op jit(solution)/shard_map/ppermute | solution.py:36
  43.1 7.5 %collective-permute-start.17 = (bf16[1,80,256]{2,1,0:T(8,128)(2,1)S(1)}, bf16[1,80,256]{2,1,0:T(8,128)(2,1)S(1)}, u32[]{:S(2)}, u32[]{:S(2)}) collective-permute-start(bf16[1,80,256]{2,1,0:T(8,128)(2,1)S(1)} %collective-permute-done.13), channel_id=1, source_target_pairs={{0,2},{1,3},{2,0},{3,1},{4,6},{5,7},{6,4},{7,5},{8,10},{9,11},{10,... | collective-permute-start | bytes 122888 | tf_op jit(solution)/shard_map/ppermute | solution.py:36
  44.6 6.0 %collective-permute-start.16 = (bf16[1,80,256]{2,1,0:T(8,128)(2,1)S(1)}, bf16[1,80,256]{2,1,0:T(8,128)(2,1)S(1)}, u32[]{:S(2)}, u32[]{:S(2)}) collective-permute-start(bf16[1,80,256]{2,1,0:T(8,128)(2,1)S(1)} %collective-permute-done.12), channel_id=1, source_target_pairs={{0,2},{1,3},{2,0},{3,1},{4,6},{5,7},{6,4},{7,5},{8,10},{9,11},{10,... | collective-permute-start | bytes 122888 | tf_op jit(solution)/shard_map/ppermute | solution.py:36
  46.6 4.0 %collective-permute-start.15 = (bf16[1,80,256]{2,1,0:T(8,128)(2,1)S(1)}, bf16[1,80,256]{2,1,0:T(8,128)(2,1)S(1)}, u32[]{:S(2)}, u32[]{:S(2)}) collective-permute-start(bf16[1,80,256]{2,1,0:T(8,128)(2,1)S(1)} %collective-permute-done.11), channel_id=1, source_target_pairs={{0,2},{1,3},{2,0},{3,1},{4,6},{5,7},{6,4},{7,5},{8,10},{9,11},{10,... | collective-permute-start | bytes 122888 | tf_op jit(solution)/shard_map/ppermute | solution.py:36
  50.7 1.7 %collective-permute-start.18 = (bf16[8,80,256]{2,1,0:T(8,128)(2,1)S(1)}, bf16[8,80,256]{2,1,0:T(8,128)(2,1)S(1)}, u32[]{:S(2)}, u32[]{:S(2)}) collective-permute-start(bf16[8,80,256]{2,1,0:T(8,128)(2,1)S(1)} %constant_dynamic-update-slice_fusion.refs_0_), channel_id=1, source_target_pairs={{0,1},{1,0},{2,3},{3,2},{4,5},{5,4},{6,7},{7,6},{8,9},{9,8},{10,11... | collective-permute-start | bytes 983048 | tf_op jit(solution)/shard_map/ppermute | solution.py:36

commit v9 on v8

--- a/solution.py
+++ b/solution.py
@@ -13,9 +13,10 @@
 EPS = 1e-06
 BF = jnp.bfloat16
 F32 = jnp.float32
-GROUP = (0, 2, 1, 3)
+FEAT_AT = 2
 PAD = 16
 LINE = ((12, 3), (8, 1), (4, 2))
+OTHERS = ((14, 7), (12, 3), (10, 5), (8, 1), (6, 6), (4, 2), (2, 4))
 TURNS = (0, 3, 1, 2, 4, 7, 5, 6)
 
 
@@ -47,45 +48,19 @@
     return jnp.transpose(jnp.broadcast_to(row, (rows, rows)))
 
 
-def message_kernel(me_ref, hf_hbm, hb_hbm, wb_hbm, far_ref, near_ref, cut_ref, head_ref, wb_ref, sems):
-    rows, width = cut_ref.shape
-    me = me_ref[0]
-
-    def columns(mask):
-        other = me ^ mask
-        quarter = (other & 1) * 2 + ((other >> 1) & 1)
-        return hf_hbm.at[:, pl.ds(pl.multiple_of(quarter * width, width), width)]
-
-    moves = [
-        pltpu.make_async_copy(source, target, sems.at[k])
-        for k, (source, target) in enumerate(
-            (
-                (columns(2), far_ref.at[:rows, :]),
-                (columns(3), far_ref.at[rows : 2 * rows, :]),
-                (hb_hbm, far_ref.at[2 * rows :, :]),
-                (columns(1), near_ref.at[:rows, :]),
-                (hb_hbm, near_ref.at[rows:, :]),
-                (columns(0), cut_ref),
-                (hb_hbm, head_ref),
-                (wb_hbm, wb_ref),
-            )
-        )
-    ]
-    for move in moves:
-        move.start()
-    for move in moves:
-        move.wait()
-
-
 def feature_kernel(
+    core_ref,
     hf_hbm,
     ht_hbm,
     wf_hbm,
     wt_hbm,
+    wb_hbm,
     lat_hbm,
     ids_hbm,
     pos_hbm,
-    out_ref,
+    near_ref,
+    cut_ref,
+    wb_ref,
     hf,
     ht,
     wf,
@@ -108,6 +83,7 @@
                 (wf_hbm, wf),
                 (ht_hbm, ht),
                 (wt_hbm, wt),
+                (wb_hbm, wb_ref),
             )
         )
     ]
@@ -128,13 +104,22 @@
     coded = jnp.where(line == 0, high, jnp.where(line == 1, low, 0.0)).astype(BF)
     coded = jnp.concatenate([coded] + [jnp.zeros((PAD, width - rows), BF)] * (width > rows), axis=1)
 
-    out_ref[2 * rows :, :] = coded
     moves[3].wait()
+    core = core_ref[0]
+    for t in range(2):
+        for ref, half in ((cut_ref, core), (near_ref, 1 - core)):
+            ref[t * rows : (t + 1) * rows, :] = hf[
+                :, pl.ds(pl.multiple_of((half * 2 + t) * width, width), width)
+            ]
     moves[4].wait()
-    out_ref[:rows, :] = (dot(hf[...], wf[...]) + zrows).astype(BF)
+    feat = (dot(hf[...], wf[...]) + zrows).astype(BF)
     moves[5].wait()
     moves[6].wait()
-    out_ref[rows : 2 * rows, :] = (dot(ht[...], wt[...]) + zrows).astype(BF)
+    feat_t = (dot(ht[...], wt[...]) + zrows).astype(BF)
+    near_ref[FEAT_AT * rows : (FEAT_AT + 1) * rows, :] = feat
+    near_ref[(FEAT_AT + 1) * rows : (FEAT_AT + 2) * rows, :] = feat_t
+    near_ref[(FEAT_AT + 2) * rows :, :] = coded
+    moves[7].wait()
 
 
 def pack_kernel(*refs):
@@ -156,35 +141,29 @@
 
 def pair_kernel(*refs, rows, total):
     base_ref, place_ref = refs[:2]
-    near_ref, far_ref, core_ref = refs[2:5]
-    feats = [(ref, 0) for ref in refs[5:9]]
-    cut_ref, wb_ref, keep_ref, sends = refs[9], refs[10], refs[11], refs[12:15]
-    hid_ref, raw_ref, back_ref, mask_ref, smat_ref, pick_ref, own_ref, wfq_ref, wbq_ref = refs[15:]
+    nears, lines, cut_ref, wb_ref = refs[2:4], refs[4:8], refs[8], refs[9]
+    keep_ref, sends = refs[10], refs[11:18]
+    hid_ref, raw_ref, back_ref, mask_ref, smat_ref, pick_ref, own_ref, wfq_ref, wbq_ref = refs[18:]
     width = wb_ref.shape[1]
     pairs = float(total * (total - 1))
-    groups = total // (4 * rows)
-    span = total // 16
+    groups = total // (2 * rows)
     wb = wb_ref[...]
     end = 2 * rows + PAD
-    heads = ((near_ref, rows), (far_ref, 2 * rows), (core_ref, rows), (core_ref, 4 * rows))
-    cuts = ((cut_ref, 0), (far_ref, 0), (core_ref, 0), (core_ref, 3 * rows))
-    segments = []
-    for (head, start), (line, _) in zip(heads, feats):
-        segments += [(head, start, rows), (line, end, 4 * span - rows)]
-    first = 0
-    for ref, start, length in segments:
-        if length <= 4 * rows:
-            hid_ref[first : first + length, :] = ref[start : start + length, :]
+    feats = [(ref, FEAT_AT * rows) for ref in nears]
+    cuts = ((cut_ref, 0), (nears[1], 0))
+    length = total // 4
+    for i, ref in enumerate(lines):
+        if length <= 8 * rows:
+            hid_ref[i * length : (i + 1) * length, :] = ref[...]
         else:
 
-            def one(i, carry, ref=ref, start=start, first=first):
-                hid_ref[pl.ds(pl.multiple_of(first + i * rows, PAD), rows), :] = ref[
-                    pl.ds(pl.multiple_of(start + i * rows, PAD), rows), :
+            def one(k, carry, ref=ref, first=i * length):
+                hid_ref[pl.ds(pl.multiple_of(first + k * rows, rows), rows), :] = ref[
+                    pl.ds(pl.multiple_of(k * rows, rows), rows), :
                 ]
                 return carry
 
             lax.fori_loop(0, length // rows, one, 0)
-        first = first + length
 
     def embed(hidden):
         raw = dot(hidden, wb)
@@ -233,9 +212,9 @@
     over_rows(first_pass)
     smat = smat_ref[...]
     s_hi, s_lo = halves(smat)
-    quarter, mine = place_ref[0], place_ref[1]
+    core, mine = place_ref[0], place_ref[1]
     half = wbq_ref.shape[0]
-    columns = pl.ds(pl.multiple_of((quarter >> 1) * half, half), half)
+    columns = pl.ds(pl.multiple_of(core * half, half), half)
 
     def rows_of(places, offset):
         return jnp.concatenate([ref[at + offset : at + offset + rows, :] for ref, at in places], axis=0)
@@ -254,7 +233,8 @@
     coef = db * (1.0 / pairs) + 1.0 / total
     norm = jnp.sum(ob * ob, axis=-1, keepdims=True)
     grad_f = (ds * (1.0 / pairs) - coef * ob).astype(BF)
-    wfq_ref[...] = dot_t(rows_of(cuts, 0), grad_f)
+    for t in range(2):
+        wfq_ref[t * width : (t + 1) * width, :] = dot_t(rows_of(cuts, t * rows), grad_f)
     squares = jnp.sum(diff * ds) - jnp.sum(db * db)
     squares = squares + LAMBDA * (jnp.sum(smat * smat) / groups - jnp.sum(norm * norm))
     sums = squares / (2.0 * pairs) - (jnp.sum(f32feat * ob) + LAMBDA * jnp.sum(norm)) / total
@@ -275,14 +255,14 @@
         wbq_ref[...] += dot_t(hid_ref[here, columns], back_ref[here, :])
 
     over_rows(second_pass)
-    wf_rows = wfq_ref.shape[0] // 4
+    wf_rows = wfq_ref.shape[0] // 8
     wb_rows = wbq_ref.shape[0] // 8
     size = wf_rows + wb_rows
 
     def block(t):
         return (
             wfq_ref[pl.ds(pl.multiple_of(t * wf_rows, wf_rows), wf_rows), :],
-            wbq_ref[pl.ds(pl.multiple_of(((quarter & 1) * 4 + t) * wb_rows, wb_rows), wb_rows), :],
+            wbq_ref[pl.ds(pl.multiple_of(t * wb_rows, wb_rows), wb_rows), :],
         )
 
     keep_ref[:wf_rows, :], keep_ref[wf_rows:size, :] = block(mine)
@@ -296,7 +276,7 @@
         n_hi.astype(F32),
         jnp.where(line == 1, n_mid.astype(F32), jnp.where(line == 2, n_lo.astype(F32), 0.0)),
     ).astype(BF)
-    for ref, (_, turn) in zip(sends, LINE):
+    for ref, (_, turn) in zip(sends, OTHERS):
         part_f, part_b = block(mine ^ turn)
         ref[:wf_rows, :] = part_f.astype(BF)
         ref[wf_rows:size, :] = part_b.astype(BF)
@@ -304,11 +284,11 @@
 
 
 def add_kernel(keep_ref, *refs):
-    sum_ref, note_ref = refs[3:]
+    sum_ref, note_ref = refs[7:]
     size, width = sum_ref.shape
     total = keep_ref[:size, :]
     note = keep_ref[size : size + 1, :1]
-    for ref in refs[:3]:
+    for ref in refs[:7]:
         total = total + ref[:size, :].astype(F32)
         coded = ref[size:, :].astype(F32)
         note = note + (coded[0:1, :1] + coded[1:2, :1] + coded[2:3, :1])
@@ -360,25 +340,20 @@
     total = size * rows
     assert bits >= 4 and size == 1 << bits and high // 4 == width == wide
 
-    far, near, cut, head, wb_copy = pl.pallas_call(
-        message_kernel,
-        in_specs=[SMEM] + [HBM] * 3,
-        out_specs=[VMEM] * 5,
+    head = hidden_b
+    for mask in reversed(beyond):
+        head = jnp.concatenate([head, swap(head, mask, size)], axis=0)
+    pieces = [swap(head, mask, size) for mask, _ in LINE]
+    core = (me & 1).astype(jnp.int32)
+    near, cut, wb_copy = pl.pallas_call(
+        feature_kernel,
+        in_specs=[SMEM] + [HBM] * 8,
+        out_specs=[VMEM] * 3,
         out_shape=[
-            jax.ShapeDtypeStruct((3 * rows, width), BF),
+            jax.ShapeDtypeStruct(((FEAT_AT + 2) * rows + PAD, width), BF),
             jax.ShapeDtypeStruct((2 * rows, width), BF),
-            jax.ShapeDtypeStruct((rows, width), BF),
-            jax.ShapeDtypeStruct(hidden_b.shape, BF),
             jax.ShapeDtypeStruct(w_b.shape, BF),
         ],
-        scratch_shapes=[pltpu.SemaphoreType.DMA((8,))],
-        compiler_params=pltpu.CompilerParams(vmem_limit_bytes=59 * 2**20),
-    )(me.astype(jnp.int32).reshape(1), hidden_f, hidden_b, w_b)
-    feats0 = pl.pallas_call(
-        feature_kernel,
-        in_specs=[HBM] * 7,
-        out_specs=VMEM,
-        out_shape=jax.ShapeDtypeStruct((2 * rows + PAD, width), BF),
         scratch_shapes=[
             pltpu.VMEM(hidden_f.shape, BF),
             pltpu.VMEM(hidden_t.shape, BF),
@@ -387,69 +362,59 @@
             pltpu.VMEM(latents.shape, BF),
             pltpu.VMEM((1, rows), jnp.int32),
             pltpu.VMEM((1, rows), jnp.int32),
-            pltpu.SemaphoreType.DMA((7,)),
+            pltpu.SemaphoreType.DMA((8,)),
         ],
-        compiler_params=pltpu.CompilerParams(vmem_limit_bytes=59 * 2**20),
-        cost_estimate=pl.CostEstimate(
-            flops=4 * rows * high * width, bytes_accessed=4 * high * (rows + width), transcendentals=0
-        ),
+        compiler_params=pltpu.CompilerParams(vmem_limit_bytes=60 * 2**20),
     )(
+        core.reshape(1),
         hidden_f,
         hidden_t,
         w_f,
         w_t,
+        w_b,
         latents,
         latent_ids.reshape(1, rows),
         positives.reshape(1, rows),
     )
-    far2 = swap(far, 2, size)
-    for mask in reversed(beyond):
-        head = jnp.concatenate([head, swap(head, mask, size)], axis=0)
-    piece12, piece8, piece4 = [swap(head, mask, size) for mask, _ in LINE]
-    to_core = pack(near, far2, after=near)
-    more = [head[rows:]] * (len(beyond) > 0)
-    second0 = pack(feats0, piece4, piece8, piece12, *more, after=to_core)
-    second2 = swap(second0, 2, size)
-    from_core = swap(to_core, 1, size)
-    second1 = swap(second0, 1, size)
-    second3 = swap(second2, 1, size)
+    near1 = swap(near, 1, size)
+    line0 = pack(head, *pieces, after=near)
+    line2 = swap(line0, 2, size)
+    line1 = swap(line0, 1, size)
+    line3 = swap(line2, 1, size)
 
     inner = reverse_bits(jnp.arange(size // 16, dtype=jnp.int32), bits - 4) << 4
-    first, others = inner[:1], inner[1:]
     bases = []
-    for core in (0, 1):
-        bases += [core ^ first] + [core ^ mask ^ inner for mask in (4, 8, 12)] + [core ^ others]
-        core = core ^ 2
-        bases += [core ^ first] + [core ^ mask ^ inner for mask in (4, 8, 12)] + [core ^ others]
+    for way in (0, 2, 1, 3):
+        bases += [way ^ inner] + [way ^ mask ^ inner for mask, _ in LINE]
     bases = ((me ^ jnp.concatenate(bases)) * rows).astype(jnp.int32)
     place = reverse_bits(me & 15, 4).astype(jnp.int32)
-    places = jnp.stack([place >> 2, place & 3])
+    places = jnp.stack([core, place & 7])
     wf_rows, wb_rows = high // 16, wide // 16
     each = wf_rows + wb_rows
     keep, *sends = pl.pallas_call(
         functools.partial(pair_kernel, rows=rows, total=total),
-        in_specs=[SMEM] * 2 + [VMEM] * 9,
-        out_specs=[VMEM] * 4,
+        in_specs=[SMEM] * 2 + [VMEM] * 8,
+        out_specs=[VMEM] * 8,
         out_shape=[jax.ShapeDtypeStruct((each + PAD, width), F32)]
-        + [jax.ShapeDtypeStruct((each + PAD, width), BF)] * 3,
+        + [jax.ShapeDtypeStruct((each + PAD, width), BF)] * 7,
         scratch_shapes=[
             pltpu.VMEM((total, wide), BF),
             pltpu.VMEM((total, width), F32),
             pltpu.VMEM((total, width), BF),
-            pltpu.VMEM((4 * rows, min(total, 16 * rows)), BF),
+            pltpu.VMEM((2 * rows, min(total, 16 * rows)), BF),
             pltpu.VMEM((width, width), F32),
-            pltpu.VMEM((4 * rows, wide), F32),
-            pltpu.VMEM((4 * rows, wide), BF),
-            pltpu.VMEM((width, width), F32),
+            pltpu.VMEM((2 * rows, wide), F32),
+            pltpu.VMEM((2 * rows, wide), BF),
+            pltpu.VMEM((2 * width, width), F32),
             pltpu.VMEM((wide // 2, width), F32),
         ],
         compiler_params=pltpu.CompilerParams(vmem_limit_bytes=15 * 2**20 + total * width * 10),
-    )(bases, places, near, far2, from_core, second0, second2, second1, second3, cut, wb_copy)
-
-    got = [swap(part, mask, size) for part, (mask, _) in zip(sends, LINE)]
+    )(bases, places, near, near1, line0, line2, line1, line3, cut, wb_copy)
+
+    got = [swap(part, mask, size) for part, (mask, _) in zip(sends, OTHERS)]
     result, note = pl.pallas_call(
         add_kernel,
-        in_specs=[VMEM] * 4,
+        in_specs=[VMEM] * 8,
         out_specs=[VMEM] * 2,
         out_shape=[
             jax.ShapeDtypeStruct((each, width), F32 if beyond else BF),

time: 53.7 us -> 59.5 us (1.11)
  starting transfers between devices: 22.2 us -> 26.1 us
  waiting for transfers between devices: 19.5 us -> 22.4 us
  Pallas kernels: 10.3 us -> 9.29 us
    ppermute x19 -> x22, starting transfers between devices: 22.2 us -> 26.1 us  [swap(): return lax.ppermute(array, 'fa', [(i, i ^ mask) for i in range(size)])]
    ppermute x19 -> x22, waiting for transfers between devices: 19.5 us -> 22.4 us  [swap(): return lax.ppermute(array, 'fa', [(i, i ^ mask) for i in range(size)])]
    pallas_call x3 -> x2, Pallas kernels: 5.09 us -> 3.24 us  [the longest x1 2.71 us: body(): pl.pallas_call(feature_kernel, in_specs=[SMEM] + [HBM] * 8, out_specs=[VM...]
    pallas_call x2 -> x1, Pallas kernels: 0.05 us -> 1.01 us  [pack(): pl.pallas_call(pack_kernel, in_specs=[VMEM] * (len(arrays) + 1), out_spec...]
  transfers between devices with their start and end apart: 19 -> 22, of which waited for: 10 -> 13; matrix products, arithmetic and copies ran while one was open for 0% -> 0% of each run, Pallas kernels for 5% -> 5%
where the time goes in v9:
time: 59.5 us; the launch traced here: 59.3 us
  starting transfers between devices  26.1 us (44%)
  waiting for transfers between devices  22.4 us (38%)
  Pallas kernels  9.29 us (16%)
  between operations  0.75 us (1%)
  local copies, waits for them, and re-layouts  0.63 us (1%)
    ppermute x22, starting transfers between devices, swap(): return lax.ppermute(array, 'fa', [(i, i ^ mask) for i in range(size)])  26.1 us
    ppermute x22, waiting for transfers between devices, swap(): return lax.ppermute(array, 'fa', [(i, i ^ mask) for i in range(size)])  22.4 us
    pallas_call x1, Pallas kernels, body(): pl.pallas_call(functools.partial(pair_kernel, rows=rows, total=total), in...  3.9 us
    pallas_call x1, Pallas kernels, body(): pl.pallas_call(feature_kernel, in_specs=[SMEM] + [HBM] * 8, out_specs=[VM...  2.71 us
  transfers between devices with their start and end apart: 22, of which 13 were waited for; matrix products, arithmetic and copies ran while one was open for 0% of the time, Pallas kernels for 5%

profile of v9, /device:TPU:0, one launch (start us, length us, event | category | flops | bytes accessed | tf_op | source)
XLA Modules:
  0.0 59.3 jit_solution(15296052466178802427)
XLA Ops:
  0.6 4.1 %collective-permute-start.2 = (bf16[128,256]{1,0:T(8,128)(2,1)}, bf16[128,256]{1,0:T(8,128)(2,1)S(1)}, u32[]{:S(2)}, u32[]{:S(2)}) collective-permute-start(bf16[128,256]{1,0:T(8,128)(2,1)} %refs_0_.1), channel_id=1, source_target_pairs={{0,8},{1,9},{2,10},{3,11},{4,12},{5,13},{6,14},{7,15},{8,0},{9,1},... | collective-permute-start | bytes 196616 | tf_op jit(solution)/shard_map/ppermute | solution.py:37
  4.7 1.3 %collective-permute-start.1 = (bf16[128,256]{1,0:T(8,128)(2,1)}, bf16[128,256]{1,0:T(8,128)(2,1)S(1)}, u32[]{:S(2)}, u32[]{:S(2)}) collective-permute-start(bf16[128,256]{1,0:T(8,128)(2,1)} %refs_0_.1), channel_id=1, source_target_pairs={{0,12},{1,13},{2,14},{3,15},{4,8},{5,9},{6,10},{7,11},{8,4},{9,5},... | collective-permute-start | bytes 196616 | tf_op jit(solution)/shard_map/ppermute | solution.py:37
  6.1 0.2 collective-permute-start.3
  6.3 0.0 copy-start.2
  6.3 2.7 %shard_map.112 = (bf16[528,256]{1,0:T(8,128)(2,1)}, bf16[256,256]{1,0:T(8,128)(2,1)}, bf16[256,256]{1,0:T(8,128)(2,1)}) custom-call(s32[1]{0:T(128)} %bitcast.1.core_ref, bf16[128,1024]{1,0:T(8,128)(2,1)} %hf_hbm.1, bf16[128,1024]{1,0:T(8,128)(2,1)} %ht_hbm.1, bf16[1024,256]{1,0:T(8,128)(2,1)} %wf_hbm.1, bf16[1024,256]{1,0:T(8,128)(2,1)} %wt_hbm.1, ...), custom_call_target="tpu_custom_call" | custom-call | tf_op jit(solution)/shard_map/pallas_call | solution.py:348
  9.0 0.0 collective-permute-done.2.refs_2_
  9.0 2.1 %collective-permute-done.1.refs_1_ = bf16[128,256]{1,0:T(8,128)(2,1)S(1)} collective-permute-done((bf16[128,256]{1,0:T(8,128)(2,1)}, bf16[128,256]{1,0:T(8,128)(2,1)S(1)}, u32[]{:S(2)}, u32[]{:S(2)}) %collective-permute-start.1) | collective-permute-done | bytes 65568 | tf_op jit(solution)/shard_map/ppermute | solution.py:37
  11.2 0.1 collective-permute-done.3.refs_3_
  11.3 0.0 copy-done.2
  11.3 0.0 copy-start
  11.3 0.0 copy-start.1
  11.3 1.0 %shard_map.113.refs_4_ = bf16[512,256]{1,0:T(8,128)(2,1)S(1)} custom-call(bf16[128,256]{1,0:T(8,128)(2,1)S(1)} %copy-done.2, bf16[128,256]{1,0:T(8,128)(2,1)S(1)} %collective-permute-done.1.refs_1_, bf16[128,256]{1,0:T(8,128)(2,1)S(1)} %collective-permute-done.2.refs_2_, bf16[128,256]{1,0:T(8,128)(2,1)S(1)} %collective-permute-done.3.refs_3_, ...), custom_call_target="tpu_custom_call" | custom-call | tf_op jit(solution)/shard_map/pallas_call | solution.py:133
  12.3 1.6 %collective-permute-start.4 = (bf16[512,256]{1,0:T(8,128)(2,1)S(1)}, bf16[512,256]{1,0:T(8,128)(2,1)S(1)}, u32[]{:S(2)}, u32[]{:S(2)}) collective-permute-start(bf16[512,256]{1,0:T(8,128)(2,1)S(1)} %shard_map.113.refs_4_), channel_id=1, source_target_pairs={{0,2},{1,3},{2,0},{3,1},{4,6},{5,7},{6,4},{7,5},{8,10},{9,11},{10,... | collective-permute-start | bytes 786440 | tf_op jit(solution)/shard_map/ppermute | solution.py:37
  13.9 0.0 collective-permute-start
  13.9 0.5 collective-permute-start.5
  14.4 4.5 %collective-permute-done.4.refs_5_ = bf16[512,256]{1,0:T(8,128)(2,1)S(1)} collective-permute-done((bf16[512,256]{1,0:T(8,128)(2,1)S(1)}, bf16[512,256]{1,0:T(8,128)(2,1)S(1)}, u32[]{:S(2)}, u32[]{:S(2)}) %collective-permute-start.4) | collective-permute-done | bytes 262176 | tf_op jit(solution)/shard_map/ppermute | solution.py:37
  18.9 0.0 collective-permute-start.6
  18.9 0.0 copy-start.3
  18.9 0.1 pad_add_fusion.refs_1_
  19.0 0.6 copy-done.3
  19.6 0.0 collective-permute-done.refs_3_
  19.6 0.0 collective-permute-done.5.refs_6_
  19.6 0.9 %collective-permute-done.6.refs_7_ = bf16[512,256]{1,0:T(8,128)(2,1)S(1)} collective-permute-done((bf16[512,256]{1,0:T(8,128)(2,1)S(1)}, bf16[512,256]{1,0:T(8,128)(2,1)S(1)}, u32[]{:S(2)}, u32[]{:S(2)}) %collective-permute-start.6) | collective-permute-done | bytes 262176 | tf_op jit(solution)/shard_map/ppermute | solution.py:37
  20.5 0.0 copy-done
  20.5 0.0 copy-done.1
  20.5 3.9 %shard_map.114 = (f32[96,256]{1,0:T(8,128)S(1)}, bf16[96,256]{1,0:T(8,128)(2,1)S(1)}, bf16[96,256]{1,0:T(8,128)(2,1)S(1)}, bf16[96,256]{1,0:T(8,128)(2,1)S(1)}, ...) custom-call(s32[16]{0:T(128)S(1)} %xor_multiply_fusion.refs_0_, ...), custom_call_target="tpu_custom_call" | custom-call | tf_op jit(solution)/shard_map/pallas_call | solution.py:394
  24.4 4.8 %collective-permute-start.7 = (bf16[96,256]{1,0:T(8,128)(2,1)S(1)}, bf16[96,256]{1,0:T(8,128)(2,1)S(1)}, u32[]{:S(2)}, u32[]{:S(2)}) collective-permute-start(bf16[96,256]{1,0:T(8,128)(2,1)S(1)} %get-tuple-element.22), channel_id=1, source_target_pairs={{0,14},{1,15},{2,12},{3,13},{4,10},{5,11},{6,8},{7,9},{8,6},{9,7},... | collective-permute-start | bytes 147464 | tf_op jit(solution)/shard_map/ppermute | solution.py:37
  29.2 0.3 collective-permute-start.8
  29.4 2.0 %collective-permute-start.9 = (bf16[96,256]{1,0:T(8,128)(2,1)S(1)}, bf16[96,256]{1,0:T(8,128)(2,1)S(1)}, u32[]{:S(2)}, u32[]{:S(2)}) collective-permute-start(bf16[96,256]{1,0:T(8,128)(2,1)S(1)} %get-tuple-element.24), channel_id=1, source_target_pairs={{0,10},{1,11},{2,8},{3,9},{4,14},{5,15},{6,12},{7,13},{8,2},{9,3},... | collective-permute-start | bytes 147464 | tf_op jit(solution)/shard_map/ppermute | solution.py:37
  31.4 0.8 %collective-permute-start.10 = (bf16[96,256]{1,0:T(8,128)(2,1)S(1)}, bf16[96,256]{1,0:T(8,128)(2,1)S(1)}, u32[]{:S(2)}, u32[]{:S(2)}) collective-permute-start(bf16[96,256]{1,0:T(8,128)(2,1)S(1)} %get-tuple-element.25), channel_id=1, source_target_pairs={{0,8},{1,9},{2,10},{3,11},{4,12},{5,13},{6,14},{7,15},{8,0},{9,1},... | collective-permute-start | bytes 147464 | tf_op jit(solution)/shard_map/ppermute | solution.py:37
  32.2 2.3 %collective-permute-start.11 = (bf16[96,256]{1,0:T(8,128)(2,1)S(1)}, bf16[96,256]{1,0:T(8,128)(2,1)S(1)}, u32[]{:S(2)}, u32[]{:S(2)}) collective-permute-start(bf16[96,256]{1,0:T(8,128)(2,1)S(1)} %get-tuple-element.26), channel_id=1, source_target_pairs={{0,6},{1,7},{2,4},{3,5},{4,2},{5,3},{6,0},{7,1},{8,14},{9,15},{10,... | collective-permute-start | bytes 147464 | tf_op jit(solution)/shard_map/ppermute | solution.py:37
  34.4 0.0 collective-permute-done.7.refs_0_
  34.4 1.8 %collective-permute-start.12 = (bf16[96,256]{1,0:T(8,128)(2,1)S(1)}, bf16[96,256]{1,0:T(8,128)(2,1)S(1)}, u32[]{:S(2)}, u32[]{:S(2)}) collective-permute-start(bf16[96,256]{1,0:T(8,128)(2,1)S(1)} %get-tuple-element.27), channel_id=1, source_target_pairs={{0,4},{1,5},{2,6},{3,7},{4,0},{5,1},{6,2},{7,3},{8,12},{9,13},{10,... | collective-permute-start | bytes 147464 | tf_op jit(solution)/shard_map/ppermute | solution.py:37
  36.2 0.0 collective-permute-done.8.refs_1_
  36.2 0.0 collective-permute-start.13
  36.2 0.6 %collective-permute-done.9.refs_2_ = bf16[96,256]{1,0:T(8,128)(2,1)S(1)} collective-permute-done((bf16[96,256]{1,0:T(8,128)(2,1)S(1)}, bf16[96,256]{1,0:T(8,128)(2,1)S(1)}, u32[]{:S(2)}, u32[]{:S(2)}) %collective-permute-start.9) | collective-permute-done | bytes 49184 | tf_op jit(solution)/shard_map/ppermute | solution.py:37
  36.8 1.6 %collective-permute-done.10.refs_3_ = bf16[96,256]{1,0:T(8,128)(2,1)S(1)} collective-permute-done((bf16[96,256]{1,0:T(8,128)(2,1)S(1)}, bf16[96,256]{1,0:T(8,128)(2,1)S(1)}, u32[]{:S(2)}, u32[]{:S(2)}) %collective-permute-start.10) | collective-permute-done | bytes 49184 | tf_op jit(solution)/shard_map/ppermute | solution.py:37
  38.4 0.3 collective-permute-done.11.refs_4_
  38.7 0.4 collective-permute-done.12.refs_5_
  39.2 1.1 %collective-permute-done.13.refs_6_ = bf16[96,256]{1,0:T(8,128)(2,1)S(1)} collective-permute-done((bf16[96,256]{1,0:T(8,128)(2,1)S(1)}, bf16[96,256]{1,0:T(8,128)(2,1)S(1)}, u32[]{:S(2)}, u32[]{:S(2)}) %collective-permute-start.13) | collective-permute-done | bytes 49184 | tf_op jit(solution)/shard_map/ppermute | solution.py:37
  40.3 0.5 shard_map.115
  40.8 0.2 collective-permute-start.17
  41.0 1.2 %collective-permute-start.16 = (bf16[1,80,256]{2,1,0:T(8,128)(2,1)S(1)}, bf16[1,80,256]{2,1,0:T(8,128)(2,1)S(1)}, u32[]{:S(2)}, u32[]{:S(2)}) collective-permute-start(bf16[1,80,256]{2,1,0:T(8,128)(2,1)S(1)} %bitcast.9), channel_id=1, source_target_pairs={{0,4},{1,5},{2,6},{3,7},{4,0},{5,1},{6,2},{7,3},{8,12},{9,13},{10,... | collective-permute-start | bytes 122888 | tf_op jit(solution)/shard_map/ppermute | solution.py:37
  42.2 4.4 %collective-permute-start.15 = (bf16[1,80,256]{2,1,0:T(8,128)(2,1)S(1)}, bf16[1,80,256]{2,1,0:T(8,128)(2,1)S(1)}, u32[]{:S(2)}, u32[]{:S(2)}) collective-permute-start(bf16[1,80,256]{2,1,0:T(8,128)(2,1)S(1)} %bitcast.10), channel_id=1, source_target_pairs={{0,8},{1,9},{2,10},{3,11},{4,12},{5,13},{6,14},{7,15},{8,0},{9,1},... | collective-permute-start | bytes 122888 | tf_op jit(solution)/shard_map/ppermute | solution.py:37
  46.6 0.0 collective-permute-start.14
  46.6 0.0 collective-permute-done.16
  46.6 0.7 %collective-permute-start.20 = (bf16[1,80,256]{2,1,0:T(8,128)(2,1)S(1)}, bf16[1,80,256]{2,1,0:T(8,128)(2,1)S(1)}, u32[]{:S(2)}, u32[]{:S(2)}) collective-permute-start(bf16[1,80,256]{2,1,0:T(8,128)(2,1)S(1)} %collective-permute-done.16), channel_id=1, source_target_pairs={{0,2},{1,3},{2,0},{3,1},{4,6},{5,7},{6,4},{7,5},{8,10},{9,11},{10,... | collective-permute-start | bytes 122888 | tf_op jit(solution)/shard_map/ppermute | solution.py:37
  47.3 1.6 %collective-permute-done.15 = bf16[1,80,256]{2,1,0:T(8,128)(2,1)S(1)} collective-permute-done((bf16[1,80,256]{2,1,0:T(8,128)(2,1)S(1)}, bf16[1,80,256]{2,1,0:T(8,128)(2,1)S(1)}, u32[]{:S(2)}, u32[]{:S(2)}) %collective-permute-start.15) | collective-permute-done | bytes 40992 | tf_op jit(solution)/shard_map/ppermute | solution.py:37
  48.9 0.0 collective-permute-start.19
  48.9 3.5 %collective-permute-done.14 = bf16[1,80,256]{2,1,0:T(8,128)(2,1)S(1)} collective-permute-done((bf16[1,80,256]{2,1,0:T(8,128)(2,1)S(1)}, bf16[1,80,256]{2,1,0:T(8,128)(2,1)S(1)}, u32[]{:S(2)}, u32[]{:S(2)}) %collective-permute-start.14) | collective-permute-done | bytes 40992 | tf_op jit(solution)/shard_map/ppermute | solution.py:37
  52.4 0.0 collective-permute-start.18
  52.4 0.0 collective-permute-done.17
  52.4 3.9 %collective-permute-done.18 = bf16[1,80,256]{2,1,0:T(8,128)(2,1)S(1)} collective-permute-done((bf16[1,80,256]{2,1,0:T(8,128)(2,1)S(1)}, bf16[1,80,256]{2,1,0:T(8,128)(2,1)S(1)}, u32[]{:S(2)}, u32[]{:S(2)}) %collective-permute-start.18) | collective-permute-done | bytes 40992 | tf_op jit(solution)/shard_map/ppermute | solution.py:37
  56.4 0.0 collective-permute-done.19
  56.4 0.0 collective-permute-done.20
  56.4 0.1 collective-permute-start.21
  56.5 1.6 %collective-permute-done.21.refs_1_ = bf16[8,80,256]{2,1,0:T(8,128)(2,1)S(1)} collective-permute-done((bf16[8,80,256]{2,1,0:T(8,128)(2,1)S(1)}, bf16[8,80,256]{2,1,0:T(8,128)(2,1)S(1)}, u32[]{:S(2)}, u32[]{:S(2)}) %collective-permute-start.21) | collective-permute-done | bytes 327712 | tf_op jit(solution)/shard_map/ppermute | solution.py:37
  58.1 1.1 %shard_map.116 = (f32[1024,256]{1,0:T(8,128)}, f32[256,256]{1,0:T(8,128)}) custom-call(s32[1]{0:T(128)} %bitcast.place_ref, bf16[8,80,256]{2,1,0:T(8,128)(2,1)S(1)} %constant_dynamic-update-slice_fusion.refs_0_, bf16[8,80,256]{2,1,0:T(8,128)(2,1)S(1)} %collective-permute-done.21.refs_1_), custom_call_target="tpu_custom_call" | custom-call | tf_op jit(solution)/shard_map/pallas_call | solution.py:432
  (9 shorter events, 0.0 us)
Async XLA Ops:
  0.6 8.4 %collective-permute-start.2 = (bf16[128,256]{1,0:T(8,128)(2,1)}, bf16[128,256]{1,0:T(8,128)(2,1)S(1)}, u32[]{:S(2)}, u32[]{:S(2)}) collective-permute-start(bf16[128,256]{1,0:T(8,128)(2,1)} %refs_0_.1), channel_id=1, source_target_pairs={{0,8},{1,9},{2,10},{3,11},{4,12},{5,13},{6,14},{7,15},{8,0},{9,1},... | collective-permute-start | bytes 196616 | tf_op jit(solution)/shard_map/ppermute | solution.py:37
  4.7 6.4 %collective-permute-start.1 = (bf16[128,256]{1,0:T(8,128)(2,1)}, bf16[128,256]{1,0:T(8,128)(2,1)S(1)}, u32[]{:S(2)}, u32[]{:S(2)}) collective-permute-start(bf16[128,256]{1,0:T(8,128)(2,1)} %refs_0_.1), channel_id=1, source_target_pairs={{0,12},{1,13},{2,14},{3,15},{4,8},{5,9},{6,10},{7,11},{8,4},{9,5},... | collective-permute-start | bytes 196616 | tf_op jit(solution)/shard_map/ppermute | solution.py:37
  6.1 5.2 %collective-permute-start.3 = (bf16[128,256]{1,0:T(8,128)(2,1)}, bf16[128,256]{1,0:T(8,128)(2,1)S(1)}, u32[]{:S(2)}, u32[]{:S(2)}) collective-permute-start(bf16[128,256]{1,0:T(8,128)(2,1)} %refs_0_.1), channel_id=1, source_target_pairs={{0,4},{1,5},{2,6},{3,7},{4,0},{5,1},{6,2},{7,3},{8,12},{9,13},{10,... | collective-permute-start | bytes 196616 | tf_op jit(solution)/shard_map/ppermute | solution.py:37
  6.3 5.0 %copy-start.2 = (bf16[128,256]{1,0:T(8,128)(2,1)S(1)}, bf16[128,256]{1,0:T(8,128)(2,1)}, u32[]{:S(2)}) copy-start(bf16[128,256]{1,0:T(8,128)(2,1)} %refs_0_.1) | copy-start | bytes 196612
  11.3 9.2 %copy-start = (bf16[256,256]{1,0:T(8,128)(2,1)S(1)}, bf16[256,256]{1,0:T(8,128)(2,1)}, u32[]{:S(2)}) copy-start(bf16[256,256]{1,0:T(8,128)(2,1)} %get-tuple-element.19.refs_8_) | copy-start | bytes 393220
  11.3 9.2 %copy-start.1 = (bf16[256,256]{1,0:T(8,128)(2,1)S(1)}, bf16[256,256]{1,0:T(8,128)(2,1)}, u32[]{:S(2)}) copy-start(bf16[256,256]{1,0:T(8,128)(2,1)} %get-tuple-element.20.refs_9_) | copy-start | bytes 393220
  12.3 6.6 %collective-permute-start.4 = (bf16[512,256]{1,0:T(8,128)(2,1)S(1)}, bf16[512,256]{1,0:T(8,128)(2,1)S(1)}, u32[]{:S(2)}, u32[]{:S(2)}) collective-permute-start(bf16[512,256]{1,0:T(8,128)(2,1)S(1)} %shard_map.113.refs_4_), channel_id=1, source_target_pairs={{0,2},{1,3},{2,0},{3,1},{4,6},{5,7},{6,4},{7,5},{8,10},{9,11},{10,... | collective-permute-start | bytes 786440 | tf_op jit(solution)/shard_map/ppermute | solution.py:37
  13.9 5.7 %collective-permute-start = (bf16[528,256]{1,0:T(8,128)(2,1)}, bf16[528,256]{1,0:T(8,128)(2,1)S(1)}, u32[]{:S(2)}, u32[]{:S(2)}) collective-permute-start(bf16[528,256]{1,0:T(8,128)(2,1)} %get-tuple-element.18.refs_4_.refs_2_), channel_id=1, source_target_pairs={{0,1},{1,0},{2,3},{3,2},{4,5},{5,4},{6,7},{7,6},{8,9},{9,8},{10,11... | collective-permute-start | bytes 811016 | tf_op jit(solution)/shard_map/ppermute | solution.py:37
  13.9 5.7 %collective-permute-start.5 = (bf16[512,256]{1,0:T(8,128)(2,1)S(1)}, bf16[512,256]{1,0:T(8,128)(2,1)S(1)}, u32[]{:S(2)}, u32[]{:S(2)}) collective-permute-start(bf16[512,256]{1,0:T(8,128)(2,1)S(1)} %shard_map.113.refs_4_), channel_id=1, source_target_pairs={{0,1},{1,0},{2,3},{3,2},{4,5},{5,4},{6,7},{7,6},{8,9},{9,8},{10,11... | collective-permute-start | bytes 786440 | tf_op jit(solution)/shard_map/ppermute | solution.py:37
  18.9 1.5 %collective-permute-start.6 = (bf16[512,256]{1,0:T(8,128)(2,1)S(1)}, bf16[512,256]{1,0:T(8,128)(2,1)S(1)}, u32[]{:S(2)}, u32[]{:S(2)}) collective-permute-start(bf16[512,256]{1,0:T(8,128)(2,1)S(1)} %collective-permute-done.4.refs_5_), channel_id=1, source_target_pairs={{0,1},{1,0},{2,3},{3,2},{4,5},{5,4},{6,7},{7,6},{8,9},{9,8},{10,11... | collective-permute-start | bytes 786440 | tf_op jit(solution)/shard_map/ppermute | solution.py:37
  18.9 0.7 %copy-start.3 = (s32[16]{0:T(128)S(1)}, s32[16]{0:T(128)}, u32[]{:S(2)}) copy-start(s32[16]{0:T(128)} %constant.24.clone.1) | copy-start | bytes 196
  24.4 10.1 %collective-permute-start.7 = (bf16[96,256]{1,0:T(8,128)(2,1)S(1)}, bf16[96,256]{1,0:T(8,128)(2,1)S(1)}, u32[]{:S(2)}, u32[]{:S(2)}) collective-permute-start(bf16[96,256]{1,0:T(8,128)(2,1)S(1)} %get-tuple-element.22), channel_id=1, source_target_pairs={{0,14},{1,15},{2,12},{3,13},{4,10},{5,11},{6,8},{7,9},{8,6},{9,7},... | collective-permute-start | bytes 147464 | tf_op jit(solution)/shard_map/ppermute | solution.py:37
  29.2 7.1 %collective-permute-start.8 = (bf16[96,256]{1,0:T(8,128)(2,1)S(1)}, bf16[96,256]{1,0:T(8,128)(2,1)S(1)}, u32[]{:S(2)}, u32[]{:S(2)}) collective-permute-start(bf16[96,256]{1,0:T(8,128)(2,1)S(1)} %get-tuple-element.23), channel_id=1, source_target_pairs={{0,12},{1,13},{2,14},{3,15},{4,8},{5,9},{6,10},{7,11},{8,4},{9,5},... | collective-permute-start | bytes 147464 | tf_op jit(solution)/shard_map/ppermute | solution.py:37
  29.4 7.4 %collective-permute-start.9 = (bf16[96,256]{1,0:T(8,128)(2,1)S(1)}, bf16[96,256]{1,0:T(8,128)(2,1)S(1)}, u32[]{:S(2)}, u32[]{:S(2)}) collective-permute-start(bf16[96,256]{1,0:T(8,128)(2,1)S(1)} %get-tuple-element.24), channel_id=1, source_target_pairs={{0,10},{1,11},{2,8},{3,9},{4,14},{5,15},{6,12},{7,13},{8,2},{9,3},... | collective-permute-start | bytes 147464 | tf_op jit(solution)/shard_map/ppermute | solution.py:37
  31.4 7.0 %collective-permute-start.10 = (bf16[96,256]{1,0:T(8,128)(2,1)S(1)}, bf16[96,256]{1,0:T(8,128)(2,1)S(1)}, u32[]{:S(2)}, u32[]{:S(2)}) collective-permute-start(bf16[96,256]{1,0:T(8,128)(2,1)S(1)} %get-tuple-element.25), channel_id=1, source_target_pairs={{0,8},{1,9},{2,10},{3,11},{4,12},{5,13},{6,14},{7,15},{8,0},{9,1},... | collective-permute-start | bytes 147464 | tf_op jit(solution)/shard_map/ppermute | solution.py:37
  32.2 6.6 %collective-permute-start.11 = (bf16[96,256]{1,0:T(8,128)(2,1)S(1)}, bf16[96,256]{1,0:T(8,128)(2,1)S(1)}, u32[]{:S(2)}, u32[]{:S(2)}) collective-permute-start(bf16[96,256]{1,0:T(8,128)(2,1)S(1)} %get-tuple-element.26), channel_id=1, source_target_pairs={{0,6},{1,7},{2,4},{3,5},{4,2},{5,3},{6,0},{7,1},{8,14},{9,15},{10,... | collective-permute-start | bytes 147464 | tf_op jit(solution)/shard_map/ppermute | solution.py:37
  34.4 4.7 %collective-permute-start.12 = (bf16[96,256]{1,0:T(8,128)(2,1)S(1)}, bf16[96,256]{1,0:T(8,128)(2,1)S(1)}, u32[]{:S(2)}, u32[]{:S(2)}) collective-permute-start(bf16[96,256]{1,0:T(8,128)(2,1)S(1)} %get-tuple-element.27), channel_id=1, source_target_pairs={{0,4},{1,5},{2,6},{3,7},{4,0},{5,1},{6,2},{7,3},{8,12},{9,13},{10,... | collective-permute-start | bytes 147464 | tf_op jit(solution)/shard_map/ppermute | solution.py:37
  36.2 4.1 %collective-permute-start.13 = (bf16[96,256]{1,0:T(8,128)(2,1)S(1)}, bf16[96,256]{1,0:T(8,128)(2,1)S(1)}, u32[]{:S(2)}, u32[]{:S(2)}) collective-permute-start(bf16[96,256]{1,0:T(8,128)(2,1)S(1)} %get-tuple-element.28), channel_id=1, source_target_pairs={{0,2},{1,3},{2,0},{3,1},{4,6},{5,7},{6,4},{7,5},{8,10},{9,11},{10,... | collective-permute-start | bytes 147464 | tf_op jit(solution)/shard_map/ppermute | solution.py:37
  40.8 11.6 %collective-permute-start.17 = (bf16[1,80,256]{2,1,0:T(8,128)(2,1)S(1)}, bf16[1,80,256]{2,1,0:T(8,128)(2,1)S(1)}, u32[]{:S(2)}, u32[]{:S(2)}) collective-permute-start(bf16[1,80,256]{2,1,0:T(8,128)(2,1)S(1)} %bitcast.8), channel_id=1, source_target_pairs={{0,2},{1,3},{2,0},{3,1},{4,6},{5,7},{6,4},{7,5},{8,10},{9,11},{10,... | collective-permute-start | bytes 122888 | tf_op jit(solution)/shard_map/ppermute | solution.py:37
  41.0 5.6 %collective-permute-start.16 = (bf16[1,80,256]{2,1,0:T(8,128)(2,1)S(1)}, bf16[1,80,256]{2,1,0:T(8,128)(2,1)S(1)}, u32[]{:S(2)}, u32[]{:S(2)}) collective-permute-start(bf16[1,80,256]{2,1,0:T(8,128)(2,1)S(1)} %bitcast.9), channel_id=1, source_target_pairs={{0,4},{1,5},{2,6},{3,7},{4,0},{5,1},{6,2},{7,3},{8,12},{9,13},{10,... | collective-permute-start | bytes 122888 | tf_op jit(solution)/shard_map/ppermute | solution.py:37
  42.2 6.6 %collective-permute-start.15 = (bf16[1,80,256]{2,1,0:T(8,128)(2,1)S(1)}, bf16[1,80,256]{2,1,0:T(8,128)(2,1)S(1)}, u32[]{:S(2)}, u32[]{:S(2)}) collective-permute-start(bf16[1,80,256]{2,1,0:T(8,128)(2,1)S(1)} %bitcast.10), channel_id=1, source_target_pairs={{0,8},{1,9},{2,10},{3,11},{4,12},{5,13},{6,14},{7,15},{8,0},{9,1},... | collective-permute-start | bytes 122888 | tf_op jit(solution)/shard_map/ppermute | solution.py:37
  46.6 5.8 %collective-permute-start.14 = (bf16[1,80,256]{2,1,0:T(8,128)(2,1)S(1)}, bf16[1,80,256]{2,1,0:T(8,128)(2,1)S(1)}, u32[]{:S(2)}, u32[]{:S(2)}) collective-permute-start(bf16[1,80,256]{2,1,0:T(8,128)(2,1)S(1)} %bitcast.11), channel_id=1, source_target_pairs={{0,12},{1,13},{2,14},{3,15},{4,8},{5,9},{6,10},{7,11},{8,4},{9,5},... | collective-permute-start | bytes 122888 | tf_op jit(solution)/shard_map/ppermute | solution.py:37
  46.6 9.8 %collective-permute-start.20 = (bf16[1,80,256]{2,1,0:T(8,128)(2,1)S(1)}, bf16[1,80,256]{2,1,0:T(8,128)(2,1)S(1)}, u32[]{:S(2)}, u32[]{:S(2)}) collective-permute-start(bf16[1,80,256]{2,1,0:T(8,128)(2,1)S(1)} %collective-permute-done.16), channel_id=1, source_target_pairs={{0,2},{1,3},{2,0},{3,1},{4,6},{5,7},{6,4},{7,5},{8,10},{9,11},{10,... | collective-permute-start | bytes 122888 | tf_op jit(solution)/shard_map/ppermute | solution.py:37
  48.9 7.5 %collective-permute-start.19 = (bf16[1,80,256]{2,1,0:T(8,128)(2,1)S(1)}, bf16[1,80,256]{2,1,0:T(8,128)(2,1)S(1)}, u32[]{:S(2)}, u32[]{:S(2)}) collective-permute-start(bf16[1,80,256]{2,1,0:T(8,128)(2,1)S(1)} %collective-permute-done.15), channel_id=1, source_target_pairs={{0,2},{1,3},{2,0},{3,1},{4,6},{5,7},{6,4},{7,5},{8,10},{9,11},{10,... | collective-permute-start | bytes 122888 | tf_op jit(solution)/shard_map/ppermute | solution.py:37
  52.4 4.0 %collective-permute-start.18 = (bf16[1,80,256]{2,1,0:T(8,128)(2,1)S(1)}, bf16[1,80,256]{2,1,0:T(8,128)(2,1)S(1)}, u32[]{:S(2)}, u32[]{:S(2)}) collective-permute-start(bf16[1,80,256]{2,1,0:T(8,128)(2,1)S(1)} %collective-permute-done.14), channel_id=1, source_target_pairs={{0,2},{1,3},{2,0},{3,1},{4,6},{5,7},{6,4},{7,5},{8,10},{9,11},{10,... | collective-permute-start | bytes 122888 | tf_op jit(solution)/shard_map/ppermute | solution.py:37
  56.4 1.7 %collective-permute-start.21 = (bf16[8,80,256]{2,1,0:T(8,128)(2,1)S(1)}, bf16[8,80,256]{2,1,0:T(8,128)(2,1)S(1)}, u32[]{:S(2)}, u32[]{:S(2)}) collective-permute-start(bf16[8,80,256]{2,1,0:T(8,128)(2,1)S(1)} %constant_dynamic-update-slice_fusion.refs_0_), channel_id=1, source_target_pairs={{0,1},{1,0},{2,3},{3,2},{4,5},{5,4},{6,7},{7,6},{8,9},{9,8},{10,11... | collective-permute-start | bytes 983048 | tf_op jit(solution)/shard_map/ppermute | solution.py:37

commit v10 on v9

--- a/solution.py
+++ b/solution.py
@@ -13,10 +13,12 @@
 EPS = 1e-06
 BF = jnp.bfloat16
 F32 = jnp.float32
-FEAT_AT = 2
+GROUP = (0, 2, 1, 3)
+CUT_AT = (0, 0, 0, 1)
+HEAD_AT = (1, 2, 1, 2)
+FEAT_AT = (2, 3, 2, 3)
 PAD = 16
 LINE = ((12, 3), (8, 1), (4, 2))
-OTHERS = ((14, 7), (12, 3), (10, 5), (8, 1), (6, 6), (4, 2), (2, 4))
 TURNS = (0, 3, 1, 2, 4, 7, 5, 6)
 
 
@@ -49,17 +51,20 @@
 
 
 def feature_kernel(
-    core_ref,
+    me_ref,
     hf_hbm,
     ht_hbm,
+    hb_hbm,
     wf_hbm,
     wt_hbm,
     wb_hbm,
     lat_hbm,
     ids_hbm,
     pos_hbm,
+    far_ref,
     near_ref,
     cut_ref,
+    head_ref,
     wb_ref,
     hf,
     ht,
@@ -83,6 +88,7 @@
                 (wf_hbm, wf),
                 (ht_hbm, ht),
                 (wt_hbm, wt),
+                (hb_hbm, head_ref),
                 (wb_hbm, wb_ref),
             )
         )
@@ -104,22 +110,29 @@
     coded = jnp.where(line == 0, high, jnp.where(line == 1, low, 0.0)).astype(BF)
     coded = jnp.concatenate([coded] + [jnp.zeros((PAD, width - rows), BF)] * (width > rows), axis=1)
 
+    def piece(slot):
+        other = me_ref[0] ^ GROUP[slot]
+        quarter = (other & 1) * 2 + ((other >> 1) & 1)
+        return hf[:, pl.ds(pl.multiple_of(quarter * width, width), width)]
+
     moves[3].wait()
-    core = core_ref[0]
-    for t in range(2):
-        for ref, half in ((cut_ref, core), (near_ref, 1 - core)):
-            ref[t * rows : (t + 1) * rows, :] = hf[
-                :, pl.ds(pl.multiple_of((half * 2 + t) * width, width), width)
-            ]
+    cut_ref[...] = piece(0)
+    far_ref[:rows, :] = piece(1)
+    near_ref[:rows, :] = piece(2)
+    far_ref[rows : 2 * rows, :] = piece(3)
     moves[4].wait()
     feat = (dot(hf[...], wf[...]) + zrows).astype(BF)
     moves[5].wait()
     moves[6].wait()
     feat_t = (dot(ht[...], wt[...]) + zrows).astype(BF)
-    near_ref[FEAT_AT * rows : (FEAT_AT + 1) * rows, :] = feat
-    near_ref[(FEAT_AT + 1) * rows : (FEAT_AT + 2) * rows, :] = feat_t
-    near_ref[(FEAT_AT + 2) * rows :, :] = coded
     moves[7].wait()
+    head = head_ref[...]
+    for ref, at in ((far_ref, HEAD_AT[1]), (near_ref, HEAD_AT[2])):
+        ref[at * rows : (at + 1) * rows, :] = head
+        ref[(at + 1) * rows : (at + 2) * rows, :] = feat
+        ref[(at + 2) * rows : (at + 3) * rows, :] = feat_t
+        ref[(at + 3) * rows :, :] = coded
+    moves[8].wait()
 
 
 def pack_kernel(*refs):
@@ -140,30 +153,39 @@
 
 
 def pair_kernel(*refs, rows, total):
-    base_ref, place_ref = refs[:2]
-    nears, lines, cut_ref, wb_ref = refs[2:4], refs[4:8], refs[8], refs[9]
-    keep_ref, sends = refs[10], refs[11:18]
-    hid_ref, raw_ref, back_ref, mask_ref, smat_ref, pick_ref, own_ref, wfq_ref, wbq_ref = refs[18:]
+    me_ref = refs[0]
+    mails, lines, cut_ref, wb_ref = refs[1:5], refs[5:9], refs[9], refs[10]
+    keep_ref, sends = refs[11], refs[12:15]
+    hid_ref, raw_ref, back_ref, mask_ref, smat_ref, pick_ref, own_ref, wfq_ref, wbq_ref = refs[15:]
     width = wb_ref.shape[1]
     pairs = float(total * (total - 1))
-    groups = total // (2 * rows)
+    groups = total // (4 * rows)
     wb = wb_ref[...]
     end = 2 * rows + PAD
-    feats = [(ref, FEAT_AT * rows) for ref in nears]
-    cuts = ((cut_ref, 0), (nears[1], 0))
+    me = me_ref[0]
+    feats = [(ref, at * rows) for ref, at in zip(mails, FEAT_AT)]
+    cuts = [(ref, at * rows) for ref, at in zip((cut_ref,) + mails[1:], CUT_AT)]
     length = total // 4
-    for i, ref in enumerate(lines):
+    for i, (mail, line) in enumerate(zip(mails, lines)):
+        first, start = i * length, HEAD_AT[i] * rows
+        hid_ref[first : first + rows, :] = mail[start : start + rows, :]
         if length <= 8 * rows:
-            hid_ref[i * length : (i + 1) * length, :] = ref[...]
+            hid_ref[first + rows : first + length, :] = line[...]
         else:
 
-            def one(k, carry, ref=ref, first=i * length):
-                hid_ref[pl.ds(pl.multiple_of(first + k * rows, rows), rows), :] = ref[
+            def one(k, carry, line=line, first=first + rows):
+                hid_ref[pl.ds(pl.multiple_of(first + k * rows, rows), rows), :] = line[
                     pl.ds(pl.multiple_of(k * rows, rows), rows), :
                 ]
                 return carry
 
-            lax.fori_loop(0, length // rows, one, 0)
+            lax.fori_loop(0, length // rows - 1, one, 0)
+
+    def base(block):
+        per = total // (16 * rows)
+        way, along, within = block // (4 * per), (block // per) % 4, block % per
+        other = (way >> 1) | ((way & 1) << 1) | ((16 - 4 * along) & 15)
+        return (me ^ (other | (reverse_bits(within, per.bit_length() - 1) << 4))) * rows
 
     def embed(hidden):
         raw = dot(hidden, wb)
@@ -200,7 +222,7 @@
             raw_ref[here, :] = raw
             back_ref[here, :] = back
         for t in range(big // rows):
-            ids = (lanes + base_ref[step * (big // rows) + t]).astype(F32)
+            ids = (lanes + base(step * (big // rows) + t)).astype(F32)
             for g, want in enumerate(wanted):
                 mask_ref[g * rows : (g + 1) * rows, t * rows : (t + 1) * rows] = jnp.where(
                     want == ids, 1.0, 0.0
@@ -212,9 +234,10 @@
     over_rows(first_pass)
     smat = smat_ref[...]
     s_hi, s_lo = halves(smat)
-    core, mine = place_ref[0], place_ref[1]
+    place = reverse_bits(me & 15, 4)
+    quarter, mine = place >> 2, place & 3
     half = wbq_ref.shape[0]
-    columns = pl.ds(pl.multiple_of(core * half, half), half)
+    columns = pl.ds(pl.multiple_of((quarter >> 1) * half, half), half)
 
     def rows_of(places, offset):
         return jnp.concatenate([ref[at + offset : at + offset + rows, :] for ref, at in places], axis=0)
@@ -233,8 +256,7 @@
     coef = db * (1.0 / pairs) + 1.0 / total
     norm = jnp.sum(ob * ob, axis=-1, keepdims=True)
     grad_f = (ds * (1.0 / pairs) - coef * ob).astype(BF)
-    for t in range(2):
-        wfq_ref[t * width : (t + 1) * width, :] = dot_t(rows_of(cuts, t * rows), grad_f)
+    wfq_ref[...] = dot_t(rows_of(cuts, 0), grad_f)
     squares = jnp.sum(diff * ds) - jnp.sum(db * db)
     squares = squares + LAMBDA * (jnp.sum(smat * smat) / groups - jnp.sum(norm * norm))
     sums = squares / (2.0 * pairs) - (jnp.sum(f32feat * ob) + LAMBDA * jnp.sum(norm)) / total
@@ -255,14 +277,14 @@
         wbq_ref[...] += dot_t(hid_ref[here, columns], back_ref[here, :])
 
     over_rows(second_pass)
-    wf_rows = wfq_ref.shape[0] // 8
+    wf_rows = wfq_ref.shape[0] // 4
     wb_rows = wbq_ref.shape[0] // 8
     size = wf_rows + wb_rows
 
     def block(t):
         return (
             wfq_ref[pl.ds(pl.multiple_of(t * wf_rows, wf_rows), wf_rows), :],
-            wbq_ref[pl.ds(pl.multiple_of(t * wb_rows, wb_rows), wb_rows), :],
+            wbq_ref[pl.ds(pl.multiple_of(((quarter & 1) * 4 + t) * wb_rows, wb_rows), wb_rows), :],
         )
 
     keep_ref[:wf_rows, :], keep_ref[wf_rows:size, :] = block(mine)
@@ -276,7 +298,7 @@
         n_hi.astype(F32),
         jnp.where(line == 1, n_mid.astype(F32), jnp.where(line == 2, n_lo.astype(F32), 0.0)),
     ).astype(BF)
-    for ref, (_, turn) in zip(sends, OTHERS):
+    for ref, (_, turn) in zip(sends, LINE):
         part_f, part_b = block(mine ^ turn)
         ref[:wf_rows, :] = part_f.astype(BF)
         ref[wf_rows:size, :] = part_b.astype(BF)
@@ -284,11 +306,11 @@
 
 
 def add_kernel(keep_ref, *refs):
-    sum_ref, note_ref = refs[7:]
+    sum_ref, note_ref = refs[3:]
     size, width = sum_ref.shape
     total = keep_ref[:size, :]
     note = keep_ref[size : size + 1, :1]
-    for ref in refs[:7]:
+    for ref in refs[:3]:
         total = total + ref[:size, :].astype(F32)
         coded = ref[size:, :].astype(F32)
         note = note + (coded[0:1, :1] + coded[1:2, :1] + coded[2:3, :1])
@@ -296,22 +318,8 @@
     note_ref[...] = note * (1.0 / width)
 
 
-def assemble_kernel(place_ref, *refs, wf_rows, wb_rows, factor_f, factor_b):
-    place = place_ref[0]
-    wf_ref, wb_ref = refs[4:]
-    for offset, ref in zip((0, 4, 8, 12), refs):
-        for e, turn in enumerate((0,) + tuple(turn for _, turn in LINE)):
-            to = place ^ (offset + turn)
-            wf_ref[pl.ds(pl.multiple_of(to * wf_rows, wf_rows), wf_rows), :] = (
-                ref[e, :wf_rows, :].astype(F32) * factor_f
-            )
-            wb_ref[pl.ds(pl.multiple_of(to * wb_rows, wb_rows), wb_rows), :] = (
-                ref[e, wf_rows:, :].astype(F32) * factor_b
-            )
-
-
-def assemble_kernel(place_ref, *refs, wf_rows, wb_rows, factor_f, factor_b):
-    place = place_ref[0]
+def assemble_kernel(me_ref, *refs, wf_rows, wb_rows, factor_f, factor_b):
+    place = reverse_bits(me_ref[0] & 15, 4)
     wf_ref, wb_ref = refs[2:]
     for offset, ref in zip((0, 8), refs):
         for e, turn in enumerate(TURNS):
@@ -340,18 +348,17 @@
     total = size * rows
     assert bits >= 4 and size == 1 << bits and high // 4 == width == wide
 
-    head = hidden_b
-    for mask in reversed(beyond):
-        head = jnp.concatenate([head, swap(head, mask, size)], axis=0)
-    pieces = [swap(head, mask, size) for mask, _ in LINE]
-    core = (me & 1).astype(jnp.int32)
-    near, cut, wb_copy = pl.pallas_call(
+    me = me.astype(jnp.int32).reshape(1)
+    ends = [(at + 2) * rows + PAD for at in FEAT_AT]
+    far, near, cut, head, wb_copy = pl.pallas_call(
         feature_kernel,
-        in_specs=[SMEM] + [HBM] * 8,
-        out_specs=[VMEM] * 3,
+        in_specs=[SMEM] + [HBM] * 9,
+        out_specs=[VMEM] * 5,
         out_shape=[
-            jax.ShapeDtypeStruct(((FEAT_AT + 2) * rows + PAD, width), BF),
-            jax.ShapeDtypeStruct((2 * rows, width), BF),
+            jax.ShapeDtypeStruct((ends[1], width), BF),
+            jax.ShapeDtypeStruct((ends[2], width), BF),
+            jax.ShapeDtypeStruct((rows, width), BF),
+            jax.ShapeDtypeStruct(hidden_b.shape, BF),
             jax.ShapeDtypeStruct(w_b.shape, BF),
         ],
         scratch_shapes=[
@@ -362,13 +369,17 @@
             pltpu.VMEM(latents.shape, BF),
             pltpu.VMEM((1, rows), jnp.int32),
             pltpu.VMEM((1, rows), jnp.int32),
-            pltpu.SemaphoreType.DMA((8,)),
+            pltpu.SemaphoreType.DMA((9,)),
         ],
         compiler_params=pltpu.CompilerParams(vmem_limit_bytes=60 * 2**20),
+        cost_estimate=pl.CostEstimate(
+            flops=4 * rows * high * width, bytes_accessed=4 * high * (rows + width), transcendentals=0
+        ),
     )(
-        core.reshape(1),
+        me,
         hidden_f,
         hidden_t,
+        hidden_b,
         w_f,
         w_t,
         w_b,
@@ -376,45 +387,43 @@
         latent_ids.reshape(1, rows),
         positives.reshape(1, rows),
     )
+    for mask in reversed(beyond):
+        head = jnp.concatenate([head, swap(head, mask, size)], axis=0)
+    line = [head[rows:]] * (len(beyond) > 0) + [swap(head, mask, size) for mask, _ in LINE]
+    far2 = swap(far, 2, size)
+    line0 = pack(*line, after=far2)
+    line2 = swap(line0, 2, size)
     near1 = swap(near, 1, size)
-    line0 = pack(head, *pieces, after=near)
-    line2 = swap(line0, 2, size)
+    far3 = swap(far2, 1, size)
     line1 = swap(line0, 1, size)
     line3 = swap(line2, 1, size)
 
-    inner = reverse_bits(jnp.arange(size // 16, dtype=jnp.int32), bits - 4) << 4
-    bases = []
-    for way in (0, 2, 1, 3):
-        bases += [way ^ inner] + [way ^ mask ^ inner for mask, _ in LINE]
-    bases = ((me ^ jnp.concatenate(bases)) * rows).astype(jnp.int32)
-    place = reverse_bits(me & 15, 4).astype(jnp.int32)
-    places = jnp.stack([core, place & 7])
     wf_rows, wb_rows = high // 16, wide // 16
     each = wf_rows + wb_rows
     keep, *sends = pl.pallas_call(
         functools.partial(pair_kernel, rows=rows, total=total),
-        in_specs=[SMEM] * 2 + [VMEM] * 8,
-        out_specs=[VMEM] * 8,
+        in_specs=[SMEM] + [VMEM] * 10,
+        out_specs=[VMEM] * 4,
         out_shape=[jax.ShapeDtypeStruct((each + PAD, width), F32)]
-        + [jax.ShapeDtypeStruct((each + PAD, width), BF)] * 7,
+        + [jax.ShapeDtypeStruct((each + PAD, width), BF)] * 3,
         scratch_shapes=[
             pltpu.VMEM((total, wide), BF),
             pltpu.VMEM((total, width), F32),
             pltpu.VMEM((total, width), BF),
-            pltpu.VMEM((2 * rows, min(total, 16 * rows)), BF),
+            pltpu.VMEM((4 * rows, min(total, 16 * rows)), BF),
             pltpu.VMEM((width, width), F32),
-            pltpu.VMEM((2 * rows, wide), F32),
-            pltpu.VMEM((2 * rows, wide), BF),
-            pltpu.VMEM((2 * width, width), F32),
+            pltpu.VMEM((4 * rows, wide), F32),
+            pltpu.VMEM((4 * rows, wide), BF),
+            pltpu.VMEM((width, width), F32),
             pltpu.VMEM((wide // 2, width), F32),
         ],
         compiler_params=pltpu.CompilerParams(vmem_limit_bytes=15 * 2**20 + total * width * 10),
-    )(bases, places, near, near1, line0, line2, line1, line3, cut, wb_copy)
-
-    got = [swap(part, mask, size) for part, (mask, _) in zip(sends, OTHERS)]
+    )(me, near, far2, near1, far3, line0, line2, line1, line3, cut, wb_copy)
+
+    got = [swap(part, mask, size) for part, (mask, _) in zip(sends, LINE)]
     result, note = pl.pallas_call(
         add_kernel,
-        in_specs=[VMEM] * 8,
+        in_specs=[VMEM] * 4,
         out_specs=[VMEM] * 2,
         out_shape=[
             jax.ShapeDtypeStruct((each, width), F32 if beyond else BF),
@@ -444,7 +453,7 @@
             jax.ShapeDtypeStruct((wide, width), F32),
         ],
         compiler_params=pltpu.CompilerParams(vmem_limit_bytes=16 * 2**20),
-    )(place.reshape(1), near, far)
+    )(me, near, far)
     return (grad_wf, grad_wb, note.reshape(1))
 
 

time: 59.5 us -> 52.5 us (0.88)
  starting transfers between devices: 26.1 us -> 21.5 us
  Pallas kernels: 9.29 us -> 8.1 us
    ppermute x22 -> x20, starting transfers between devices: 26.1 us -> 21.5 us  [swap(): return lax.ppermute(array, 'fa', [(i, i ^ mask) for i in range(size)])]
    pallas_call x1, Pallas kernels: 1.01 us -> 0.01 us  [pack(): pl.pallas_call(pack_kernel, in_specs=[VMEM] * (len(arrays) + 1), out_spec...]
    ppermute x22 -> x20, waiting for transfers between devices: 22.4 us -> 22 us  [swap(): return lax.ppermute(array, 'fa', [(i, i ^ mask) for i in range(size)])]
  transfers between devices with their start and end apart: 22 -> 20, of which waited for: 13 -> 10; matrix products, arithmetic and copies ran while one was open for 0% -> 0% of each run, Pallas kernels for 5% -> 0%
where the time goes in v10:
time: 52.5 us; the launch traced here: 52.4 us
  waiting for transfers between devices  22 us (42%)
  starting transfers between devices  21.5 us (41%)
  Pallas kernels  8.1 us (15%)
  between operations  0.75 us (1%)
    ppermute x20, waiting for transfers between devices, swap(): return lax.ppermute(array, 'fa', [(i, i ^ mask) for i in range(size)])  22 us
    ppermute x20, starting transfers between devices, swap(): return lax.ppermute(array, 'fa', [(i, i ^ mask) for i in range(size)])  21.5 us
    pallas_call x1, Pallas kernels, body(): pl.pallas_call(functools.partial(pair_kernel, rows=rows, total=total), in...  3.56 us
    pallas_call x1, Pallas kernels, body(): pl.pallas_call(feature_kernel, in_specs=[SMEM] + [HBM] * 9, out_specs=[VM...  2.83 us
    pallas_call x1, Pallas kernels, body(): pl.pallas_call(functools.partial(assemble_kernel, wf_rows=wf_rows, wb_row...  1.16 us
  transfers between devices with their start and end apart: 20, of which 10 were waited for; matrix products, arithmetic and copies ran while one was open for 0% of the time, Pallas kernels for 0%

profile of v10, /device:TPU:0, one launch (start us, length us, event | category | flops | bytes accessed | tf_op | source)
XLA Modules:
  0.0 52.4 jit_solution(197643289443836566)
XLA Ops:
  0.6 2.8 %shard_map.112 = (bf16[656,256]{1,0:T(8,128)(2,1)}, bf16[528,256]{1,0:T(8,128)(2,1)}, bf16[128,256]{1,0:T(8,128)(2,1)}, bf16[128,256]{1,0:T(8,128)(2,1)}, bf16[256,256]{1,0:T(8,128)(2,1)}) custom-call(s32[1]{0:T(128)} %bitcast.me_ref.refs_0_, bf16[128,1024]{1,0:T(8,128)(2,1)} %hf_hbm.1, bf16[128,1024]{1,0:T(8,128)(2,1)} %ht_hbm.1, bf16[128,256]{1,0:T(8,128)(2,1)} %hb_hbm.1, ...), custom_call_target="tpu_custom_call" | custom-call | flops 134217728 | bytes 1572864 | tf_op jit(solution)/shard_map/pallas_call | solution.py:353
  3.5 3.0 %collective-permute-start = (bf16[656,256]{1,0:T(8,128)(2,1)}, bf16[656,256]{1,0:T(8,128)(2,1)S(1)}, u32[]{:S(2)}, u32[]{:S(2)}) collective-permute-start(bf16[656,256]{1,0:T(8,128)(2,1)} %get-tuple-element.17), channel_id=1, source_target_pairs={{0,2},{1,3},{2,0},{3,1},{4,6},{5,7},{6,4},{7,5},{8,10},{9,11},{10,... | collective-permute-start | bytes 1007624 | tf_op jit(solution)/shard_map/ppermute | solution.py:39
  6.5 0.0 copy-start
  6.5 0.0 copy-start.1
  6.5 0.0 copy-start.2
  6.5 1.6 %collective-permute-start.5 = (bf16[128,256]{1,0:T(8,128)(2,1)}, bf16[128,256]{1,0:T(8,128)(2,1)S(1)}, u32[]{:S(2)}, u32[]{:S(2)}) collective-permute-start(bf16[128,256]{1,0:T(8,128)(2,1)} %get-tuple-element.18), channel_id=1, source_target_pairs={{0,4},{1,5},{2,6},{3,7},{4,0},{5,1},{6,2},{7,3},{8,12},{9,13},{10,... | collective-permute-start | bytes 196616 | tf_op jit(solution)/shard_map/ppermute | solution.py:39
  8.1 2.6 %collective-permute-start.4 = (bf16[128,256]{1,0:T(8,128)(2,1)}, bf16[128,256]{1,0:T(8,128)(2,1)S(1)}, u32[]{:S(2)}, u32[]{:S(2)}) collective-permute-start(bf16[128,256]{1,0:T(8,128)(2,1)} %get-tuple-element.18), channel_id=1, source_target_pairs={{0,8},{1,9},{2,10},{3,11},{4,12},{5,13},{6,14},{7,15},{8,0},{9,1},... | collective-permute-start | bytes 196616 | tf_op jit(solution)/shard_map/ppermute | solution.py:39
  10.7 0.2 collective-permute-start.3
  10.9 0.1 collective-permute-done.5.refs_2_
  11.0 4.3 %collective-permute-done.4.refs_1_ = bf16[128,256]{1,0:T(8,128)(2,1)S(1)} collective-permute-done((bf16[128,256]{1,0:T(8,128)(2,1)}, bf16[128,256]{1,0:T(8,128)(2,1)S(1)}, u32[]{:S(2)}, u32[]{:S(2)}) %collective-permute-start.4) | collective-permute-done | bytes 65568 | tf_op jit(solution)/shard_map/ppermute | solution.py:39
  15.3 1.7 %collective-permute-done.3.refs_0_ = bf16[128,256]{1,0:T(8,128)(2,1)S(1)} collective-permute-done((bf16[128,256]{1,0:T(8,128)(2,1)}, bf16[128,256]{1,0:T(8,128)(2,1)S(1)}, u32[]{:S(2)}, u32[]{:S(2)}) %collective-permute-start.3) | collective-permute-done | bytes 65568 | tf_op jit(solution)/shard_map/ppermute | solution.py:39
  17.0 0.0 collective-permute-done.refs_3_.refs_2_
  17.0 0.6 %collective-permute-start.6 = (bf16[384,256]{1,0:T(8,128)(2,1)S(1)}, bf16[384,256]{1,0:T(8,128)(2,1)S(1)}, u32[]{:S(2)}, u32[]{:S(2)}) collective-permute-start(bf16[384,256]{1,0:T(8,128)(2,1)S(1)} %shard_map.113.refs_5_), channel_id=1, source_target_pairs={{0,2},{1,3},{2,0},{3,1},{4,6},{5,7},{6,4},{7,5},{8,10},{9,11},{10,... | collective-permute-start | bytes 589832 | tf_op jit(solution)/shard_map/ppermute | solution.py:39
  17.5 0.0 collective-permute-start.2
  17.5 0.0 copy-done
  17.6 0.5 collective-permute-start.1
  18.1 0.0 collective-permute-start.7
  18.1 4.6 %collective-permute-done.6.refs_6_ = bf16[384,256]{1,0:T(8,128)(2,1)S(1)} collective-permute-done((bf16[384,256]{1,0:T(8,128)(2,1)S(1)}, bf16[384,256]{1,0:T(8,128)(2,1)S(1)}, u32[]{:S(2)}, u32[]{:S(2)}) %collective-permute-start.6) | collective-permute-done | bytes 196640 | tf_op jit(solution)/shard_map/ppermute | solution.py:39
  22.7 0.0 collective-permute-start.8
  22.7 0.0 collective-permute-done.1.refs_3_
  22.7 0.0 collective-permute-done.7.refs_7_
  22.7 0.0 collective-permute-done.2.refs_4_
  22.7 1.4 %collective-permute-done.8.refs_8_ = bf16[384,256]{1,0:T(8,128)(2,1)S(1)} collective-permute-done((bf16[384,256]{1,0:T(8,128)(2,1)S(1)}, bf16[384,256]{1,0:T(8,128)(2,1)S(1)}, u32[]{:S(2)}, u32[]{:S(2)}) %collective-permute-start.8) | collective-permute-done | bytes 196640 | tf_op jit(solution)/shard_map/ppermute | solution.py:39
  24.2 0.0 copy-done.1
  24.2 0.0 copy-done.2
  24.2 3.6 %shard_map.114 = (f32[96,256]{1,0:T(8,128)S(1)}, bf16[96,256]{1,0:T(8,128)(2,1)S(1)}, bf16[96,256]{1,0:T(8,128)(2,1)S(1)}, bf16[96,256]{1,0:T(8,128)(2,1)S(1)}) custom-call(s32[1]{0:T(128)} %bitcast.me_ref.refs_0_, bf16[528,256]{1,0:T(8,128)(2,1)S(1)} %copy-done, bf16[656,256]{1,0:T(8,128)(2,1)S(1)} %collective-permute-done.refs_3_.refs_2_, ...), custom_call_target="tpu_custom_call" | custom-call | tf_op jit(solution)/shard_map/pallas_call | solution.py:403
  27.7 1.6 %collective-permute-start.9 = (bf16[96,256]{1,0:T(8,128)(2,1)S(1)}, bf16[96,256]{1,0:T(8,128)(2,1)S(1)}, u32[]{:S(2)}, u32[]{:S(2)}) collective-permute-start(bf16[96,256]{1,0:T(8,128)(2,1)S(1)} %get-tuple-element.22), channel_id=1, source_target_pairs={{0,12},{1,13},{2,14},{3,15},{4,8},{5,9},{6,10},{7,11},{8,4},{9,5},... | collective-permute-start | bytes 147464 | tf_op jit(solution)/shard_map/ppermute | solution.py:39
  29.4 0.0 collective-permute-start.10
  29.4 2.8 %collective-permute-start.11 = (bf16[96,256]{1,0:T(8,128)(2,1)S(1)}, bf16[96,256]{1,0:T(8,128)(2,1)S(1)}, u32[]{:S(2)}, u32[]{:S(2)}) collective-permute-start(bf16[96,256]{1,0:T(8,128)(2,1)S(1)} %get-tuple-element.24), channel_id=1, source_target_pairs={{0,4},{1,5},{2,6},{3,7},{4,0},{5,1},{6,2},{7,3},{8,12},{9,13},{10,... | collective-permute-start | bytes 147464 | tf_op jit(solution)/shard_map/ppermute | solution.py:39
  32.2 1.8 %collective-permute-done.9.refs_0_ = bf16[96,256]{1,0:T(8,128)(2,1)S(1)} collective-permute-done((bf16[96,256]{1,0:T(8,128)(2,1)S(1)}, bf16[96,256]{1,0:T(8,128)(2,1)S(1)}, u32[]{:S(2)}, u32[]{:S(2)}) %collective-permute-start.9) | collective-permute-done | bytes 49184 | tf_op jit(solution)/shard_map/ppermute | solution.py:39
  34.0 1.5 %collective-permute-done.10.refs_1_ = bf16[96,256]{1,0:T(8,128)(2,1)S(1)} collective-permute-done((bf16[96,256]{1,0:T(8,128)(2,1)S(1)}, bf16[96,256]{1,0:T(8,128)(2,1)S(1)}, u32[]{:S(2)}, u32[]{:S(2)}) %collective-permute-start.10) | collective-permute-done | bytes 49184 | tf_op jit(solution)/shard_map/ppermute | solution.py:39
  35.5 0.0 collective-permute-done.11.refs_2_
  35.5 0.5 %shard_map.115 = (bf16[80,256]{1,0:T(8,128)(2,1)S(1)}, f32[1,1]{1,0:T(1,128)}) custom-call(f32[96,256]{1,0:T(8,128)S(1)} %get-tuple-element.21.keep_ref, bf16[96,256]{1,0:T(8,128)(2,1)S(1)} %collective-permute-done.9.refs_0_, bf16[96,256]{1,0:T(8,128)(2,1)S(1)} %collective-permute-done.10.refs_1_, bf16[96,256]{1,0:T(8,128)(2,1)S(1)} %collective-permute-done.11.refs_2_), custom_call_target="tpu_custom_call" | custom-call | tf_op jit(solution)/shard_map/pallas_call | solution.py:424
  36.0 0.5 collective-permute-start.15
  36.5 0.8 %collective-permute-start.14 = (bf16[1,80,256]{2,1,0:T(8,128)(2,1)S(1)}, bf16[1,80,256]{2,1,0:T(8,128)(2,1)S(1)}, u32[]{:S(2)}, u32[]{:S(2)}) collective-permute-start(bf16[1,80,256]{2,1,0:T(8,128)(2,1)S(1)} %bitcast.7), channel_id=1, source_target_pairs={{0,4},{1,5},{2,6},{3,7},{4,0},{5,1},{6,2},{7,3},{8,12},{9,13},{10,... | collective-permute-start | bytes 122888 | tf_op jit(solution)/shard_map/ppermute | solution.py:39
  37.3 2.4 %collective-permute-start.13 = (bf16[1,80,256]{2,1,0:T(8,128)(2,1)S(1)}, bf16[1,80,256]{2,1,0:T(8,128)(2,1)S(1)}, u32[]{:S(2)}, u32[]{:S(2)}) collective-permute-start(bf16[1,80,256]{2,1,0:T(8,128)(2,1)S(1)} %bitcast.8), channel_id=1, source_target_pairs={{0,8},{1,9},{2,10},{3,11},{4,12},{5,13},{6,14},{7,15},{8,0},{9,1},... | collective-permute-start | bytes 122888 | tf_op jit(solution)/shard_map/ppermute | solution.py:39
  39.7 1.3 %collective-permute-start.12 = (bf16[1,80,256]{2,1,0:T(8,128)(2,1)S(1)}, bf16[1,80,256]{2,1,0:T(8,128)(2,1)S(1)}, u32[]{:S(2)}, u32[]{:S(2)}) collective-permute-start(bf16[1,80,256]{2,1,0:T(8,128)(2,1)S(1)} %bitcast.9), channel_id=1, source_target_pairs={{0,12},{1,13},{2,14},{3,15},{4,8},{5,9},{6,10},{7,11},{8,4},{9,5},... | collective-permute-start | bytes 122888 | tf_op jit(solution)/shard_map/ppermute | solution.py:39
  40.9 0.0 collective-permute-done.14
  40.9 1.5 %collective-permute-start.18 = (bf16[1,80,256]{2,1,0:T(8,128)(2,1)S(1)}, bf16[1,80,256]{2,1,0:T(8,128)(2,1)S(1)}, u32[]{:S(2)}, u32[]{:S(2)}) collective-permute-start(bf16[1,80,256]{2,1,0:T(8,128)(2,1)S(1)} %collective-permute-done.14), channel_id=1, source_target_pairs={{0,2},{1,3},{2,0},{3,1},{4,6},{5,7},{6,4},{7,5},{8,10},{9,11},{10,... | collective-permute-start | bytes 122888 | tf_op jit(solution)/shard_map/ppermute | solution.py:39
  42.4 0.0 collective-permute-done.13
  42.4 1.3 %collective-permute-start.17 = (bf16[1,80,256]{2,1,0:T(8,128)(2,1)S(1)}, bf16[1,80,256]{2,1,0:T(8,128)(2,1)S(1)}, u32[]{:S(2)}, u32[]{:S(2)}) collective-permute-start(bf16[1,80,256]{2,1,0:T(8,128)(2,1)S(1)} %collective-permute-done.13), channel_id=1, source_target_pairs={{0,2},{1,3},{2,0},{3,1},{4,6},{5,7},{6,4},{7,5},{8,10},{9,11},{10,... | collective-permute-start | bytes 122888 | tf_op jit(solution)/shard_map/ppermute | solution.py:39
  43.7 1.7 %collective-permute-done.12 = bf16[1,80,256]{2,1,0:T(8,128)(2,1)S(1)} collective-permute-done((bf16[1,80,256]{2,1,0:T(8,128)(2,1)S(1)}, bf16[1,80,256]{2,1,0:T(8,128)(2,1)S(1)}, u32[]{:S(2)}, u32[]{:S(2)}) %collective-permute-start.12) | collective-permute-done | bytes 40992 | tf_op jit(solution)/shard_map/ppermute | solution.py:39
  45.5 0.8 %collective-permute-start.16 = (bf16[1,80,256]{2,1,0:T(8,128)(2,1)S(1)}, bf16[1,80,256]{2,1,0:T(8,128)(2,1)S(1)}, u32[]{:S(2)}, u32[]{:S(2)}) collective-permute-start(bf16[1,80,256]{2,1,0:T(8,128)(2,1)S(1)} %collective-permute-done.12), channel_id=1, source_target_pairs={{0,2},{1,3},{2,0},{3,1},{4,6},{5,7},{6,4},{7,5},{8,10},{9,11},{10,... | collective-permute-start | bytes 122888 | tf_op jit(solution)/shard_map/ppermute | solution.py:39
  46.3 0.0 collective-permute-done.15
  46.3 3.2 %collective-permute-done.16 = bf16[1,80,256]{2,1,0:T(8,128)(2,1)S(1)} collective-permute-done((bf16[1,80,256]{2,1,0:T(8,128)(2,1)S(1)}, bf16[1,80,256]{2,1,0:T(8,128)(2,1)S(1)}, u32[]{:S(2)}, u32[]{:S(2)}) %collective-permute-start.16) | collective-permute-done | bytes 40992 | tf_op jit(solution)/shard_map/ppermute | solution.py:39
  49.5 0.0 collective-permute-done.17
  49.5 0.0 collective-permute-done.18
  49.5 0.1 collective-permute-start.19
  49.6 1.6 %collective-permute-done.19.refs_1_ = bf16[8,80,256]{2,1,0:T(8,128)(2,1)S(1)} collective-permute-done((bf16[8,80,256]{2,1,0:T(8,128)(2,1)S(1)}, bf16[8,80,256]{2,1,0:T(8,128)(2,1)S(1)}, u32[]{:S(2)}, u32[]{:S(2)}) %collective-permute-start.19) | collective-permute-done | bytes 327712 | tf_op jit(solution)/shard_map/ppermute | solution.py:39
  51.2 1.2 %shard_map.116 = (f32[1024,256]{1,0:T(8,128)}, f32[256,256]{1,0:T(8,128)}) custom-call(s32[1]{0:T(128)} %bitcast.me_ref.refs_0_, bf16[8,80,256]{2,1,0:T(8,128)(2,1)S(1)} %constant_dynamic-update-slice_fusion.refs_0_, bf16[8,80,256]{2,1,0:T(8,128)(2,1)S(1)} %collective-permute-done.19.refs_1_), custom_call_target="tpu_custom_call" | custom-call | tf_op jit(solution)/shard_map/pallas_call | solution.py:441
  (9 shorter events, 0.0 us)
Async XLA Ops:
  3.5 13.5 %collective-permute-start = (bf16[656,256]{1,0:T(8,128)(2,1)}, bf16[656,256]{1,0:T(8,128)(2,1)S(1)}, u32[]{:S(2)}, u32[]{:S(2)}) collective-permute-start(bf16[656,256]{1,0:T(8,128)(2,1)} %get-tuple-element.17), channel_id=1, source_target_pairs={{0,2},{1,3},{2,0},{3,1},{4,6},{5,7},{6,4},{7,5},{8,10},{9,11},{10,... | collective-permute-start | bytes 1007624 | tf_op jit(solution)/shard_map/ppermute | solution.py:39
  6.5 11.0 %copy-start = (bf16[528,256]{1,0:T(8,128)(2,1)S(1)}, bf16[528,256]{1,0:T(8,128)(2,1)}, u32[]{:S(2)}) copy-start(bf16[528,256]{1,0:T(8,128)(2,1)} %get-tuple-element.16.refs_1_) | copy-start | bytes 811012
  6.5 17.6 %copy-start.1 = (bf16[256,256]{1,0:T(8,128)(2,1)S(1)}, bf16[256,256]{1,0:T(8,128)(2,1)}, u32[]{:S(2)}) copy-start(bf16[256,256]{1,0:T(8,128)(2,1)} %get-tuple-element.20.refs_10_) | copy-start | bytes 393220
  6.5 17.6 %copy-start.2 = (bf16[128,256]{1,0:T(8,128)(2,1)S(1)}, bf16[128,256]{1,0:T(8,128)(2,1)}, u32[]{:S(2)}) copy-start(bf16[128,256]{1,0:T(8,128)(2,1)} %get-tuple-element.19.refs_9_) | copy-start | bytes 196612
  6.5 4.5 %collective-permute-start.5 = (bf16[128,256]{1,0:T(8,128)(2,1)}, bf16[128,256]{1,0:T(8,128)(2,1)S(1)}, u32[]{:S(2)}, u32[]{:S(2)}) collective-permute-start(bf16[128,256]{1,0:T(8,128)(2,1)} %get-tuple-element.18), channel_id=1, source_target_pairs={{0,4},{1,5},{2,6},{3,7},{4,0},{5,1},{6,2},{7,3},{8,12},{9,13},{10,... | collective-permute-start | bytes 196616 | tf_op jit(solution)/shard_map/ppermute | solution.py:39
  8.1 7.2 %collective-permute-start.4 = (bf16[128,256]{1,0:T(8,128)(2,1)}, bf16[128,256]{1,0:T(8,128)(2,1)S(1)}, u32[]{:S(2)}, u32[]{:S(2)}) collective-permute-start(bf16[128,256]{1,0:T(8,128)(2,1)} %get-tuple-element.18), channel_id=1, source_target_pairs={{0,8},{1,9},{2,10},{3,11},{4,12},{5,13},{6,14},{7,15},{8,0},{9,1},... | collective-permute-start | bytes 196616 | tf_op jit(solution)/shard_map/ppermute | solution.py:39
  10.7 6.3 %collective-permute-start.3 = (bf16[128,256]{1,0:T(8,128)(2,1)}, bf16[128,256]{1,0:T(8,128)(2,1)S(1)}, u32[]{:S(2)}, u32[]{:S(2)}) collective-permute-start(bf16[128,256]{1,0:T(8,128)(2,1)} %get-tuple-element.18), channel_id=1, source_target_pairs={{0,12},{1,13},{2,14},{3,15},{4,8},{5,9},{6,10},{7,11},{8,4},{9,5},... | collective-permute-start | bytes 196616 | tf_op jit(solution)/shard_map/ppermute | solution.py:39
  17.0 5.7 %collective-permute-start.6 = (bf16[384,256]{1,0:T(8,128)(2,1)S(1)}, bf16[384,256]{1,0:T(8,128)(2,1)S(1)}, u32[]{:S(2)}, u32[]{:S(2)}) collective-permute-start(bf16[384,256]{1,0:T(8,128)(2,1)S(1)} %shard_map.113.refs_5_), channel_id=1, source_target_pairs={{0,2},{1,3},{2,0},{3,1},{4,6},{5,7},{6,4},{7,5},{8,10},{9,11},{10,... | collective-permute-start | bytes 589832 | tf_op jit(solution)/shard_map/ppermute | solution.py:39
  17.5 5.2 %collective-permute-start.2 = (bf16[656,256]{1,0:T(8,128)(2,1)S(1)}, bf16[656,256]{1,0:T(8,128)(2,1)S(1)}, u32[]{:S(2)}, u32[]{:S(2)}) collective-permute-start(bf16[656,256]{1,0:T(8,128)(2,1)S(1)} %collective-permute-done.refs_3_.refs_2_), channel_id=1, source_target_pairs={{0,1},{1,0},{2,3},{3,2},{4,5},{5,4},{6,7},{7,6},{8,9},{9,8},{10,11... | collective-permute-start | bytes 1007624 | tf_op jit(solution)/shard_map/ppermute | solution.py:39
  17.6 5.2 %collective-permute-start.1 = (bf16[528,256]{1,0:T(8,128)(2,1)S(1)}, bf16[528,256]{1,0:T(8,128)(2,1)S(1)}, u32[]{:S(2)}, u32[]{:S(2)}) collective-permute-start(bf16[528,256]{1,0:T(8,128)(2,1)S(1)} %copy-done), channel_id=1, source_target_pairs={{0,1},{1,0},{2,3},{3,2},{4,5},{5,4},{6,7},{7,6},{8,9},{9,8},{10,11... | collective-permute-start | bytes 811016 | tf_op jit(solution)/shard_map/ppermute | solution.py:39
  18.1 4.7 %collective-permute-start.7 = (bf16[384,256]{1,0:T(8,128)(2,1)S(1)}, bf16[384,256]{1,0:T(8,128)(2,1)S(1)}, u32[]{:S(2)}, u32[]{:S(2)}) collective-permute-start(bf16[384,256]{1,0:T(8,128)(2,1)S(1)} %shard_map.113.refs_5_), channel_id=1, source_target_pairs={{0,1},{1,0},{2,3},{3,2},{4,5},{5,4},{6,7},{7,6},{8,9},{9,8},{10,11... | collective-permute-start | bytes 589832 | tf_op jit(solution)/shard_map/ppermute | solution.py:39
  22.7 1.4 %collective-permute-start.8 = (bf16[384,256]{1,0:T(8,128)(2,1)S(1)}, bf16[384,256]{1,0:T(8,128)(2,1)S(1)}, u32[]{:S(2)}, u32[]{:S(2)}) collective-permute-start(bf16[384,256]{1,0:T(8,128)(2,1)S(1)} %collective-permute-done.6.refs_6_), channel_id=1, source_target_pairs={{0,1},{1,0},{2,3},{3,2},{4,5},{5,4},{6,7},{7,6},{8,9},{9,8},{10,11... | collective-permute-start | bytes 589832 | tf_op jit(solution)/shard_map/ppermute | solution.py:39
  27.7 6.3 %collective-permute-start.9 = (bf16[96,256]{1,0:T(8,128)(2,1)S(1)}, bf16[96,256]{1,0:T(8,128)(2,1)S(1)}, u32[]{:S(2)}, u32[]{:S(2)}) collective-permute-start(bf16[96,256]{1,0:T(8,128)(2,1)S(1)} %get-tuple-element.22), channel_id=1, source_target_pairs={{0,12},{1,13},{2,14},{3,15},{4,8},{5,9},{6,10},{7,11},{8,4},{9,5},... | collective-permute-start | bytes 147464 | tf_op jit(solution)/shard_map/ppermute | solution.py:39
  29.4 6.1 %collective-permute-start.10 = (bf16[96,256]{1,0:T(8,128)(2,1)S(1)}, bf16[96,256]{1,0:T(8,128)(2,1)S(1)}, u32[]{:S(2)}, u32[]{:S(2)}) collective-permute-start(bf16[96,256]{1,0:T(8,128)(2,1)S(1)} %get-tuple-element.23), channel_id=1, source_target_pairs={{0,8},{1,9},{2,10},{3,11},{4,12},{5,13},{6,14},{7,15},{8,0},{9,1},... | collective-permute-start | bytes 147464 | tf_op jit(solution)/shard_map/ppermute | solution.py:39
  29.4 6.1 %collective-permute-start.11 = (bf16[96,256]{1,0:T(8,128)(2,1)S(1)}, bf16[96,256]{1,0:T(8,128)(2,1)S(1)}, u32[]{:S(2)}, u32[]{:S(2)}) collective-permute-start(bf16[96,256]{1,0:T(8,128)(2,1)S(1)} %get-tuple-element.24), channel_id=1, source_target_pairs={{0,4},{1,5},{2,6},{3,7},{4,0},{5,1},{6,2},{7,3},{8,12},{9,13},{10,... | collective-permute-start | bytes 147464 | tf_op jit(solution)/shard_map/ppermute | solution.py:39
  36.0 10.3 %collective-permute-start.15 = (bf16[1,80,256]{2,1,0:T(8,128)(2,1)S(1)}, bf16[1,80,256]{2,1,0:T(8,128)(2,1)S(1)}, u32[]{:S(2)}, u32[]{:S(2)}) collective-permute-start(bf16[1,80,256]{2,1,0:T(8,128)(2,1)S(1)} %bitcast.6), channel_id=1, source_target_pairs={{0,2},{1,3},{2,0},{3,1},{4,6},{5,7},{6,4},{7,5},{8,10},{9,11},{10,... | collective-permute-start | bytes 122888 | tf_op jit(solution)/shard_map/ppermute | solution.py:39
  36.5 4.4 %collective-permute-start.14 = (bf16[1,80,256]{2,1,0:T(8,128)(2,1)S(1)}, bf16[1,80,256]{2,1,0:T(8,128)(2,1)S(1)}, u32[]{:S(2)}, u32[]{:S(2)}) collective-permute-start(bf16[1,80,256]{2,1,0:T(8,128)(2,1)S(1)} %bitcast.7), channel_id=1, source_target_pairs={{0,4},{1,5},{2,6},{3,7},{4,0},{5,1},{6,2},{7,3},{8,12},{9,13},{10,... | collective-permute-start | bytes 122888 | tf_op jit(solution)/shard_map/ppermute | solution.py:39
  37.3 5.1 %collective-permute-start.13 = (bf16[1,80,256]{2,1,0:T(8,128)(2,1)S(1)}, bf16[1,80,256]{2,1,0:T(8,128)(2,1)S(1)}, u32[]{:S(2)}, u32[]{:S(2)}) collective-permute-start(bf16[1,80,256]{2,1,0:T(8,128)(2,1)S(1)} %bitcast.8), channel_id=1, source_target_pairs={{0,8},{1,9},{2,10},{3,11},{4,12},{5,13},{6,14},{7,15},{8,0},{9,1},... | collective-permute-start | bytes 122888 | tf_op jit(solution)/shard_map/ppermute | solution.py:39
  39.7 5.8 %collective-permute-start.12 = (bf16[1,80,256]{2,1,0:T(8,128)(2,1)S(1)}, bf16[1,80,256]{2,1,0:T(8,128)(2,1)S(1)}, u32[]{:S(2)}, u32[]{:S(2)}) collective-permute-start(bf16[1,80,256]{2,1,0:T(8,128)(2,1)S(1)} %bitcast.9), channel_id=1, source_target_pairs={{0,12},{1,13},{2,14},{3,15},{4,8},{5,9},{6,10},{7,11},{8,4},{9,5},... | collective-permute-start | bytes 122888 | tf_op jit(solution)/shard_map/ppermute | solution.py:39
  40.9 8.6 %collective-permute-start.18 = (bf16[1,80,256]{2,1,0:T(8,128)(2,1)S(1)}, bf16[1,80,256]{2,1,0:T(8,128)(2,1)S(1)}, u32[]{:S(2)}, u32[]{:S(2)}) collective-permute-start(bf16[1,80,256]{2,1,0:T(8,128)(2,1)S(1)} %collective-permute-done.14), channel_id=1, source_target_pairs={{0,2},{1,3},{2,0},{3,1},{4,6},{5,7},{6,4},{7,5},{8,10},{9,11},{10,... | collective-permute-start | bytes 122888 | tf_op jit(solution)/shard_map/ppermute | solution.py:39
  42.4 7.0 %collective-permute-start.17 = (bf16[1,80,256]{2,1,0:T(8,128)(2,1)S(1)}, bf16[1,80,256]{2,1,0:T(8,128)(2,1)S(1)}, u32[]{:S(2)}, u32[]{:S(2)}) collective-permute-start(bf16[1,80,256]{2,1,0:T(8,128)(2,1)S(1)} %collective-permute-done.13), channel_id=1, source_target_pairs={{0,2},{1,3},{2,0},{3,1},{4,6},{5,7},{6,4},{7,5},{8,10},{9,11},{10,... | collective-permute-start | bytes 122888 | tf_op jit(solution)/shard_map/ppermute | solution.py:39
  45.5 4.0 %collective-permute-start.16 = (bf16[1,80,256]{2,1,0:T(8,128)(2,1)S(1)}, bf16[1,80,256]{2,1,0:T(8,128)(2,1)S(1)}, u32[]{:S(2)}, u32[]{:S(2)}) collective-permute-start(bf16[1,80,256]{2,1,0:T(8,128)(2,1)S(1)} %collective-permute-done.12), channel_id=1, source_target_pairs={{0,2},{1,3},{2,0},{3,1},{4,6},{5,7},{6,4},{7,5},{8,10},{9,11},{10,... | collective-permute-start | bytes 122888 | tf_op jit(solution)/shard_map/ppermute | solution.py:39
  49.5 1.7 %collective-permute-start.19 = (bf16[8,80,256]{2,1,0:T(8,128)(2,1)S(1)}, bf16[8,80,256]{2,1,0:T(8,128)(2,1)S(1)}, u32[]{:S(2)}, u32[]{:S(2)}) collective-permute-start(bf16[8,80,256]{2,1,0:T(8,128)(2,1)S(1)} %constant_dynamic-update-slice_fusion.refs_0_), channel_id=1, source_target_pairs={{0,1},{1,0},{2,3},{3,2},{4,5},{5,4},{6,7},{7,6},{8,9},{9,8},{10,11... | collective-permute-start | bytes 983048 | tf_op jit(solution)/shard_map/ppermute | solution.py:39

commit v11 on v10

--- a/solution.py
+++ b/solution.py
@@ -19,7 +19,7 @@
 FEAT_AT = (2, 3, 2, 3)
 PAD = 16
 LINE = ((12, 3), (8, 1), (4, 2))
-TURNS = (0, 3, 1, 2, 4, 7, 5, 6)
+TURNS = (0, 2, 1, 3, 4, 6, 5, 7)
 
 
 def dot(left, right):
@@ -391,10 +391,13 @@
         head = jnp.concatenate([head, swap(head, mask, size)], axis=0)
     line = [head[rows:]] * (len(beyond) > 0) + [swap(head, mask, size) for mask, _ in LINE]
     far2 = swap(far, 2, size)
-    line0 = pack(*line, after=far2)
-    line2 = swap(line0, 2, size)
+    over = [swap(piece, 2, size) for piece in line[-2:]]
+    gated = pack(*line[:-2], after=far2)
+    line = [gated] + line[-2:]
+    over = [swap(gated, 2, size)] + over
     near1 = swap(near, 1, size)
     far3 = swap(far2, 1, size)
+    line0, line2 = [jnp.concatenate(part, axis=0) for part in (line, over)]
     line1 = swap(line0, 1, size)
     line3 = swap(line2, 1, size)
 
@@ -435,7 +438,7 @@
         result = result + swap(result, mask, size)
         note = note + swap(note, mask, size)
     result = result.astype(BF).reshape(1, each, width)
-    pieces = [result] + [swap(result, mask, size) for mask, _ in LINE]
+    pieces = [result] + [swap(result, mask, size) for mask, _ in reversed(LINE)]
     near = jnp.concatenate(pieces + [swap(piece, 2, size) for piece in pieces], axis=0)
     far = swap(near, 1, size)
     grad_wf, grad_wb = pl.pallas_call(

time: 52.5 us -> 51.8 us (0.987)
  waiting for transfers between devices: 22 us -> 20.6 us
    ppermute x20 -> x22, waiting for transfers between devices: 22 us -> 20.6 us  [swap(): return lax.ppermute(array, 'fa', [(i, i ^ mask) for i in range(size)])]
    ppermute x20 -> x22, starting transfers between devices: 21.5 us -> 22 us  [swap(): return lax.ppermute(array, 'fa', [(i, i ^ mask) for i in range(size)])]
  transfers between devices with their start and end apart: 20 -> 22, of which waited for: 10 -> 11; matrix products, arithmetic and copies ran while one was open for 0% -> 0% of each run, Pallas kernels for 0% -> 0%
where the time goes in v11:
time: 51.8 us; the launch traced here: 51.6 us
  starting transfers between devices  22 us (42%)
  waiting for transfers between devices  20.6 us (40%)
  Pallas kernels  8.1 us (16%)
  between operations  0.81 us (2%)
    ppermute x22, starting transfers between devices, swap(): return lax.ppermute(array, 'fa', [(i, i ^ mask) for i in range(size)])  22 us
    ppermute x22, waiting for transfers between devices, swap(): return lax.ppermute(array, 'fa', [(i, i ^ mask) for i in range(size)])  20.6 us
    pallas_call x1, Pallas kernels, body(): pl.pallas_call(functools.partial(pair_kernel, rows=rows, total=total), in...  3.57 us
    pallas_call x1, Pallas kernels, body(): pl.pallas_call(feature_kernel, in_specs=[SMEM] + [HBM] * 9, out_specs=[VM...  2.83 us
    pallas_call x1, Pallas kernels, body(): pl.pallas_call(functools.partial(assemble_kernel, wf_rows=wf_rows, wb_row...  1.16 us
  transfers between devices with their start and end apart: 22, of which 11 were waited for; matrix products, arithmetic and copies ran while one was open for 0% of the time, Pallas kernels for 0%

profile of v11, /device:TPU:0, one launch (start us, length us, event | category | flops | bytes accessed | tf_op | source)
XLA Modules:
  0.0 51.6 jit_solution(2181705722716715996)
XLA Ops:
  0.6 2.8 %shard_map.112 = (bf16[656,256]{1,0:T(8,128)(2,1)}, bf16[528,256]{1,0:T(8,128)(2,1)}, bf16[128,256]{1,0:T(8,128)(2,1)}, bf16[128,256]{1,0:T(8,128)(2,1)}, bf16[256,256]{1,0:T(8,128)(2,1)}) custom-call(s32[1]{0:T(128)} %bitcast.me_ref.refs_0_, bf16[128,1024]{1,0:T(8,128)(2,1)} %hf_hbm.1, bf16[128,1024]{1,0:T(8,128)(2,1)} %ht_hbm.1, bf16[128,256]{1,0:T(8,128)(2,1)} %hb_hbm.1, ...), custom_call_target="tpu_custom_call" | custom-call | flops 134217728 | bytes 1572864 | tf_op jit(solution)/shard_map/pallas_call | solution.py:353
  3.5 3.0 %collective-permute-start = (bf16[656,256]{1,0:T(8,128)(2,1)}, bf16[656,256]{1,0:T(8,128)(2,1)S(1)}, u32[]{:S(2)}, u32[]{:S(2)}) collective-permute-start(bf16[656,256]{1,0:T(8,128)(2,1)} %get-tuple-element.17), channel_id=1, source_target_pairs={{0,2},{1,3},{2,0},{3,1},{4,6},{5,7},{6,4},{7,5},{8,10},{9,11},{10,... | collective-permute-start | bytes 1007624 | tf_op jit(solution)/shard_map/ppermute | solution.py:39
  6.5 1.6 %collective-permute-start.5 = (bf16[128,256]{1,0:T(8,128)(2,1)}, bf16[128,256]{1,0:T(8,128)(2,1)S(1)}, u32[]{:S(2)}, u32[]{:S(2)}) collective-permute-start(bf16[128,256]{1,0:T(8,128)(2,1)} %get-tuple-element.18), channel_id=1, source_target_pairs={{0,4},{1,5},{2,6},{3,7},{4,0},{5,1},{6,2},{7,3},{8,12},{9,13},{10,... | collective-permute-start | bytes 196616 | tf_op jit(solution)/shard_map/ppermute | solution.py:39
  8.1 2.6 %collective-permute-start.4 = (bf16[128,256]{1,0:T(8,128)(2,1)}, bf16[128,256]{1,0:T(8,128)(2,1)S(1)}, u32[]{:S(2)}, u32[]{:S(2)}) collective-permute-start(bf16[128,256]{1,0:T(8,128)(2,1)} %get-tuple-element.18), channel_id=1, source_target_pairs={{0,8},{1,9},{2,10},{3,11},{4,12},{5,13},{6,14},{7,15},{8,0},{9,1},... | collective-permute-start | bytes 196616 | tf_op jit(solution)/shard_map/ppermute | solution.py:39
  10.7 0.2 collective-permute-start.3
  10.9 0.0 collective-permute-start.1
  10.9 0.1 collective-permute-done.5
  11.0 0.3 collective-permute-start.8
  11.3 4.0 %collective-permute-done.4 = bf16[128,256]{1,0:T(8,128)(2,1)S(1)} collective-permute-done((bf16[128,256]{1,0:T(8,128)(2,1)}, bf16[128,256]{1,0:T(8,128)(2,1)S(1)}, u32[]{:S(2)}, u32[]{:S(2)}) %collective-permute-start.4) | collective-permute-done | bytes 65568 | tf_op jit(solution)/shard_map/ppermute | solution.py:39
  15.3 0.5 collective-permute-start.7
  15.8 1.1 %collective-permute-done.3.refs_0_ = bf16[128,256]{1,0:T(8,128)(2,1)S(1)} collective-permute-done((bf16[128,256]{1,0:T(8,128)(2,1)}, bf16[128,256]{1,0:T(8,128)(2,1)S(1)}, u32[]{:S(2)}, u32[]{:S(2)}) %collective-permute-start.3) | collective-permute-done | bytes 65568 | tf_op jit(solution)/shard_map/ppermute | solution.py:39
  16.9 0.0 collective-permute-done.refs_1_.refs_2_
  17.0 0.6 %collective-permute-start.6 = (bf16[128,256]{1,0:T(8,128)(2,1)S(1)}, bf16[128,256]{1,0:T(8,128)(2,1)S(1)}, u32[]{:S(2)}, u32[]{:S(2)}) collective-permute-start(bf16[128,256]{1,0:T(8,128)(2,1)S(1)} %shard_map.113), channel_id=1, source_target_pairs={{0,2},{1,3},{2,0},{3,1},{4,6},{5,7},{6,4},{7,5},{8,10},{9,11},{10,... | collective-permute-start | bytes 196616 | tf_op jit(solution)/shard_map/ppermute | solution.py:39
  17.5 0.0 copy-start.1
  17.6 0.0 copy-start
  17.6 0.1 collective-permute-start.9
  17.6 3.6 %collective-permute-done.6 = bf16[128,256]{1,0:T(8,128)(2,1)S(1)} collective-permute-done((bf16[128,256]{1,0:T(8,128)(2,1)S(1)}, bf16[128,256]{1,0:T(8,128)(2,1)S(1)}, u32[]{:S(2)}, u32[]{:S(2)}) %collective-permute-start.6) | collective-permute-done | bytes 65568 | tf_op jit(solution)/shard_map/ppermute | solution.py:39
  21.3 0.0 collective-permute-start.2
  21.3 0.0 collective-permute-done.7
  21.3 0.0 copy-start.2
  21.3 0.0 collective-permute-done.8
  21.4 0.6 %collective-permute-start.10 = (bf16[384,256]{1,0:T(8,128)(2,1)S(1)}, bf16[384,256]{1,0:T(8,128)(2,1)S(1)}, u32[]{:S(2)}, u32[]{:S(2)}) collective-permute-start(bf16[384,256]{1,0:T(8,128)(2,1)S(1)} %constant_dynamic-update-slice_fusion.refs_6_), channel_id=1, source_target_pairs={{0,1},{1,0},{2,3},{3,2},{4,5},{5,4},{6,7},{7,6},{8,9},{9,8},{10,11... | collective-permute-start | bytes 589832 | tf_op jit(solution)/shard_map/ppermute | solution.py:39
  21.9 0.0 collective-permute-done.1.refs_3_
  21.9 0.0 collective-permute-done.9.refs_7_
  21.9 1.3 %collective-permute-done.10.refs_8_ = bf16[384,256]{1,0:T(8,128)(2,1)S(1)} collective-permute-done((bf16[384,256]{1,0:T(8,128)(2,1)S(1)}, bf16[384,256]{1,0:T(8,128)(2,1)S(1)}, u32[]{:S(2)}, u32[]{:S(2)}) %collective-permute-start.10) | collective-permute-done | bytes 196640 | tf_op jit(solution)/shard_map/ppermute | solution.py:39
  23.2 0.0 collective-permute-done.2.refs_4_
  23.2 0.0 copy-done.1
  23.2 0.0 copy-done
  23.2 0.0 copy-done.2
  23.2 3.6 %shard_map.114 = (f32[96,256]{1,0:T(8,128)S(1)}, bf16[96,256]{1,0:T(8,128)(2,1)S(1)}, bf16[96,256]{1,0:T(8,128)(2,1)S(1)}, bf16[96,256]{1,0:T(8,128)(2,1)S(1)}) custom-call(s32[1]{0:T(128)} %bitcast.me_ref.refs_0_, bf16[528,256]{1,0:T(8,128)(2,1)S(1)} %copy-done, bf16[656,256]{1,0:T(8,128)(2,1)S(1)} %collective-permute-done.refs_1_.refs_2_, ...), custom_call_target="tpu_custom_call" | custom-call | tf_op jit(solution)/shard_map/pallas_call | solution.py:406
  26.8 2.2 %collective-permute-start.11 = (bf16[96,256]{1,0:T(8,128)(2,1)S(1)}, bf16[96,256]{1,0:T(8,128)(2,1)S(1)}, u32[]{:S(2)}, u32[]{:S(2)}) collective-permute-start(bf16[96,256]{1,0:T(8,128)(2,1)S(1)} %get-tuple-element.22), channel_id=1, source_target_pairs={{0,12},{1,13},{2,14},{3,15},{4,8},{5,9},{6,10},{7,11},{8,4},{9,5},... | collective-permute-start | bytes 147464 | tf_op jit(solution)/shard_map/ppermute | solution.py:39
  29.0 0.0 collective-permute-start.12
  29.0 2.2 %collective-permute-start.13 = (bf16[96,256]{1,0:T(8,128)(2,1)S(1)}, bf16[96,256]{1,0:T(8,128)(2,1)S(1)}, u32[]{:S(2)}, u32[]{:S(2)}) collective-permute-start(bf16[96,256]{1,0:T(8,128)(2,1)S(1)} %get-tuple-element.24), channel_id=1, source_target_pairs={{0,4},{1,5},{2,6},{3,7},{4,0},{5,1},{6,2},{7,3},{8,12},{9,13},{10,... | collective-permute-start | bytes 147464 | tf_op jit(solution)/shard_map/ppermute | solution.py:39
  31.3 1.8 %collective-permute-done.11.refs_0_ = bf16[96,256]{1,0:T(8,128)(2,1)S(1)} collective-permute-done((bf16[96,256]{1,0:T(8,128)(2,1)S(1)}, bf16[96,256]{1,0:T(8,128)(2,1)S(1)}, u32[]{:S(2)}, u32[]{:S(2)}) %collective-permute-start.11) | collective-permute-done | bytes 49184 | tf_op jit(solution)/shard_map/ppermute | solution.py:39
  33.1 1.5 %collective-permute-done.12.refs_1_ = bf16[96,256]{1,0:T(8,128)(2,1)S(1)} collective-permute-done((bf16[96,256]{1,0:T(8,128)(2,1)S(1)}, bf16[96,256]{1,0:T(8,128)(2,1)S(1)}, u32[]{:S(2)}, u32[]{:S(2)}) %collective-permute-start.12) | collective-permute-done | bytes 49184 | tf_op jit(solution)/shard_map/ppermute | solution.py:39
  34.6 0.0 collective-permute-done.13.refs_2_
  34.6 0.5 %shard_map.115 = (bf16[80,256]{1,0:T(8,128)(2,1)S(1)}, f32[1,1]{1,0:T(1,128)}) custom-call(f32[96,256]{1,0:T(8,128)S(1)} %get-tuple-element.21.keep_ref, bf16[96,256]{1,0:T(8,128)(2,1)S(1)} %collective-permute-done.11.refs_0_, bf16[96,256]{1,0:T(8,128)(2,1)S(1)} %collective-permute-done.12.refs_1_, bf16[96,256]{1,0:T(8,128)(2,1)S(1)} %collective-permute-done.13.refs_2_), custom_call_target="tpu_custom_call" | custom-call | tf_op jit(solution)/shard_map/pallas_call | solution.py:427
  35.1 1.4 %collective-permute-start.17 = (bf16[1,80,256]{2,1,0:T(8,128)(2,1)S(1)}, bf16[1,80,256]{2,1,0:T(8,128)(2,1)S(1)}, u32[]{:S(2)}, u32[]{:S(2)}) collective-permute-start(bf16[1,80,256]{2,1,0:T(8,128)(2,1)S(1)} %bitcast.6), channel_id=1, source_target_pairs={{0,2},{1,3},{2,0},{3,1},{4,6},{5,7},{6,4},{7,5},{8,10},{9,11},{10,... | collective-permute-start | bytes 122888 | tf_op jit(solution)/shard_map/ppermute | solution.py:39
  36.5 2.2 %collective-permute-start.16 = (bf16[1,80,256]{2,1,0:T(8,128)(2,1)S(1)}, bf16[1,80,256]{2,1,0:T(8,128)(2,1)S(1)}, u32[]{:S(2)}, u32[]{:S(2)}) collective-permute-start(bf16[1,80,256]{2,1,0:T(8,128)(2,1)S(1)} %bitcast.7), channel_id=1, source_target_pairs={{0,12},{1,13},{2,14},{3,15},{4,8},{5,9},{6,10},{7,11},{8,4},{9,5},... | collective-permute-start | bytes 122888 | tf_op jit(solution)/shard_map/ppermute | solution.py:39
  38.7 0.2 collective-permute-start.15
  38.9 2.0 %collective-permute-start.14 = (bf16[1,80,256]{2,1,0:T(8,128)(2,1)S(1)}, bf16[1,80,256]{2,1,0:T(8,128)(2,1)S(1)}, u32[]{:S(2)}, u32[]{:S(2)}) collective-permute-start(bf16[1,80,256]{2,1,0:T(8,128)(2,1)S(1)} %bitcast.9), channel_id=1, source_target_pairs={{0,4},{1,5},{2,6},{3,7},{4,0},{5,1},{6,2},{7,3},{8,12},{9,13},{10,... | collective-permute-start | bytes 122888 | tf_op jit(solution)/shard_map/ppermute | solution.py:39
  40.9 1.8 %collective-permute-done.16 = bf16[1,80,256]{2,1,0:T(8,128)(2,1)S(1)} collective-permute-done((bf16[1,80,256]{2,1,0:T(8,128)(2,1)S(1)}, bf16[1,80,256]{2,1,0:T(8,128)(2,1)S(1)}, u32[]{:S(2)}, u32[]{:S(2)}) %collective-permute-start.16) | collective-permute-done | bytes 40992 | tf_op jit(solution)/shard_map/ppermute | solution.py:39
  42.7 0.3 collective-permute-start.20
  43.0 0.9 %collective-permute-done.15 = bf16[1,80,256]{2,1,0:T(8,128)(2,1)S(1)} collective-permute-done((bf16[1,80,256]{2,1,0:T(8,128)(2,1)S(1)}, bf16[1,80,256]{2,1,0:T(8,128)(2,1)S(1)}, u32[]{:S(2)}, u32[]{:S(2)}) %collective-permute-start.15) | collective-permute-done | bytes 40992 | tf_op jit(solution)/shard_map/ppermute | solution.py:39
  43.8 0.9 %collective-permute-start.19 = (bf16[1,80,256]{2,1,0:T(8,128)(2,1)S(1)}, bf16[1,80,256]{2,1,0:T(8,128)(2,1)S(1)}, u32[]{:S(2)}, u32[]{:S(2)}) collective-permute-start(bf16[1,80,256]{2,1,0:T(8,128)(2,1)S(1)} %collective-permute-done.15), channel_id=1, source_target_pairs={{0,2},{1,3},{2,0},{3,1},{4,6},{5,7},{6,4},{7,5},{8,10},{9,11},{10,... | collective-permute-start | bytes 122888 | tf_op jit(solution)/shard_map/ppermute | solution.py:39
  44.7 0.0 collective-permute-done.14
  44.7 1.1 %collective-permute-start.18 = (bf16[1,80,256]{2,1,0:T(8,128)(2,1)S(1)}, bf16[1,80,256]{2,1,0:T(8,128)(2,1)S(1)}, u32[]{:S(2)}, u32[]{:S(2)}) collective-permute-start(bf16[1,80,256]{2,1,0:T(8,128)(2,1)S(1)} %collective-permute-done.14), channel_id=1, source_target_pairs={{0,2},{1,3},{2,0},{3,1},{4,6},{5,7},{6,4},{7,5},{8,10},{9,11},{10,... | collective-permute-start | bytes 122888 | tf_op jit(solution)/shard_map/ppermute | solution.py:39
  45.9 0.0 collective-permute-done.17
  45.9 2.8 %collective-permute-done.18 = bf16[1,80,256]{2,1,0:T(8,128)(2,1)S(1)} collective-permute-done((bf16[1,80,256]{2,1,0:T(8,128)(2,1)S(1)}, bf16[1,80,256]{2,1,0:T(8,128)(2,1)S(1)}, u32[]{:S(2)}, u32[]{:S(2)}) %collective-permute-start.18) | collective-permute-done | bytes 40992 | tf_op jit(solution)/shard_map/ppermute | solution.py:39
  48.7 0.0 collective-permute-done.19
  48.7 0.0 collective-permute-done.20
  48.8 0.1 collective-permute-start.21
  48.8 1.6 %collective-permute-done.21.refs_1_ = bf16[8,80,256]{2,1,0:T(8,128)(2,1)S(1)} collective-permute-done((bf16[8,80,256]{2,1,0:T(8,128)(2,1)S(1)}, bf16[8,80,256]{2,1,0:T(8,128)(2,1)S(1)}, u32[]{:S(2)}, u32[]{:S(2)}) %collective-permute-start.21) | collective-permute-done | bytes 327712 | tf_op jit(solution)/shard_map/ppermute | solution.py:39
  50.5 1.2 %shard_map.116 = (f32[1024,256]{1,0:T(8,128)}, f32[256,256]{1,0:T(8,128)}) custom-call(s32[1]{0:T(128)} %bitcast.me_ref.refs_0_, bf16[8,80,256]{2,1,0:T(8,128)(2,1)S(1)} %constant_dynamic-update-slice_fusion.3.refs_0_, bf16[8,80,256]{2,1,0:T(8,128)(2,1)S(1)} %collective-permute-done.21.refs_1_), custom_call_target="tpu_custom_call" | custom-call | tf_op jit(solution)/shard_map/pallas_call | solution.py:444
  (13 shorter events, 0.1 us)
Async XLA Ops:
  3.5 13.5 %collective-permute-start = (bf16[656,256]{1,0:T(8,128)(2,1)}, bf16[656,256]{1,0:T(8,128)(2,1)S(1)}, u32[]{:S(2)}, u32[]{:S(2)}) collective-permute-start(bf16[656,256]{1,0:T(8,128)(2,1)} %get-tuple-element.17), channel_id=1, source_target_pairs={{0,2},{1,3},{2,0},{3,1},{4,6},{5,7},{6,4},{7,5},{8,10},{9,11},{10,... | collective-permute-start | bytes 1007624 | tf_op jit(solution)/shard_map/ppermute | solution.py:39
  6.5 4.5 %collective-permute-start.5 = (bf16[128,256]{1,0:T(8,128)(2,1)}, bf16[128,256]{1,0:T(8,128)(2,1)S(1)}, u32[]{:S(2)}, u32[]{:S(2)}) collective-permute-start(bf16[128,256]{1,0:T(8,128)(2,1)} %get-tuple-element.18), channel_id=1, source_target_pairs={{0,4},{1,5},{2,6},{3,7},{4,0},{5,1},{6,2},{7,3},{8,12},{9,13},{10,... | collective-permute-start | bytes 196616 | tf_op jit(solution)/shard_map/ppermute | solution.py:39
  8.1 7.2 %collective-permute-start.4 = (bf16[128,256]{1,0:T(8,128)(2,1)}, bf16[128,256]{1,0:T(8,128)(2,1)S(1)}, u32[]{:S(2)}, u32[]{:S(2)}) collective-permute-start(bf16[128,256]{1,0:T(8,128)(2,1)} %get-tuple-element.18), channel_id=1, source_target_pairs={{0,8},{1,9},{2,10},{3,11},{4,12},{5,13},{6,14},{7,15},{8,0},{9,1},... | collective-permute-start | bytes 196616 | tf_op jit(solution)/shard_map/ppermute | solution.py:39
  10.7 6.3 %collective-permute-start.3 = (bf16[128,256]{1,0:T(8,128)(2,1)}, bf16[128,256]{1,0:T(8,128)(2,1)S(1)}, u32[]{:S(2)}, u32[]{:S(2)}) collective-permute-start(bf16[128,256]{1,0:T(8,128)(2,1)} %get-tuple-element.18), channel_id=1, source_target_pairs={{0,12},{1,13},{2,14},{3,15},{4,8},{5,9},{6,10},{7,11},{8,4},{9,5},... | collective-permute-start | bytes 196616 | tf_op jit(solution)/shard_map/ppermute | solution.py:39
  10.9 11.0 %collective-permute-start.1 = (bf16[528,256]{1,0:T(8,128)(2,1)}, bf16[528,256]{1,0:T(8,128)(2,1)S(1)}, u32[]{:S(2)}, u32[]{:S(2)}) collective-permute-start(bf16[528,256]{1,0:T(8,128)(2,1)} %get-tuple-element.16.refs_1_), channel_id=1, source_target_pairs={{0,1},{1,0},{2,3},{3,2},{4,5},{5,4},{6,7},{7,6},{8,9},{9,8},{10,11... | collective-permute-start | bytes 811016 | tf_op jit(solution)/shard_map/ppermute | solution.py:39
  11.0 10.4 %collective-permute-start.8 = (bf16[128,256]{1,0:T(8,128)(2,1)S(1)}, bf16[128,256]{1,0:T(8,128)(2,1)S(1)}, u32[]{:S(2)}, u32[]{:S(2)}) collective-permute-start(bf16[128,256]{1,0:T(8,128)(2,1)S(1)} %collective-permute-done.5), channel_id=1, source_target_pairs={{0,2},{1,3},{2,0},{3,1},{4,6},{5,7},{6,4},{7,5},{8,10},{9,11},{10,... | collective-permute-start | bytes 196616 | tf_op jit(solution)/shard_map/ppermute | solution.py:39
  15.3 6.0 %collective-permute-start.7 = (bf16[128,256]{1,0:T(8,128)(2,1)S(1)}, bf16[128,256]{1,0:T(8,128)(2,1)S(1)}, u32[]{:S(2)}, u32[]{:S(2)}) collective-permute-start(bf16[128,256]{1,0:T(8,128)(2,1)S(1)} %collective-permute-done.4), channel_id=1, source_target_pairs={{0,2},{1,3},{2,0},{3,1},{4,6},{5,7},{6,4},{7,5},{8,10},{9,11},{10,... | collective-permute-start | bytes 196616 | tf_op jit(solution)/shard_map/ppermute | solution.py:39
  17.0 4.3 %collective-permute-start.6 = (bf16[128,256]{1,0:T(8,128)(2,1)S(1)}, bf16[128,256]{1,0:T(8,128)(2,1)S(1)}, u32[]{:S(2)}, u32[]{:S(2)}) collective-permute-start(bf16[128,256]{1,0:T(8,128)(2,1)S(1)} %shard_map.113), channel_id=1, source_target_pairs={{0,2},{1,3},{2,0},{3,1},{4,6},{5,7},{6,4},{7,5},{8,10},{9,11},{10,... | collective-permute-start | bytes 196616 | tf_op jit(solution)/shard_map/ppermute | solution.py:39
  17.5 5.7 %copy-start.1 = (bf16[256,256]{1,0:T(8,128)(2,1)S(1)}, bf16[256,256]{1,0:T(8,128)(2,1)}, u32[]{:S(2)}) copy-start(bf16[256,256]{1,0:T(8,128)(2,1)} %get-tuple-element.20.refs_10_) | copy-start | bytes 393220
  17.6 5.7 %copy-start = (bf16[528,256]{1,0:T(8,128)(2,1)S(1)}, bf16[528,256]{1,0:T(8,128)(2,1)}, u32[]{:S(2)}) copy-start(bf16[528,256]{1,0:T(8,128)(2,1)} %get-tuple-element.16.refs_1_) | copy-start | bytes 811012
  17.6 4.4 %collective-permute-start.9 = (bf16[384,256]{1,0:T(8,128)(2,1)S(1)}, bf16[384,256]{1,0:T(8,128)(2,1)S(1)}, u32[]{:S(2)}, u32[]{:S(2)}) collective-permute-start(bf16[384,256]{1,0:T(8,128)(2,1)S(1)} %pad_maximum_fusion.refs_5_), channel_id=1, source_target_pairs={{0,1},{1,0},{2,3},{3,2},{4,5},{5,4},{6,7},{7,6},{8,9},{9,8},{10,11... | collective-permute-start | bytes 589832 | tf_op jit(solution)/shard_map/ppermute | solution.py:39
  21.3 1.9 %collective-permute-start.2 = (bf16[656,256]{1,0:T(8,128)(2,1)S(1)}, bf16[656,256]{1,0:T(8,128)(2,1)S(1)}, u32[]{:S(2)}, u32[]{:S(2)}) collective-permute-start(bf16[656,256]{1,0:T(8,128)(2,1)S(1)} %collective-permute-done.refs_1_.refs_2_), channel_id=1, source_target_pairs={{0,1},{1,0},{2,3},{3,2},{4,5},{5,4},{6,7},{7,6},{8,9},{9,8},{10,11... | collective-permute-start | bytes 1007624 | tf_op jit(solution)/shard_map/ppermute | solution.py:39
  21.3 1.9 %copy-start.2 = (bf16[128,256]{1,0:T(8,128)(2,1)S(1)}, bf16[128,256]{1,0:T(8,128)(2,1)}, u32[]{:S(2)}) copy-start(bf16[128,256]{1,0:T(8,128)(2,1)} %get-tuple-element.19.refs_9_) | copy-start | bytes 196612
  21.4 1.8 %collective-permute-start.10 = (bf16[384,256]{1,0:T(8,128)(2,1)S(1)}, bf16[384,256]{1,0:T(8,128)(2,1)S(1)}, u32[]{:S(2)}, u32[]{:S(2)}) collective-permute-start(bf16[384,256]{1,0:T(8,128)(2,1)S(1)} %constant_dynamic-update-slice_fusion.refs_6_), channel_id=1, source_target_pairs={{0,1},{1,0},{2,3},{3,2},{4,5},{5,4},{6,7},{7,6},{8,9},{9,8},{10,11... | collective-permute-start | bytes 589832 | tf_op jit(solution)/shard_map/ppermute | solution.py:39
  26.8 6.3 %collective-permute-start.11 = (bf16[96,256]{1,0:T(8,128)(2,1)S(1)}, bf16[96,256]{1,0:T(8,128)(2,1)S(1)}, u32[]{:S(2)}, u32[]{:S(2)}) collective-permute-start(bf16[96,256]{1,0:T(8,128)(2,1)S(1)} %get-tuple-element.22), channel_id=1, source_target_pairs={{0,12},{1,13},{2,14},{3,15},{4,8},{5,9},{6,10},{7,11},{8,4},{9,5},... | collective-permute-start | bytes 147464 | tf_op jit(solution)/shard_map/ppermute | solution.py:39
  29.0 5.5 %collective-permute-start.12 = (bf16[96,256]{1,0:T(8,128)(2,1)S(1)}, bf16[96,256]{1,0:T(8,128)(2,1)S(1)}, u32[]{:S(2)}, u32[]{:S(2)}) collective-permute-start(bf16[96,256]{1,0:T(8,128)(2,1)S(1)} %get-tuple-element.23), channel_id=1, source_target_pairs={{0,8},{1,9},{2,10},{3,11},{4,12},{5,13},{6,14},{7,15},{8,0},{9,1},... | collective-permute-start | bytes 147464 | tf_op jit(solution)/shard_map/ppermute | solution.py:39
  29.0 5.5 %collective-permute-start.13 = (bf16[96,256]{1,0:T(8,128)(2,1)S(1)}, bf16[96,256]{1,0:T(8,128)(2,1)S(1)}, u32[]{:S(2)}, u32[]{:S(2)}) collective-permute-start(bf16[96,256]{1,0:T(8,128)(2,1)S(1)} %get-tuple-element.24), channel_id=1, source_target_pairs={{0,4},{1,5},{2,6},{3,7},{4,0},{5,1},{6,2},{7,3},{8,12},{9,13},{10,... | collective-permute-start | bytes 147464 | tf_op jit(solution)/shard_map/ppermute | solution.py:39
  35.1 10.8 %collective-permute-start.17 = (bf16[1,80,256]{2,1,0:T(8,128)(2,1)S(1)}, bf16[1,80,256]{2,1,0:T(8,128)(2,1)S(1)}, u32[]{:S(2)}, u32[]{:S(2)}) collective-permute-start(bf16[1,80,256]{2,1,0:T(8,128)(2,1)S(1)} %bitcast.6), channel_id=1, source_target_pairs={{0,2},{1,3},{2,0},{3,1},{4,6},{5,7},{6,4},{7,5},{8,10},{9,11},{10,... | collective-permute-start | bytes 122888 | tf_op jit(solution)/shard_map/ppermute | solution.py:39
  36.5 6.2 %collective-permute-start.16 = (bf16[1,80,256]{2,1,0:T(8,128)(2,1)S(1)}, bf16[1,80,256]{2,1,0:T(8,128)(2,1)S(1)}, u32[]{:S(2)}, u32[]{:S(2)}) collective-permute-start(bf16[1,80,256]{2,1,0:T(8,128)(2,1)S(1)} %bitcast.7), channel_id=1, source_target_pairs={{0,12},{1,13},{2,14},{3,15},{4,8},{5,9},{6,10},{7,11},{8,4},{9,5},... | collective-permute-start | bytes 122888 | tf_op jit(solution)/shard_map/ppermute | solution.py:39
  38.7 5.2 %collective-permute-start.15 = (bf16[1,80,256]{2,1,0:T(8,128)(2,1)S(1)}, bf16[1,80,256]{2,1,0:T(8,128)(2,1)S(1)}, u32[]{:S(2)}, u32[]{:S(2)}) collective-permute-start(bf16[1,80,256]{2,1,0:T(8,128)(2,1)S(1)} %bitcast.8), channel_id=1, source_target_pairs={{0,8},{1,9},{2,10},{3,11},{4,12},{5,13},{6,14},{7,15},{8,0},{9,1},... | collective-permute-start | bytes 122888 | tf_op jit(solution)/shard_map/ppermute | solution.py:39
  38.9 5.9 %collective-permute-start.14 = (bf16[1,80,256]{2,1,0:T(8,128)(2,1)S(1)}, bf16[1,80,256]{2,1,0:T(8,128)(2,1)S(1)}, u32[]{:S(2)}, u32[]{:S(2)}) collective-permute-start(bf16[1,80,256]{2,1,0:T(8,128)(2,1)S(1)} %bitcast.9), channel_id=1, source_target_pairs={{0,4},{1,5},{2,6},{3,7},{4,0},{5,1},{6,2},{7,3},{8,12},{9,13},{10,... | collective-permute-start | bytes 122888 | tf_op jit(solution)/shard_map/ppermute | solution.py:39
  42.7 6.1 %collective-permute-start.20 = (bf16[1,80,256]{2,1,0:T(8,128)(2,1)S(1)}, bf16[1,80,256]{2,1,0:T(8,128)(2,1)S(1)}, u32[]{:S(2)}, u32[]{:S(2)}) collective-permute-start(bf16[1,80,256]{2,1,0:T(8,128)(2,1)S(1)} %collective-permute-done.16), channel_id=1, source_target_pairs={{0,2},{1,3},{2,0},{3,1},{4,6},{5,7},{6,4},{7,5},{8,10},{9,11},{10,... | collective-permute-start | bytes 122888 | tf_op jit(solution)/shard_map/ppermute | solution.py:39
  43.8 4.9 %collective-permute-start.19 = (bf16[1,80,256]{2,1,0:T(8,128)(2,1)S(1)}, bf16[1,80,256]{2,1,0:T(8,128)(2,1)S(1)}, u32[]{:S(2)}, u32[]{:S(2)}) collective-permute-start(bf16[1,80,256]{2,1,0:T(8,128)(2,1)S(1)} %collective-permute-done.15), channel_id=1, source_target_pairs={{0,2},{1,3},{2,0},{3,1},{4,6},{5,7},{6,4},{7,5},{8,10},{9,11},{10,... | collective-permute-start | bytes 122888 | tf_op jit(solution)/shard_map/ppermute | solution.py:39
  44.7 4.0 %collective-permute-start.18 = (bf16[1,80,256]{2,1,0:T(8,128)(2,1)S(1)}, bf16[1,80,256]{2,1,0:T(8,128)(2,1)S(1)}, u32[]{:S(2)}, u32[]{:S(2)}) collective-permute-start(bf16[1,80,256]{2,1,0:T(8,128)(2,1)S(1)} %collective-permute-done.14), channel_id=1, source_target_pairs={{0,2},{1,3},{2,0},{3,1},{4,6},{5,7},{6,4},{7,5},{8,10},{9,11},{10,... | collective-permute-start | bytes 122888 | tf_op jit(solution)/shard_map/ppermute | solution.py:39
  48.8 1.7 %collective-permute-start.21 = (bf16[8,80,256]{2,1,0:T(8,128)(2,1)S(1)}, bf16[8,80,256]{2,1,0:T(8,128)(2,1)S(1)}, u32[]{:S(2)}, u32[]{:S(2)}) collective-permute-start(bf16[8,80,256]{2,1,0:T(8,128)(2,1)S(1)} %constant_dynamic-update-slice_fusion.3.refs_0_), channel_id=1, source_target_pairs={{0,1},{1,0},{2,3},{3,2},{4,5},{5,4},{6,7},{7,6},{8,9},{9,8},{10,11... | collective-permute-start | bytes 983048 | tf_op jit(solution)/shard_map/ppermute | solution.py:39

commit v12 on v11

--- a/solution.py
+++ b/solution.py
@@ -19,7 +19,7 @@
 FEAT_AT = (2, 3, 2, 3)
 PAD = 16
 LINE = ((12, 3), (8, 1), (4, 2))
-TURNS = (0, 2, 1, 3, 4, 6, 5, 7)
+TURNS = (0, 4, 2, 1, 3, 6, 5, 7)
 
 
 def dot(left, right):
@@ -184,7 +184,7 @@
     def base(block):
         per = total // (16 * rows)
         way, along, within = block // (4 * per), (block // per) % 4, block % per
-        other = (way >> 1) | ((way & 1) << 1) | ((16 - 4 * along) & 15)
+        other = (way >> 1) | ((way & 1) << 1) | (4 * along)
         return (me ^ (other | (reverse_bits(within, per.bit_length() - 1) << 4))) * rows
 
     def embed(hidden):
@@ -389,7 +389,8 @@
     )
     for mask in reversed(beyond):
         head = jnp.concatenate([head, swap(head, mask, size)], axis=0)
-    line = [head[rows:]] * (len(beyond) > 0) + [swap(head, mask, size) for mask, _ in LINE]
+    line = [swap(head, mask, size) for mask, _ in reversed(LINE)]
+    line = [head[rows:]] * (len(beyond) > 0) + line
     far2 = swap(far, 2, size)
     over = [swap(piece, 2, size) for piece in line[-2:]]
     gated = pack(*line[:-2], after=far2)
@@ -438,8 +439,9 @@
         result = result + swap(result, mask, size)
         note = note + swap(note, mask, size)
     result = result.astype(BF).reshape(1, each, width)
-    pieces = [result] + [swap(result, mask, size) for mask, _ in reversed(LINE)]
-    near = jnp.concatenate(pieces + [swap(piece, 2, size) for piece in pieces], axis=0)
+    pieces = [swap(result, mask, size) for mask, _ in reversed(LINE)]
+    near = [result, swap(result, 2, size)] + pieces + [swap(piece, 2, size) for piece in pieces]
+    near = jnp.concatenate(near, axis=0)
     far = swap(near, 1, size)
     grad_wf, grad_wb = pl.pallas_call(
         functools.partial(

time: 51.8 us -> 50.9 us (0.983)
  waiting for transfers between devices: 20.6 us -> 17.2 us
  starting transfers between devices: 22 us -> 24.6 us
    ppermute x22, waiting for transfers between devices: 20.6 us -> 17.2 us  [swap(): return lax.ppermute(array, 'fa', [(i, i ^ mask) for i in range(size)])]
    ppermute x22, starting transfers between devices: 22 us -> 24.6 us  [swap(): return lax.ppermute(array, 'fa', [(i, i ^ mask) for i in range(size)])]
  transfers between devices with their start and end apart: 22 -> 22, of which waited for: 11 -> 8; matrix products, arithmetic and copies ran while one was open for 0% -> 0% of each run, Pallas kernels for 0% -> 0%
where the time goes in v12:
time: 50.9 us; the launch traced here: 50.7 us
  starting transfers between devices  24.6 us (48%)
  waiting for transfers between devices  17.2 us (34%)
  Pallas kernels  8.09 us (16%)
  between operations  0.8 us (2%)
    ppermute x22, starting transfers between devices, swap(): return lax.ppermute(array, 'fa', [(i, i ^ mask) for i in range(size)])  24.6 us
    ppermute x22, waiting for transfers between devices, swap(): return lax.ppermute(array, 'fa', [(i, i ^ mask) for i in range(size)])  17.2 us
    pallas_call x1, Pallas kernels, body(): pl.pallas_call(functools.partial(pair_kernel, rows=rows, total=total), in...  3.57 us
    pallas_call x1, Pallas kernels, body(): pl.pallas_call(feature_kernel, in_specs=[SMEM] + [HBM] * 9, out_specs=[VM...  2.83 us
    pallas_call x1, Pallas kernels, body(): pl.pallas_call(functools.partial(assemble_kernel, wf_rows=wf_rows, wb_row...  1.16 us
  transfers between devices with their start and end apart: 22, of which 8 were waited for; matrix products, arithmetic and copies ran while one was open for 0% of the time, Pallas kernels for 0%

profile of v12, /device:TPU:0, one launch (start us, length us, event | category | flops | bytes accessed | tf_op | source)
XLA Modules:
  0.0 50.7 jit_solution(4624867609488819320)
XLA Ops:
  0.6 2.8 %shard_map.112 = (bf16[656,256]{1,0:T(8,128)(2,1)}, bf16[528,256]{1,0:T(8,128)(2,1)}, bf16[128,256]{1,0:T(8,128)(2,1)}, bf16[128,256]{1,0:T(8,128)(2,1)}, bf16[256,256]{1,0:T(8,128)(2,1)}) custom-call(s32[1]{0:T(128)} %bitcast.me_ref.refs_0_, bf16[128,1024]{1,0:T(8,128)(2,1)} %hf_hbm.1, bf16[128,1024]{1,0:T(8,128)(2,1)} %ht_hbm.1, bf16[128,256]{1,0:T(8,128)(2,1)} %hb_hbm.1, ...), custom_call_target="tpu_custom_call" | custom-call | flops 134217728 | bytes 1572864 | tf_op jit(solution)/shard_map/pallas_call | solution.py:353
  3.5 3.0 %collective-permute-start = (bf16[656,256]{1,0:T(8,128)(2,1)}, bf16[656,256]{1,0:T(8,128)(2,1)S(1)}, u32[]{:S(2)}, u32[]{:S(2)}) collective-permute-start(bf16[656,256]{1,0:T(8,128)(2,1)} %get-tuple-element.17), channel_id=1, source_target_pairs={{0,2},{1,3},{2,0},{3,1},{4,6},{5,7},{6,4},{7,5},{8,10},{9,11},{10,... | collective-permute-start | bytes 1007624 | tf_op jit(solution)/shard_map/ppermute | solution.py:39
  6.5 3.6 %collective-permute-start.5 = (bf16[128,256]{1,0:T(8,128)(2,1)}, bf16[128,256]{1,0:T(8,128)(2,1)S(1)}, u32[]{:S(2)}, u32[]{:S(2)}) collective-permute-start(bf16[128,256]{1,0:T(8,128)(2,1)} %get-tuple-element.18), channel_id=1, source_target_pairs={{0,12},{1,13},{2,14},{3,15},{4,8},{5,9},{6,10},{7,11},{8,4},{9,5},... | collective-permute-start | bytes 196616 | tf_op jit(solution)/shard_map/ppermute | solution.py:39
  10.1 0.0 collective-permute-start.4
  10.1 0.8 %collective-permute-start.3 = (bf16[128,256]{1,0:T(8,128)(2,1)}, bf16[128,256]{1,0:T(8,128)(2,1)S(1)}, u32[]{:S(2)}, u32[]{:S(2)}) collective-permute-start(bf16[128,256]{1,0:T(8,128)(2,1)} %get-tuple-element.18), channel_id=1, source_target_pairs={{0,4},{1,5},{2,6},{3,7},{4,0},{5,1},{6,2},{7,3},{8,12},{9,13},{10,... | collective-permute-start | bytes 196616 | tf_op jit(solution)/shard_map/ppermute | solution.py:39
  10.9 0.0 collective-permute-start.1
  10.9 2.7 %collective-permute-done.5 = bf16[128,256]{1,0:T(8,128)(2,1)S(1)} collective-permute-done((bf16[128,256]{1,0:T(8,128)(2,1)}, bf16[128,256]{1,0:T(8,128)(2,1)S(1)}, u32[]{:S(2)}, u32[]{:S(2)}) %collective-permute-start.5) | collective-permute-done | bytes 65568 | tf_op jit(solution)/shard_map/ppermute | solution.py:39
  13.6 0.0 collective-permute-start.8
  13.6 2.1 %collective-permute-done.4 = bf16[128,256]{1,0:T(8,128)(2,1)S(1)} collective-permute-done((bf16[128,256]{1,0:T(8,128)(2,1)}, bf16[128,256]{1,0:T(8,128)(2,1)S(1)}, u32[]{:S(2)}, u32[]{:S(2)}) %collective-permute-start.4) | collective-permute-done | bytes 65568 | tf_op jit(solution)/shard_map/ppermute | solution.py:39
  15.7 0.5 collective-permute-start.7
  16.2 0.0 collective-permute-done.3.refs_0_
  16.2 0.0 collective-permute-done.refs_1_.refs_2_
  16.2 1.6 %collective-permute-start.6 = (bf16[128,256]{1,0:T(8,128)(2,1)S(1)}, bf16[128,256]{1,0:T(8,128)(2,1)S(1)}, u32[]{:S(2)}, u32[]{:S(2)}) collective-permute-start(bf16[128,256]{1,0:T(8,128)(2,1)S(1)} %shard_map.113), channel_id=1, source_target_pairs={{0,2},{1,3},{2,0},{3,1},{4,6},{5,7},{6,4},{7,5},{8,10},{9,11},{10,... | collective-permute-start | bytes 196616 | tf_op jit(solution)/shard_map/ppermute | solution.py:39
  17.8 0.0 copy-start.1
  17.8 0.0 copy-start
  17.8 0.1 collective-permute-start.9
  17.9 2.8 %collective-permute-done.6 = bf16[128,256]{1,0:T(8,128)(2,1)S(1)} collective-permute-done((bf16[128,256]{1,0:T(8,128)(2,1)S(1)}, bf16[128,256]{1,0:T(8,128)(2,1)S(1)}, u32[]{:S(2)}, u32[]{:S(2)}) %collective-permute-start.6) | collective-permute-done | bytes 65568 | tf_op jit(solution)/shard_map/ppermute | solution.py:39
  20.7 0.0 collective-permute-start.2
  20.7 0.0 collective-permute-done.7
  20.7 0.0 copy-start.2
  20.7 0.0 collective-permute-done.8
  20.7 0.6 %collective-permute-start.10 = (bf16[384,256]{1,0:T(8,128)(2,1)S(1)}, bf16[384,256]{1,0:T(8,128)(2,1)S(1)}, u32[]{:S(2)}, u32[]{:S(2)}) collective-permute-start(bf16[384,256]{1,0:T(8,128)(2,1)S(1)} %constant_dynamic-update-slice_fusion.refs_6_), channel_id=1, source_target_pairs={{0,1},{1,0},{2,3},{3,2},{4,5},{5,4},{6,7},{7,6},{8,9},{9,8},{10,11... | collective-permute-start | bytes 589832 | tf_op jit(solution)/shard_map/ppermute | solution.py:39
  21.3 0.0 collective-permute-done.1.refs_3_
  21.3 0.0 collective-permute-done.9.refs_7_
  21.3 1.3 %collective-permute-done.10.refs_8_ = bf16[384,256]{1,0:T(8,128)(2,1)S(1)} collective-permute-done((bf16[384,256]{1,0:T(8,128)(2,1)S(1)}, bf16[384,256]{1,0:T(8,128)(2,1)S(1)}, u32[]{:S(2)}, u32[]{:S(2)}) %collective-permute-start.10) | collective-permute-done | bytes 196640 | tf_op jit(solution)/shard_map/ppermute | solution.py:39
  22.6 0.0 collective-permute-done.2.refs_4_
  22.6 0.0 copy-done.1
  22.6 0.0 copy-done
  22.6 0.0 copy-done.2
  22.6 3.6 %shard_map.114 = (f32[96,256]{1,0:T(8,128)S(1)}, bf16[96,256]{1,0:T(8,128)(2,1)S(1)}, bf16[96,256]{1,0:T(8,128)(2,1)S(1)}, bf16[96,256]{1,0:T(8,128)(2,1)S(1)}) custom-call(s32[1]{0:T(128)} %bitcast.me_ref.refs_0_, bf16[528,256]{1,0:T(8,128)(2,1)S(1)} %copy-done, bf16[656,256]{1,0:T(8,128)(2,1)S(1)} %collective-permute-done.refs_1_.refs_2_, ...), custom_call_target="tpu_custom_call" | custom-call | tf_op jit(solution)/shard_map/pallas_call | solution.py:407
  26.2 3.0 %collective-permute-start.11 = (bf16[96,256]{1,0:T(8,128)(2,1)S(1)}, bf16[96,256]{1,0:T(8,128)(2,1)S(1)}, u32[]{:S(2)}, u32[]{:S(2)}) collective-permute-start(bf16[96,256]{1,0:T(8,128)(2,1)S(1)} %get-tuple-element.22), channel_id=1, source_target_pairs={{0,12},{1,13},{2,14},{3,15},{4,8},{5,9},{6,10},{7,11},{8,4},{9,5},... | collective-permute-start | bytes 147464 | tf_op jit(solution)/shard_map/ppermute | solution.py:39
  29.2 0.0 collective-permute-start.12
  29.2 1.4 %collective-permute-start.13 = (bf16[96,256]{1,0:T(8,128)(2,1)S(1)}, bf16[96,256]{1,0:T(8,128)(2,1)S(1)}, u32[]{:S(2)}, u32[]{:S(2)}) collective-permute-start(bf16[96,256]{1,0:T(8,128)(2,1)S(1)} %get-tuple-element.24), channel_id=1, source_target_pairs={{0,4},{1,5},{2,6},{3,7},{4,0},{5,1},{6,2},{7,3},{8,12},{9,13},{10,... | collective-permute-start | bytes 147464 | tf_op jit(solution)/shard_map/ppermute | solution.py:39
  30.6 1.8 %collective-permute-done.11.refs_0_ = bf16[96,256]{1,0:T(8,128)(2,1)S(1)} collective-permute-done((bf16[96,256]{1,0:T(8,128)(2,1)S(1)}, bf16[96,256]{1,0:T(8,128)(2,1)S(1)}, u32[]{:S(2)}, u32[]{:S(2)}) %collective-permute-start.11) | collective-permute-done | bytes 49184 | tf_op jit(solution)/shard_map/ppermute | solution.py:39
  32.5 1.8 %collective-permute-done.12.refs_1_ = bf16[96,256]{1,0:T(8,128)(2,1)S(1)} collective-permute-done((bf16[96,256]{1,0:T(8,128)(2,1)S(1)}, bf16[96,256]{1,0:T(8,128)(2,1)S(1)}, u32[]{:S(2)}, u32[]{:S(2)}) %collective-permute-start.12) | collective-permute-done | bytes 49184 | tf_op jit(solution)/shard_map/ppermute | solution.py:39
  34.2 0.0 collective-permute-done.13.refs_2_
  34.2 0.5 %shard_map.115 = (bf16[80,256]{1,0:T(8,128)(2,1)S(1)}, f32[1,1]{1,0:T(1,128)}) custom-call(f32[96,256]{1,0:T(8,128)S(1)} %get-tuple-element.21.keep_ref, bf16[96,256]{1,0:T(8,128)(2,1)S(1)} %collective-permute-done.11.refs_0_, bf16[96,256]{1,0:T(8,128)(2,1)S(1)} %collective-permute-done.12.refs_1_, bf16[96,256]{1,0:T(8,128)(2,1)S(1)} %collective-permute-done.13.refs_2_), custom_call_target="tpu_custom_call" | custom-call | tf_op jit(solution)/shard_map/pallas_call | solution.py:428
  34.8 2.4 %collective-permute-start.17 = (bf16[1,80,256]{2,1,0:T(8,128)(2,1)S(1)}, bf16[1,80,256]{2,1,0:T(8,128)(2,1)S(1)}, u32[]{:S(2)}, u32[]{:S(2)}) collective-permute-start(bf16[1,80,256]{2,1,0:T(8,128)(2,1)S(1)} %bitcast.6), channel_id=1, source_target_pairs={{0,12},{1,13},{2,14},{3,15},{4,8},{5,9},{6,10},{7,11},{8,4},{9,5},... | collective-permute-start | bytes 122888 | tf_op jit(solution)/shard_map/ppermute | solution.py:39
  37.1 0.0 collective-permute-start.16
  37.1 2.0 %collective-permute-start.15 = (bf16[1,80,256]{2,1,0:T(8,128)(2,1)S(1)}, bf16[1,80,256]{2,1,0:T(8,128)(2,1)S(1)}, u32[]{:S(2)}, u32[]{:S(2)}) collective-permute-start(bf16[1,80,256]{2,1,0:T(8,128)(2,1)S(1)} %bitcast.8), channel_id=1, source_target_pairs={{0,4},{1,5},{2,6},{3,7},{4,0},{5,1},{6,2},{7,3},{8,12},{9,13},{10,... | collective-permute-start | bytes 122888 | tf_op jit(solution)/shard_map/ppermute | solution.py:39
  39.2 1.8 %collective-permute-start.14 = (bf16[1,80,256]{2,1,0:T(8,128)(2,1)S(1)}, bf16[1,80,256]{2,1,0:T(8,128)(2,1)S(1)}, u32[]{:S(2)}, u32[]{:S(2)}) collective-permute-start(bf16[1,80,256]{2,1,0:T(8,128)(2,1)S(1)} %bitcast.9), channel_id=1, source_target_pairs={{0,2},{1,3},{2,0},{3,1},{4,6},{5,7},{6,4},{7,5},{8,10},{9,11},{10,... | collective-permute-start | bytes 122888 | tf_op jit(solution)/shard_map/ppermute | solution.py:39
  40.9 0.0 collective-permute-done.17
  40.9 1.7 %collective-permute-start.20 = (bf16[1,80,256]{2,1,0:T(8,128)(2,1)S(1)}, bf16[1,80,256]{2,1,0:T(8,128)(2,1)S(1)}, u32[]{:S(2)}, u32[]{:S(2)}) collective-permute-start(bf16[1,80,256]{2,1,0:T(8,128)(2,1)S(1)} %collective-permute-done.17), channel_id=1, source_target_pairs={{0,2},{1,3},{2,0},{3,1},{4,6},{5,7},{6,4},{7,5},{8,10},{9,11},{10,... | collective-permute-start | bytes 122888 | tf_op jit(solution)/shard_map/ppermute | solution.py:39
  42.6 0.0 collective-permute-done.16
  42.6 1.2 %collective-permute-start.19 = (bf16[1,80,256]{2,1,0:T(8,128)(2,1)S(1)}, bf16[1,80,256]{2,1,0:T(8,128)(2,1)S(1)}, u32[]{:S(2)}, u32[]{:S(2)}) collective-permute-start(bf16[1,80,256]{2,1,0:T(8,128)(2,1)S(1)} %collective-permute-done.16), channel_id=1, source_target_pairs={{0,2},{1,3},{2,0},{3,1},{4,6},{5,7},{6,4},{7,5},{8,10},{9,11},{10,... | collective-permute-start | bytes 122888 | tf_op jit(solution)/shard_map/ppermute | solution.py:39
  43.8 0.0 collective-permute-done.15
  43.8 0.8 %collective-permute-start.18 = (bf16[1,80,256]{2,1,0:T(8,128)(2,1)S(1)}, bf16[1,80,256]{2,1,0:T(8,128)(2,1)S(1)}, u32[]{:S(2)}, u32[]{:S(2)}) collective-permute-start(bf16[1,80,256]{2,1,0:T(8,128)(2,1)S(1)} %collective-permute-done.15), channel_id=1, source_target_pairs={{0,2},{1,3},{2,0},{3,1},{4,6},{5,7},{6,4},{7,5},{8,10},{9,11},{10,... | collective-permute-start | bytes 122888 | tf_op jit(solution)/shard_map/ppermute | solution.py:39
  44.7 0.0 collective-permute-done.14
  44.7 3.1 %collective-permute-done.18 = bf16[1,80,256]{2,1,0:T(8,128)(2,1)S(1)} collective-permute-done((bf16[1,80,256]{2,1,0:T(8,128)(2,1)S(1)}, bf16[1,80,256]{2,1,0:T(8,128)(2,1)S(1)}, u32[]{:S(2)}, u32[]{:S(2)}) %collective-permute-start.18) | collective-permute-done | bytes 40992 | tf_op jit(solution)/shard_map/ppermute | solution.py:39
  47.8 0.0 collective-permute-done.19
  47.9 0.0 collective-permute-done.20
  47.9 0.1 collective-permute-start.21
  48.0 1.6 %collective-permute-done.21.refs_1_ = bf16[8,80,256]{2,1,0:T(8,128)(2,1)S(1)} collective-permute-done((bf16[8,80,256]{2,1,0:T(8,128)(2,1)S(1)}, bf16[8,80,256]{2,1,0:T(8,128)(2,1)S(1)}, u32[]{:S(2)}, u32[]{:S(2)}) %collective-permute-start.21) | collective-permute-done | bytes 327712 | tf_op jit(solution)/shard_map/ppermute | solution.py:39
  49.6 1.2 %shard_map.116 = (f32[1024,256]{1,0:T(8,128)}, f32[256,256]{1,0:T(8,128)}) custom-call(s32[1]{0:T(128)} %bitcast.me_ref.refs_0_, bf16[8,80,256]{2,1,0:T(8,128)(2,1)S(1)} %constant_dynamic-update-slice_fusion.3.refs_0_, bf16[8,80,256]{2,1,0:T(8,128)(2,1)S(1)} %collective-permute-done.21.refs_1_), custom_call_target="tpu_custom_call" | custom-call | tf_op jit(solution)/shard_map/pallas_call | solution.py:446
  (13 shorter events, 0.1 us)
Async XLA Ops:
  3.5 12.7 %collective-permute-start = (bf16[656,256]{1,0:T(8,128)(2,1)}, bf16[656,256]{1,0:T(8,128)(2,1)S(1)}, u32[]{:S(2)}, u32[]{:S(2)}) collective-permute-start(bf16[656,256]{1,0:T(8,128)(2,1)} %get-tuple-element.17), channel_id=1, source_target_pairs={{0,2},{1,3},{2,0},{3,1},{4,6},{5,7},{6,4},{7,5},{8,10},{9,11},{10,... | collective-permute-start | bytes 1007624 | tf_op jit(solution)/shard_map/ppermute | solution.py:39
  6.5 7.1 %collective-permute-start.5 = (bf16[128,256]{1,0:T(8,128)(2,1)}, bf16[128,256]{1,0:T(8,128)(2,1)S(1)}, u32[]{:S(2)}, u32[]{:S(2)}) collective-permute-start(bf16[128,256]{1,0:T(8,128)(2,1)} %get-tuple-element.18), channel_id=1, source_target_pairs={{0,12},{1,13},{2,14},{3,15},{4,8},{5,9},{6,10},{7,11},{8,4},{9,5},... | collective-permute-start | bytes 196616 | tf_op jit(solution)/shard_map/ppermute | solution.py:39
  10.1 5.6 %collective-permute-start.4 = (bf16[128,256]{1,0:T(8,128)(2,1)}, bf16[128,256]{1,0:T(8,128)(2,1)S(1)}, u32[]{:S(2)}, u32[]{:S(2)}) collective-permute-start(bf16[128,256]{1,0:T(8,128)(2,1)} %get-tuple-element.18), channel_id=1, source_target_pairs={{0,8},{1,9},{2,10},{3,11},{4,12},{5,13},{6,14},{7,15},{8,0},{9,1},... | collective-permute-start | bytes 196616 | tf_op jit(solution)/shard_map/ppermute | solution.py:39
  10.1 6.0 %collective-permute-start.3 = (bf16[128,256]{1,0:T(8,128)(2,1)}, bf16[128,256]{1,0:T(8,128)(2,1)S(1)}, u32[]{:S(2)}, u32[]{:S(2)}) collective-permute-start(bf16[128,256]{1,0:T(8,128)(2,1)} %get-tuple-element.18), channel_id=1, source_target_pairs={{0,4},{1,5},{2,6},{3,7},{4,0},{5,1},{6,2},{7,3},{8,12},{9,13},{10,... | collective-permute-start | bytes 196616 | tf_op jit(solution)/shard_map/ppermute | solution.py:39
  10.9 10.4 %collective-permute-start.1 = (bf16[528,256]{1,0:T(8,128)(2,1)}, bf16[528,256]{1,0:T(8,128)(2,1)S(1)}, u32[]{:S(2)}, u32[]{:S(2)}) collective-permute-start(bf16[528,256]{1,0:T(8,128)(2,1)} %get-tuple-element.16.refs_1_), channel_id=1, source_target_pairs={{0,1},{1,0},{2,3},{3,2},{4,5},{5,4},{6,7},{7,6},{8,9},{9,8},{10,11... | collective-permute-start | bytes 811016 | tf_op jit(solution)/shard_map/ppermute | solution.py:39
  13.6 7.1 %collective-permute-start.8 = (bf16[128,256]{1,0:T(8,128)(2,1)S(1)}, bf16[128,256]{1,0:T(8,128)(2,1)S(1)}, u32[]{:S(2)}, u32[]{:S(2)}) collective-permute-start(bf16[128,256]{1,0:T(8,128)(2,1)S(1)} %collective-permute-done.5), channel_id=1, source_target_pairs={{0,2},{1,3},{2,0},{3,1},{4,6},{5,7},{6,4},{7,5},{8,10},{9,11},{10,... | collective-permute-start | bytes 196616 | tf_op jit(solution)/shard_map/ppermute | solution.py:39
  15.7 5.0 %collective-permute-start.7 = (bf16[128,256]{1,0:T(8,128)(2,1)S(1)}, bf16[128,256]{1,0:T(8,128)(2,1)S(1)}, u32[]{:S(2)}, u32[]{:S(2)}) collective-permute-start(bf16[128,256]{1,0:T(8,128)(2,1)S(1)} %collective-permute-done.4), channel_id=1, source_target_pairs={{0,2},{1,3},{2,0},{3,1},{4,6},{5,7},{6,4},{7,5},{8,10},{9,11},{10,... | collective-permute-start | bytes 196616 | tf_op jit(solution)/shard_map/ppermute | solution.py:39
  16.2 4.5 %collective-permute-start.6 = (bf16[128,256]{1,0:T(8,128)(2,1)S(1)}, bf16[128,256]{1,0:T(8,128)(2,1)S(1)}, u32[]{:S(2)}, u32[]{:S(2)}) collective-permute-start(bf16[128,256]{1,0:T(8,128)(2,1)S(1)} %shard_map.113), channel_id=1, source_target_pairs={{0,2},{1,3},{2,0},{3,1},{4,6},{5,7},{6,4},{7,5},{8,10},{9,11},{10,... | collective-permute-start | bytes 196616 | tf_op jit(solution)/shard_map/ppermute | solution.py:39
  17.8 4.8 %copy-start.1 = (bf16[256,256]{1,0:T(8,128)(2,1)S(1)}, bf16[256,256]{1,0:T(8,128)(2,1)}, u32[]{:S(2)}) copy-start(bf16[256,256]{1,0:T(8,128)(2,1)} %get-tuple-element.20.refs_10_) | copy-start | bytes 393220
  17.8 4.8 %copy-start = (bf16[528,256]{1,0:T(8,128)(2,1)S(1)}, bf16[528,256]{1,0:T(8,128)(2,1)}, u32[]{:S(2)}) copy-start(bf16[528,256]{1,0:T(8,128)(2,1)} %get-tuple-element.16.refs_1_) | copy-start | bytes 811012
  17.8 3.5 %collective-permute-start.9 = (bf16[384,256]{1,0:T(8,128)(2,1)S(1)}, bf16[384,256]{1,0:T(8,128)(2,1)S(1)}, u32[]{:S(2)}, u32[]{:S(2)}) collective-permute-start(bf16[384,256]{1,0:T(8,128)(2,1)S(1)} %pad_maximum_fusion.refs_5_), channel_id=1, source_target_pairs={{0,1},{1,0},{2,3},{3,2},{4,5},{5,4},{6,7},{7,6},{8,9},{9,8},{10,11... | collective-permute-start | bytes 589832 | tf_op jit(solution)/shard_map/ppermute | solution.py:39
  20.7 1.9 %collective-permute-start.2 = (bf16[656,256]{1,0:T(8,128)(2,1)S(1)}, bf16[656,256]{1,0:T(8,128)(2,1)S(1)}, u32[]{:S(2)}, u32[]{:S(2)}) collective-permute-start(bf16[656,256]{1,0:T(8,128)(2,1)S(1)} %collective-permute-done.refs_1_.refs_2_), channel_id=1, source_target_pairs={{0,1},{1,0},{2,3},{3,2},{4,5},{5,4},{6,7},{7,6},{8,9},{9,8},{10,11... | collective-permute-start | bytes 1007624 | tf_op jit(solution)/shard_map/ppermute | solution.py:39
  20.7 1.9 %copy-start.2 = (bf16[128,256]{1,0:T(8,128)(2,1)S(1)}, bf16[128,256]{1,0:T(8,128)(2,1)}, u32[]{:S(2)}) copy-start(bf16[128,256]{1,0:T(8,128)(2,1)} %get-tuple-element.19.refs_9_) | copy-start | bytes 196612
  20.7 1.8 %collective-permute-start.10 = (bf16[384,256]{1,0:T(8,128)(2,1)S(1)}, bf16[384,256]{1,0:T(8,128)(2,1)S(1)}, u32[]{:S(2)}, u32[]{:S(2)}) collective-permute-start(bf16[384,256]{1,0:T(8,128)(2,1)S(1)} %constant_dynamic-update-slice_fusion.refs_6_), channel_id=1, source_target_pairs={{0,1},{1,0},{2,3},{3,2},{4,5},{5,4},{6,7},{7,6},{8,9},{9,8},{10,11... | collective-permute-start | bytes 589832 | tf_op jit(solution)/shard_map/ppermute | solution.py:39
  26.2 6.3 %collective-permute-start.11 = (bf16[96,256]{1,0:T(8,128)(2,1)S(1)}, bf16[96,256]{1,0:T(8,128)(2,1)S(1)}, u32[]{:S(2)}, u32[]{:S(2)}) collective-permute-start(bf16[96,256]{1,0:T(8,128)(2,1)S(1)} %get-tuple-element.22), channel_id=1, source_target_pairs={{0,12},{1,13},{2,14},{3,15},{4,8},{5,9},{6,10},{7,11},{8,4},{9,5},... | collective-permute-start | bytes 147464 | tf_op jit(solution)/shard_map/ppermute | solution.py:39
  29.2 5.1 %collective-permute-start.12 = (bf16[96,256]{1,0:T(8,128)(2,1)S(1)}, bf16[96,256]{1,0:T(8,128)(2,1)S(1)}, u32[]{:S(2)}, u32[]{:S(2)}) collective-permute-start(bf16[96,256]{1,0:T(8,128)(2,1)S(1)} %get-tuple-element.23), channel_id=1, source_target_pairs={{0,8},{1,9},{2,10},{3,11},{4,12},{5,13},{6,14},{7,15},{8,0},{9,1},... | collective-permute-start | bytes 147464 | tf_op jit(solution)/shard_map/ppermute | solution.py:39
  29.2 5.1 %collective-permute-start.13 = (bf16[96,256]{1,0:T(8,128)(2,1)S(1)}, bf16[96,256]{1,0:T(8,128)(2,1)S(1)}, u32[]{:S(2)}, u32[]{:S(2)}) collective-permute-start(bf16[96,256]{1,0:T(8,128)(2,1)S(1)} %get-tuple-element.24), channel_id=1, source_target_pairs={{0,4},{1,5},{2,6},{3,7},{4,0},{5,1},{6,2},{7,3},{8,12},{9,13},{10,... | collective-permute-start | bytes 147464 | tf_op jit(solution)/shard_map/ppermute | solution.py:39
  34.8 6.2 %collective-permute-start.17 = (bf16[1,80,256]{2,1,0:T(8,128)(2,1)S(1)}, bf16[1,80,256]{2,1,0:T(8,128)(2,1)S(1)}, u32[]{:S(2)}, u32[]{:S(2)}) collective-permute-start(bf16[1,80,256]{2,1,0:T(8,128)(2,1)S(1)} %bitcast.6), channel_id=1, source_target_pairs={{0,12},{1,13},{2,14},{3,15},{4,8},{5,9},{6,10},{7,11},{8,4},{9,5},... | collective-permute-start | bytes 122888 | tf_op jit(solution)/shard_map/ppermute | solution.py:39
  37.1 5.5 %collective-permute-start.16 = (bf16[1,80,256]{2,1,0:T(8,128)(2,1)S(1)}, bf16[1,80,256]{2,1,0:T(8,128)(2,1)S(1)}, u32[]{:S(2)}, u32[]{:S(2)}) collective-permute-start(bf16[1,80,256]{2,1,0:T(8,128)(2,1)S(1)} %bitcast.7), channel_id=1, source_target_pairs={{0,8},{1,9},{2,10},{3,11},{4,12},{5,13},{6,14},{7,15},{8,0},{9,1},... | collective-permute-start | bytes 122888 | tf_op jit(solution)/shard_map/ppermute | solution.py:39
  37.1 6.7 %collective-permute-start.15 = (bf16[1,80,256]{2,1,0:T(8,128)(2,1)S(1)}, bf16[1,80,256]{2,1,0:T(8,128)(2,1)S(1)}, u32[]{:S(2)}, u32[]{:S(2)}) collective-permute-start(bf16[1,80,256]{2,1,0:T(8,128)(2,1)S(1)} %bitcast.8), channel_id=1, source_target_pairs={{0,4},{1,5},{2,6},{3,7},{4,0},{5,1},{6,2},{7,3},{8,12},{9,13},{10,... | collective-permute-start | bytes 122888 | tf_op jit(solution)/shard_map/ppermute | solution.py:39
  39.2 5.5 %collective-permute-start.14 = (bf16[1,80,256]{2,1,0:T(8,128)(2,1)S(1)}, bf16[1,80,256]{2,1,0:T(8,128)(2,1)S(1)}, u32[]{:S(2)}, u32[]{:S(2)}) collective-permute-start(bf16[1,80,256]{2,1,0:T(8,128)(2,1)S(1)} %bitcast.9), channel_id=1, source_target_pairs={{0,2},{1,3},{2,0},{3,1},{4,6},{5,7},{6,4},{7,5},{8,10},{9,11},{10,... | collective-permute-start | bytes 122888 | tf_op jit(solution)/shard_map/ppermute | solution.py:39
  40.9 6.9 %collective-permute-start.20 = (bf16[1,80,256]{2,1,0:T(8,128)(2,1)S(1)}, bf16[1,80,256]{2,1,0:T(8,128)(2,1)S(1)}, u32[]{:S(2)}, u32[]{:S(2)}) collective-permute-start(bf16[1,80,256]{2,1,0:T(8,128)(2,1)S(1)} %collective-permute-done.17), channel_id=1, source_target_pairs={{0,2},{1,3},{2,0},{3,1},{4,6},{5,7},{6,4},{7,5},{8,10},{9,11},{10,... | collective-permute-start | bytes 122888 | tf_op jit(solution)/shard_map/ppermute | solution.py:39
  42.6 5.2 %collective-permute-start.19 = (bf16[1,80,256]{2,1,0:T(8,128)(2,1)S(1)}, bf16[1,80,256]{2,1,0:T(8,128)(2,1)S(1)}, u32[]{:S(2)}, u32[]{:S(2)}) collective-permute-start(bf16[1,80,256]{2,1,0:T(8,128)(2,1)S(1)} %collective-permute-done.16), channel_id=1, source_target_pairs={{0,2},{1,3},{2,0},{3,1},{4,6},{5,7},{6,4},{7,5},{8,10},{9,11},{10,... | collective-permute-start | bytes 122888 | tf_op jit(solution)/shard_map/ppermute | solution.py:39
  43.8 4.0 %collective-permute-start.18 = (bf16[1,80,256]{2,1,0:T(8,128)(2,1)S(1)}, bf16[1,80,256]{2,1,0:T(8,128)(2,1)S(1)}, u32[]{:S(2)}, u32[]{:S(2)}) collective-permute-start(bf16[1,80,256]{2,1,0:T(8,128)(2,1)S(1)} %collective-permute-done.15), channel_id=1, source_target_pairs={{0,2},{1,3},{2,0},{3,1},{4,6},{5,7},{6,4},{7,5},{8,10},{9,11},{10,... | collective-permute-start | bytes 122888 | tf_op jit(solution)/shard_map/ppermute | solution.py:39
  47.9 1.7 %collective-permute-start.21 = (bf16[8,80,256]{2,1,0:T(8,128)(2,1)S(1)}, bf16[8,80,256]{2,1,0:T(8,128)(2,1)S(1)}, u32[]{:S(2)}, u32[]{:S(2)}) collective-permute-start(bf16[8,80,256]{2,1,0:T(8,128)(2,1)S(1)} %constant_dynamic-update-slice_fusion.3.refs_0_), channel_id=1, source_target_pairs={{0,1},{1,0},{2,3},{3,2},{4,5},{5,4},{6,7},{7,6},{8,9},{9,8},{10,11... | collective-permute-start | bytes 983048 | tf_op jit(solution)/shard_map/ppermute | solution.py:39

commit v13 on v12

--- a/solution.py
+++ b/solution.py
@@ -318,23 +318,28 @@
     note_ref[...] = note * (1.0 / width)
 
 
-def assemble_kernel(me_ref, *refs, wf_rows, wb_rows, factor_f, factor_b):
-    place = reverse_bits(me_ref[0] & 15, 4)
-    wf_ref, wb_ref = refs[2:]
-    for offset, ref in zip((0, 8), refs):
-        for e, turn in enumerate(TURNS):
-            to = place ^ (offset + turn)
-            wf_ref[pl.ds(pl.multiple_of(to * wf_rows, wf_rows), wf_rows), :] = (
-                ref[e, :wf_rows, :].astype(F32) * factor_f
+def assemble_kernel(me_ref, part_ref, *refs, offset, wf_rows, wb_rows, factor_f, factor_b):
+    wf_hbm, wb_hbm, wf_buf, wb_buf, sems = refs[-5:]
+    place = reverse_bits(me_ref[0] & 15, 4) ^ offset
+    moves = []
+    for e, turn in enumerate(TURNS):
+        to = place ^ turn
+        wf_buf[e] = part_ref[e, :wf_rows, :].astype(F32) * factor_f
+        wb_buf[e] = part_ref[e, wf_rows:, :].astype(F32) * factor_b
+        for k, (buf, hbm, rows) in enumerate(((wf_buf, wf_hbm, wf_rows), (wb_buf, wb_hbm, wb_rows))):
+            move = pltpu.make_async_copy(
+                buf.at[e], hbm.at[pl.ds(pl.multiple_of(to * rows, rows), rows), :], sems.at[2 * e + k]
             )
-            wb_ref[pl.ds(pl.multiple_of(to * wb_rows, wb_rows), wb_rows), :] = (
-                ref[e, wf_rows:, :].astype(F32) * factor_b
-            )
+            move.start()
+            moves.append(move)
+    for move in moves:
+        move.wait()
 
 
 SMEM = pl.BlockSpec(memory_space=pltpu.SMEM)
 VMEM = pl.BlockSpec(memory_space=pltpu.VMEM)
 HBM = pl.BlockSpec(memory_space=pltpu.HBM)
+ANY = pl.BlockSpec(memory_space=pl.ANY)
 
 
 def body(hidden_f, hidden_t, hidden_b, w_f, w_t, w_b, latents, latent_ids, positives):
@@ -443,22 +448,33 @@
     near = [result, swap(result, 2, size)] + pieces + [swap(piece, 2, size) for piece in pieces]
     near = jnp.concatenate(near, axis=0)
     far = swap(near, 1, size)
-    grad_wf, grad_wb = pl.pallas_call(
-        functools.partial(
-            assemble_kernel,
-            wf_rows=wf_rows,
-            wb_rows=wb_rows,
-            factor_f=math.sqrt(high),
-            factor_b=math.sqrt(wide),
-        ),
-        in_specs=[SMEM] + [VMEM] * 2,
-        out_specs=[VMEM] * 2,
-        out_shape=[
-            jax.ShapeDtypeStruct((high, width), F32),
-            jax.ShapeDtypeStruct((wide, width), F32),
-        ],
-        compiler_params=pltpu.CompilerParams(vmem_limit_bytes=16 * 2**20),
-    )(me, near, far)
+
+    def assemble(part, offset, *begun):
+        return pl.pallas_call(
+            functools.partial(
+                assemble_kernel,
+                offset=offset,
+                wf_rows=wf_rows,
+                wb_rows=wb_rows,
+                factor_f=math.sqrt(high),
+                factor_b=math.sqrt(wide),
+            ),
+            in_specs=[SMEM, VMEM] + [ANY] * len(begun),
+            out_specs=[ANY] * 2,
+            out_shape=[
+                jax.ShapeDtypeStruct((high, width), F32),
+                jax.ShapeDtypeStruct((wide, width), F32),
+            ],
+            scratch_shapes=[
+                pltpu.VMEM((8, wf_rows, width), F32),
+                pltpu.VMEM((8, wb_rows, width), F32),
+                pltpu.SemaphoreType.DMA((16,)),
+            ],
+            input_output_aliases={2 + k: k for k in range(len(begun))},
+            compiler_params=pltpu.CompilerParams(vmem_limit_bytes=8 * 2**20),
+        )(me, part, *begun)
+
+    grad_wf, grad_wb = assemble(far, 8, *assemble(near, 0))
     return (grad_wf, grad_wb, note.reshape(1))
 
 

time: 50.9 us -> 50.7 us (level)
  waiting for transfers between devices: 17.2 us -> 16.2 us
  Pallas kernels: 8.09 us -> 8.86 us
    ppermute x22, waiting for transfers between devices: 17.2 us -> 16.2 us  [swap(): return lax.ppermute(array, 'fa', [(i, i ^ mask) for i in range(size)])]
    pallas_call x1 -> x2, Pallas kernels: 1.16 us -> 1.93 us  [assemble(): pl.pallas_call(functools.partial(assemble_kernel, offset=offset, wf_rows=...]
  transfers between devices with their start and end apart: 22 -> 22, of which waited for: 8 -> 8; matrix products, arithmetic and copies ran while one was open for 0% -> 0% of each run, Pallas kernels for 0% -> 2%
where the time goes in v13:
time: 50.7 us; the launch traced here: 50.5 us
  starting transfers between devices  24.6 us (49%)
  waiting for transfers between devices  16.2 us (32%)
  Pallas kernels  8.86 us (17%)
  between operations  0.81 us (2%)
    ppermute x22, starting transfers between devices, swap(): return lax.ppermute(array, 'fa', [(i, i ^ mask) for i in range(size)])  24.6 us
    ppermute x22, waiting for transfers between devices, swap(): return lax.ppermute(array, 'fa', [(i, i ^ mask) for i in range(size)])  16.2 us
    pallas_call x1, Pallas kernels, body(): pl.pallas_call(functools.partial(pair_kernel, rows=rows, total=total), in...  3.57 us
    pallas_call x1, Pallas kernels, body(): pl.pallas_call(feature_kernel, in_specs=[SMEM] + [HBM] * 9, out_specs=[VM...  2.83 us
    pallas_call x2, Pallas kernels, assemble(): pl.pallas_call(functools.partial(assemble_kernel, offset=offset, wf_rows=...  1.93 us
  transfers between devices with their start and end apart: 22, of which 8 were waited for; matrix products, arithmetic and copies ran while one was open for 0% of the time, Pallas kernels for 2%

profile of v13, /device:TPU:0, one launch (start us, length us, event | category | flops | bytes accessed | tf_op | source)
XLA Modules:
  0.0 50.5 jit_solution(14375450680771192361)
XLA Ops:
  0.6 2.8 %shard_map.112 = (bf16[656,256]{1,0:T(8,128)(2,1)}, bf16[528,256]{1,0:T(8,128)(2,1)}, bf16[128,256]{1,0:T(8,128)(2,1)}, bf16[128,256]{1,0:T(8,128)(2,1)}, bf16[256,256]{1,0:T(8,128)(2,1)}) custom-call(s32[1]{0:T(128)} %bitcast.me_ref.refs_0_, bf16[128,1024]{1,0:T(8,128)(2,1)} %hf_hbm.1, bf16[128,1024]{1,0:T(8,128)(2,1)} %ht_hbm.1, bf16[128,256]{1,0:T(8,128)(2,1)} %hb_hbm.1, ...), custom_call_target="tpu_custom_call" | custom-call | flops 134217728 | bytes 1572864 | tf_op jit(solution)/shard_map/pallas_call | solution.py:358
  3.5 3.0 %collective-permute-start = (bf16[656,256]{1,0:T(8,128)(2,1)}, bf16[656,256]{1,0:T(8,128)(2,1)S(1)}, u32[]{:S(2)}, u32[]{:S(2)}) collective-permute-start(bf16[656,256]{1,0:T(8,128)(2,1)} %get-tuple-element.19), channel_id=1, source_target_pairs={{0,2},{1,3},{2,0},{3,1},{4,6},{5,7},{6,4},{7,5},{8,10},{9,11},{10,... | collective-permute-start | bytes 1007624 | tf_op jit(solution)/shard_map/ppermute | solution.py:39
  6.5 3.6 %collective-permute-start.5 = (bf16[128,256]{1,0:T(8,128)(2,1)}, bf16[128,256]{1,0:T(8,128)(2,1)S(1)}, u32[]{:S(2)}, u32[]{:S(2)}) collective-permute-start(bf16[128,256]{1,0:T(8,128)(2,1)} %get-tuple-element.20), channel_id=1, source_target_pairs={{0,12},{1,13},{2,14},{3,15},{4,8},{5,9},{6,10},{7,11},{8,4},{9,5},... | collective-permute-start | bytes 196616 | tf_op jit(solution)/shard_map/ppermute | solution.py:39
  10.1 0.0 collective-permute-start.4
  10.1 0.8 %collective-permute-start.3 = (bf16[128,256]{1,0:T(8,128)(2,1)}, bf16[128,256]{1,0:T(8,128)(2,1)S(1)}, u32[]{:S(2)}, u32[]{:S(2)}) collective-permute-start(bf16[128,256]{1,0:T(8,128)(2,1)} %get-tuple-element.20), channel_id=1, source_target_pairs={{0,4},{1,5},{2,6},{3,7},{4,0},{5,1},{6,2},{7,3},{8,12},{9,13},{10,... | collective-permute-start | bytes 196616 | tf_op jit(solution)/shard_map/ppermute | solution.py:39
  10.9 0.0 collective-permute-start.1
  10.9 2.7 %collective-permute-done.5 = bf16[128,256]{1,0:T(8,128)(2,1)S(1)} collective-permute-done((bf16[128,256]{1,0:T(8,128)(2,1)}, bf16[128,256]{1,0:T(8,128)(2,1)S(1)}, u32[]{:S(2)}, u32[]{:S(2)}) %collective-permute-start.5) | collective-permute-done | bytes 65568 | tf_op jit(solution)/shard_map/ppermute | solution.py:39
  13.6 0.0 collective-permute-start.8
  13.6 2.1 %collective-permute-done.4 = bf16[128,256]{1,0:T(8,128)(2,1)S(1)} collective-permute-done((bf16[128,256]{1,0:T(8,128)(2,1)}, bf16[128,256]{1,0:T(8,128)(2,1)S(1)}, u32[]{:S(2)}, u32[]{:S(2)}) %collective-permute-start.4) | collective-permute-done | bytes 65568 | tf_op jit(solution)/shard_map/ppermute | solution.py:39
  15.7 0.5 collective-permute-start.7
  16.2 0.0 collective-permute-done.3.refs_0_
  16.2 0.0 collective-permute-done.refs_1_.refs_2_
  16.2 1.6 %collective-permute-start.6 = (bf16[128,256]{1,0:T(8,128)(2,1)S(1)}, bf16[128,256]{1,0:T(8,128)(2,1)S(1)}, u32[]{:S(2)}, u32[]{:S(2)}) collective-permute-start(bf16[128,256]{1,0:T(8,128)(2,1)S(1)} %shard_map.113), channel_id=1, source_target_pairs={{0,2},{1,3},{2,0},{3,1},{4,6},{5,7},{6,4},{7,5},{8,10},{9,11},{10,... | collective-permute-start | bytes 196616 | tf_op jit(solution)/shard_map/ppermute | solution.py:39
  17.8 0.0 copy-start.1
  17.8 0.0 copy-start
  17.8 0.1 collective-permute-start.9
  17.9 2.8 %collective-permute-done.6 = bf16[128,256]{1,0:T(8,128)(2,1)S(1)} collective-permute-done((bf16[128,256]{1,0:T(8,128)(2,1)S(1)}, bf16[128,256]{1,0:T(8,128)(2,1)S(1)}, u32[]{:S(2)}, u32[]{:S(2)}) %collective-permute-start.6) | collective-permute-done | bytes 65568 | tf_op jit(solution)/shard_map/ppermute | solution.py:39
  20.7 0.0 collective-permute-start.2
  20.7 0.0 collective-permute-done.7
  20.7 0.0 copy-start.2
  20.7 0.0 collective-permute-done.8
  20.7 0.6 %collective-permute-start.10 = (bf16[384,256]{1,0:T(8,128)(2,1)S(1)}, bf16[384,256]{1,0:T(8,128)(2,1)S(1)}, u32[]{:S(2)}, u32[]{:S(2)}) collective-permute-start(bf16[384,256]{1,0:T(8,128)(2,1)S(1)} %constant_dynamic-update-slice_fusion.refs_6_), channel_id=1, source_target_pairs={{0,1},{1,0},{2,3},{3,2},{4,5},{5,4},{6,7},{7,6},{8,9},{9,8},{10,11... | collective-permute-start | bytes 589832 | tf_op jit(solution)/shard_map/ppermute | solution.py:39
  21.3 0.0 collective-permute-done.1.refs_3_
  21.3 0.0 collective-permute-done.9.refs_7_
  21.3 1.3 %collective-permute-done.10.refs_8_ = bf16[384,256]{1,0:T(8,128)(2,1)S(1)} collective-permute-done((bf16[384,256]{1,0:T(8,128)(2,1)S(1)}, bf16[384,256]{1,0:T(8,128)(2,1)S(1)}, u32[]{:S(2)}, u32[]{:S(2)}) %collective-permute-start.10) | collective-permute-done | bytes 196640 | tf_op jit(solution)/shard_map/ppermute | solution.py:39
  22.6 0.0 collective-permute-done.2.refs_4_
  22.6 0.0 copy-done.1
  22.6 0.0 copy-done
  22.6 0.0 copy-done.2
  22.6 3.6 %shard_map.114 = (f32[96,256]{1,0:T(8,128)S(1)}, bf16[96,256]{1,0:T(8,128)(2,1)S(1)}, bf16[96,256]{1,0:T(8,128)(2,1)S(1)}, bf16[96,256]{1,0:T(8,128)(2,1)S(1)}) custom-call(s32[1]{0:T(128)} %bitcast.me_ref.refs_0_, bf16[528,256]{1,0:T(8,128)(2,1)S(1)} %copy-done, bf16[656,256]{1,0:T(8,128)(2,1)S(1)} %collective-permute-done.refs_1_.refs_2_, ...), custom_call_target="tpu_custom_call" | custom-call | tf_op jit(solution)/shard_map/pallas_call | solution.py:412
  26.2 3.0 %collective-permute-start.11 = (bf16[96,256]{1,0:T(8,128)(2,1)S(1)}, bf16[96,256]{1,0:T(8,128)(2,1)S(1)}, u32[]{:S(2)}, u32[]{:S(2)}) collective-permute-start(bf16[96,256]{1,0:T(8,128)(2,1)S(1)} %get-tuple-element.24), channel_id=1, source_target_pairs={{0,12},{1,13},{2,14},{3,15},{4,8},{5,9},{6,10},{7,11},{8,4},{9,5},... | collective-permute-start | bytes 147464 | tf_op jit(solution)/shard_map/ppermute | solution.py:39
  29.2 0.0 collective-permute-start.12
  29.2 1.4 %collective-permute-start.13 = (bf16[96,256]{1,0:T(8,128)(2,1)S(1)}, bf16[96,256]{1,0:T(8,128)(2,1)S(1)}, u32[]{:S(2)}, u32[]{:S(2)}) collective-permute-start(bf16[96,256]{1,0:T(8,128)(2,1)S(1)} %get-tuple-element.26), channel_id=1, source_target_pairs={{0,4},{1,5},{2,6},{3,7},{4,0},{5,1},{6,2},{7,3},{8,12},{9,13},{10,... | collective-permute-start | bytes 147464 | tf_op jit(solution)/shard_map/ppermute | solution.py:39
  30.6 1.8 %collective-permute-done.11.refs_0_ = bf16[96,256]{1,0:T(8,128)(2,1)S(1)} collective-permute-done((bf16[96,256]{1,0:T(8,128)(2,1)S(1)}, bf16[96,256]{1,0:T(8,128)(2,1)S(1)}, u32[]{:S(2)}, u32[]{:S(2)}) %collective-permute-start.11) | collective-permute-done | bytes 49184 | tf_op jit(solution)/shard_map/ppermute | solution.py:39
  32.5 1.8 %collective-permute-done.12.refs_1_ = bf16[96,256]{1,0:T(8,128)(2,1)S(1)} collective-permute-done((bf16[96,256]{1,0:T(8,128)(2,1)S(1)}, bf16[96,256]{1,0:T(8,128)(2,1)S(1)}, u32[]{:S(2)}, u32[]{:S(2)}) %collective-permute-start.12) | collective-permute-done | bytes 49184 | tf_op jit(solution)/shard_map/ppermute | solution.py:39
  34.2 0.0 collective-permute-done.13.refs_2_
  34.2 0.5 %shard_map.115 = (bf16[80,256]{1,0:T(8,128)(2,1)S(1)}, f32[1,1]{1,0:T(1,128)}) custom-call(f32[96,256]{1,0:T(8,128)S(1)} %get-tuple-element.23.keep_ref, bf16[96,256]{1,0:T(8,128)(2,1)S(1)} %collective-permute-done.11.refs_0_, bf16[96,256]{1,0:T(8,128)(2,1)S(1)} %collective-permute-done.12.refs_1_, bf16[96,256]{1,0:T(8,128)(2,1)S(1)} %collective-permute-done.13.refs_2_), custom_call_target="tpu_custom_call" | custom-call | tf_op jit(solution)/shard_map/pallas_call | solution.py:433
  34.8 2.4 %collective-permute-start.17 = (bf16[1,80,256]{2,1,0:T(8,128)(2,1)S(1)}, bf16[1,80,256]{2,1,0:T(8,128)(2,1)S(1)}, u32[]{:S(2)}, u32[]{:S(2)}) collective-permute-start(bf16[1,80,256]{2,1,0:T(8,128)(2,1)S(1)} %bitcast.6), channel_id=1, source_target_pairs={{0,12},{1,13},{2,14},{3,15},{4,8},{5,9},{6,10},{7,11},{8,4},{9,5},... | collective-permute-start | bytes 122888 | tf_op jit(solution)/shard_map/ppermute | solution.py:39
  37.1 0.0 collective-permute-start.16
  37.1 2.0 %collective-permute-start.15 = (bf16[1,80,256]{2,1,0:T(8,128)(2,1)S(1)}, bf16[1,80,256]{2,1,0:T(8,128)(2,1)S(1)}, u32[]{:S(2)}, u32[]{:S(2)}) collective-permute-start(bf16[1,80,256]{2,1,0:T(8,128)(2,1)S(1)} %bitcast.8), channel_id=1, source_target_pairs={{0,4},{1,5},{2,6},{3,7},{4,0},{5,1},{6,2},{7,3},{8,12},{9,13},{10,... | collective-permute-start | bytes 122888 | tf_op jit(solution)/shard_map/ppermute | solution.py:39
  39.2 1.8 %collective-permute-start.14 = (bf16[1,80,256]{2,1,0:T(8,128)(2,1)S(1)}, bf16[1,80,256]{2,1,0:T(8,128)(2,1)S(1)}, u32[]{:S(2)}, u32[]{:S(2)}) collective-permute-start(bf16[1,80,256]{2,1,0:T(8,128)(2,1)S(1)} %bitcast.9), channel_id=1, source_target_pairs={{0,2},{1,3},{2,0},{3,1},{4,6},{5,7},{6,4},{7,5},{8,10},{9,11},{10,... | collective-permute-start | bytes 122888 | tf_op jit(solution)/shard_map/ppermute | solution.py:39
  40.9 0.0 collective-permute-done.17
  40.9 1.7 %collective-permute-start.20 = (bf16[1,80,256]{2,1,0:T(8,128)(2,1)S(1)}, bf16[1,80,256]{2,1,0:T(8,128)(2,1)S(1)}, u32[]{:S(2)}, u32[]{:S(2)}) collective-permute-start(bf16[1,80,256]{2,1,0:T(8,128)(2,1)S(1)} %collective-permute-done.17), channel_id=1, source_target_pairs={{0,2},{1,3},{2,0},{3,1},{4,6},{5,7},{6,4},{7,5},{8,10},{9,11},{10,... | collective-permute-start | bytes 122888 | tf_op jit(solution)/shard_map/ppermute | solution.py:39
  42.6 0.0 collective-permute-done.16
  42.6 1.2 %collective-permute-start.19 = (bf16[1,80,256]{2,1,0:T(8,128)(2,1)S(1)}, bf16[1,80,256]{2,1,0:T(8,128)(2,1)S(1)}, u32[]{:S(2)}, u32[]{:S(2)}) collective-permute-start(bf16[1,80,256]{2,1,0:T(8,128)(2,1)S(1)} %collective-permute-done.16), channel_id=1, source_target_pairs={{0,2},{1,3},{2,0},{3,1},{4,6},{5,7},{6,4},{7,5},{8,10},{9,11},{10,... | collective-permute-start | bytes 122888 | tf_op jit(solution)/shard_map/ppermute | solution.py:39
  43.8 0.0 collective-permute-done.15
  43.8 0.8 %collective-permute-start.18 = (bf16[1,80,256]{2,1,0:T(8,128)(2,1)S(1)}, bf16[1,80,256]{2,1,0:T(8,128)(2,1)S(1)}, u32[]{:S(2)}, u32[]{:S(2)}) collective-permute-start(bf16[1,80,256]{2,1,0:T(8,128)(2,1)S(1)} %collective-permute-done.15), channel_id=1, source_target_pairs={{0,2},{1,3},{2,0},{3,1},{4,6},{5,7},{6,4},{7,5},{8,10},{9,11},{10,... | collective-permute-start | bytes 122888 | tf_op jit(solution)/shard_map/ppermute | solution.py:39
  44.7 0.0 collective-permute-done.14
  44.7 3.1 %collective-permute-done.18 = bf16[1,80,256]{2,1,0:T(8,128)(2,1)S(1)} collective-permute-done((bf16[1,80,256]{2,1,0:T(8,128)(2,1)S(1)}, bf16[1,80,256]{2,1,0:T(8,128)(2,1)S(1)}, u32[]{:S(2)}, u32[]{:S(2)}) %collective-permute-start.18) | collective-permute-done | bytes 40992 | tf_op jit(solution)/shard_map/ppermute | solution.py:39
  47.8 0.0 collective-permute-done.19
  47.9 0.0 collective-permute-done.20
  47.9 0.1 collective-permute-start.21
  48.0 1.0 %shard_map.116 = (f32[1024,256]{1,0:T(8,128)}, f32[256,256]{1,0:T(8,128)}) custom-call(s32[1]{0:T(128)} %bitcast.me_ref.refs_0_, bf16[8,80,256]{2,1,0:T(8,128)(2,1)S(1)} %constant_dynamic-update-slice_fusion.3.part_ref), custom_call_target="tpu_custom_call" | custom-call | tf_op jit(solution)/shard_map/pallas_call | solution.py:453
  48.9 0.6 %collective-permute-done.21.part_ref = bf16[8,80,256]{2,1,0:T(8,128)(2,1)S(1)} collective-permute-done((bf16[8,80,256]{2,1,0:T(8,128)(2,1)S(1)}, bf16[8,80,256]{2,1,0:T(8,128)(2,1)S(1)}, u32[]{:S(2)}, u32[]{:S(2)}) %collective-permute-start.21) | collective-permute-done | bytes 327712 | tf_op jit(solution)/shard_map/ppermute | solution.py:39
  49.6 1.0 %shard_map.117 = (f32[1024,256]{1,0:T(8,128)}, f32[256,256]{1,0:T(8,128)}) custom-call(s32[1]{0:T(128)} %bitcast.me_ref.refs_0_, bf16[8,80,256]{2,1,0:T(8,128)(2,1)S(1)} %collective-permute-done.21.part_ref, f32[1024,256]{1,0:T(8,128)} %get-tuple-element.28.refs_0_, f32[256,256]{1,0:T(8,128)} %get-tuple-element.29.refs_1_), custom_call_target="tpu_custom_call", output_to_operand_aliasing={{0}: (2, {}), {1}: (3, {})} | custom-call | tf_op jit(solution)/shard_map/pallas_call | solution.py:453
  (13 shorter events, 0.1 us)
Async XLA Ops:
  3.5 12.7 %collective-permute-start = (bf16[656,256]{1,0:T(8,128)(2,1)}, bf16[656,256]{1,0:T(8,128)(2,1)S(1)}, u32[]{:S(2)}, u32[]{:S(2)}) collective-permute-start(bf16[656,256]{1,0:T(8,128)(2,1)} %get-tuple-element.19), channel_id=1, source_target_pairs={{0,2},{1,3},{2,0},{3,1},{4,6},{5,7},{6,4},{7,5},{8,10},{9,11},{10,... | collective-permute-start | bytes 1007624 | tf_op jit(solution)/shard_map/ppermute | solution.py:39
  6.5 7.1 %collective-permute-start.5 = (bf16[128,256]{1,0:T(8,128)(2,1)}, bf16[128,256]{1,0:T(8,128)(2,1)S(1)}, u32[]{:S(2)}, u32[]{:S(2)}) collective-permute-start(bf16[128,256]{1,0:T(8,128)(2,1)} %get-tuple-element.20), channel_id=1, source_target_pairs={{0,12},{1,13},{2,14},{3,15},{4,8},{5,9},{6,10},{7,11},{8,4},{9,5},... | collective-permute-start | bytes 196616 | tf_op jit(solution)/shard_map/ppermute | solution.py:39
  10.1 5.6 %collective-permute-start.4 = (bf16[128,256]{1,0:T(8,128)(2,1)}, bf16[128,256]{1,0:T(8,128)(2,1)S(1)}, u32[]{:S(2)}, u32[]{:S(2)}) collective-permute-start(bf16[128,256]{1,0:T(8,128)(2,1)} %get-tuple-element.20), channel_id=1, source_target_pairs={{0,8},{1,9},{2,10},{3,11},{4,12},{5,13},{6,14},{7,15},{8,0},{9,1},... | collective-permute-start | bytes 196616 | tf_op jit(solution)/shard_map/ppermute | solution.py:39
  10.1 6.0 %collective-permute-start.3 = (bf16[128,256]{1,0:T(8,128)(2,1)}, bf16[128,256]{1,0:T(8,128)(2,1)S(1)}, u32[]{:S(2)}, u32[]{:S(2)}) collective-permute-start(bf16[128,256]{1,0:T(8,128)(2,1)} %get-tuple-element.20), channel_id=1, source_target_pairs={{0,4},{1,5},{2,6},{3,7},{4,0},{5,1},{6,2},{7,3},{8,12},{9,13},{10,... | collective-permute-start | bytes 196616 | tf_op jit(solution)/shard_map/ppermute | solution.py:39
  10.9 10.4 %collective-permute-start.1 = (bf16[528,256]{1,0:T(8,128)(2,1)}, bf16[528,256]{1,0:T(8,128)(2,1)S(1)}, u32[]{:S(2)}, u32[]{:S(2)}) collective-permute-start(bf16[528,256]{1,0:T(8,128)(2,1)} %get-tuple-element.18.refs_1_), channel_id=1, source_target_pairs={{0,1},{1,0},{2,3},{3,2},{4,5},{5,4},{6,7},{7,6},{8,9},{9,8},{10,11... | collective-permute-start | bytes 811016 | tf_op jit(solution)/shard_map/ppermute | solution.py:39
  13.6 7.1 %collective-permute-start.8 = (bf16[128,256]{1,0:T(8,128)(2,1)S(1)}, bf16[128,256]{1,0:T(8,128)(2,1)S(1)}, u32[]{:S(2)}, u32[]{:S(2)}) collective-permute-start(bf16[128,256]{1,0:T(8,128)(2,1)S(1)} %collective-permute-done.5), channel_id=1, source_target_pairs={{0,2},{1,3},{2,0},{3,1},{4,6},{5,7},{6,4},{7,5},{8,10},{9,11},{10,... | collective-permute-start | bytes 196616 | tf_op jit(solution)/shard_map/ppermute | solution.py:39
  15.7 5.0 %collective-permute-start.7 = (bf16[128,256]{1,0:T(8,128)(2,1)S(1)}, bf16[128,256]{1,0:T(8,128)(2,1)S(1)}, u32[]{:S(2)}, u32[]{:S(2)}) collective-permute-start(bf16[128,256]{1,0:T(8,128)(2,1)S(1)} %collective-permute-done.4), channel_id=1, source_target_pairs={{0,2},{1,3},{2,0},{3,1},{4,6},{5,7},{6,4},{7,5},{8,10},{9,11},{10,... | collective-permute-start | bytes 196616 | tf_op jit(solution)/shard_map/ppermute | solution.py:39
  16.2 4.5 %collective-permute-start.6 = (bf16[128,256]{1,0:T(8,128)(2,1)S(1)}, bf16[128,256]{1,0:T(8,128)(2,1)S(1)}, u32[]{:S(2)}, u32[]{:S(2)}) collective-permute-start(bf16[128,256]{1,0:T(8,128)(2,1)S(1)} %shard_map.113), channel_id=1, source_target_pairs={{0,2},{1,3},{2,0},{3,1},{4,6},{5,7},{6,4},{7,5},{8,10},{9,11},{10,... | collective-permute-start | bytes 196616 | tf_op jit(solution)/shard_map/ppermute | solution.py:39
  17.8 4.8 %copy-start.1 = (bf16[256,256]{1,0:T(8,128)(2,1)S(1)}, bf16[256,256]{1,0:T(8,128)(2,1)}, u32[]{:S(2)}) copy-start(bf16[256,256]{1,0:T(8,128)(2,1)} %get-tuple-element.22.refs_10_) | copy-start | bytes 393220
  17.8 4.8 %copy-start = (bf16[528,256]{1,0:T(8,128)(2,1)S(1)}, bf16[528,256]{1,0:T(8,128)(2,1)}, u32[]{:S(2)}) copy-start(bf16[528,256]{1,0:T(8,128)(2,1)} %get-tuple-element.18.refs_1_) | copy-start | bytes 811012
  17.8 3.5 %collective-permute-start.9 = (bf16[384,256]{1,0:T(8,128)(2,1)S(1)}, bf16[384,256]{1,0:T(8,128)(2,1)S(1)}, u32[]{:S(2)}, u32[]{:S(2)}) collective-permute-start(bf16[384,256]{1,0:T(8,128)(2,1)S(1)} %pad_maximum_fusion.refs_5_), channel_id=1, source_target_pairs={{0,1},{1,0},{2,3},{3,2},{4,5},{5,4},{6,7},{7,6},{8,9},{9,8},{10,11... | collective-permute-start | bytes 589832 | tf_op jit(solution)/shard_map/ppermute | solution.py:39
  20.7 1.9 %collective-permute-start.2 = (bf16[656,256]{1,0:T(8,128)(2,1)S(1)}, bf16[656,256]{1,0:T(8,128)(2,1)S(1)}, u32[]{:S(2)}, u32[]{:S(2)}) collective-permute-start(bf16[656,256]{1,0:T(8,128)(2,1)S(1)} %collective-permute-done.refs_1_.refs_2_), channel_id=1, source_target_pairs={{0,1},{1,0},{2,3},{3,2},{4,5},{5,4},{6,7},{7,6},{8,9},{9,8},{10,11... | collective-permute-start | bytes 1007624 | tf_op jit(solution)/shard_map/ppermute | solution.py:39
  20.7 1.9 %copy-start.2 = (bf16[128,256]{1,0:T(8,128)(2,1)S(1)}, bf16[128,256]{1,0:T(8,128)(2,1)}, u32[]{:S(2)}) copy-start(bf16[128,256]{1,0:T(8,128)(2,1)} %get-tuple-element.21.refs_9_) | copy-start | bytes 196612
  20.7 1.8 %collective-permute-start.10 = (bf16[384,256]{1,0:T(8,128)(2,1)S(1)}, bf16[384,256]{1,0:T(8,128)(2,1)S(1)}, u32[]{:S(2)}, u32[]{:S(2)}) collective-permute-start(bf16[384,256]{1,0:T(8,128)(2,1)S(1)} %constant_dynamic-update-slice_fusion.refs_6_), channel_id=1, source_target_pairs={{0,1},{1,0},{2,3},{3,2},{4,5},{5,4},{6,7},{7,6},{8,9},{9,8},{10,11... | collective-permute-start | bytes 589832 | tf_op jit(solution)/shard_map/ppermute | solution.py:39
  26.2 6.3 %collective-permute-start.11 = (bf16[96,256]{1,0:T(8,128)(2,1)S(1)}, bf16[96,256]{1,0:T(8,128)(2,1)S(1)}, u32[]{:S(2)}, u32[]{:S(2)}) collective-permute-start(bf16[96,256]{1,0:T(8,128)(2,1)S(1)} %get-tuple-element.24), channel_id=1, source_target_pairs={{0,12},{1,13},{2,14},{3,15},{4,8},{5,9},{6,10},{7,11},{8,4},{9,5},... | collective-permute-start | bytes 147464 | tf_op jit(solution)/shard_map/ppermute | solution.py:39
  29.2 5.1 %collective-permute-start.12 = (bf16[96,256]{1,0:T(8,128)(2,1)S(1)}, bf16[96,256]{1,0:T(8,128)(2,1)S(1)}, u32[]{:S(2)}, u32[]{:S(2)}) collective-permute-start(bf16[96,256]{1,0:T(8,128)(2,1)S(1)} %get-tuple-element.25), channel_id=1, source_target_pairs={{0,8},{1,9},{2,10},{3,11},{4,12},{5,13},{6,14},{7,15},{8,0},{9,1},... | collective-permute-start | bytes 147464 | tf_op jit(solution)/shard_map/ppermute | solution.py:39
  29.2 5.1 %collective-permute-start.13 = (bf16[96,256]{1,0:T(8,128)(2,1)S(1)}, bf16[96,256]{1,0:T(8,128)(2,1)S(1)}, u32[]{:S(2)}, u32[]{:S(2)}) collective-permute-start(bf16[96,256]{1,0:T(8,128)(2,1)S(1)} %get-tuple-element.26), channel_id=1, source_target_pairs={{0,4},{1,5},{2,6},{3,7},{4,0},{5,1},{6,2},{7,3},{8,12},{9,13},{10,... | collective-permute-start | bytes 147464 | tf_op jit(solution)/shard_map/ppermute | solution.py:39
  34.8 6.2 %collective-permute-start.17 = (bf16[1,80,256]{2,1,0:T(8,128)(2,1)S(1)}, bf16[1,80,256]{2,1,0:T(8,128)(2,1)S(1)}, u32[]{:S(2)}, u32[]{:S(2)}) collective-permute-start(bf16[1,80,256]{2,1,0:T(8,128)(2,1)S(1)} %bitcast.6), channel_id=1, source_target_pairs={{0,12},{1,13},{2,14},{3,15},{4,8},{5,9},{6,10},{7,11},{8,4},{9,5},... | collective-permute-start | bytes 122888 | tf_op jit(solution)/shard_map/ppermute | solution.py:39
  37.1 5.5 %collective-permute-start.16 = (bf16[1,80,256]{2,1,0:T(8,128)(2,1)S(1)}, bf16[1,80,256]{2,1,0:T(8,128)(2,1)S(1)}, u32[]{:S(2)}, u32[]{:S(2)}) collective-permute-start(bf16[1,80,256]{2,1,0:T(8,128)(2,1)S(1)} %bitcast.7), channel_id=1, source_target_pairs={{0,8},{1,9},{2,10},{3,11},{4,12},{5,13},{6,14},{7,15},{8,0},{9,1},... | collective-permute-start | bytes 122888 | tf_op jit(solution)/shard_map/ppermute | solution.py:39
  37.1 6.7 %collective-permute-start.15 = (bf16[1,80,256]{2,1,0:T(8,128)(2,1)S(1)}, bf16[1,80,256]{2,1,0:T(8,128)(2,1)S(1)}, u32[]{:S(2)}, u32[]{:S(2)}) collective-permute-start(bf16[1,80,256]{2,1,0:T(8,128)(2,1)S(1)} %bitcast.8), channel_id=1, source_target_pairs={{0,4},{1,5},{2,6},{3,7},{4,0},{5,1},{6,2},{7,3},{8,12},{9,13},{10,... | collective-permute-start | bytes 122888 | tf_op jit(solution)/shard_map/ppermute | solution.py:39
  39.2 5.5 %collective-permute-start.14 = (bf16[1,80,256]{2,1,0:T(8,128)(2,1)S(1)}, bf16[1,80,256]{2,1,0:T(8,128)(2,1)S(1)}, u32[]{:S(2)}, u32[]{:S(2)}) collective-permute-start(bf16[1,80,256]{2,1,0:T(8,128)(2,1)S(1)} %bitcast.9), channel_id=1, source_target_pairs={{0,2},{1,3},{2,0},{3,1},{4,6},{5,7},{6,4},{7,5},{8,10},{9,11},{10,... | collective-permute-start | bytes 122888 | tf_op jit(solution)/shard_map/ppermute | solution.py:39
  40.9 6.9 %collective-permute-start.20 = (bf16[1,80,256]{2,1,0:T(8,128)(2,1)S(1)}, bf16[1,80,256]{2,1,0:T(8,128)(2,1)S(1)}, u32[]{:S(2)}, u32[]{:S(2)}) collective-permute-start(bf16[1,80,256]{2,1,0:T(8,128)(2,1)S(1)} %collective-permute-done.17), channel_id=1, source_target_pairs={{0,2},{1,3},{2,0},{3,1},{4,6},{5,7},{6,4},{7,5},{8,10},{9,11},{10,... | collective-permute-start | bytes 122888 | tf_op jit(solution)/shard_map/ppermute | solution.py:39
  42.6 5.2 %collective-permute-start.19 = (bf16[1,80,256]{2,1,0:T(8,128)(2,1)S(1)}, bf16[1,80,256]{2,1,0:T(8,128)(2,1)S(1)}, u32[]{:S(2)}, u32[]{:S(2)}) collective-permute-start(bf16[1,80,256]{2,1,0:T(8,128)(2,1)S(1)} %collective-permute-done.16), channel_id=1, source_target_pairs={{0,2},{1,3},{2,0},{3,1},{4,6},{5,7},{6,4},{7,5},{8,10},{9,11},{10,... | collective-permute-start | bytes 122888 | tf_op jit(solution)/shard_map/ppermute | solution.py:39
  43.8 4.0 %collective-permute-start.18 = (bf16[1,80,256]{2,1,0:T(8,128)(2,1)S(1)}, bf16[1,80,256]{2,1,0:T(8,128)(2,1)S(1)}, u32[]{:S(2)}, u32[]{:S(2)}) collective-permute-start(bf16[1,80,256]{2,1,0:T(8,128)(2,1)S(1)} %collective-permute-done.15), channel_id=1, source_target_pairs={{0,2},{1,3},{2,0},{3,1},{4,6},{5,7},{6,4},{7,5},{8,10},{9,11},{10,... | collective-permute-start | bytes 122888 | tf_op jit(solution)/shard_map/ppermute | solution.py:39
  47.9 1.7 %collective-permute-start.21 = (bf16[8,80,256]{2,1,0:T(8,128)(2,1)S(1)}, bf16[8,80,256]{2,1,0:T(8,128)(2,1)S(1)}, u32[]{:S(2)}, u32[]{:S(2)}) collective-permute-start(bf16[8,80,256]{2,1,0:T(8,128)(2,1)S(1)} %constant_dynamic-update-slice_fusion.3.part_ref), channel_id=1, source_target_pairs={{0,1},{1,0},{2,3},{3,2},{4,5},{5,4},{6,7},{7,6},{8,9},{9,8},{10,11... | collective-permute-start | bytes 983048 | tf_op jit(solution)/shard_map/ppermute | solution.py:39

commit v14 on v13

--- a/solution.py
+++ b/solution.py
@@ -19,7 +19,7 @@
 FEAT_AT = (2, 3, 2, 3)
 PAD = 16
 LINE = ((12, 3), (8, 1), (4, 2))
-TURNS = (0, 4, 2, 1, 3, 6, 5, 7)
+TURNS = (2, 1, 3, 0, 6, 5, 7, 4)
 
 
 def dot(left, right):
@@ -444,9 +444,9 @@
         result = result + swap(result, mask, size)
         note = note + swap(note, mask, size)
     result = result.astype(BF).reshape(1, each, width)
-    pieces = [swap(result, mask, size) for mask, _ in reversed(LINE)]
-    near = [result, swap(result, 2, size)] + pieces + [swap(piece, 2, size) for piece in pieces]
-    near = jnp.concatenate(near, axis=0)
+    piece12, piece8, piece4 = [swap(result, mask, size) for mask, _ in LINE]
+    pairs = [jnp.concatenate(pair, axis=0) for pair in ((piece4, piece8), (piece12, result))]
+    near = jnp.concatenate(pairs + [swap(pair, 2, size) for pair in pairs], axis=0)
     far = swap(near, 1, size)
 
     def assemble(part, offset, *begun):

time: 50.7 us -> 50.1 us (0.988)
  starting transfers between devices: 24.6 us -> 22.4 us
  waiting for transfers between devices: 16.2 us -> 17.8 us
    ppermute x22 -> x20, starting transfers between devices: 24.6 us -> 22.4 us  [swap(): return lax.ppermute(array, 'fa', [(i, i ^ mask) for i in range(size)])]
    ppermute x22 -> x20, waiting for transfers between devices: 16.2 us -> 17.8 us  [swap(): return lax.ppermute(array, 'fa', [(i, i ^ mask) for i in range(size)])]
  transfers between devices with their start and end apart: 22 -> 20, of which waited for: 8 -> 9; matrix products, arithmetic and copies ran while one was open for 0% -> 0% of each run, Pallas kernels for 2% -> 2%
where the time goes in v14:
time: 50.1 us; the launch traced here: 49.9 us
  starting transfers between devices  22.4 us (45%)
  waiting for transfers between devices  17.8 us (36%)
  Pallas kernels  8.86 us (18%)
  between operations  0.81 us (2%)
    ppermute x20, starting transfers between devices, swap(): return lax.ppermute(array, 'fa', [(i, i ^ mask) for i in range(size)])  22.4 us
    ppermute x20, waiting for transfers between devices, swap(): return lax.ppermute(array, 'fa', [(i, i ^ mask) for i in range(size)])  17.8 us
    pallas_call x1, Pallas kernels, body(): pl.pallas_call(functools.partial(pair_kernel, rows=rows, total=total), in...  3.57 us
    pallas_call x1, Pallas kernels, body(): pl.pallas_call(feature_kernel, in_specs=[SMEM] + [HBM] * 9, out_specs=[VM...  2.83 us
    pallas_call x2, Pallas kernels, assemble(): pl.pallas_call(functools.partial(assemble_kernel, offset=offset, wf_rows=...  1.93 us
  transfers between devices with their start and end apart: 20, of which 9 were waited for; matrix products, arithmetic and copies ran while one was open for 0% of the time, Pallas kernels for 2%

profile of v14, /device:TPU:0, one launch (start us, length us, event | category | flops | bytes accessed | tf_op | source)
XLA Modules:
  0.0 49.9 jit_solution(16234393990875949877)
XLA Ops:
  0.6 2.8 %shard_map.112 = (bf16[656,256]{1,0:T(8,128)(2,1)}, bf16[528,256]{1,0:T(8,128)(2,1)}, bf16[128,256]{1,0:T(8,128)(2,1)}, bf16[128,256]{1,0:T(8,128)(2,1)}, bf16[256,256]{1,0:T(8,128)(2,1)}) custom-call(s32[1]{0:T(128)} %bitcast.me_ref.refs_0_, bf16[128,1024]{1,0:T(8,128)(2,1)} %hf_hbm.1, bf16[128,1024]{1,0:T(8,128)(2,1)} %ht_hbm.1, bf16[128,256]{1,0:T(8,128)(2,1)} %hb_hbm.1, ...), custom_call_target="tpu_custom_call" | custom-call | flops 134217728 | bytes 1572864 | tf_op jit(solution)/shard_map/pallas_call | solution.py:358
  3.5 3.0 %collective-permute-start = (bf16[656,256]{1,0:T(8,128)(2,1)}, bf16[656,256]{1,0:T(8,128)(2,1)S(1)}, u32[]{:S(2)}, u32[]{:S(2)}) collective-permute-start(bf16[656,256]{1,0:T(8,128)(2,1)} %get-tuple-element.19), channel_id=1, source_target_pairs={{0,2},{1,3},{2,0},{3,1},{4,6},{5,7},{6,4},{7,5},{8,10},{9,11},{10,... | collective-permute-start | bytes 1007624 | tf_op jit(solution)/shard_map/ppermute | solution.py:39
  6.5 3.6 %collective-permute-start.5 = (bf16[128,256]{1,0:T(8,128)(2,1)}, bf16[128,256]{1,0:T(8,128)(2,1)S(1)}, u32[]{:S(2)}, u32[]{:S(2)}) collective-permute-start(bf16[128,256]{1,0:T(8,128)(2,1)} %get-tuple-element.20), channel_id=1, source_target_pairs={{0,12},{1,13},{2,14},{3,15},{4,8},{5,9},{6,10},{7,11},{8,4},{9,5},... | collective-permute-start | bytes 196616 | tf_op jit(solution)/shard_map/ppermute | solution.py:39
  10.1 0.0 collective-permute-start.4
  10.1 0.8 %collective-permute-start.3 = (bf16[128,256]{1,0:T(8,128)(2,1)}, bf16[128,256]{1,0:T(8,128)(2,1)S(1)}, u32[]{:S(2)}, u32[]{:S(2)}) collective-permute-start(bf16[128,256]{1,0:T(8,128)(2,1)} %get-tuple-element.20), channel_id=1, source_target_pairs={{0,4},{1,5},{2,6},{3,7},{4,0},{5,1},{6,2},{7,3},{8,12},{9,13},{10,... | collective-permute-start | bytes 196616 | tf_op jit(solution)/shard_map/ppermute | solution.py:39
  10.9 0.0 collective-permute-start.1
  10.9 2.7 %collective-permute-done.5 = bf16[128,256]{1,0:T(8,128)(2,1)S(1)} collective-permute-done((bf16[128,256]{1,0:T(8,128)(2,1)}, bf16[128,256]{1,0:T(8,128)(2,1)S(1)}, u32[]{:S(2)}, u32[]{:S(2)}) %collective-permute-start.5) | collective-permute-done | bytes 65568 | tf_op jit(solution)/shard_map/ppermute | solution.py:39
  13.6 0.0 collective-permute-start.8
  13.6 2.1 %collective-permute-done.4 = bf16[128,256]{1,0:T(8,128)(2,1)S(1)} collective-permute-done((bf16[128,256]{1,0:T(8,128)(2,1)}, bf16[128,256]{1,0:T(8,128)(2,1)S(1)}, u32[]{:S(2)}, u32[]{:S(2)}) %collective-permute-start.4) | collective-permute-done | bytes 65568 | tf_op jit(solution)/shard_map/ppermute | solution.py:39
  15.7 0.5 collective-permute-start.7
  16.2 0.0 collective-permute-done.3.refs_0_
  16.2 0.0 collective-permute-done.refs_1_.refs_2_
  16.2 1.6 %collective-permute-start.6 = (bf16[128,256]{1,0:T(8,128)(2,1)S(1)}, bf16[128,256]{1,0:T(8,128)(2,1)S(1)}, u32[]{:S(2)}, u32[]{:S(2)}) collective-permute-start(bf16[128,256]{1,0:T(8,128)(2,1)S(1)} %shard_map.113), channel_id=1, source_target_pairs={{0,2},{1,3},{2,0},{3,1},{4,6},{5,7},{6,4},{7,5},{8,10},{9,11},{10,... | collective-permute-start | bytes 196616 | tf_op jit(solution)/shard_map/ppermute | solution.py:39
  17.8 0.0 copy-start.1
  17.8 0.0 copy-start
  17.8 0.1 collective-permute-start.9
  17.9 2.8 %collective-permute-done.6 = bf16[128,256]{1,0:T(8,128)(2,1)S(1)} collective-permute-done((bf16[128,256]{1,0:T(8,128)(2,1)S(1)}, bf16[128,256]{1,0:T(8,128)(2,1)S(1)}, u32[]{:S(2)}, u32[]{:S(2)}) %collective-permute-start.6) | collective-permute-done | bytes 65568 | tf_op jit(solution)/shard_map/ppermute | solution.py:39
  20.7 0.0 collective-permute-start.2
  20.7 0.0 collective-permute-done.7
  20.7 0.0 copy-start.2
  20.7 0.0 collective-permute-done.8
  20.7 0.6 %collective-permute-start.10 = (bf16[384,256]{1,0:T(8,128)(2,1)S(1)}, bf16[384,256]{1,0:T(8,128)(2,1)S(1)}, u32[]{:S(2)}, u32[]{:S(2)}) collective-permute-start(bf16[384,256]{1,0:T(8,128)(2,1)S(1)} %constant_dynamic-update-slice_fusion.refs_6_), channel_id=1, source_target_pairs={{0,1},{1,0},{2,3},{3,2},{4,5},{5,4},{6,7},{7,6},{8,9},{9,8},{10,11... | collective-permute-start | bytes 589832 | tf_op jit(solution)/shard_map/ppermute | solution.py:39
  21.3 0.0 collective-permute-done.1.refs_3_
  21.3 0.0 collective-permute-done.9.refs_7_
  21.3 1.3 %collective-permute-done.10.refs_8_ = bf16[384,256]{1,0:T(8,128)(2,1)S(1)} collective-permute-done((bf16[384,256]{1,0:T(8,128)(2,1)S(1)}, bf16[384,256]{1,0:T(8,128)(2,1)S(1)}, u32[]{:S(2)}, u32[]{:S(2)}) %collective-permute-start.10) | collective-permute-done | bytes 196640 | tf_op jit(solution)/shard_map/ppermute | solution.py:39
  22.6 0.0 collective-permute-done.2.refs_4_
  22.6 0.0 copy-done.1
  22.6 0.0 copy-done
  22.6 0.0 copy-done.2
  22.6 3.6 %shard_map.114 = (f32[96,256]{1,0:T(8,128)S(1)}, bf16[96,256]{1,0:T(8,128)(2,1)S(1)}, bf16[96,256]{1,0:T(8,128)(2,1)S(1)}, bf16[96,256]{1,0:T(8,128)(2,1)S(1)}) custom-call(s32[1]{0:T(128)} %bitcast.me_ref.refs_0_, bf16[528,256]{1,0:T(8,128)(2,1)S(1)} %copy-done, bf16[656,256]{1,0:T(8,128)(2,1)S(1)} %collective-permute-done.refs_1_.refs_2_, ...), custom_call_target="tpu_custom_call" | custom-call | tf_op jit(solution)/shard_map/pallas_call | solution.py:412
  26.2 3.0 %collective-permute-start.11 = (bf16[96,256]{1,0:T(8,128)(2,1)S(1)}, bf16[96,256]{1,0:T(8,128)(2,1)S(1)}, u32[]{:S(2)}, u32[]{:S(2)}) collective-permute-start(bf16[96,256]{1,0:T(8,128)(2,1)S(1)} %get-tuple-element.24), channel_id=1, source_target_pairs={{0,12},{1,13},{2,14},{3,15},{4,8},{5,9},{6,10},{7,11},{8,4},{9,5},... | collective-permute-start | bytes 147464 | tf_op jit(solution)/shard_map/ppermute | solution.py:39
  29.2 0.0 collective-permute-start.12
  29.2 1.4 %collective-permute-start.13 = (bf16[96,256]{1,0:T(8,128)(2,1)S(1)}, bf16[96,256]{1,0:T(8,128)(2,1)S(1)}, u32[]{:S(2)}, u32[]{:S(2)}) collective-permute-start(bf16[96,256]{1,0:T(8,128)(2,1)S(1)} %get-tuple-element.26), channel_id=1, source_target_pairs={{0,4},{1,5},{2,6},{3,7},{4,0},{5,1},{6,2},{7,3},{8,12},{9,13},{10,... | collective-permute-start | bytes 147464 | tf_op jit(solution)/shard_map/ppermute | solution.py:39
  30.6 1.8 %collective-permute-done.11.refs_0_ = bf16[96,256]{1,0:T(8,128)(2,1)S(1)} collective-permute-done((bf16[96,256]{1,0:T(8,128)(2,1)S(1)}, bf16[96,256]{1,0:T(8,128)(2,1)S(1)}, u32[]{:S(2)}, u32[]{:S(2)}) %collective-permute-start.11) | collective-permute-done | bytes 49184 | tf_op jit(solution)/shard_map/ppermute | solution.py:39
  32.5 1.8 %collective-permute-done.12.refs_1_ = bf16[96,256]{1,0:T(8,128)(2,1)S(1)} collective-permute-done((bf16[96,256]{1,0:T(8,128)(2,1)S(1)}, bf16[96,256]{1,0:T(8,128)(2,1)S(1)}, u32[]{:S(2)}, u32[]{:S(2)}) %collective-permute-start.12) | collective-permute-done | bytes 49184 | tf_op jit(solution)/shard_map/ppermute | solution.py:39
  34.2 0.0 collective-permute-done.13.refs_2_
  34.2 0.5 %shard_map.115 = (bf16[80,256]{1,0:T(8,128)(2,1)S(1)}, f32[1,1]{1,0:T(1,128)}) custom-call(f32[96,256]{1,0:T(8,128)S(1)} %get-tuple-element.23.keep_ref, bf16[96,256]{1,0:T(8,128)(2,1)S(1)} %collective-permute-done.11.refs_0_, bf16[96,256]{1,0:T(8,128)(2,1)S(1)} %collective-permute-done.12.refs_1_, bf16[96,256]{1,0:T(8,128)(2,1)S(1)} %collective-permute-done.13.refs_2_), custom_call_target="tpu_custom_call" | custom-call | tf_op jit(solution)/shard_map/pallas_call | solution.py:433
  34.8 2.4 %collective-permute-start.16 = (bf16[1,80,256]{2,1,0:T(8,128)(2,1)S(1)}, bf16[1,80,256]{2,1,0:T(8,128)(2,1)S(1)}, u32[]{:S(2)}, u32[]{:S(2)}) collective-permute-start(bf16[1,80,256]{2,1,0:T(8,128)(2,1)S(1)} %bitcast.6), channel_id=1, source_target_pairs={{0,12},{1,13},{2,14},{3,15},{4,8},{5,9},{6,10},{7,11},{8,4},{9,5},... | collective-permute-start | bytes 122888 | tf_op jit(solution)/shard_map/ppermute | solution.py:39
  37.1 0.0 collective-permute-start.15
  37.1 2.0 %collective-permute-start.14 = (bf16[1,80,256]{2,1,0:T(8,128)(2,1)S(1)}, bf16[1,80,256]{2,1,0:T(8,128)(2,1)S(1)}, u32[]{:S(2)}, u32[]{:S(2)}) collective-permute-start(bf16[1,80,256]{2,1,0:T(8,128)(2,1)S(1)} %bitcast.8), channel_id=1, source_target_pairs={{0,4},{1,5},{2,6},{3,7},{4,0},{5,1},{6,2},{7,3},{8,12},{9,13},{10,... | collective-permute-start | bytes 122888 | tf_op jit(solution)/shard_map/ppermute | solution.py:39
  39.2 1.4 %collective-permute-done.16 = bf16[1,80,256]{2,1,0:T(8,128)(2,1)S(1)} collective-permute-done((bf16[1,80,256]{2,1,0:T(8,128)(2,1)S(1)}, bf16[1,80,256]{2,1,0:T(8,128)(2,1)S(1)}, u32[]{:S(2)}, u32[]{:S(2)}) %collective-permute-start.16) | collective-permute-done | bytes 40992 | tf_op jit(solution)/shard_map/ppermute | solution.py:39
  40.6 2.1 %collective-permute-start.18 = (bf16[2,80,256]{2,1,0:T(8,128)(2,1)S(1)}, bf16[2,80,256]{2,1,0:T(8,128)(2,1)S(1)}, u32[]{:S(2)}, u32[]{:S(2)}) collective-permute-start(bf16[2,80,256]{2,1,0:T(8,128)(2,1)S(1)} %pad_maximum_fusion.2), channel_id=1, source_target_pairs={{0,2},{1,3},{2,0},{3,1},{4,6},{5,7},{6,4},{7,5},{8,10},{9,11},{10,... | collective-permute-start | bytes 245768 | tf_op jit(solution)/shard_map/ppermute | solution.py:39
  42.7 0.0 collective-permute-done.15
  42.7 0.0 collective-permute-done.14
  42.7 1.2 %collective-permute-start.17 = (bf16[2,80,256]{2,1,0:T(8,128)(2,1)S(1)}, bf16[2,80,256]{2,1,0:T(8,128)(2,1)S(1)}, u32[]{:S(2)}, u32[]{:S(2)}) collective-permute-start(bf16[2,80,256]{2,1,0:T(8,128)(2,1)S(1)} %pad_maximum_fusion.1), channel_id=1, source_target_pairs={{0,2},{1,3},{2,0},{3,1},{4,6},{5,7},{6,4},{7,5},{8,10},{9,11},{10,... | collective-permute-start | bytes 245768 | tf_op jit(solution)/shard_map/ppermute | solution.py:39
  44.0 3.3 %collective-permute-done.17 = bf16[2,80,256]{2,1,0:T(8,128)(2,1)S(1)} collective-permute-done((bf16[2,80,256]{2,1,0:T(8,128)(2,1)S(1)}, bf16[2,80,256]{2,1,0:T(8,128)(2,1)S(1)}, u32[]{:S(2)}, u32[]{:S(2)}) %collective-permute-start.17) | collective-permute-done | bytes 81952 | tf_op jit(solution)/shard_map/ppermute | solution.py:39
  47.2 0.0 collective-permute-done.18
  47.3 0.1 collective-permute-start.19
  47.3 1.0 %shard_map.116 = (f32[1024,256]{1,0:T(8,128)}, f32[256,256]{1,0:T(8,128)}) custom-call(s32[1]{0:T(128)} %bitcast.me_ref.refs_0_, bf16[8,80,256]{2,1,0:T(8,128)(2,1)S(1)} %constant_dynamic-update-slice_fusion.3.part_ref), custom_call_target="tpu_custom_call" | custom-call | tf_op jit(solution)/shard_map/pallas_call | solution.py:453
  48.3 0.6 %collective-permute-done.19.part_ref = bf16[8,80,256]{2,1,0:T(8,128)(2,1)S(1)} collective-permute-done((bf16[8,80,256]{2,1,0:T(8,128)(2,1)S(1)}, bf16[8,80,256]{2,1,0:T(8,128)(2,1)S(1)}, u32[]{:S(2)}, u32[]{:S(2)}) %collective-permute-start.19) | collective-permute-done | bytes 327712 | tf_op jit(solution)/shard_map/ppermute | solution.py:39
  49.0 1.0 %shard_map.117 = (f32[1024,256]{1,0:T(8,128)}, f32[256,256]{1,0:T(8,128)}) custom-call(s32[1]{0:T(128)} %bitcast.me_ref.refs_0_, bf16[8,80,256]{2,1,0:T(8,128)(2,1)S(1)} %collective-permute-done.19.part_ref, f32[1024,256]{1,0:T(8,128)} %get-tuple-element.28.refs_0_, f32[256,256]{1,0:T(8,128)} %get-tuple-element.29.refs_1_), custom_call_target="tpu_custom_call", output_to_operand_aliasing={{0}: (2, {}), {1}: (3, {})} | custom-call | tf_op jit(solution)/shard_map/pallas_call | solution.py:453
  (13 shorter events, 0.1 us)
Async XLA Ops:
  3.5 12.7 %collective-permute-start = (bf16[656,256]{1,0:T(8,128)(2,1)}, bf16[656,256]{1,0:T(8,128)(2,1)S(1)}, u32[]{:S(2)}, u32[]{:S(2)}) collective-permute-start(bf16[656,256]{1,0:T(8,128)(2,1)} %get-tuple-element.19), channel_id=1, source_target_pairs={{0,2},{1,3},{2,0},{3,1},{4,6},{5,7},{6,4},{7,5},{8,10},{9,11},{10,... | collective-permute-start | bytes 1007624 | tf_op jit(solution)/shard_map/ppermute | solution.py:39
  6.5 7.1 %collective-permute-start.5 = (bf16[128,256]{1,0:T(8,128)(2,1)}, bf16[128,256]{1,0:T(8,128)(2,1)S(1)}, u32[]{:S(2)}, u32[]{:S(2)}) collective-permute-start(bf16[128,256]{1,0:T(8,128)(2,1)} %get-tuple-element.20), channel_id=1, source_target_pairs={{0,12},{1,13},{2,14},{3,15},{4,8},{5,9},{6,10},{7,11},{8,4},{9,5},... | collective-permute-start | bytes 196616 | tf_op jit(solution)/shard_map/ppermute | solution.py:39
  10.1 5.6 %collective-permute-start.4 = (bf16[128,256]{1,0:T(8,128)(2,1)}, bf16[128,256]{1,0:T(8,128)(2,1)S(1)}, u32[]{:S(2)}, u32[]{:S(2)}) collective-permute-start(bf16[128,256]{1,0:T(8,128)(2,1)} %get-tuple-element.20), channel_id=1, source_target_pairs={{0,8},{1,9},{2,10},{3,11},{4,12},{5,13},{6,14},{7,15},{8,0},{9,1},... | collective-permute-start | bytes 196616 | tf_op jit(solution)/shard_map/ppermute | solution.py:39
  10.1 6.0 %collective-permute-start.3 = (bf16[128,256]{1,0:T(8,128)(2,1)}, bf16[128,256]{1,0:T(8,128)(2,1)S(1)}, u32[]{:S(2)}, u32[]{:S(2)}) collective-permute-start(bf16[128,256]{1,0:T(8,128)(2,1)} %get-tuple-element.20), channel_id=1, source_target_pairs={{0,4},{1,5},{2,6},{3,7},{4,0},{5,1},{6,2},{7,3},{8,12},{9,13},{10,... | collective-permute-start | bytes 196616 | tf_op jit(solution)/shard_map/ppermute | solution.py:39
  10.9 10.4 %collective-permute-start.1 = (bf16[528,256]{1,0:T(8,128)(2,1)}, bf16[528,256]{1,0:T(8,128)(2,1)S(1)}, u32[]{:S(2)}, u32[]{:S(2)}) collective-permute-start(bf16[528,256]{1,0:T(8,128)(2,1)} %get-tuple-element.18.refs_1_), channel_id=1, source_target_pairs={{0,1},{1,0},{2,3},{3,2},{4,5},{5,4},{6,7},{7,6},{8,9},{9,8},{10,11... | collective-permute-start | bytes 811016 | tf_op jit(solution)/shard_map/ppermute | solution.py:39
  13.6 7.1 %collective-permute-start.8 = (bf16[128,256]{1,0:T(8,128)(2,1)S(1)}, bf16[128,256]{1,0:T(8,128)(2,1)S(1)}, u32[]{:S(2)}, u32[]{:S(2)}) collective-permute-start(bf16[128,256]{1,0:T(8,128)(2,1)S(1)} %collective-permute-done.5), channel_id=1, source_target_pairs={{0,2},{1,3},{2,0},{3,1},{4,6},{5,7},{6,4},{7,5},{8,10},{9,11},{10,... | collective-permute-start | bytes 196616 | tf_op jit(solution)/shard_map/ppermute | solution.py:39
  15.7 5.0 %collective-permute-start.7 = (bf16[128,256]{1,0:T(8,128)(2,1)S(1)}, bf16[128,256]{1,0:T(8,128)(2,1)S(1)}, u32[]{:S(2)}, u32[]{:S(2)}) collective-permute-start(bf16[128,256]{1,0:T(8,128)(2,1)S(1)} %collective-permute-done.4), channel_id=1, source_target_pairs={{0,2},{1,3},{2,0},{3,1},{4,6},{5,7},{6,4},{7,5},{8,10},{9,11},{10,... | collective-permute-start | bytes 196616 | tf_op jit(solution)/shard_map/ppermute | solution.py:39
  16.2 4.5 %collective-permute-start.6 = (bf16[128,256]{1,0:T(8,128)(2,1)S(1)}, bf16[128,256]{1,0:T(8,128)(2,1)S(1)}, u32[]{:S(2)}, u32[]{:S(2)}) collective-permute-start(bf16[128,256]{1,0:T(8,128)(2,1)S(1)} %shard_map.113), channel_id=1, source_target_pairs={{0,2},{1,3},{2,0},{3,1},{4,6},{5,7},{6,4},{7,5},{8,10},{9,11},{10,... | collective-permute-start | bytes 196616 | tf_op jit(solution)/shard_map/ppermute | solution.py:39
  17.8 4.8 %copy-start.1 = (bf16[256,256]{1,0:T(8,128)(2,1)S(1)}, bf16[256,256]{1,0:T(8,128)(2,1)}, u32[]{:S(2)}) copy-start(bf16[256,256]{1,0:T(8,128)(2,1)} %get-tuple-element.22.refs_10_) | copy-start | bytes 393220
  17.8 4.8 %copy-start = (bf16[528,256]{1,0:T(8,128)(2,1)S(1)}, bf16[528,256]{1,0:T(8,128)(2,1)}, u32[]{:S(2)}) copy-start(bf16[528,256]{1,0:T(8,128)(2,1)} %get-tuple-element.18.refs_1_) | copy-start | bytes 811012
  17.8 3.5 %collective-permute-start.9 = (bf16[384,256]{1,0:T(8,128)(2,1)S(1)}, bf16[384,256]{1,0:T(8,128)(2,1)S(1)}, u32[]{:S(2)}, u32[]{:S(2)}) collective-permute-start(bf16[384,256]{1,0:T(8,128)(2,1)S(1)} %pad_maximum_fusion.refs_5_), channel_id=1, source_target_pairs={{0,1},{1,0},{2,3},{3,2},{4,5},{5,4},{6,7},{7,6},{8,9},{9,8},{10,11... | collective-permute-start | bytes 589832 | tf_op jit(solution)/shard_map/ppermute | solution.py:39
  20.7 1.9 %collective-permute-start.2 = (bf16[656,256]{1,0:T(8,128)(2,1)S(1)}, bf16[656,256]{1,0:T(8,128)(2,1)S(1)}, u32[]{:S(2)}, u32[]{:S(2)}) collective-permute-start(bf16[656,256]{1,0:T(8,128)(2,1)S(1)} %collective-permute-done.refs_1_.refs_2_), channel_id=1, source_target_pairs={{0,1},{1,0},{2,3},{3,2},{4,5},{5,4},{6,7},{7,6},{8,9},{9,8},{10,11... | collective-permute-start | bytes 1007624 | tf_op jit(solution)/shard_map/ppermute | solution.py:39
  20.7 1.9 %copy-start.2 = (bf16[128,256]{1,0:T(8,128)(2,1)S(1)}, bf16[128,256]{1,0:T(8,128)(2,1)}, u32[]{:S(2)}) copy-start(bf16[128,256]{1,0:T(8,128)(2,1)} %get-tuple-element.21.refs_9_) | copy-start | bytes 196612
  20.7 1.8 %collective-permute-start.10 = (bf16[384,256]{1,0:T(8,128)(2,1)S(1)}, bf16[384,256]{1,0:T(8,128)(2,1)S(1)}, u32[]{:S(2)}, u32[]{:S(2)}) collective-permute-start(bf16[384,256]{1,0:T(8,128)(2,1)S(1)} %constant_dynamic-update-slice_fusion.refs_6_), channel_id=1, source_target_pairs={{0,1},{1,0},{2,3},{3,2},{4,5},{5,4},{6,7},{7,6},{8,9},{9,8},{10,11... | collective-permute-start | bytes 589832 | tf_op jit(solution)/shard_map/ppermute | solution.py:39
  26.2 6.3 %collective-permute-start.11 = (bf16[96,256]{1,0:T(8,128)(2,1)S(1)}, bf16[96,256]{1,0:T(8,128)(2,1)S(1)}, u32[]{:S(2)}, u32[]{:S(2)}) collective-permute-start(bf16[96,256]{1,0:T(8,128)(2,1)S(1)} %get-tuple-element.24), channel_id=1, source_target_pairs={{0,12},{1,13},{2,14},{3,15},{4,8},{5,9},{6,10},{7,11},{8,4},{9,5},... | collective-permute-start | bytes 147464 | tf_op jit(solution)/shard_map/ppermute | solution.py:39
  29.2 5.1 %collective-permute-start.12 = (bf16[96,256]{1,0:T(8,128)(2,1)S(1)}, bf16[96,256]{1,0:T(8,128)(2,1)S(1)}, u32[]{:S(2)}, u32[]{:S(2)}) collective-permute-start(bf16[96,256]{1,0:T(8,128)(2,1)S(1)} %get-tuple-element.25), channel_id=1, source_target_pairs={{0,8},{1,9},{2,10},{3,11},{4,12},{5,13},{6,14},{7,15},{8,0},{9,1},... | collective-permute-start | bytes 147464 | tf_op jit(solution)/shard_map/ppermute | solution.py:39
  29.2 5.1 %collective-permute-start.13 = (bf16[96,256]{1,0:T(8,128)(2,1)S(1)}, bf16[96,256]{1,0:T(8,128)(2,1)S(1)}, u32[]{:S(2)}, u32[]{:S(2)}) collective-permute-start(bf16[96,256]{1,0:T(8,128)(2,1)S(1)} %get-tuple-element.26), channel_id=1, source_target_pairs={{0,4},{1,5},{2,6},{3,7},{4,0},{5,1},{6,2},{7,3},{8,12},{9,13},{10,... | collective-permute-start | bytes 147464 | tf_op jit(solution)/shard_map/ppermute | solution.py:39
  34.8 5.8 %collective-permute-start.16 = (bf16[1,80,256]{2,1,0:T(8,128)(2,1)S(1)}, bf16[1,80,256]{2,1,0:T(8,128)(2,1)S(1)}, u32[]{:S(2)}, u32[]{:S(2)}) collective-permute-start(bf16[1,80,256]{2,1,0:T(8,128)(2,1)S(1)} %bitcast.6), channel_id=1, source_target_pairs={{0,12},{1,13},{2,14},{3,15},{4,8},{5,9},{6,10},{7,11},{8,4},{9,5},... | collective-permute-start | bytes 122888 | tf_op jit(solution)/shard_map/ppermute | solution.py:39
  37.1 5.6 %collective-permute-start.15 = (bf16[1,80,256]{2,1,0:T(8,128)(2,1)S(1)}, bf16[1,80,256]{2,1,0:T(8,128)(2,1)S(1)}, u32[]{:S(2)}, u32[]{:S(2)}) collective-permute-start(bf16[1,80,256]{2,1,0:T(8,128)(2,1)S(1)} %bitcast.7), channel_id=1, source_target_pairs={{0,8},{1,9},{2,10},{3,11},{4,12},{5,13},{6,14},{7,15},{8,0},{9,1},... | collective-permute-start | bytes 122888 | tf_op jit(solution)/shard_map/ppermute | solution.py:39
  37.1 5.6 %collective-permute-start.14 = (bf16[1,80,256]{2,1,0:T(8,128)(2,1)S(1)}, bf16[1,80,256]{2,1,0:T(8,128)(2,1)S(1)}, u32[]{:S(2)}, u32[]{:S(2)}) collective-permute-start(bf16[1,80,256]{2,1,0:T(8,128)(2,1)S(1)} %bitcast.8), channel_id=1, source_target_pairs={{0,4},{1,5},{2,6},{3,7},{4,0},{5,1},{6,2},{7,3},{8,12},{9,13},{10,... | collective-permute-start | bytes 122888 | tf_op jit(solution)/shard_map/ppermute | solution.py:39
  40.6 6.6 %collective-permute-start.18 = (bf16[2,80,256]{2,1,0:T(8,128)(2,1)S(1)}, bf16[2,80,256]{2,1,0:T(8,128)(2,1)S(1)}, u32[]{:S(2)}, u32[]{:S(2)}) collective-permute-start(bf16[2,80,256]{2,1,0:T(8,128)(2,1)S(1)} %pad_maximum_fusion.2), channel_id=1, source_target_pairs={{0,2},{1,3},{2,0},{3,1},{4,6},{5,7},{6,4},{7,5},{8,10},{9,11},{10,... | collective-permute-start | bytes 245768 | tf_op jit(solution)/shard_map/ppermute | solution.py:39
  42.7 4.5 %collective-permute-start.17 = (bf16[2,80,256]{2,1,0:T(8,128)(2,1)S(1)}, bf16[2,80,256]{2,1,0:T(8,128)(2,1)S(1)}, u32[]{:S(2)}, u32[]{:S(2)}) collective-permute-start(bf16[2,80,256]{2,1,0:T(8,128)(2,1)S(1)} %pad_maximum_fusion.1), channel_id=1, source_target_pairs={{0,2},{1,3},{2,0},{3,1},{4,6},{5,7},{6,4},{7,5},{8,10},{9,11},{10,... | collective-permute-start | bytes 245768 | tf_op jit(solution)/shard_map/ppermute | solution.py:39
  47.3 1.7 %collective-permute-start.19 = (bf16[8,80,256]{2,1,0:T(8,128)(2,1)S(1)}, bf16[8,80,256]{2,1,0:T(8,128)(2,1)S(1)}, u32[]{:S(2)}, u32[]{:S(2)}) collective-permute-start(bf16[8,80,256]{2,1,0:T(8,128)(2,1)S(1)} %constant_dynamic-update-slice_fusion.3.part_ref), channel_id=1, source_target_pairs={{0,1},{1,0},{2,3},{3,2},{4,5},{5,4},{6,7},{7,6},{8,9},{9,8},{10,11... | collective-permute-start | bytes 983048 | tf_op jit(solution)/shard_map/ppermute | solution.py:39

commit v15 on v14

--- a/solution.py
+++ b/solution.py
@@ -322,16 +322,17 @@
     wf_hbm, wb_hbm, wf_buf, wb_buf, sems = refs[-5:]
     place = reverse_bits(me_ref[0] & 15, 4) ^ offset
     moves = []
-    for e, turn in enumerate(TURNS):
-        to = place ^ turn
-        wf_buf[e] = part_ref[e, :wf_rows, :].astype(F32) * factor_f
-        wb_buf[e] = part_ref[e, wf_rows:, :].astype(F32) * factor_b
-        for k, (buf, hbm, rows) in enumerate(((wf_buf, wf_hbm, wf_rows), (wb_buf, wb_hbm, wb_rows))):
-            move = pltpu.make_async_copy(
-                buf.at[e], hbm.at[pl.ds(pl.multiple_of(to * rows, rows), rows), :], sems.at[2 * e + k]
+    kinds = ((wf_buf, wf_hbm, 0, wf_rows, factor_f), (wb_buf, wb_hbm, wf_rows, wb_rows, factor_b))
+    for k, (buf, hbm, first, rows, factor) in enumerate(kinds):
+        for e, turn in enumerate(TURNS):
+            to = (place ^ turn) & 7
+            buf[pl.ds(pl.multiple_of(to * rows, rows), rows), :] = (
+                part_ref[e, first : first + rows, :].astype(F32) * factor
             )
-            move.start()
-            moves.append(move)
+        start = pl.multiple_of((place >> 3) * (8 * rows), 8 * rows)
+        move = pltpu.make_async_copy(buf, hbm.at[pl.ds(start, 8 * rows), :], sems.at[k])
+        move.start()
+        moves.append(move)
     for move in moves:
         move.wait()
 
@@ -466,9 +467,9 @@
                 jax.ShapeDtypeStruct((wide, width), F32),
             ],
             scratch_shapes=[
-                pltpu.VMEM((8, wf_rows, width), F32),
-                pltpu.VMEM((8, wb_rows, width), F32),
-                pltpu.SemaphoreType.DMA((16,)),
+                pltpu.VMEM((8 * wf_rows, width), F32),
+                pltpu.VMEM((8 * wb_rows, width), F32),
+                pltpu.SemaphoreType.DMA((2,)),
             ],
             input_output_aliases={2 + k: k for k in range(len(begun))},
             compiler_params=pltpu.CompilerParams(vmem_limit_bytes=8 * 2**20),

time: 50.1 us -> 50 us (level)
  no operation moved by 1% of the time
where the time goes in v15:
time: 50 us; the launch traced here: 49.8 us
  starting transfers between devices  22.4 us (45%)
  waiting for transfers between devices  17.8 us (36%)
  Pallas kernels  8.72 us (17%)
  between operations  0.81 us (2%)
    ppermute x20, starting transfers between devices, swap(): return lax.ppermute(array, 'fa', [(i, i ^ mask) for i in range(size)])  22.4 us
    ppermute x20, waiting for transfers between devices, swap(): return lax.ppermute(array, 'fa', [(i, i ^ mask) for i in range(size)])  17.8 us
    pallas_call x1, Pallas kernels, body(): pl.pallas_call(functools.partial(pair_kernel, rows=rows, total=total), in...  3.57 us
    pallas_call x1, Pallas kernels, body(): pl.pallas_call(feature_kernel, in_specs=[SMEM] + [HBM] * 9, out_specs=[VM...  2.83 us
    pallas_call x2, Pallas kernels, assemble(): pl.pallas_call(functools.partial(assemble_kernel, offset=offset, wf_rows=...  1.79 us
  transfers between devices with their start and end apart: 20, of which 9 were waited for; matrix products, arithmetic and copies ran while one was open for 0% of the time, Pallas kernels for 2%

profile of v15, /device:TPU:0, one launch (start us, length us, event | category | flops | bytes accessed | tf_op | source)
XLA Modules:
  0.0 49.8 jit_solution(15194318826107857299)
XLA Ops:
  0.6 2.8 %shard_map.112 = (bf16[656,256]{1,0:T(8,128)(2,1)}, bf16[528,256]{1,0:T(8,128)(2,1)}, bf16[128,256]{1,0:T(8,128)(2,1)}, bf16[128,256]{1,0:T(8,128)(2,1)}, bf16[256,256]{1,0:T(8,128)(2,1)}) custom-call(s32[1]{0:T(128)} %bitcast.me_ref.refs_0_, bf16[128,1024]{1,0:T(8,128)(2,1)} %hf_hbm.1, bf16[128,1024]{1,0:T(8,128)(2,1)} %ht_hbm.1, bf16[128,256]{1,0:T(8,128)(2,1)} %hb_hbm.1, ...), custom_call_target="tpu_custom_call" | custom-call | flops 134217728 | bytes 1572864 | tf_op jit(solution)/shard_map/pallas_call | solution.py:359
  3.5 3.0 %collective-permute-start = (bf16[656,256]{1,0:T(8,128)(2,1)}, bf16[656,256]{1,0:T(8,128)(2,1)S(1)}, u32[]{:S(2)}, u32[]{:S(2)}) collective-permute-start(bf16[656,256]{1,0:T(8,128)(2,1)} %get-tuple-element.19), channel_id=1, source_target_pairs={{0,2},{1,3},{2,0},{3,1},{4,6},{5,7},{6,4},{7,5},{8,10},{9,11},{10,... | collective-permute-start | bytes 1007624 | tf_op jit(solution)/shard_map/ppermute | solution.py:39
  6.5 3.6 %collective-permute-start.5 = (bf16[128,256]{1,0:T(8,128)(2,1)}, bf16[128,256]{1,0:T(8,128)(2,1)S(1)}, u32[]{:S(2)}, u32[]{:S(2)}) collective-permute-start(bf16[128,256]{1,0:T(8,128)(2,1)} %get-tuple-element.20), channel_id=1, source_target_pairs={{0,12},{1,13},{2,14},{3,15},{4,8},{5,9},{6,10},{7,11},{8,4},{9,5},... | collective-permute-start | bytes 196616 | tf_op jit(solution)/shard_map/ppermute | solution.py:39
  10.1 0.0 collective-permute-start.4
  10.1 0.8 %collective-permute-start.3 = (bf16[128,256]{1,0:T(8,128)(2,1)}, bf16[128,256]{1,0:T(8,128)(2,1)S(1)}, u32[]{:S(2)}, u32[]{:S(2)}) collective-permute-start(bf16[128,256]{1,0:T(8,128)(2,1)} %get-tuple-element.20), channel_id=1, source_target_pairs={{0,4},{1,5},{2,6},{3,7},{4,0},{5,1},{6,2},{7,3},{8,12},{9,13},{10,... | collective-permute-start | bytes 196616 | tf_op jit(solution)/shard_map/ppermute | solution.py:39
  10.9 0.0 collective-permute-start.1
  10.9 2.7 %collective-permute-done.5 = bf16[128,256]{1,0:T(8,128)(2,1)S(1)} collective-permute-done((bf16[128,256]{1,0:T(8,128)(2,1)}, bf16[128,256]{1,0:T(8,128)(2,1)S(1)}, u32[]{:S(2)}, u32[]{:S(2)}) %collective-permute-start.5) | collective-permute-done | bytes 65568 | tf_op jit(solution)/shard_map/ppermute | solution.py:39
  13.6 0.0 collective-permute-start.8
  13.6 2.1 %collective-permute-done.4 = bf16[128,256]{1,0:T(8,128)(2,1)S(1)} collective-permute-done((bf16[128,256]{1,0:T(8,128)(2,1)}, bf16[128,256]{1,0:T(8,128)(2,1)S(1)}, u32[]{:S(2)}, u32[]{:S(2)}) %collective-permute-start.4) | collective-permute-done | bytes 65568 | tf_op jit(solution)/shard_map/ppermute | solution.py:39
  15.7 0.5 collective-permute-start.7
  16.2 0.0 collective-permute-done.3.refs_0_
  16.2 0.0 collective-permute-done.refs_1_.refs_2_
  16.2 1.6 %collective-permute-start.6 = (bf16[128,256]{1,0:T(8,128)(2,1)S(1)}, bf16[128,256]{1,0:T(8,128)(2,1)S(1)}, u32[]{:S(2)}, u32[]{:S(2)}) collective-permute-start(bf16[128,256]{1,0:T(8,128)(2,1)S(1)} %shard_map.113), channel_id=1, source_target_pairs={{0,2},{1,3},{2,0},{3,1},{4,6},{5,7},{6,4},{7,5},{8,10},{9,11},{10,... | collective-permute-start | bytes 196616 | tf_op jit(solution)/shard_map/ppermute | solution.py:39
  17.8 0.0 copy-start.1
  17.8 0.0 copy-start
  17.8 0.1 collective-permute-start.9
  17.9 2.8 %collective-permute-done.6 = bf16[128,256]{1,0:T(8,128)(2,1)S(1)} collective-permute-done((bf16[128,256]{1,0:T(8,128)(2,1)S(1)}, bf16[128,256]{1,0:T(8,128)(2,1)S(1)}, u32[]{:S(2)}, u32[]{:S(2)}) %collective-permute-start.6) | collective-permute-done | bytes 65568 | tf_op jit(solution)/shard_map/ppermute | solution.py:39
  20.7 0.0 collective-permute-start.2
  20.7 0.0 collective-permute-done.7
  20.7 0.0 copy-start.2
  20.7 0.0 collective-permute-done.8
  20.7 0.6 %collective-permute-start.10 = (bf16[384,256]{1,0:T(8,128)(2,1)S(1)}, bf16[384,256]{1,0:T(8,128)(2,1)S(1)}, u32[]{:S(2)}, u32[]{:S(2)}) collective-permute-start(bf16[384,256]{1,0:T(8,128)(2,1)S(1)} %constant_dynamic-update-slice_fusion.refs_6_), channel_id=1, source_target_pairs={{0,1},{1,0},{2,3},{3,2},{4,5},{5,4},{6,7},{7,6},{8,9},{9,8},{10,11... | collective-permute-start | bytes 589832 | tf_op jit(solution)/shard_map/ppermute | solution.py:39
  21.3 0.0 collective-permute-done.1.refs_3_
  21.3 0.0 collective-permute-done.9.refs_7_
  21.3 1.3 %collective-permute-done.10.refs_8_ = bf16[384,256]{1,0:T(8,128)(2,1)S(1)} collective-permute-done((bf16[384,256]{1,0:T(8,128)(2,1)S(1)}, bf16[384,256]{1,0:T(8,128)(2,1)S(1)}, u32[]{:S(2)}, u32[]{:S(2)}) %collective-permute-start.10) | collective-permute-done | bytes 196640 | tf_op jit(solution)/shard_map/ppermute | solution.py:39
  22.6 0.0 collective-permute-done.2.refs_4_
  22.6 0.0 copy-done.1
  22.6 0.0 copy-done
  22.6 0.0 copy-done.2
  22.6 3.6 %shard_map.114 = (f32[96,256]{1,0:T(8,128)S(1)}, bf16[96,256]{1,0:T(8,128)(2,1)S(1)}, bf16[96,256]{1,0:T(8,128)(2,1)S(1)}, bf16[96,256]{1,0:T(8,128)(2,1)S(1)}) custom-call(s32[1]{0:T(128)} %bitcast.me_ref.refs_0_, bf16[528,256]{1,0:T(8,128)(2,1)S(1)} %copy-done, bf16[656,256]{1,0:T(8,128)(2,1)S(1)} %collective-permute-done.refs_1_.refs_2_, ...), custom_call_target="tpu_custom_call" | custom-call | tf_op jit(solution)/shard_map/pallas_call | solution.py:413
  26.2 3.0 %collective-permute-start.11 = (bf16[96,256]{1,0:T(8,128)(2,1)S(1)}, bf16[96,256]{1,0:T(8,128)(2,1)S(1)}, u32[]{:S(2)}, u32[]{:S(2)}) collective-permute-start(bf16[96,256]{1,0:T(8,128)(2,1)S(1)} %get-tuple-element.24), channel_id=1, source_target_pairs={{0,12},{1,13},{2,14},{3,15},{4,8},{5,9},{6,10},{7,11},{8,4},{9,5},... | collective-permute-start | bytes 147464 | tf_op jit(solution)/shard_map/ppermute | solution.py:39
  29.2 0.0 collective-permute-start.12
  29.2 1.4 %collective-permute-start.13 = (bf16[96,256]{1,0:T(8,128)(2,1)S(1)}, bf16[96,256]{1,0:T(8,128)(2,1)S(1)}, u32[]{:S(2)}, u32[]{:S(2)}) collective-permute-start(bf16[96,256]{1,0:T(8,128)(2,1)S(1)} %get-tuple-element.26), channel_id=1, source_target_pairs={{0,4},{1,5},{2,6},{3,7},{4,0},{5,1},{6,2},{7,3},{8,12},{9,13},{10,... | collective-permute-start | bytes 147464 | tf_op jit(solution)/shard_map/ppermute | solution.py:39
  30.6 1.8 %collective-permute-done.11.refs_0_ = bf16[96,256]{1,0:T(8,128)(2,1)S(1)} collective-permute-done((bf16[96,256]{1,0:T(8,128)(2,1)S(1)}, bf16[96,256]{1,0:T(8,128)(2,1)S(1)}, u32[]{:S(2)}, u32[]{:S(2)}) %collective-permute-start.11) | collective-permute-done | bytes 49184 | tf_op jit(solution)/shard_map/ppermute | solution.py:39
  32.5 1.8 %collective-permute-done.12.refs_1_ = bf16[96,256]{1,0:T(8,128)(2,1)S(1)} collective-permute-done((bf16[96,256]{1,0:T(8,128)(2,1)S(1)}, bf16[96,256]{1,0:T(8,128)(2,1)S(1)}, u32[]{:S(2)}, u32[]{:S(2)}) %collective-permute-start.12) | collective-permute-done | bytes 49184 | tf_op jit(solution)/shard_map/ppermute | solution.py:39
  34.2 0.0 collective-permute-done.13.refs_2_
  34.2 0.5 %shard_map.115 = (bf16[80,256]{1,0:T(8,128)(2,1)S(1)}, f32[1,1]{1,0:T(1,128)}) custom-call(f32[96,256]{1,0:T(8,128)S(1)} %get-tuple-element.23.keep_ref, bf16[96,256]{1,0:T(8,128)(2,1)S(1)} %collective-permute-done.11.refs_0_, bf16[96,256]{1,0:T(8,128)(2,1)S(1)} %collective-permute-done.12.refs_1_, bf16[96,256]{1,0:T(8,128)(2,1)S(1)} %collective-permute-done.13.refs_2_), custom_call_target="tpu_custom_call" | custom-call | tf_op jit(solution)/shard_map/pallas_call | solution.py:434
  34.8 2.4 %collective-permute-start.16 = (bf16[1,80,256]{2,1,0:T(8,128)(2,1)S(1)}, bf16[1,80,256]{2,1,0:T(8,128)(2,1)S(1)}, u32[]{:S(2)}, u32[]{:S(2)}) collective-permute-start(bf16[1,80,256]{2,1,0:T(8,128)(2,1)S(1)} %bitcast.6), channel_id=1, source_target_pairs={{0,12},{1,13},{2,14},{3,15},{4,8},{5,9},{6,10},{7,11},{8,4},{9,5},... | collective-permute-start | bytes 122888 | tf_op jit(solution)/shard_map/ppermute | solution.py:39
  37.1 0.0 collective-permute-start.15
  37.1 2.0 %collective-permute-start.14 = (bf16[1,80,256]{2,1,0:T(8,128)(2,1)S(1)}, bf16[1,80,256]{2,1,0:T(8,128)(2,1)S(1)}, u32[]{:S(2)}, u32[]{:S(2)}) collective-permute-start(bf16[1,80,256]{2,1,0:T(8,128)(2,1)S(1)} %bitcast.8), channel_id=1, source_target_pairs={{0,4},{1,5},{2,6},{3,7},{4,0},{5,1},{6,2},{7,3},{8,12},{9,13},{10,... | collective-permute-start | bytes 122888 | tf_op jit(solution)/shard_map/ppermute | solution.py:39
  39.2 1.4 %collective-permute-done.16 = bf16[1,80,256]{2,1,0:T(8,128)(2,1)S(1)} collective-permute-done((bf16[1,80,256]{2,1,0:T(8,128)(2,1)S(1)}, bf16[1,80,256]{2,1,0:T(8,128)(2,1)S(1)}, u32[]{:S(2)}, u32[]{:S(2)}) %collective-permute-start.16) | collective-permute-done | bytes 40992 | tf_op jit(solution)/shard_map/ppermute | solution.py:39
  40.6 2.1 %collective-permute-start.18 = (bf16[2,80,256]{2,1,0:T(8,128)(2,1)S(1)}, bf16[2,80,256]{2,1,0:T(8,128)(2,1)S(1)}, u32[]{:S(2)}, u32[]{:S(2)}) collective-permute-start(bf16[2,80,256]{2,1,0:T(8,128)(2,1)S(1)} %pad_maximum_fusion.2), channel_id=1, source_target_pairs={{0,2},{1,3},{2,0},{3,1},{4,6},{5,7},{6,4},{7,5},{8,10},{9,11},{10,... | collective-permute-start | bytes 245768 | tf_op jit(solution)/shard_map/ppermute | solution.py:39
  42.7 0.0 collective-permute-done.15
  42.7 0.0 collective-permute-done.14
  42.7 1.2 %collective-permute-start.17 = (bf16[2,80,256]{2,1,0:T(8,128)(2,1)S(1)}, bf16[2,80,256]{2,1,0:T(8,128)(2,1)S(1)}, u32[]{:S(2)}, u32[]{:S(2)}) collective-permute-start(bf16[2,80,256]{2,1,0:T(8,128)(2,1)S(1)} %pad_maximum_fusion.1), channel_id=1, source_target_pairs={{0,2},{1,3},{2,0},{3,1},{4,6},{5,7},{6,4},{7,5},{8,10},{9,11},{10,... | collective-permute-start | bytes 245768 | tf_op jit(solution)/shard_map/ppermute | solution.py:39
  44.0 3.3 %collective-permute-done.17 = bf16[2,80,256]{2,1,0:T(8,128)(2,1)S(1)} collective-permute-done((bf16[2,80,256]{2,1,0:T(8,128)(2,1)S(1)}, bf16[2,80,256]{2,1,0:T(8,128)(2,1)S(1)}, u32[]{:S(2)}, u32[]{:S(2)}) %collective-permute-start.17) | collective-permute-done | bytes 81952 | tf_op jit(solution)/shard_map/ppermute | solution.py:39
  47.2 0.0 collective-permute-done.18
  47.3 0.1 collective-permute-start.19
  47.3 0.9 %shard_map.116 = (f32[1024,256]{1,0:T(8,128)}, f32[256,256]{1,0:T(8,128)}) custom-call(s32[1]{0:T(128)} %bitcast.me_ref.refs_0_, bf16[8,80,256]{2,1,0:T(8,128)(2,1)S(1)} %constant_dynamic-update-slice_fusion.3.part_ref), custom_call_target="tpu_custom_call" | custom-call | tf_op jit(solution)/shard_map/pallas_call | solution.py:454
  48.2 0.7 %collective-permute-done.19.part_ref = bf16[8,80,256]{2,1,0:T(8,128)(2,1)S(1)} collective-permute-done((bf16[8,80,256]{2,1,0:T(8,128)(2,1)S(1)}, bf16[8,80,256]{2,1,0:T(8,128)(2,1)S(1)}, u32[]{:S(2)}, u32[]{:S(2)}) %collective-permute-start.19) | collective-permute-done | bytes 327712 | tf_op jit(solution)/shard_map/ppermute | solution.py:39
  49.0 0.9 %shard_map.117 = (f32[1024,256]{1,0:T(8,128)}, f32[256,256]{1,0:T(8,128)}) custom-call(s32[1]{0:T(128)} %bitcast.me_ref.refs_0_, bf16[8,80,256]{2,1,0:T(8,128)(2,1)S(1)} %collective-permute-done.19.part_ref, f32[1024,256]{1,0:T(8,128)} %get-tuple-element.28.refs_0_, f32[256,256]{1,0:T(8,128)} %get-tuple-element.29.refs_1_), custom_call_target="tpu_custom_call", output_to_operand_aliasing={{0}: (2, {}), {1}: (3, {})} | custom-call | tf_op jit(solution)/shard_map/pallas_call | solution.py:454
  (13 shorter events, 0.1 us)
Async XLA Ops:
  3.5 12.7 %collective-permute-start = (bf16[656,256]{1,0:T(8,128)(2,1)}, bf16[656,256]{1,0:T(8,128)(2,1)S(1)}, u32[]{:S(2)}, u32[]{:S(2)}) collective-permute-start(bf16[656,256]{1,0:T(8,128)(2,1)} %get-tuple-element.19), channel_id=1, source_target_pairs={{0,2},{1,3},{2,0},{3,1},{4,6},{5,7},{6,4},{7,5},{8,10},{9,11},{10,... | collective-permute-start | bytes 1007624 | tf_op jit(solution)/shard_map/ppermute | solution.py:39
  6.5 7.1 %collective-permute-start.5 = (bf16[128,256]{1,0:T(8,128)(2,1)}, bf16[128,256]{1,0:T(8,128)(2,1)S(1)}, u32[]{:S(2)}, u32[]{:S(2)}) collective-permute-start(bf16[128,256]{1,0:T(8,128)(2,1)} %get-tuple-element.20), channel_id=1, source_target_pairs={{0,12},{1,13},{2,14},{3,15},{4,8},{5,9},{6,10},{7,11},{8,4},{9,5},... | collective-permute-start | bytes 196616 | tf_op jit(solution)/shard_map/ppermute | solution.py:39
  10.1 5.6 %collective-permute-start.4 = (bf16[128,256]{1,0:T(8,128)(2,1)}, bf16[128,256]{1,0:T(8,128)(2,1)S(1)}, u32[]{:S(2)}, u32[]{:S(2)}) collective-permute-start(bf16[128,256]{1,0:T(8,128)(2,1)} %get-tuple-element.20), channel_id=1, source_target_pairs={{0,8},{1,9},{2,10},{3,11},{4,12},{5,13},{6,14},{7,15},{8,0},{9,1},... | collective-permute-start | bytes 196616 | tf_op jit(solution)/shard_map/ppermute | solution.py:39
  10.1 6.0 %collective-permute-start.3 = (bf16[128,256]{1,0:T(8,128)(2,1)}, bf16[128,256]{1,0:T(8,128)(2,1)S(1)}, u32[]{:S(2)}, u32[]{:S(2)}) collective-permute-start(bf16[128,256]{1,0:T(8,128)(2,1)} %get-tuple-element.20), channel_id=1, source_target_pairs={{0,4},{1,5},{2,6},{3,7},{4,0},{5,1},{6,2},{7,3},{8,12},{9,13},{10,... | collective-permute-start | bytes 196616 | tf_op jit(solution)/shard_map/ppermute | solution.py:39
  10.9 10.4 %collective-permute-start.1 = (bf16[528,256]{1,0:T(8,128)(2,1)}, bf16[528,256]{1,0:T(8,128)(2,1)S(1)}, u32[]{:S(2)}, u32[]{:S(2)}) collective-permute-start(bf16[528,256]{1,0:T(8,128)(2,1)} %get-tuple-element.18.refs_1_), channel_id=1, source_target_pairs={{0,1},{1,0},{2,3},{3,2},{4,5},{5,4},{6,7},{7,6},{8,9},{9,8},{10,11... | collective-permute-start | bytes 811016 | tf_op jit(solution)/shard_map/ppermute | solution.py:39
  13.6 7.1 %collective-permute-start.8 = (bf16[128,256]{1,0:T(8,128)(2,1)S(1)}, bf16[128,256]{1,0:T(8,128)(2,1)S(1)}, u32[]{:S(2)}, u32[]{:S(2)}) collective-permute-start(bf16[128,256]{1,0:T(8,128)(2,1)S(1)} %collective-permute-done.5), channel_id=1, source_target_pairs={{0,2},{1,3},{2,0},{3,1},{4,6},{5,7},{6,4},{7,5},{8,10},{9,11},{10,... | collective-permute-start | bytes 196616 | tf_op jit(solution)/shard_map/ppermute | solution.py:39
  15.7 5.0 %collective-permute-start.7 = (bf16[128,256]{1,0:T(8,128)(2,1)S(1)}, bf16[128,256]{1,0:T(8,128)(2,1)S(1)}, u32[]{:S(2)}, u32[]{:S(2)}) collective-permute-start(bf16[128,256]{1,0:T(8,128)(2,1)S(1)} %collective-permute-done.4), channel_id=1, source_target_pairs={{0,2},{1,3},{2,0},{3,1},{4,6},{5,7},{6,4},{7,5},{8,10},{9,11},{10,... | collective-permute-start | bytes 196616 | tf_op jit(solution)/shard_map/ppermute | solution.py:39
  16.2 4.5 %collective-permute-start.6 = (bf16[128,256]{1,0:T(8,128)(2,1)S(1)}, bf16[128,256]{1,0:T(8,128)(2,1)S(1)}, u32[]{:S(2)}, u32[]{:S(2)}) collective-permute-start(bf16[128,256]{1,0:T(8,128)(2,1)S(1)} %shard_map.113), channel_id=1, source_target_pairs={{0,2},{1,3},{2,0},{3,1},{4,6},{5,7},{6,4},{7,5},{8,10},{9,11},{10,... | collective-permute-start | bytes 196616 | tf_op jit(solution)/shard_map/ppermute | solution.py:39
  17.8 4.8 %copy-start.1 = (bf16[256,256]{1,0:T(8,128)(2,1)S(1)}, bf16[256,256]{1,0:T(8,128)(2,1)}, u32[]{:S(2)}) copy-start(bf16[256,256]{1,0:T(8,128)(2,1)} %get-tuple-element.22.refs_10_) | copy-start | bytes 393220
  17.8 4.8 %copy-start = (bf16[528,256]{1,0:T(8,128)(2,1)S(1)}, bf16[528,256]{1,0:T(8,128)(2,1)}, u32[]{:S(2)}) copy-start(bf16[528,256]{1,0:T(8,128)(2,1)} %get-tuple-element.18.refs_1_) | copy-start | bytes 811012
  17.8 3.5 %collective-permute-start.9 = (bf16[384,256]{1,0:T(8,128)(2,1)S(1)}, bf16[384,256]{1,0:T(8,128)(2,1)S(1)}, u32[]{:S(2)}, u32[]{:S(2)}) collective-permute-start(bf16[384,256]{1,0:T(8,128)(2,1)S(1)} %pad_maximum_fusion.refs_5_), channel_id=1, source_target_pairs={{0,1},{1,0},{2,3},{3,2},{4,5},{5,4},{6,7},{7,6},{8,9},{9,8},{10,11... | collective-permute-start | bytes 589832 | tf_op jit(solution)/shard_map/ppermute | solution.py:39
  20.7 1.9 %collective-permute-start.2 = (bf16[656,256]{1,0:T(8,128)(2,1)S(1)}, bf16[656,256]{1,0:T(8,128)(2,1)S(1)}, u32[]{:S(2)}, u32[]{:S(2)}) collective-permute-start(bf16[656,256]{1,0:T(8,128)(2,1)S(1)} %collective-permute-done.refs_1_.refs_2_), channel_id=1, source_target_pairs={{0,1},{1,0},{2,3},{3,2},{4,5},{5,4},{6,7},{7,6},{8,9},{9,8},{10,11... | collective-permute-start | bytes 1007624 | tf_op jit(solution)/shard_map/ppermute | solution.py:39
  20.7 1.9 %copy-start.2 = (bf16[128,256]{1,0:T(8,128)(2,1)S(1)}, bf16[128,256]{1,0:T(8,128)(2,1)}, u32[]{:S(2)}) copy-start(bf16[128,256]{1,0:T(8,128)(2,1)} %get-tuple-element.21.refs_9_) | copy-start | bytes 196612
  20.7 1.8 %collective-permute-start.10 = (bf16[384,256]{1,0:T(8,128)(2,1)S(1)}, bf16[384,256]{1,0:T(8,128)(2,1)S(1)}, u32[]{:S(2)}, u32[]{:S(2)}) collective-permute-start(bf16[384,256]{1,0:T(8,128)(2,1)S(1)} %constant_dynamic-update-slice_fusion.refs_6_), channel_id=1, source_target_pairs={{0,1},{1,0},{2,3},{3,2},{4,5},{5,4},{6,7},{7,6},{8,9},{9,8},{10,11... | collective-permute-start | bytes 589832 | tf_op jit(solution)/shard_map/ppermute | solution.py:39
  26.2 6.3 %collective-permute-start.11 = (bf16[96,256]{1,0:T(8,128)(2,1)S(1)}, bf16[96,256]{1,0:T(8,128)(2,1)S(1)}, u32[]{:S(2)}, u32[]{:S(2)}) collective-permute-start(bf16[96,256]{1,0:T(8,128)(2,1)S(1)} %get-tuple-element.24), channel_id=1, source_target_pairs={{0,12},{1,13},{2,14},{3,15},{4,8},{5,9},{6,10},{7,11},{8,4},{9,5},... | collective-permute-start | bytes 147464 | tf_op jit(solution)/shard_map/ppermute | solution.py:39
  29.2 5.1 %collective-permute-start.12 = (bf16[96,256]{1,0:T(8,128)(2,1)S(1)}, bf16[96,256]{1,0:T(8,128)(2,1)S(1)}, u32[]{:S(2)}, u32[]{:S(2)}) collective-permute-start(bf16[96,256]{1,0:T(8,128)(2,1)S(1)} %get-tuple-element.25), channel_id=1, source_target_pairs={{0,8},{1,9},{2,10},{3,11},{4,12},{5,13},{6,14},{7,15},{8,0},{9,1},... | collective-permute-start | bytes 147464 | tf_op jit(solution)/shard_map/ppermute | solution.py:39
  29.2 5.1 %collective-permute-start.13 = (bf16[96,256]{1,0:T(8,128)(2,1)S(1)}, bf16[96,256]{1,0:T(8,128)(2,1)S(1)}, u32[]{:S(2)}, u32[]{:S(2)}) collective-permute-start(bf16[96,256]{1,0:T(8,128)(2,1)S(1)} %get-tuple-element.26), channel_id=1, source_target_pairs={{0,4},{1,5},{2,6},{3,7},{4,0},{5,1},{6,2},{7,3},{8,12},{9,13},{10,... | collective-permute-start | bytes 147464 | tf_op jit(solution)/shard_map/ppermute | solution.py:39
  34.8 5.8 %collective-permute-start.16 = (bf16[1,80,256]{2,1,0:T(8,128)(2,1)S(1)}, bf16[1,80,256]{2,1,0:T(8,128)(2,1)S(1)}, u32[]{:S(2)}, u32[]{:S(2)}) collective-permute-start(bf16[1,80,256]{2,1,0:T(8,128)(2,1)S(1)} %bitcast.6), channel_id=1, source_target_pairs={{0,12},{1,13},{2,14},{3,15},{4,8},{5,9},{6,10},{7,11},{8,4},{9,5},... | collective-permute-start | bytes 122888 | tf_op jit(solution)/shard_map/ppermute | solution.py:39
  37.1 5.6 %collective-permute-start.15 = (bf16[1,80,256]{2,1,0:T(8,128)(2,1)S(1)}, bf16[1,80,256]{2,1,0:T(8,128)(2,1)S(1)}, u32[]{:S(2)}, u32[]{:S(2)}) collective-permute-start(bf16[1,80,256]{2,1,0:T(8,128)(2,1)S(1)} %bitcast.7), channel_id=1, source_target_pairs={{0,8},{1,9},{2,10},{3,11},{4,12},{5,13},{6,14},{7,15},{8,0},{9,1},... | collective-permute-start | bytes 122888 | tf_op jit(solution)/shard_map/ppermute | solution.py:39
  37.1 5.6 %collective-permute-start.14 = (bf16[1,80,256]{2,1,0:T(8,128)(2,1)S(1)}, bf16[1,80,256]{2,1,0:T(8,128)(2,1)S(1)}, u32[]{:S(2)}, u32[]{:S(2)}) collective-permute-start(bf16[1,80,256]{2,1,0:T(8,128)(2,1)S(1)} %bitcast.8), channel_id=1, source_target_pairs={{0,4},{1,5},{2,6},{3,7},{4,0},{5,1},{6,2},{7,3},{8,12},{9,13},{10,... | collective-permute-start | bytes 122888 | tf_op jit(solution)/shard_map/ppermute | solution.py:39
  40.6 6.6 %collective-permute-start.18 = (bf16[2,80,256]{2,1,0:T(8,128)(2,1)S(1)}, bf16[2,80,256]{2,1,0:T(8,128)(2,1)S(1)}, u32[]{:S(2)}, u32[]{:S(2)}) collective-permute-start(bf16[2,80,256]{2,1,0:T(8,128)(2,1)S(1)} %pad_maximum_fusion.2), channel_id=1, source_target_pairs={{0,2},{1,3},{2,0},{3,1},{4,6},{5,7},{6,4},{7,5},{8,10},{9,11},{10,... | collective-permute-start | bytes 245768 | tf_op jit(solution)/shard_map/ppermute | solution.py:39
  42.7 4.5 %collective-permute-start.17 = (bf16[2,80,256]{2,1,0:T(8,128)(2,1)S(1)}, bf16[2,80,256]{2,1,0:T(8,128)(2,1)S(1)}, u32[]{:S(2)}, u32[]{:S(2)}) collective-permute-start(bf16[2,80,256]{2,1,0:T(8,128)(2,1)S(1)} %pad_maximum_fusion.1), channel_id=1, source_target_pairs={{0,2},{1,3},{2,0},{3,1},{4,6},{5,7},{6,4},{7,5},{8,10},{9,11},{10,... | collective-permute-start | bytes 245768 | tf_op jit(solution)/shard_map/ppermute | solution.py:39
  47.3 1.7 %collective-permute-start.19 = (bf16[8,80,256]{2,1,0:T(8,128)(2,1)S(1)}, bf16[8,80,256]{2,1,0:T(8,128)(2,1)S(1)}, u32[]{:S(2)}, u32[]{:S(2)}) collective-permute-start(bf16[8,80,256]{2,1,0:T(8,128)(2,1)S(1)} %constant_dynamic-update-slice_fusion.3.part_ref), channel_id=1, source_target_pairs={{0,1},{1,0},{2,3},{3,2},{4,5},{5,4},{6,7},{7,6},{8,9},{9,8},{10,11... | collective-permute-start | bytes 983048 | tf_op jit(solution)/shard_map/ppermute | solution.py:39

commit v16 on v15

--- a/solution.py
+++ b/solution.py
@@ -81,13 +81,13 @@
         pltpu.make_async_copy(source, target, sems.at[k])
         for k, (source, target) in enumerate(
             (
-                (ids_hbm, ids),
-                (pos_hbm, pos),
-                (lat_hbm, lat),
                 (hf_hbm, hf),
                 (wf_hbm, wf),
                 (ht_hbm, ht),
                 (wt_hbm, wt),
+                (lat_hbm, lat),
+                (ids_hbm, ids),
+                (pos_hbm, pos),
                 (hb_hbm, head_ref),
                 (wb_hbm, wb_ref),
             )
@@ -95,7 +95,22 @@
     ]
     for move in moves:
         move.start()
-    for move in moves[:3]:
+    def piece(slot):
+        other = me_ref[0] ^ GROUP[slot]
+        quarter = (other & 1) * 2 + ((other >> 1) & 1)
+        return hf[:, pl.ds(pl.multiple_of(quarter * width, width), width)]
+
+    moves[0].wait()
+    cut_ref[...] = piece(0)
+    far_ref[:rows, :] = piece(1)
+    near_ref[:rows, :] = piece(2)
+    far_ref[rows : 2 * rows, :] = piece(3)
+    moves[1].wait()
+    feat = dot(hf[...], wf[...])
+    moves[2].wait()
+    moves[3].wait()
+    feat_t = dot(ht[...], wt[...])
+    for move in moves[4:7]:
         move.wait()
     who = columns_of(ids[...].astype(F32), rows)
     lanes = lax.broadcasted_iota(jnp.int32, (rows, rows), 1).astype(F32)
@@ -110,21 +125,8 @@
     coded = jnp.where(line == 0, high, jnp.where(line == 1, low, 0.0)).astype(BF)
     coded = jnp.concatenate([coded] + [jnp.zeros((PAD, width - rows), BF)] * (width > rows), axis=1)
 
-    def piece(slot):
-        other = me_ref[0] ^ GROUP[slot]
-        quarter = (other & 1) * 2 + ((other >> 1) & 1)
-        return hf[:, pl.ds(pl.multiple_of(quarter * width, width), width)]
-
-    moves[3].wait()
-    cut_ref[...] = piece(0)
-    far_ref[:rows, :] = piece(1)
-    near_ref[:rows, :] = piece(2)
-    far_ref[rows : 2 * rows, :] = piece(3)
-    moves[4].wait()
-    feat = (dot(hf[...], wf[...]) + zrows).astype(BF)
-    moves[5].wait()
-    moves[6].wait()
-    feat_t = (dot(ht[...], wt[...]) + zrows).astype(BF)
+    feat = (feat + zrows).astype(BF)
+    feat_t = (feat_t + zrows).astype(BF)
     moves[7].wait()
     head = head_ref[...]
     for ref, at in ((far_ref, HEAD_AT[1]), (near_ref, HEAD_AT[2])):

time: 50 us -> 50.1 us (level)
  no operation moved by 1% of the time
where the time goes in v16:
time: 50.1 us; the launch traced here: 49.9 us
  starting transfers between devices  22.4 us (45%)
  waiting for transfers between devices  17.9 us (36%)
  Pallas kernels  8.71 us (17%)
  between operations  0.81 us (2%)
    ppermute x20, starting transfers between devices, swap(): return lax.ppermute(array, 'fa', [(i, i ^ mask) for i in range(size)])  22.4 us
    ppermute x20, waiting for transfers between devices, swap(): return lax.ppermute(array, 'fa', [(i, i ^ mask) for i in range(size)])  17.9 us
    pallas_call x1, Pallas kernels, body(): pl.pallas_call(functools.partial(pair_kernel, rows=rows, total=total), in...  3.57 us
    pallas_call x1, Pallas kernels, body(): pl.pallas_call(feature_kernel, in_specs=[SMEM] + [HBM] * 9, out_specs=[VM...  2.82 us
    pallas_call x2, Pallas kernels, assemble(): pl.pallas_call(functools.partial(assemble_kernel, offset=offset, wf_rows=...  1.79 us
  transfers between devices with their start and end apart: 20, of which 9 were waited for; matrix products, arithmetic and copies ran while one was open for 0% of the time, Pallas kernels for 2%

profile of v16, /device:TPU:0, one launch (start us, length us, event | category | flops | bytes accessed | tf_op | source)
XLA Modules:
  0.0 49.9 jit_solution(11008331138872355335)
XLA Ops:
  0.6 2.8 %shard_map.112 = (bf16[656,256]{1,0:T(8,128)(2,1)}, bf16[528,256]{1,0:T(8,128)(2,1)}, bf16[128,256]{1,0:T(8,128)(2,1)}, bf16[128,256]{1,0:T(8,128)(2,1)}, bf16[256,256]{1,0:T(8,128)(2,1)}) custom-call(s32[1]{0:T(128)} %bitcast.me_ref.refs_0_, bf16[128,1024]{1,0:T(8,128)(2,1)} %hf_hbm.1, bf16[128,1024]{1,0:T(8,128)(2,1)} %ht_hbm.1, bf16[128,256]{1,0:T(8,128)(2,1)} %hb_hbm.1, ...), custom_call_target="tpu_custom_call" | custom-call | flops 134217728 | bytes 1572864 | tf_op jit(solution)/shard_map/pallas_call | solution.py:361
  3.5 3.0 %collective-permute-start = (bf16[656,256]{1,0:T(8,128)(2,1)}, bf16[656,256]{1,0:T(8,128)(2,1)S(1)}, u32[]{:S(2)}, u32[]{:S(2)}) collective-permute-start(bf16[656,256]{1,0:T(8,128)(2,1)} %get-tuple-element.19), channel_id=1, source_target_pairs={{0,2},{1,3},{2,0},{3,1},{4,6},{5,7},{6,4},{7,5},{8,10},{9,11},{10,... | collective-permute-start | bytes 1007624 | tf_op jit(solution)/shard_map/ppermute | solution.py:39
  6.5 3.6 %collective-permute-start.5 = (bf16[128,256]{1,0:T(8,128)(2,1)}, bf16[128,256]{1,0:T(8,128)(2,1)S(1)}, u32[]{:S(2)}, u32[]{:S(2)}) collective-permute-start(bf16[128,256]{1,0:T(8,128)(2,1)} %get-tuple-element.20), channel_id=1, source_target_pairs={{0,12},{1,13},{2,14},{3,15},{4,8},{5,9},{6,10},{7,11},{8,4},{9,5},... | collective-permute-start | bytes 196616 | tf_op jit(solution)/shard_map/ppermute | solution.py:39
  10.1 0.0 collective-permute-start.4
  10.1 0.8 %collective-permute-start.3 = (bf16[128,256]{1,0:T(8,128)(2,1)}, bf16[128,256]{1,0:T(8,128)(2,1)S(1)}, u32[]{:S(2)}, u32[]{:S(2)}) collective-permute-start(bf16[128,256]{1,0:T(8,128)(2,1)} %get-tuple-element.20), channel_id=1, source_target_pairs={{0,4},{1,5},{2,6},{3,7},{4,0},{5,1},{6,2},{7,3},{8,12},{9,13},{10,... | collective-permute-start | bytes 196616 | tf_op jit(solution)/shard_map/ppermute | solution.py:39
  10.9 0.0 collective-permute-start.1
  10.9 2.7 %collective-permute-done.5 = bf16[128,256]{1,0:T(8,128)(2,1)S(1)} collective-permute-done((bf16[128,256]{1,0:T(8,128)(2,1)}, bf16[128,256]{1,0:T(8,128)(2,1)S(1)}, u32[]{:S(2)}, u32[]{:S(2)}) %collective-permute-start.5) | collective-permute-done | bytes 65568 | tf_op jit(solution)/shard_map/ppermute | solution.py:39
  13.6 0.0 collective-permute-start.8
  13.6 2.1 %collective-permute-done.4 = bf16[128,256]{1,0:T(8,128)(2,1)S(1)} collective-permute-done((bf16[128,256]{1,0:T(8,128)(2,1)}, bf16[128,256]{1,0:T(8,128)(2,1)S(1)}, u32[]{:S(2)}, u32[]{:S(2)}) %collective-permute-start.4) | collective-permute-done | bytes 65568 | tf_op jit(solution)/shard_map/ppermute | solution.py:39
  15.7 0.5 collective-permute-start.7
  16.2 0.0 collective-permute-done.3.refs_0_
  16.2 0.0 collective-permute-done.refs_1_.refs_2_
  16.2 1.6 %collective-permute-start.6 = (bf16[128,256]{1,0:T(8,128)(2,1)S(1)}, bf16[128,256]{1,0:T(8,128)(2,1)S(1)}, u32[]{:S(2)}, u32[]{:S(2)}) collective-permute-start(bf16[128,256]{1,0:T(8,128)(2,1)S(1)} %shard_map.113), channel_id=1, source_target_pairs={{0,2},{1,3},{2,0},{3,1},{4,6},{5,7},{6,4},{7,5},{8,10},{9,11},{10,... | collective-permute-start | bytes 196616 | tf_op jit(solution)/shard_map/ppermute | solution.py:39
  17.8 0.0 copy-start.1
  17.8 0.0 copy-start
  17.8 0.1 collective-permute-start.9
  17.9 2.8 %collective-permute-done.6 = bf16[128,256]{1,0:T(8,128)(2,1)S(1)} collective-permute-done((bf16[128,256]{1,0:T(8,128)(2,1)S(1)}, bf16[128,256]{1,0:T(8,128)(2,1)S(1)}, u32[]{:S(2)}, u32[]{:S(2)}) %collective-permute-start.6) | collective-permute-done | bytes 65568 | tf_op jit(solution)/shard_map/ppermute | solution.py:39
  20.7 0.0 collective-permute-start.2
  20.7 0.0 collective-permute-done.7
  20.7 0.0 copy-start.2
  20.7 0.0 collective-permute-done.8
  20.7 0.6 %collective-permute-start.10 = (bf16[384,256]{1,0:T(8,128)(2,1)S(1)}, bf16[384,256]{1,0:T(8,128)(2,1)S(1)}, u32[]{:S(2)}, u32[]{:S(2)}) collective-permute-start(bf16[384,256]{1,0:T(8,128)(2,1)S(1)} %constant_dynamic-update-slice_fusion.refs_6_), channel_id=1, source_target_pairs={{0,1},{1,0},{2,3},{3,2},{4,5},{5,4},{6,7},{7,6},{8,9},{9,8},{10,11... | collective-permute-start | bytes 589832 | tf_op jit(solution)/shard_map/ppermute | solution.py:39
  21.3 0.0 collective-permute-done.1.refs_3_
  21.3 0.0 collective-permute-done.9.refs_7_
  21.3 1.3 %collective-permute-done.10.refs_8_ = bf16[384,256]{1,0:T(8,128)(2,1)S(1)} collective-permute-done((bf16[384,256]{1,0:T(8,128)(2,1)S(1)}, bf16[384,256]{1,0:T(8,128)(2,1)S(1)}, u32[]{:S(2)}, u32[]{:S(2)}) %collective-permute-start.10) | collective-permute-done | bytes 196640 | tf_op jit(solution)/shard_map/ppermute | solution.py:39
  22.6 0.0 collective-permute-done.2.refs_4_
  22.6 0.0 copy-done.1
  22.6 0.0 copy-done
  22.6 0.0 copy-done.2
  22.6 3.6 %shard_map.114 = (f32[96,256]{1,0:T(8,128)S(1)}, bf16[96,256]{1,0:T(8,128)(2,1)S(1)}, bf16[96,256]{1,0:T(8,128)(2,1)S(1)}, bf16[96,256]{1,0:T(8,128)(2,1)S(1)}) custom-call(s32[1]{0:T(128)} %bitcast.me_ref.refs_0_, bf16[528,256]{1,0:T(8,128)(2,1)S(1)} %copy-done, bf16[656,256]{1,0:T(8,128)(2,1)S(1)} %collective-permute-done.refs_1_.refs_2_, ...), custom_call_target="tpu_custom_call" | custom-call | tf_op jit(solution)/shard_map/pallas_call | solution.py:415
  26.2 3.0 %collective-permute-start.11 = (bf16[96,256]{1,0:T(8,128)(2,1)S(1)}, bf16[96,256]{1,0:T(8,128)(2,1)S(1)}, u32[]{:S(2)}, u32[]{:S(2)}) collective-permute-start(bf16[96,256]{1,0:T(8,128)(2,1)S(1)} %get-tuple-element.24), channel_id=1, source_target_pairs={{0,12},{1,13},{2,14},{3,15},{4,8},{5,9},{6,10},{7,11},{8,4},{9,5},... | collective-permute-start | bytes 147464 | tf_op jit(solution)/shard_map/ppermute | solution.py:39
  29.2 0.0 collective-permute-start.12
  29.2 1.4 %collective-permute-start.13 = (bf16[96,256]{1,0:T(8,128)(2,1)S(1)}, bf16[96,256]{1,0:T(8,128)(2,1)S(1)}, u32[]{:S(2)}, u32[]{:S(2)}) collective-permute-start(bf16[96,256]{1,0:T(8,128)(2,1)S(1)} %get-tuple-element.26), channel_id=1, source_target_pairs={{0,4},{1,5},{2,6},{3,7},{4,0},{5,1},{6,2},{7,3},{8,12},{9,13},{10,... | collective-permute-start | bytes 147464 | tf_op jit(solution)/shard_map/ppermute | solution.py:39
  30.6 1.9 %collective-permute-done.11.refs_0_ = bf16[96,256]{1,0:T(8,128)(2,1)S(1)} collective-permute-done((bf16[96,256]{1,0:T(8,128)(2,1)S(1)}, bf16[96,256]{1,0:T(8,128)(2,1)S(1)}, u32[]{:S(2)}, u32[]{:S(2)}) %collective-permute-start.11) | collective-permute-done | bytes 49184 | tf_op jit(solution)/shard_map/ppermute | solution.py:39
  32.5 1.8 %collective-permute-done.12.refs_1_ = bf16[96,256]{1,0:T(8,128)(2,1)S(1)} collective-permute-done((bf16[96,256]{1,0:T(8,128)(2,1)S(1)}, bf16[96,256]{1,0:T(8,128)(2,1)S(1)}, u32[]{:S(2)}, u32[]{:S(2)}) %collective-permute-start.12) | collective-permute-done | bytes 49184 | tf_op jit(solution)/shard_map/ppermute | solution.py:39
  34.2 0.0 collective-permute-done.13.refs_2_
  34.2 0.5 %shard_map.115 = (bf16[80,256]{1,0:T(8,128)(2,1)S(1)}, f32[1,1]{1,0:T(1,128)}) custom-call(f32[96,256]{1,0:T(8,128)S(1)} %get-tuple-element.23.keep_ref, bf16[96,256]{1,0:T(8,128)(2,1)S(1)} %collective-permute-done.11.refs_0_, bf16[96,256]{1,0:T(8,128)(2,1)S(1)} %collective-permute-done.12.refs_1_, bf16[96,256]{1,0:T(8,128)(2,1)S(1)} %collective-permute-done.13.refs_2_), custom_call_target="tpu_custom_call" | custom-call | tf_op jit(solution)/shard_map/pallas_call | solution.py:436
  34.8 2.4 %collective-permute-start.16 = (bf16[1,80,256]{2,1,0:T(8,128)(2,1)S(1)}, bf16[1,80,256]{2,1,0:T(8,128)(2,1)S(1)}, u32[]{:S(2)}, u32[]{:S(2)}) collective-permute-start(bf16[1,80,256]{2,1,0:T(8,128)(2,1)S(1)} %bitcast.6), channel_id=1, source_target_pairs={{0,12},{1,13},{2,14},{3,15},{4,8},{5,9},{6,10},{7,11},{8,4},{9,5},... | collective-permute-start | bytes 122888 | tf_op jit(solution)/shard_map/ppermute | solution.py:39
  37.1 0.0 collective-permute-start.15
  37.1 2.0 %collective-permute-start.14 = (bf16[1,80,256]{2,1,0:T(8,128)(2,1)S(1)}, bf16[1,80,256]{2,1,0:T(8,128)(2,1)S(1)}, u32[]{:S(2)}, u32[]{:S(2)}) collective-permute-start(bf16[1,80,256]{2,1,0:T(8,128)(2,1)S(1)} %bitcast.8), channel_id=1, source_target_pairs={{0,4},{1,5},{2,6},{3,7},{4,0},{5,1},{6,2},{7,3},{8,12},{9,13},{10,... | collective-permute-start | bytes 122888 | tf_op jit(solution)/shard_map/ppermute | solution.py:39
  39.2 1.4 %collective-permute-done.16 = bf16[1,80,256]{2,1,0:T(8,128)(2,1)S(1)} collective-permute-done((bf16[1,80,256]{2,1,0:T(8,128)(2,1)S(1)}, bf16[1,80,256]{2,1,0:T(8,128)(2,1)S(1)}, u32[]{:S(2)}, u32[]{:S(2)}) %collective-permute-start.16) | collective-permute-done | bytes 40992 | tf_op jit(solution)/shard_map/ppermute | solution.py:39
  40.6 2.2 %collective-permute-start.18 = (bf16[2,80,256]{2,1,0:T(8,128)(2,1)S(1)}, bf16[2,80,256]{2,1,0:T(8,128)(2,1)S(1)}, u32[]{:S(2)}, u32[]{:S(2)}) collective-permute-start(bf16[2,80,256]{2,1,0:T(8,128)(2,1)S(1)} %pad_maximum_fusion.2), channel_id=1, source_target_pairs={{0,2},{1,3},{2,0},{3,1},{4,6},{5,7},{6,4},{7,5},{8,10},{9,11},{10,... | collective-permute-start | bytes 245768 | tf_op jit(solution)/shard_map/ppermute | solution.py:39
  42.8 0.0 collective-permute-done.15
  42.8 0.0 collective-permute-done.14
  42.8 1.1 %collective-permute-start.17 = (bf16[2,80,256]{2,1,0:T(8,128)(2,1)S(1)}, bf16[2,80,256]{2,1,0:T(8,128)(2,1)S(1)}, u32[]{:S(2)}, u32[]{:S(2)}) collective-permute-start(bf16[2,80,256]{2,1,0:T(8,128)(2,1)S(1)} %pad_maximum_fusion.1), channel_id=1, source_target_pairs={{0,2},{1,3},{2,0},{3,1},{4,6},{5,7},{6,4},{7,5},{8,10},{9,11},{10,... | collective-permute-start | bytes 245768 | tf_op jit(solution)/shard_map/ppermute | solution.py:39
  43.9 3.3 %collective-permute-done.17 = bf16[2,80,256]{2,1,0:T(8,128)(2,1)S(1)} collective-permute-done((bf16[2,80,256]{2,1,0:T(8,128)(2,1)S(1)}, bf16[2,80,256]{2,1,0:T(8,128)(2,1)S(1)}, u32[]{:S(2)}, u32[]{:S(2)}) %collective-permute-start.17) | collective-permute-done | bytes 81952 | tf_op jit(solution)/shard_map/ppermute | solution.py:39
  47.3 0.0 collective-permute-done.18
  47.3 0.1 collective-permute-start.19
  47.4 0.9 %shard_map.116 = (f32[1024,256]{1,0:T(8,128)}, f32[256,256]{1,0:T(8,128)}) custom-call(s32[1]{0:T(128)} %bitcast.me_ref.refs_0_, bf16[8,80,256]{2,1,0:T(8,128)(2,1)S(1)} %constant_dynamic-update-slice_fusion.3.part_ref), custom_call_target="tpu_custom_call" | custom-call | tf_op jit(solution)/shard_map/pallas_call | solution.py:456
  48.3 0.7 %collective-permute-done.19.part_ref = bf16[8,80,256]{2,1,0:T(8,128)(2,1)S(1)} collective-permute-done((bf16[8,80,256]{2,1,0:T(8,128)(2,1)S(1)}, bf16[8,80,256]{2,1,0:T(8,128)(2,1)S(1)}, u32[]{:S(2)}, u32[]{:S(2)}) %collective-permute-start.19) | collective-permute-done | bytes 327712 | tf_op jit(solution)/shard_map/ppermute | solution.py:39
  49.0 0.9 %shard_map.117 = (f32[1024,256]{1,0:T(8,128)}, f32[256,256]{1,0:T(8,128)}) custom-call(s32[1]{0:T(128)} %bitcast.me_ref.refs_0_, bf16[8,80,256]{2,1,0:T(8,128)(2,1)S(1)} %collective-permute-done.19.part_ref, f32[1024,256]{1,0:T(8,128)} %get-tuple-element.28.refs_0_, f32[256,256]{1,0:T(8,128)} %get-tuple-element.29.refs_1_), custom_call_target="tpu_custom_call", output_to_operand_aliasing={{0}: (2, {}), {1}: (3, {})} | custom-call | tf_op jit(solution)/shard_map/pallas_call | solution.py:456
  (13 shorter events, 0.1 us)
Async XLA Ops:
  3.5 12.7 %collective-permute-start = (bf16[656,256]{1,0:T(8,128)(2,1)}, bf16[656,256]{1,0:T(8,128)(2,1)S(1)}, u32[]{:S(2)}, u32[]{:S(2)}) collective-permute-start(bf16[656,256]{1,0:T(8,128)(2,1)} %get-tuple-element.19), channel_id=1, source_target_pairs={{0,2},{1,3},{2,0},{3,1},{4,6},{5,7},{6,4},{7,5},{8,10},{9,11},{10,... | collective-permute-start | bytes 1007624 | tf_op jit(solution)/shard_map/ppermute | solution.py:39
  6.5 7.1 %collective-permute-start.5 = (bf16[128,256]{1,0:T(8,128)(2,1)}, bf16[128,256]{1,0:T(8,128)(2,1)S(1)}, u32[]{:S(2)}, u32[]{:S(2)}) collective-permute-start(bf16[128,256]{1,0:T(8,128)(2,1)} %get-tuple-element.20), channel_id=1, source_target_pairs={{0,12},{1,13},{2,14},{3,15},{4,8},{5,9},{6,10},{7,11},{8,4},{9,5},... | collective-permute-start | bytes 196616 | tf_op jit(solution)/shard_map/ppermute | solution.py:39
  10.1 5.6 %collective-permute-start.4 = (bf16[128,256]{1,0:T(8,128)(2,1)}, bf16[128,256]{1,0:T(8,128)(2,1)S(1)}, u32[]{:S(2)}, u32[]{:S(2)}) collective-permute-start(bf16[128,256]{1,0:T(8,128)(2,1)} %get-tuple-element.20), channel_id=1, source_target_pairs={{0,8},{1,9},{2,10},{3,11},{4,12},{5,13},{6,14},{7,15},{8,0},{9,1},... | collective-permute-start | bytes 196616 | tf_op jit(solution)/shard_map/ppermute | solution.py:39
  10.1 6.1 %collective-permute-start.3 = (bf16[128,256]{1,0:T(8,128)(2,1)}, bf16[128,256]{1,0:T(8,128)(2,1)S(1)}, u32[]{:S(2)}, u32[]{:S(2)}) collective-permute-start(bf16[128,256]{1,0:T(8,128)(2,1)} %get-tuple-element.20), channel_id=1, source_target_pairs={{0,4},{1,5},{2,6},{3,7},{4,0},{5,1},{6,2},{7,3},{8,12},{9,13},{10,... | collective-permute-start | bytes 196616 | tf_op jit(solution)/shard_map/ppermute | solution.py:39
  10.9 10.4 %collective-permute-start.1 = (bf16[528,256]{1,0:T(8,128)(2,1)}, bf16[528,256]{1,0:T(8,128)(2,1)S(1)}, u32[]{:S(2)}, u32[]{:S(2)}) collective-permute-start(bf16[528,256]{1,0:T(8,128)(2,1)} %get-tuple-element.18.refs_1_), channel_id=1, source_target_pairs={{0,1},{1,0},{2,3},{3,2},{4,5},{5,4},{6,7},{7,6},{8,9},{9,8},{10,11... | collective-permute-start | bytes 811016 | tf_op jit(solution)/shard_map/ppermute | solution.py:39
  13.6 7.1 %collective-permute-start.8 = (bf16[128,256]{1,0:T(8,128)(2,1)S(1)}, bf16[128,256]{1,0:T(8,128)(2,1)S(1)}, u32[]{:S(2)}, u32[]{:S(2)}) collective-permute-start(bf16[128,256]{1,0:T(8,128)(2,1)S(1)} %collective-permute-done.5), channel_id=1, source_target_pairs={{0,2},{1,3},{2,0},{3,1},{4,6},{5,7},{6,4},{7,5},{8,10},{9,11},{10,... | collective-permute-start | bytes 196616 | tf_op jit(solution)/shard_map/ppermute | solution.py:39
  15.7 5.0 %collective-permute-start.7 = (bf16[128,256]{1,0:T(8,128)(2,1)S(1)}, bf16[128,256]{1,0:T(8,128)(2,1)S(1)}, u32[]{:S(2)}, u32[]{:S(2)}) collective-permute-start(bf16[128,256]{1,0:T(8,128)(2,1)S(1)} %collective-permute-done.4), channel_id=1, source_target_pairs={{0,2},{1,3},{2,0},{3,1},{4,6},{5,7},{6,4},{7,5},{8,10},{9,11},{10,... | collective-permute-start | bytes 196616 | tf_op jit(solution)/shard_map/ppermute | solution.py:39
  16.2 4.5 %collective-permute-start.6 = (bf16[128,256]{1,0:T(8,128)(2,1)S(1)}, bf16[128,256]{1,0:T(8,128)(2,1)S(1)}, u32[]{:S(2)}, u32[]{:S(2)}) collective-permute-start(bf16[128,256]{1,0:T(8,128)(2,1)S(1)} %shard_map.113), channel_id=1, source_target_pairs={{0,2},{1,3},{2,0},{3,1},{4,6},{5,7},{6,4},{7,5},{8,10},{9,11},{10,... | collective-permute-start | bytes 196616 | tf_op jit(solution)/shard_map/ppermute | solution.py:39
  17.8 4.8 %copy-start.1 = (bf16[256,256]{1,0:T(8,128)(2,1)S(1)}, bf16[256,256]{1,0:T(8,128)(2,1)}, u32[]{:S(2)}) copy-start(bf16[256,256]{1,0:T(8,128)(2,1)} %get-tuple-element.22.refs_10_) | copy-start | bytes 393220
  17.8 4.8 %copy-start = (bf16[528,256]{1,0:T(8,128)(2,1)S(1)}, bf16[528,256]{1,0:T(8,128)(2,1)}, u32[]{:S(2)}) copy-start(bf16[528,256]{1,0:T(8,128)(2,1)} %get-tuple-element.18.refs_1_) | copy-start | bytes 811012
  17.8 3.5 %collective-permute-start.9 = (bf16[384,256]{1,0:T(8,128)(2,1)S(1)}, bf16[384,256]{1,0:T(8,128)(2,1)S(1)}, u32[]{:S(2)}, u32[]{:S(2)}) collective-permute-start(bf16[384,256]{1,0:T(8,128)(2,1)S(1)} %pad_maximum_fusion.refs_5_), channel_id=1, source_target_pairs={{0,1},{1,0},{2,3},{3,2},{4,5},{5,4},{6,7},{7,6},{8,9},{9,8},{10,11... | collective-permute-start | bytes 589832 | tf_op jit(solution)/shard_map/ppermute | solution.py:39
  20.7 1.9 %collective-permute-start.2 = (bf16[656,256]{1,0:T(8,128)(2,1)S(1)}, bf16[656,256]{1,0:T(8,128)(2,1)S(1)}, u32[]{:S(2)}, u32[]{:S(2)}) collective-permute-start(bf16[656,256]{1,0:T(8,128)(2,1)S(1)} %collective-permute-done.refs_1_.refs_2_), channel_id=1, source_target_pairs={{0,1},{1,0},{2,3},{3,2},{4,5},{5,4},{6,7},{7,6},{8,9},{9,8},{10,11... | collective-permute-start | bytes 1007624 | tf_op jit(solution)/shard_map/ppermute | solution.py:39
  20.7 1.9 %copy-start.2 = (bf16[128,256]{1,0:T(8,128)(2,1)S(1)}, bf16[128,256]{1,0:T(8,128)(2,1)}, u32[]{:S(2)}) copy-start(bf16[128,256]{1,0:T(8,128)(2,1)} %get-tuple-element.21.refs_9_) | copy-start | bytes 196612
  20.7 1.8 %collective-permute-start.10 = (bf16[384,256]{1,0:T(8,128)(2,1)S(1)}, bf16[384,256]{1,0:T(8,128)(2,1)S(1)}, u32[]{:S(2)}, u32[]{:S(2)}) collective-permute-start(bf16[384,256]{1,0:T(8,128)(2,1)S(1)} %constant_dynamic-update-slice_fusion.refs_6_), channel_id=1, source_target_pairs={{0,1},{1,0},{2,3},{3,2},{4,5},{5,4},{6,7},{7,6},{8,9},{9,8},{10,11... | collective-permute-start | bytes 589832 | tf_op jit(solution)/shard_map/ppermute | solution.py:39
  26.2 6.3 %collective-permute-start.11 = (bf16[96,256]{1,0:T(8,128)(2,1)S(1)}, bf16[96,256]{1,0:T(8,128)(2,1)S(1)}, u32[]{:S(2)}, u32[]{:S(2)}) collective-permute-start(bf16[96,256]{1,0:T(8,128)(2,1)S(1)} %get-tuple-element.24), channel_id=1, source_target_pairs={{0,12},{1,13},{2,14},{3,15},{4,8},{5,9},{6,10},{7,11},{8,4},{9,5},... | collective-permute-start | bytes 147464 | tf_op jit(solution)/shard_map/ppermute | solution.py:39
  29.2 5.1 %collective-permute-start.12 = (bf16[96,256]{1,0:T(8,128)(2,1)S(1)}, bf16[96,256]{1,0:T(8,128)(2,1)S(1)}, u32[]{:S(2)}, u32[]{:S(2)}) collective-permute-start(bf16[96,256]{1,0:T(8,128)(2,1)S(1)} %get-tuple-element.25), channel_id=1, source_target_pairs={{0,8},{1,9},{2,10},{3,11},{4,12},{5,13},{6,14},{7,15},{8,0},{9,1},... | collective-permute-start | bytes 147464 | tf_op jit(solution)/shard_map/ppermute | solution.py:39
  29.2 5.1 %collective-permute-start.13 = (bf16[96,256]{1,0:T(8,128)(2,1)S(1)}, bf16[96,256]{1,0:T(8,128)(2,1)S(1)}, u32[]{:S(2)}, u32[]{:S(2)}) collective-permute-start(bf16[96,256]{1,0:T(8,128)(2,1)S(1)} %get-tuple-element.26), channel_id=1, source_target_pairs={{0,4},{1,5},{2,6},{3,7},{4,0},{5,1},{6,2},{7,3},{8,12},{9,13},{10,... | collective-permute-start | bytes 147464 | tf_op jit(solution)/shard_map/ppermute | solution.py:39
  34.8 5.8 %collective-permute-start.16 = (bf16[1,80,256]{2,1,0:T(8,128)(2,1)S(1)}, bf16[1,80,256]{2,1,0:T(8,128)(2,1)S(1)}, u32[]{:S(2)}, u32[]{:S(2)}) collective-permute-start(bf16[1,80,256]{2,1,0:T(8,128)(2,1)S(1)} %bitcast.6), channel_id=1, source_target_pairs={{0,12},{1,13},{2,14},{3,15},{4,8},{5,9},{6,10},{7,11},{8,4},{9,5},... | collective-permute-start | bytes 122888 | tf_op jit(solution)/shard_map/ppermute | solution.py:39
  37.1 5.6 %collective-permute-start.15 = (bf16[1,80,256]{2,1,0:T(8,128)(2,1)S(1)}, bf16[1,80,256]{2,1,0:T(8,128)(2,1)S(1)}, u32[]{:S(2)}, u32[]{:S(2)}) collective-permute-start(bf16[1,80,256]{2,1,0:T(8,128)(2,1)S(1)} %bitcast.7), channel_id=1, source_target_pairs={{0,8},{1,9},{2,10},{3,11},{4,12},{5,13},{6,14},{7,15},{8,0},{9,1},... | collective-permute-start | bytes 122888 | tf_op jit(solution)/shard_map/ppermute | solution.py:39
  37.1 5.6 %collective-permute-start.14 = (bf16[1,80,256]{2,1,0:T(8,128)(2,1)S(1)}, bf16[1,80,256]{2,1,0:T(8,128)(2,1)S(1)}, u32[]{:S(2)}, u32[]{:S(2)}) collective-permute-start(bf16[1,80,256]{2,1,0:T(8,128)(2,1)S(1)} %bitcast.8), channel_id=1, source_target_pairs={{0,4},{1,5},{2,6},{3,7},{4,0},{5,1},{6,2},{7,3},{8,12},{9,13},{10,... | collective-permute-start | bytes 122888 | tf_op jit(solution)/shard_map/ppermute | solution.py:39
  40.6 6.7 %collective-permute-start.18 = (bf16[2,80,256]{2,1,0:T(8,128)(2,1)S(1)}, bf16[2,80,256]{2,1,0:T(8,128)(2,1)S(1)}, u32[]{:S(2)}, u32[]{:S(2)}) collective-permute-start(bf16[2,80,256]{2,1,0:T(8,128)(2,1)S(1)} %pad_maximum_fusion.2), channel_id=1, source_target_pairs={{0,2},{1,3},{2,0},{3,1},{4,6},{5,7},{6,4},{7,5},{8,10},{9,11},{10,... | collective-permute-start | bytes 245768 | tf_op jit(solution)/shard_map/ppermute | solution.py:39
  42.8 4.5 %collective-permute-start.17 = (bf16[2,80,256]{2,1,0:T(8,128)(2,1)S(1)}, bf16[2,80,256]{2,1,0:T(8,128)(2,1)S(1)}, u32[]{:S(2)}, u32[]{:S(2)}) collective-permute-start(bf16[2,80,256]{2,1,0:T(8,128)(2,1)S(1)} %pad_maximum_fusion.1), channel_id=1, source_target_pairs={{0,2},{1,3},{2,0},{3,1},{4,6},{5,7},{6,4},{7,5},{8,10},{9,11},{10,... | collective-permute-start | bytes 245768 | tf_op jit(solution)/shard_map/ppermute | solution.py:39
  47.3 1.7 %collective-permute-start.19 = (bf16[8,80,256]{2,1,0:T(8,128)(2,1)S(1)}, bf16[8,80,256]{2,1,0:T(8,128)(2,1)S(1)}, u32[]{:S(2)}, u32[]{:S(2)}) collective-permute-start(bf16[8,80,256]{2,1,0:T(8,128)(2,1)S(1)} %constant_dynamic-update-slice_fusion.3.part_ref), channel_id=1, source_target_pairs={{0,1},{1,0},{2,3},{3,2},{4,5},{5,4},{6,7},{7,6},{8,9},{9,8},{10,11... | collective-permute-start | bytes 983048 | tf_op jit(solution)/shard_map/ppermute | solution.py:39
